TPU v7x, 32 devices: a whole 2x2x4 slice. The times are simulated.
32 devices in a mesh: gx: 8 (over z, y), gy: 4 (over x, core).
Axes of the slice: x: 2, y: 2, z: 4, core: 2. Of those that a mesh axis runs over, the one named last changes fastest.
Arguments:
- hamiltonian: float32 [8, 4, 5, 128, 128], P('gx', 'gy'), may hold values from -0.25 to 0.25
- inverse_margin: float32 [8, 4, 5, 128, 128], P('gx', 'gy'), may hold values from -0.25 to 0.25
- density: float32 [2, 8, 4, 5, 128, 128], P(None, 'gx', 'gy'), may hold values from -6 to 6
- cutoff: int32 [8, 4, 5], P('gx', 'gy'), may hold values 0 or 1
- derivative: float32 [3, 8, 4, 5, 128, 128], P(None, 'gx', 'gy'), may hold values from -0.046875 to 0.046875
- atom_of: int32 [8, 4, 128], P('gx', 'gy'), may hold values from 0 to 63, as said below
Outputs:
- new_density: float32 [2, 8, 4, 5, 128, 128], P(None, 'gx', 'gy')
- forces: float32 [8, 4, 3, 64], P('gx', 'gy')
Inputs may be any that keep to these rules, and one draw needn't show every extreme that they name: `atom_of`: within each group the map never falls and each of the 64 atoms owns at least one of the 128 orbitals.
All inputs are finite; a program needn't handle non-finite values. No bound on the sum of `cutoff` on one device may be relied on, other than what follows from the above.
Results may differ from a plain program's by a relative error of at most 0.0001.
Values sent between devices are 32-bit elements; how exact they have to be, the bound alone decides.
No kernel may reach another device: no remote copies, remote signals or barrier semaphores. Data moves between devices by JAX's collectives and lax.ppermute only.
A program may use at most 64 MiB of HBM per device.

v0:
```python
import jax
import jax.numpy as jnp
from jax import lax
from jax.sharding import PartitionSpec as P

ATOMS = 64


opposite = (0, 2, 1, 4, 3)
time_step = 0.25
highest = lax.Precision.HIGHEST
positions = ((2, 1), (0, 1), (1, 2), (1, 0))


def padded_2(cells, sides, width):
    for axis, dim in sides:
        count = lax.axis_size(axis)
        head = lax.slice_in_dim(cells, 0, width, axis=dim)
        tail = lax.slice_in_dim(cells, cells.shape[dim] - width, cells.shape[dim], axis=dim)
        cells = jnp.concatenate(
            [
                lax.ppermute(tail, axis, [(i, (i + 1) % count) for i in range(count)]),
                cells,
                lax.ppermute(head, axis, [((i + 1) % count, i) for i in range(count)]),
            ],
            axis=dim,
        )
    return cells


def neighbours(padded):
    zero_blocks = jnp.stack(
        [padded[..., first_at, second_at, 0, :, :] for first_at, second_at in positions], axis=-3
    )
    back_blocks = jnp.stack(
        [
            padded[..., spot[0], spot[1], opposite[place + 1], :, :]
            for place, spot in enumerate(positions)
        ],
        axis=-3,
    )
    return (zero_blocks, back_blocks)


def matmul(left, right):
    return jnp.matmul(left, right, precision=highest)


def product(left, right, zero_blocks, back_blocks, keep):
    joined = jnp.concatenate([right[..., :1, :, :], back_blocks], axis=-3)
    diagonal = jnp.sum(matmul(left, joined), axis=-3)
    others = matmul(left[..., :1, :, :], right[..., 1:, :, :]) + matmul(
        left[..., 1:, :, :], zero_blocks
    )
    result = jnp.concatenate([diagonal[..., None, :, :], others], axis=-3)
    return result * keep[:, None, None]


def density_neighbours(current):
    padded = padded_2(current[:, None, None], (("gx", 1), ("gy", 2)), 1)
    return neighbours(padded)


def local(hamiltonian, inverse_margin, density, cutoff, derivative, atom_of):
    keep = jnp.concatenate([jnp.ones((1,), jnp.float32), cutoff[0, 0, 1:].astype(jnp.float32)])
    weight = keep[:, None, None]
    ham = hamiltonian[0, 0] * weight
    inverse = inverse_margin[0, 0] * weight
    stacked = jnp.stack([ham, inverse], axis=0)[:, None, None]
    padded = padded_2(stacked, (("gx", 1), ("gy", 2)), 1)
    near_zero, near_back = neighbours(padded)
    propagator = product(inverse, ham, near_zero[0], near_back[0], keep)
    current = density[:, 0, 0] * weight[None]
    rho_zero, rho_back = density_neighbours(current)
    left_term = product(propagator, current, rho_zero, rho_back, keep)
    mixed = product(current, ham, near_zero[0], near_back[0], keep)
    right_term = product(mixed, inverse, near_zero[1], near_back[1], keep)
    commutators = left_term - right_term
    current = jnp.stack(
        [current[0] + time_step * commutators[1], current[1] - time_step * commutators[0]], axis=0
    )
    slopes = derivative[:, 0, 0] * weight[None]
    weighted = current[0][None] * slopes
    row_part = jnp.sum(weighted, axis=(1, 3))
    column_part = jnp.sum(weighted, axis=2)
    received = padded_2(column_part[None, None], (("gx", 0), ("gy", 1)), 1)
    orbital = row_part + column_part[:, 0]
    orbital = (
        orbital
        + received[0, 1, :, 1]
        + received[2, 1, :, 2]
        + received[1, 0, :, 3]
        + received[1, 2, :, 4]
    )
    members = (atom_of[0, 0][None, :] == jnp.arange(ATOMS, dtype=jnp.int32)[:, None]).astype(
        jnp.float32
    )
    forces = -jnp.einsum("cw,aw->ca", orbital, members, precision=highest)
    return (current[:, None, None], forces[None, None])


def solution(mesh):
    placed = (
        P("gx", "gy", None, None, None),
        P("gx", "gy", None, None, None),
        P(None, "gx", "gy", None, None, None),
        P("gx", "gy", None),
        P(None, "gx", "gy", None, None, None),
        P("gx", "gy", None),
    )
    return jax.shard_map(
        local,
        mesh=mesh,
        in_specs=placed,
        out_specs=(P(None, "gx", "gy", None, None, None), P("gx", "gy", None, None)),
        check_vma=False,
    )
```

profile of v0, /device:TPU:0, one launch (start us, length us, event | category | flops | bytes accessed | tf_op | source)
XLA Modules:
  0.0 155.8 jit_solution(12921965732090164313)
XLA Ops:
  0.6 0.0 copy-start
  0.6 0.8 convert_bitcast_fusion
  1.4 0.1 pad_maximum_fusion.9
  1.5 1.2 bitcast_multiply_fusion.3
  2.7 0.0 copy-start.1
  2.7 0.0 copy-start.2
  2.8 6.1 %collective-permute-start = (f32[2,1,1,5,128,128]{5,4,0,3,2,1:T(8,128)S(1)}, f32[2,1,1,5,128,128]{5,4,0,3,2,1:T(8,128)S(1)}, u32[]{:S(2)}, u32[]{:S(2)}) collective-permute-start(f32[2,1,1,5,128,128]{5,4,0,3,2,1:T(8,128)S(1)} %maximum_bitcast_fusion), channel_id=1, source_target_pairs={{4,0},{8,4},{12,8},{16,12},{20,16},{24,20},{28,24},{0,28},{5,1},{9... | collective-permute-start | bytes 1966088 | tf_op jit(solution)/shard_map/ppermute | solution.py:24
  8.8 0.0 collective-permute-start.1
  8.8 0.0 copy-done
  8.9 0.1 copy_multiply_fusion
  9.0 4.8 %collective-permute-start.4 = (f32[2,1,1,5,128,128]{5,4,0,3,2,1:T(8,128)S(1)}, f32[2,1,1,5,128,128]{5,4,0,3,2,1:T(8,128)S(1)}, u32[]{:S(2)}, u32[]{:S(2)}) collective-permute-start(f32[2,1,1,5,128,128]{5,4,0,3,2,1:T(8,128)S(1)} %copy_multiply_fusion), channel_id=1, source_target_pairs={{4,0},{8,4},{12,8},{16,12},{20,16},{24,20},{28,24},{0,28},{5,1},{9... | collective-permute-start | bytes 1966088 | tf_op jit(solution)/shard_map/ppermute | solution.py:24
  13.7 0.0 collective-permute-start.5
  13.7 0.1 bitcast_multiply_fusion.1
  13.9 0.0 copy-done.1
  13.9 0.0 copy-done.2
  13.9 0.1 bitcast_multiply_fusion.5
  14.0 35.4 %collective-permute-done = f32[2,1,1,5,128,128]{5,4,0,3,2,1:T(8,128)S(1)} collective-permute-done((f32[2,1,1,5,128,128]{5,4,0,3,2,1:T(8,128)S(1)}, f32[2,1,1,5,128,128]{5,4,0,3,2,1:T(8,128)S(1)}, u32[]{:S(2)}, u32[]{:S(2)}) %collective-permute-start) | collective-permute-done | bytes 655392 | tf_op jit(solution)/shard_map/ppermute | solution.py:24
  49.5 0.0 collective-permute-done.1
  49.5 0.2 pad_maximum_fusion
  49.7 0.1 collective-permute-start.3
  49.7 0.4 convolution_bitcast_fusion.6
  50.1 1.8 %collective-permute-start.2 = (f32[2,3,1,5,128,128]{5,4,0,3,2,1:T(8,128)S(1)}, f32[2,3,1,5,128,128]{5,4,0,3,2,1:T(8,128)S(1)}, u32[]{:S(2)}, u32[]{:S(2)}) collective-permute-start(f32[2,3,1,5,128,128]{5,4,0,3,2,1:T(8,128)S(1)} %pad_maximum_fusion), channel_id=1, source_target_pairs={{1,0},{2,1},{3,2},{0,3},{5,4},{6,5},{7,6},{4,7},{9,8},{10,9},{11,1... | collective-permute-start | bytes 5898248 | tf_op jit(solution)/shard_map/ppermute | solution.py:24
  51.9 10.8 %collective-permute-done.4 = f32[2,1,1,5,128,128]{5,4,0,3,2,1:T(8,128)S(1)} collective-permute-done((f32[2,1,1,5,128,128]{5,4,0,3,2,1:T(8,128)S(1)}, f32[2,1,1,5,128,128]{5,4,0,3,2,1:T(8,128)S(1)}, u32[]{:S(2)}, u32[]{:S(2)}) %collective-permute-start.4) | collective-permute-done | bytes 655392 | tf_op jit(solution)/shard_map/ppermute | solution.py:24
  62.7 0.2 collective-permute-done.5
  62.8 0.2 pad_maximum_fusion.1
  63.0 1.2 collective-permute-start.6
  64.2 0.0 collective-permute-start.7
  64.3 27.7 %collective-permute-done.3 = f32[2,3,1,5,128,128]{5,4,0,3,2,1:T(8,128)S(1)} collective-permute-done((f32[2,3,1,5,128,128]{5,4,0,3,2,1:T(8,128)S(1)}, f32[2,3,1,5,128,128]{5,4,0,3,2,1:T(8,128)S(1)}, u32[]{:S(2)}, u32[]{:S(2)}) %collective-permute-start.3) | collective-permute-done | bytes 1966112 | tf_op jit(solution)/shard_map/ppermute | solution.py:22
  92.0 3.0 %collective-permute-done.2 = f32[2,3,1,5,128,128]{5,4,0,3,2,1:T(8,128)S(1)} collective-permute-done((f32[2,3,1,5,128,128]{5,4,0,3,2,1:T(8,128)S(1)}, f32[2,3,1,5,128,128]{5,4,0,3,2,1:T(8,128)S(1)}, u32[]{:S(2)}, u32[]{:S(2)}) %collective-permute-start.2) | collective-permute-done | bytes 1966112 | tf_op jit(solution)/shard_map/ppermute | solution.py:24
  95.1 0.1 pad_maximum_fusion.3
  95.2 0.5 convolution_bitcast_fusion.10
  95.7 0.4 convolution_add_fusion
  96.1 40.4 %collective-permute-done.6 = f32[2,3,1,5,128,128]{5,4,0,3,2,1:T(8,128)S(1)} collective-permute-done((f32[2,3,1,5,128,128]{5,4,0,3,2,1:T(8,128)S(1)}, f32[2,3,1,5,128,128]{5,4,0,3,2,1:T(8,128)S(1)}, u32[]{:S(2)}, u32[]{:S(2)}) %collective-permute-start.6) | collective-permute-done | bytes 1966112 | tf_op jit(solution)/shard_map/ppermute | solution.py:24
  136.5 0.1 maximum_multiply_fusion.3
  136.6 0.7 convolution_bitcast_fusion.8
  137.3 0.6 convolution_bitcast_fusion.5
  137.9 0.6 fusion.1
  138.5 0.1 maximum_multiply_fusion.1
  138.7 0.6 convolution_bitcast_fusion.4
  139.3 0.6 fusion.2
  139.8 0.0 collective-permute-done.7
  139.9 0.5 convolution_bitcast_fusion.9
  140.4 0.6 convolution_bitcast_fusion.2
  141.0 0.6 fusion
  141.6 0.7 convolution_bitcast_fusion.7
  142.3 0.0 copy-start.3
  142.3 0.1 fusion.7
  142.5 0.0 copy-start.4
  142.5 0.1 fusion.11
  142.6 0.9 copy-done.3
  143.5 0.3 fusion.6
  143.8 1.4 collective-permute-start.8
  145.2 3.8 %collective-permute-start.9 = (f32[1,1,3,5,128]{4,2,3,1,0:T(4,128)S(1)}, f32[1,1,3,5,128]{4,2,3,1,0:T(4,128)S(1)}, u32[]{:S(2)}, u32[]{:S(2)}) collective-permute-start(f32[1,1,3,5,128]{4,2,3,1,0:T(4,128)S(1)} %copy.35), channel_id=1, source_target_pairs={{4,0},{8,4},{12,8},{16,12},{20,16},{24,20},{28,24},{0,28},{5,1},{9... | collective-permute-start | bytes 23048 | tf_op jit(solution)/shard_map/ppermute | solution.py:24
  149.0 1.6 %collective-permute-done.8 = f32[1,1,3,5,128]{4,2,3,1,0:T(4,128)S(1)} collective-permute-done((f32[1,1,3,5,128]{4,2,3,1,0:T(4,128)S(1)}, f32[1,1,3,5,128]{4,2,3,1,0:T(4,128)S(1)}, u32[]{:S(2)}, u32[]{:S(2)}) %collective-permute-start.8) | collective-permute-done | bytes 7712 | tf_op jit(solution)/shard_map/ppermute | solution.py:22
  150.6 0.0 collective-permute-done.9
  150.6 1.1 collective-permute-start.11
  151.7 0.0 collective-permute-start.10
  151.7 0.9 maximum_bitcast_fusion.1
  152.6 0.8 collective-permute-done.11
  153.5 1.6 %collective-permute-done.10 = f32[3,1,3,5,128]{4,2,3,1,0:T(4,128)S(1)} collective-permute-done((f32[3,1,3,5,128]{4,2,3,1,0:T(4,128)S(1)}, f32[3,1,3,5,128]{4,2,3,1,0:T(4,128)S(1)}, u32[]{:S(2)}, u32[]{:S(2)}) %collective-permute-start.10) | collective-permute-done | bytes 23072 | tf_op jit(solution)/shard_map/ppermute | solution.py:22
  155.1 0.0 copy-done.4
  155.1 0.1 fusion.3
  155.2 0.6 copy.41
  (25 shorter events, 0.3 us)
Async XLA Ops:
  0.6 8.2 %copy-start = (f32[2,1,1,5,128,128]{5,4,3,2,1,0:T(8,128)S(1)}, f32[2,1,1,5,128,128]{5,4,3,2,1,0:T(8,128)}, u32[]{:S(2)}) copy-start(f32[2,1,1,5,128,128]{5,4,3,2,1,0:T(8,128)} %param.8) | copy-start | bytes 1966084
  2.7 11.2 %copy-start.1 = (f32[1,1,5,128,128]{4,3,2,1,0:T(8,128)S(1)}, f32[1,1,5,128,128]{4,3,2,1,0:T(8,128)}, u32[]{:S(2)}) copy-start(f32[1,1,5,128,128]{4,3,2,1,0:T(8,128)} %param.7) | copy-start | bytes 983044
  2.7 11.2 %copy-start.2 = (f32[1,1,5,128,128]{4,3,2,1,0:T(8,128)S(1)}, f32[1,1,5,128,128]{4,3,2,1,0:T(8,128)}, u32[]{:S(2)}) copy-start(f32[1,1,5,128,128]{4,3,2,1,0:T(8,128)} %param.6) | copy-start | bytes 983044
  2.8 46.7 %collective-permute-start = (f32[2,1,1,5,128,128]{5,4,0,3,2,1:T(8,128)S(1)}, f32[2,1,1,5,128,128]{5,4,0,3,2,1:T(8,128)S(1)}, u32[]{:S(2)}, u32[]{:S(2)}) collective-permute-start(f32[2,1,1,5,128,128]{5,4,0,3,2,1:T(8,128)S(1)} %maximum_bitcast_fusion), channel_id=1, source_target_pairs={{4,0},{8,4},{12,8},{16,12},{20,16},{24,20},{28,24},{0,28},{5,1},{9... | collective-permute-start | bytes 1966088 | tf_op jit(solution)/shard_map/ppermute | solution.py:24
  8.8 40.6 %collective-permute-start.1 = (f32[2,1,1,5,128,128]{5,4,0,3,2,1:T(8,128)S(1)}, f32[2,1,1,5,128,128]{5,4,0,3,2,1:T(8,128)S(1)}, u32[]{:S(2)}, u32[]{:S(2)}) collective-permute-start(f32[2,1,1,5,128,128]{5,4,0,3,2,1:T(8,128)S(1)} %maximum_bitcast_fusion), channel_id=1, source_target_pairs={{0,4},{4,8},{8,12},{12,16},{16,20},{20,24},{24,28},{28,0},{1,5},{5... | collective-permute-start | bytes 1966088 | tf_op jit(solution)/shard_map/ppermute | solution.py:22
  9.0 53.7 %collective-permute-start.4 = (f32[2,1,1,5,128,128]{5,4,0,3,2,1:T(8,128)S(1)}, f32[2,1,1,5,128,128]{5,4,0,3,2,1:T(8,128)S(1)}, u32[]{:S(2)}, u32[]{:S(2)}) collective-permute-start(f32[2,1,1,5,128,128]{5,4,0,3,2,1:T(8,128)S(1)} %copy_multiply_fusion), channel_id=1, source_target_pairs={{4,0},{8,4},{12,8},{16,12},{20,16},{24,20},{28,24},{0,28},{5,1},{9... | collective-permute-start | bytes 1966088 | tf_op jit(solution)/shard_map/ppermute | solution.py:24
  13.7 49.1 %collective-permute-start.5 = (f32[2,1,1,5,128,128]{5,4,0,3,2,1:T(8,128)S(1)}, f32[2,1,1,5,128,128]{5,4,0,3,2,1:T(8,128)S(1)}, u32[]{:S(2)}, u32[]{:S(2)}) collective-permute-start(f32[2,1,1,5,128,128]{5,4,0,3,2,1:T(8,128)S(1)} %copy_multiply_fusion), channel_id=1, source_target_pairs={{0,4},{4,8},{8,12},{12,16},{16,20},{20,24},{24,28},{28,0},{1,5},{5... | collective-permute-start | bytes 1966088 | tf_op jit(solution)/shard_map/ppermute | solution.py:22
  49.7 42.4 %collective-permute-start.3 = (f32[2,3,1,5,128,128]{5,4,0,3,2,1:T(8,128)S(1)}, f32[2,3,1,5,128,128]{5,4,0,3,2,1:T(8,128)S(1)}, u32[]{:S(2)}, u32[]{:S(2)}) collective-permute-start(f32[2,3,1,5,128,128]{5,4,0,3,2,1:T(8,128)S(1)} %pad_maximum_fusion), channel_id=1, source_target_pairs={{0,1},{1,2},{2,3},{3,0},{4,5},{5,6},{6,7},{7,4},{8,9},{9,10},{10,1... | collective-permute-start | bytes 5898248 | tf_op jit(solution)/shard_map/ppermute | solution.py:22
  50.1 45.0 %collective-permute-start.2 = (f32[2,3,1,5,128,128]{5,4,0,3,2,1:T(8,128)S(1)}, f32[2,3,1,5,128,128]{5,4,0,3,2,1:T(8,128)S(1)}, u32[]{:S(2)}, u32[]{:S(2)}) collective-permute-start(f32[2,3,1,5,128,128]{5,4,0,3,2,1:T(8,128)S(1)} %pad_maximum_fusion), channel_id=1, source_target_pairs={{1,0},{2,1},{3,2},{0,3},{5,4},{6,5},{7,6},{4,7},{9,8},{10,9},{11,1... | collective-permute-start | bytes 5898248 | tf_op jit(solution)/shard_map/ppermute | solution.py:24
  63.0 73.5 %collective-permute-start.6 = (f32[2,3,1,5,128,128]{5,4,0,3,2,1:T(8,128)S(1)}, f32[2,3,1,5,128,128]{5,4,0,3,2,1:T(8,128)S(1)}, u32[]{:S(2)}, u32[]{:S(2)}) collective-permute-start(f32[2,3,1,5,128,128]{5,4,0,3,2,1:T(8,128)S(1)} %pad_maximum_fusion.1), channel_id=1, source_target_pairs={{1,0},{2,1},{3,2},{0,3},{5,4},{6,5},{7,6},{4,7},{9,8},{10,9},{11,1... | collective-permute-start | bytes 5898248 | tf_op jit(solution)/shard_map/ppermute | solution.py:24
  64.2 75.7 %collective-permute-start.7 = (f32[2,3,1,5,128,128]{5,4,0,3,2,1:T(8,128)S(1)}, f32[2,3,1,5,128,128]{5,4,0,3,2,1:T(8,128)S(1)}, u32[]{:S(2)}, u32[]{:S(2)}) collective-permute-start(f32[2,3,1,5,128,128]{5,4,0,3,2,1:T(8,128)S(1)} %pad_maximum_fusion.1), channel_id=1, source_target_pairs={{0,1},{1,2},{2,3},{3,0},{4,5},{5,6},{6,7},{7,4},{8,9},{9,10},{10,1... | collective-permute-start | bytes 5898248 | tf_op jit(solution)/shard_map/ppermute | solution.py:22
  142.3 1.2 copy-start.3
  142.5 12.6 %copy-start.4 = (s32[1,1,128]{2,1,0:T(1,128)S(1)}, s32[1,1,128]{2,1,0:T(1,128)}, u32[]{:S(2)}) copy-start(s32[1,1,128]{2,1,0:T(1,128)} %param.11) | copy-start | bytes 1540
  143.8 6.8 %collective-permute-start.8 = (f32[1,1,3,5,128]{4,2,3,1,0:T(4,128)S(1)}, f32[1,1,3,5,128]{4,2,3,1,0:T(4,128)S(1)}, u32[]{:S(2)}, u32[]{:S(2)}) collective-permute-start(f32[1,1,3,5,128]{4,2,3,1,0:T(4,128)S(1)} %copy.35), channel_id=1, source_target_pairs={{0,4},{4,8},{8,12},{12,16},{16,20},{20,24},{24,28},{28,0},{1,5},{5... | collective-permute-start | bytes 23048 | tf_op jit(solution)/shard_map/ppermute | solution.py:22
  145.2 5.4 %collective-permute-start.9 = (f32[1,1,3,5,128]{4,2,3,1,0:T(4,128)S(1)}, f32[1,1,3,5,128]{4,2,3,1,0:T(4,128)S(1)}, u32[]{:S(2)}, u32[]{:S(2)}) collective-permute-start(f32[1,1,3,5,128]{4,2,3,1,0:T(4,128)S(1)} %copy.35), channel_id=1, source_target_pairs={{4,0},{8,4},{12,8},{16,12},{20,16},{24,20},{28,24},{0,28},{5,1},{9... | collective-permute-start | bytes 23048 | tf_op jit(solution)/shard_map/ppermute | solution.py:24
  150.6 2.8 %collective-permute-start.11 = (f32[3,1,3,5,128]{4,3,2,1,0:T(8,128)S(1)}, f32[3,1,3,5,128]{4,3,2,1,0:T(8,128)S(1)}, u32[]{:S(2)}, u32[]{:S(2)}) collective-permute-start(f32[3,1,3,5,128]{4,3,2,1,0:T(8,128)S(1)} %pad_maximum_fusion.8), channel_id=1, source_target_pairs={{1,0},{2,1},{3,2},{0,3},{5,4},{6,5},{7,6},{4,7},{9,8},{10,9},{11,1... | collective-permute-start | bytes 69128 | tf_op jit(solution)/shard_map/ppermute | solution.py:24
  151.7 3.3 %collective-permute-start.10 = (f32[3,1,3,5,128]{4,2,3,1,0:T(4,128)S(1)}, f32[3,1,3,5,128]{4,2,3,1,0:T(4,128)S(1)}, u32[]{:S(2)}, u32[]{:S(2)}) collective-permute-start(f32[3,1,3,5,128]{4,2,3,1,0:T(4,128)S(1)} %copy.39), channel_id=1, source_target_pairs={{0,1},{1,2},{2,3},{3,0},{4,5},{5,6},{6,7},{7,4},{8,9},{9,10},{10,1... | collective-permute-start | bytes 69128 | tf_op jit(solution)/shard_map/ppermute | solution.py:22
where the time goes:
time: 156 us
  waiting for transfers between devices  122 us (78%)
  starting transfers between devices  20.1 us (13%)
  matrix products  6.77 us (4%)
  other arithmetic  4.55 us (3%)
  local copies, waits for them, and re-layouts  1.81 us (1%)
    ppermute x6, waiting for transfers between devices, padded_2(): lax.ppermute(head, axis, [((i + 1) % count, i) for i in range(count)])  90.5 us
    ppermute x6, waiting for transfers between devices, padded_2(): lax.ppermute(tail, axis, [(i, (i + 1) % count) for i in range(count)])  31 us
    ppermute x6, starting transfers between devices, padded_2(): lax.ppermute(head, axis, [((i + 1) % count, i) for i in range(count)])  18.7 us
    dot_general x12, matrix products, matmul(): return jnp.matmul(left, right, precision=highest)  6.65 us
  transfers between devices with their start and end apart: 12, of which 9 were waited for; matrix products, arithmetic and copies ran while one was open for 4% of the time, Pallas kernels for 0%

commit v1 on v0

v1 whole, which is shorter than its diff:
```python
import functools

import jax
import jax.numpy as jnp
from jax import lax
from jax.experimental import pallas as pl
from jax.experimental.pallas import tpu as pltpu
from jax.sharding import PartitionSpec as P

B = 128
ATOMS = 64

opposite = (0, 2, 1, 4, 3)
time_step = 0.25
vmem = pl.BlockSpec(memory_space=pltpu.VMEM)
smem = pl.BlockSpec(memory_space=pltpu.SMEM)
f32 = jnp.float32
bf16 = jnp.bfloat16


def shifted(cells, offset):
    axis = "gx" if offset < 3 else "gy"
    count = lax.axis_size(axis)
    if offset in (1, 3):
        pairs = [((i + 1) % count, i) for i in range(count)]
    else:
        pairs = [(i, (i + 1) % count) for i in range(count)]
    return lax.ppermute(cells, axis, pairs)


def cols(offset, count=1):
    return slice(offset * B, (offset + count) * B)


def split(values):
    high = values.astype(bf16)
    return high, (values - high.astype(f32)).astype(bf16)


def dot(left, right):
    def one(a, b):
        return jnp.dot(a, b, preferred_element_type=f32)

    return one(left[0], right[0]) + (one(left[0], right[1]) + one(left[1], right[0]))


def part(pair, rows, columns):
    return pair[0][rows, columns], pair[1][rows, columns]


def keep_of(cutoff_ref, offset):
    return cutoff_ref[0, 0, offset].astype(f32)


def first_kernel(cutoff_ref, ham_ref, *outs):
    for offset in range(1, 5):
        back = opposite[offset]
        outs[offset - 1][0] = ham_ref[0, 0, 0]
        outs[offset - 1][1] = ham_ref[0, 0, back] * keep_of(cutoff_ref, back)


def second_kernel(cutoff_ref, ham_ref, inv_ref, rho_ref, send, left_high, left_low, ham_high, ham_low, start):
    for offset in range(5):
        here = cols(offset)
        keep = None if offset == 0 else keep_of(cutoff_ref, offset)
        blocks = (inv_ref[0, 0, offset], rho_ref[0, 0, 0, offset], rho_ref[1, 0, 0, offset])
        for place, block in enumerate(blocks):
            block = block if offset == 0 else block * keep
            if offset == 0:
                send[place] = block
            rows = slice(place * B, (place + 1) * B)
            left_high[rows, here], left_low[rows, here] = split(block)
        block = ham_ref[0, 0, offset]
        block = block if offset == 0 else block * keep
        ham_high[:, here], ham_low[:, here] = split(block)
    every = slice(0, 3 * B)
    left = (left_high, left_low)
    ham = (ham_high, ham_low)
    start[...] = dot(part(left, every, cols(0)), part(ham, slice(0, B), slice(0, 5 * B)))


def third_kernel(cutoff_ref, inv_ref, rho_ref, start, left_high, left_low, one, two, three, four, *outs):
    sends = outs[:4]
    mixed_high, mixed_low, base = outs[4:]
    for offset in range(1, 5):
        back = opposite[offset]
        keep = keep_of(cutoff_ref, back)
        sends[offset - 1][0] = inv_ref[0, 0, back] * keep
        sends[offset - 1][1] = rho_ref[0, 0, 0, back] * keep
        sends[offset - 1][2] = rho_ref[1, 0, 0, back] * keep
    left = (left_high, left_low)
    every = slice(0, 3 * B)
    diagonal = start[:, cols(0)]
    for offset, near in enumerate((one, two, three, four), 1):
        here = part(left, every, cols(offset))
        diagonal = diagonal + dot(here, split(near[1]))
        other = start[:, cols(offset)] + dot(here, split(near[0]))
        mixed_high[:, cols(offset)], mixed_low[:, cols(offset)] = split(other)
    mixed = split(diagonal)
    mixed_high[:, cols(0)], mixed_low[:, cols(0)] = mixed
    top = slice(0, B)
    whole = slice(0, 5 * B)
    prop = (mixed[0][top], mixed[1][top])
    rest = (mixed[0][B:], mixed[1][B:])
    inner = dot(rest, part(left, top, whole))
    base[0] = dot(prop, part(left, slice(B, 2 * B), whole)) - inner[:B]
    base[1] = dot(prop, part(left, slice(2 * B, 3 * B), whole)) - inner[B:]


def fourth_kernel(cutoff_ref, rho_ref, der_ref, base, mixed_high, mixed_low, one, two, three, four, new, row_part, *columns):
    mixed = (mixed_high, mixed_low)
    weighted = [jnp.zeros((B, B), f32) for _ in range(3)]
    for offset, near in enumerate((one, two, three, four), 1):
        keep = keep_of(cutoff_ref, offset)
        here = cols(offset)
        prop = part(mixed, slice(0, B), here)
        inner = dot(part(mixed, slice(B, 3 * B), here), split(near[0]))
        imag_comm = base[1, :, here] + dot(prop, split(near[2])) - inner[B:]
        real_new = rho_ref[0, 0, 0, offset] * keep + time_step * imag_comm
        new[0, offset - 1] = real_new
        for direction in range(3):
            product = real_new * der_ref[direction, 0, 0, offset]
            weighted[direction] = weighted[direction] + product
            columns[offset - 1][direction : direction + 1, :] = jnp.sum(product, axis=0, keepdims=True)
        real_comm = base[0, :, here] + dot(prop, split(near[1])) - inner[:B]
        new[1, offset - 1] = rho_ref[1, 0, 0, offset] * keep - time_step * real_comm
    for direction in range(3):
        row_part[direction] = weighted[direction]


def fifth_kernel(rho_ref, der_ref, atom_ref, base, mixed_high, mixed_low, new, row_part, one, two, three, four, c1, c2, c3, c4, out_ref, forces_ref):
    mixed = (mixed_high, mixed_low)
    real_comm = base[0, :, cols(0)]
    imag_comm = base[1, :, cols(0)]
    for offset, near in enumerate((one, two, three, four), 1):
        here = cols(offset)
        prop = part(mixed, slice(0, B), here)
        inner = dot(part(mixed, slice(B, 3 * B), here), split(near[0]))
        imag_comm = imag_comm + dot(prop, split(near[2])) - inner[B:]
        real_comm = real_comm + dot(prop, split(near[1])) - inner[:B]
    real_new = rho_ref[0, 0, 0, 0] + time_step * imag_comm
    out_ref[0, 0, 0, 0] = real_new
    out_ref[1, 0, 0, 0] = rho_ref[1, 0, 0, 0] - time_step * real_comm
    for offset in range(1, 5):
        out_ref[0, 0, 0, offset] = new[0, offset - 1]
        out_ref[1, 0, 0, offset] = new[1, offset - 1]
    parts = []
    for direction in range(3):
        product = real_new * der_ref[direction, 0, 0, 0]
        total = jnp.sum(product + (product + row_part[direction]).T, axis=0, keepdims=True)
        parts.append(total)
    orbital = jnp.concatenate(parts, axis=0) + ((c1[...] + c2[...]) + (c3[...] + c4[...]))
    members = (
        lax.broadcasted_iota(jnp.int32, (ATOMS, B), 0) == jnp.broadcast_to(atom_ref[0], (ATOMS, B))
    ).astype(f32)
    forces_ref[0, 0] = -lax.dot_general(
        orbital, members, (((1,), (1,)), ((), ())), precision=lax.Precision.HIGHEST, preferred_element_type=f32
    )


def call(kernel, shapes, in_specs, flops, bytes_accessed, *args):
    return pl.pallas_call(
        kernel,
        out_shape=shapes,
        in_specs=in_specs,
        out_specs=[vmem] * len(shapes),
        compiler_params=pltpu.CompilerParams(vmem_limit_bytes=32 * 2**20),
        cost_estimate=pl.CostEstimate(flops=flops, bytes_accessed=bytes_accessed, transcendentals=0),
    )(*args)


def local(hamiltonian, inverse_margin, density, cutoff, derivative, atom_of):
    shape = jax.ShapeDtypeStruct
    unit = B * B * 4
    product = 6 * B**3
    first = call(first_kernel, [shape((2, B, B), f32)] * 4, [smem, vmem], 0, 13 * unit, cutoff, hamiltonian)
    near_ham = [shifted(first[offset - 1], offset) for offset in range(1, 5)]
    pair = [shape((3 * B, 5 * B), bf16)] * 2 + [shape((B, 5 * B), bf16)] * 2
    send, left_high, left_low, ham_high, ham_low, start = call(
        second_kernel,
        [shape((3, B, B), f32)] + pair + [shape((3 * B, 5 * B), f32)],
        [smem, vmem, vmem, vmem],
        15 * product,
        60 * unit,
        cutoff,
        hamiltonian,
        inverse_margin,
        density,
    )
    near_zero = [shifted(send, offset) for offset in range(1, 5)]
    third = call(
        third_kernel,
        [shape((3, B, B), f32)] * 4 + [shape((3 * B, 5 * B), bf16)] * 2 + [shape((2, B, 5 * B), f32)],
        [smem] + [vmem] * 9,
        44 * product,
        100 * unit,
        cutoff,
        inverse_margin,
        density,
        start,
        left_high,
        left_low,
        *near_ham,
    )
    near_back = [shifted(third[offset - 1], offset) for offset in range(1, 5)]
    mixed_high, mixed_low, base = third[4:]
    fourth = call(
        fourth_kernel,
        [shape((2, 4, B, B), f32), shape((3, B, B), f32)] + [shape((3, B), f32)] * 4,
        [smem] + [vmem] * 9,
        16 * product,
        60 * unit,
        cutoff,
        density,
        derivative,
        base,
        mixed_high,
        mixed_low,
        *near_zero,
    )
    new, row_part = fourth[:2]
    columns = [shifted(fourth[offset + 1], opposite[offset]) for offset in range(1, 5)]
    return call(
        fifth_kernel,
        [shape(density.shape, f32), shape((1, 1, 3, ATOMS), f32)],
        [vmem] * 16,
        16 * product,
        60 * unit,
        density,
        derivative,
        atom_of,
        base,
        mixed_high,
        mixed_low,
        new,
        row_part,
        *near_back,
        *columns,
    )


def solution(mesh):
    placed = (
        P("gx", "gy", None, None, None),
        P("gx", "gy", None, None, None),
        P(None, "gx", "gy", None, None, None),
        P("gx", "gy", None),
        P(None, "gx", "gy", None, None, None),
        P("gx", "gy", None),
    )
    return jax.shard_map(
        lambda *args: tuple(local(*args)),
        mesh=mesh,
        in_specs=placed,
        out_specs=(P(None, "gx", "gy", None, None, None), P("gx", "gy", None, None)),
        check_vma=False,
    )
```

time: 156 us -> 53.2 us (0.34)
  the two profiles are of different devices: /device:TPU:0 before, /device:TPU:1 now
where the time goes in v1:
time: 53.2 us; the launch traced here: 53 us
  starting transfers between devices  28.7 us (54%)
  waiting for transfers between devices  12.6 us (24%)
  Pallas kernels  6.94 us (13%)
  local copies, waits for them, and re-layouts  3.98 us (7%)
  between operations  0.71 us (1%)
    ppermute x16, starting transfers between devices, shifted(): return lax.ppermute(cells, axis, pairs)  28.7 us
    ppermute x16, waiting for transfers between devices, shifted(): return lax.ppermute(cells, axis, pairs)  12.6 us
    pallas_call x5, Pallas kernels, call(): pl.pallas_call(kernel, out_shape=shapes, in_specs=in_specs, out_specs=[vm...  6.94 us
    unnamed x14, local copies, waits for them, and re-layouts  3.42 us
  transfers between devices with their start and end apart: 16, of which 6 were waited for; matrix products, arithmetic and copies ran while one was open for 0% of the time, Pallas kernels for 9%

profile of v1, /device:TPU:1, one launch (start us, length us, event | category | flops | bytes accessed | tf_op | source)
XLA Modules:
  0.0 53.0 jit_solution(1133120108373869748)
XLA Ops:
  0.6 0.0 copy-start.3
  0.6 0.0 copy-start.4
  0.6 1.0 %copy-done.4 = f32[1,1,5,128,128]{4,3,2,1,0:T(8,128)S(1)} copy-done((f32[1,1,5,128,128]{4,3,2,1,0:T(8,128)S(1)}, f32[1,1,5,128,128]{4,3,2,1,0:T(8,128)}, u32[]{:S(2)}) %copy-start.4) | copy-done | bytes 327704
  1.7 0.0 copy-start.5
  1.7 0.7 %copy-done.5 = s32[1,1,5]{2,1,0:T(1,128)S(1)} copy-done((s32[1,1,5]{2,1,0:T(1,128)S(1)}, s32[1,1,5]{2,1,0:T(1,128)}, u32[]{:S(2)}) %copy-start.5) | copy-done | bytes 44
  2.3 0.6 %shard_map.78 = (f32[2,128,128]{2,1,0:T(8,128)S(1)}, f32[2,128,128]{2,1,0:T(8,128)S(1)}, f32[2,128,128]{2,1,0:T(8,128)S(1)}, f32[2,128,128]{2,1,0:T(8,128)S(1)}) custom-call(s32[1,1,5]{2,1,0:T(1,128)S(1)} %copy-done.5, f32[1,1,5,128,128]{4,3,2,1,0:T(8,128)S(1)} %copy-done.4), custom_call_target="tpu_custom_call" | custom-call | bytes 851968 | tf_op jit(solution)/shard_map/pallas_call | solution.py:162
  2.9 5.2 %collective-permute-start = (f32[2,128,128]{2,1,0:T(8,128)S(1)}, f32[2,128,128]{2,1,0:T(8,128)S(1)}, u32[]{:S(2)}, u32[]{:S(2)}) collective-permute-start(f32[2,128,128]{2,1,0:T(8,128)S(1)} %get-tuple-element.26), channel_id=1, source_target_pairs={{4,0},{8,4},{12,8},{16,12},{20,16},{24,20},{28,24},{0,28},{5,1},{9... | collective-permute-start | bytes 393224 | tf_op jit(solution)/shard_map/ppermute | solution.py:28
  8.1 0.0 collective-permute-start.1
  8.1 0.0 copy-done.3
  8.1 0.0 copy-start
  8.1 1.1 %copy-done = f32[2,1,1,5,128,128]{5,4,3,2,1,0:T(8,128)S(1)} copy-done((f32[2,1,1,5,128,128]{5,4,3,2,1,0:T(8,128)S(1)}, f32[2,1,1,5,128,128]{5,4,3,2,1,0:T(8,128)}, u32[]{:S(2)}) %copy-start) | copy-done | bytes 655384
  9.2 0.0 copy-start.1
  9.2 1.6 %shard_map.77 = (f32[3,128,128]{2,1,0:T(8,128)S(1)}, bf16[384,640]{1,0:T(8,128)(2,1)S(1)}, bf16[384,640]{1,0:T(8,128)(2,1)S(1)}, bf16[128,640]{1,0:T(8,128)(2,1)...) custom-call(s32[1,1,5]{2,1,0:T(1,128)S(1)} %copy-done.5, f32[1,1,5,128,128]{4,3,2,1,0:T(8,128)S(1)} %copy-done.4, ...), custom_call_target="tpu_custom_call" | custom-call | flops 188743680 | bytes 3932160 | tf_op jit(solution)/shard_map/pallas_call | solution.py:162
  10.7 2.0 %collective-permute-start.7 = (f32[3,128,128]{2,1,0:T(8,128)S(1)}, f32[3,128,128]{2,1,0:T(8,128)S(1)}, u32[]{:S(2)}, u32[]{:S(2)}) collective-permute-start(f32[3,128,128]{2,1,0:T(8,128)S(1)} %get-tuple-element.33), channel_id=1, source_target_pairs={{0,1},{1,2},{2,3},{3,0},{4,5},{5,6},{6,7},{7,4},{8,9},{9,10},{10,1... | collective-permute-start | bytes 589832 | tf_op jit(solution)/shard_map/ppermute | solution.py:28
  12.8 0.0 collective-permute-start.6
  12.8 0.0 collective-permute-start.5
  12.8 0.0 collective-permute-done.one
  12.8 0.6 %collective-permute-start.2 = (f32[2,128,128]{2,1,0:T(8,128)S(1)}, f32[2,128,128]{2,1,0:T(8,128)S(1)}, u32[]{:S(2)}, u32[]{:S(2)}) collective-permute-start(f32[2,128,128]{2,1,0:T(8,128)S(1)} %get-tuple-element.28), channel_id=1, source_target_pairs={{1,0},{2,1},{3,2},{0,3},{5,4},{6,5},{7,6},{4,7},{9,8},{10,9},{11,1... | collective-permute-start | bytes 393224 | tf_op jit(solution)/shard_map/ppermute | solution.py:28
  13.4 1.1 %collective-permute-done.1.two = f32[2,128,128]{2,1,0:T(8,128)S(1)} collective-permute-done((f32[2,128,128]{2,1,0:T(8,128)S(1)}, f32[2,128,128]{2,1,0:T(8,128)S(1)}, u32[]{:S(2)}, u32[]{:S(2)}) %collective-permute-start.1) | collective-permute-done | bytes 131104 | tf_op jit(solution)/shard_map/ppermute | solution.py:28
  14.6 3.2 %collective-permute-start.3 = (f32[2,128,128]{2,1,0:T(8,128)S(1)}, f32[2,128,128]{2,1,0:T(8,128)S(1)}, u32[]{:S(2)}, u32[]{:S(2)}) collective-permute-start(f32[2,128,128]{2,1,0:T(8,128)S(1)} %get-tuple-element.29), channel_id=1, source_target_pairs={{0,1},{1,2},{2,3},{3,0},{4,5},{5,6},{6,7},{7,4},{8,9},{9,10},{10,1... | collective-permute-start | bytes 393224 | tf_op jit(solution)/shard_map/ppermute | solution.py:28
  17.8 2.7 %collective-permute-done.2.three = f32[2,128,128]{2,1,0:T(8,128)S(1)} collective-permute-done((f32[2,128,128]{2,1,0:T(8,128)S(1)}, f32[2,128,128]{2,1,0:T(8,128)S(1)}, u32[]{:S(2)}, u32[]{:S(2)}) %collective-permute-start.2) | collective-permute-done | bytes 131104 | tf_op jit(solution)/shard_map/ppermute | solution.py:28
  20.4 5.0 %collective-permute-start.4 = (f32[3,128,128]{2,1,0:T(8,128)S(1)}, f32[3,128,128]{2,1,0:T(8,128)S(1)}, u32[]{:S(2)}, u32[]{:S(2)}) collective-permute-start(f32[3,128,128]{2,1,0:T(8,128)S(1)} %get-tuple-element.33), channel_id=1, source_target_pairs={{4,0},{8,4},{12,8},{16,12},{20,16},{24,20},{28,24},{0,28},{5,1},{9... | collective-permute-start | bytes 589832 | tf_op jit(solution)/shard_map/ppermute | solution.py:28
  25.4 0.0 collective-permute-done.3.four
  25.4 0.0 copy-done.1
  25.5 0.0 copy-start.2
  25.5 2.0 %shard_map.79 = (f32[3,128,128]{2,1,0:T(8,128)S(1)}, f32[3,128,128]{2,1,0:T(8,128)S(1)}, f32[3,128,128]{2,1,0:T(8,128)S(1)}, f32[3,128,128]{2,1,0:T(8,128)S(1)},...) custom-call(s32[1,1,5]{2,1,0:T(1,128)S(1)} %copy-done.5, ...), custom_call_target="tpu_custom_call" | custom-call | flops 553648128 | bytes 6553600 | tf_op jit(solution)/shard_map/pallas_call | solution.py:162
  27.4 0.1 collective-permute-start.8
  27.5 0.0 collective-permute-done.7.four
  27.5 1.4 %collective-permute-start.9 = (f32[3,128,128]{2,1,0:T(8,128)S(1)}, f32[3,128,128]{2,1,0:T(8,128)S(1)}, u32[]{:S(2)}, u32[]{:S(2)}) collective-permute-start(f32[3,128,128]{2,1,0:T(8,128)S(1)} %get-tuple-element.37), channel_id=1, source_target_pairs={{0,4},{4,8},{8,12},{12,16},{16,20},{20,24},{24,28},{28,0},{1,5},{5... | collective-permute-start | bytes 589832 | tf_op jit(solution)/shard_map/ppermute | solution.py:28
  28.9 0.0 collective-permute-done.6.three
  28.9 0.5 %collective-permute-start.10 = (f32[3,128,128]{2,1,0:T(8,128)S(1)}, f32[3,128,128]{2,1,0:T(8,128)S(1)}, u32[]{:S(2)}, u32[]{:S(2)}) collective-permute-start(f32[3,128,128]{2,1,0:T(8,128)S(1)} %get-tuple-element.38), channel_id=1, source_target_pairs={{1,0},{2,1},{3,2},{0,3},{5,4},{6,5},{7,6},{4,7},{9,8},{10,9},{11,1... | collective-permute-start | bytes 589832 | tf_op jit(solution)/shard_map/ppermute | solution.py:28
  29.5 0.0 collective-permute-done.5.two
  29.5 1.2 %collective-permute-start.11 = (f32[3,128,128]{2,1,0:T(8,128)S(1)}, f32[3,128,128]{2,1,0:T(8,128)S(1)}, u32[]{:S(2)}, u32[]{:S(2)}) collective-permute-start(f32[3,128,128]{2,1,0:T(8,128)S(1)} %get-tuple-element.39), channel_id=1, source_target_pairs={{0,1},{1,2},{2,3},{3,0},{4,5},{5,6},{6,7},{7,4},{8,9},{9,10},{10,1... | collective-permute-start | bytes 589832 | tf_op jit(solution)/shard_map/ppermute | solution.py:28
  30.7 0.0 collective-permute-done.4.one
  30.7 0.0 copy-done.2
  30.7 1.2 %shard_map.80 = (f32[2,4,128,128]{3,2,1,0:T(8,128)S(1)}, f32[3,128,128]{2,1,0:T(8,128)S(1)}, f32[3,128]{1,0:T(4,128)S(1)}, f32[3,128]{1,0:T(4,128)S(1)}, f32[3,128]{1,0:T(4,128)S(1)}, /*index=5*/f32[3,128]{1,0:T(4,128)S(1)}) custom-call(s32[1,1,5]{2,1,0:T(1,128)S(1)} %copy-done.5, f32[2,1,1,5,128,128]{5,4,3,2,1,0:T(8,128)S(1)} %copy-done.1, ...), custom_call_target="tpu_custom_call" | custom-call | flops 201326592 | bytes 3932160 | tf_op jit(solution)/shard_map/pallas_call | solution.py:162
  31.9 0.1 collective-permute-start.12
  32.0 5.2 %collective-permute-done.12.c1 = f32[3,128]{1,0:T(4,128)S(1)} collective-permute-done((f32[3,128]{1,0:T(4,128)S(1)}, f32[3,128]{1,0:T(4,128)S(1)}, u32[]{:S(2)}, u32[]{:S(2)}) %collective-permute-start.12) | collective-permute-done | bytes 1568 | tf_op jit(solution)/shard_map/ppermute | solution.py:28
  37.2 5.2 %collective-permute-start.13 = (f32[3,128]{1,0:T(4,128)S(1)}, f32[3,128]{1,0:T(4,128)S(1)}, u32[]{:S(2)}, u32[]{:S(2)}) collective-permute-start(f32[3,128]{1,0:T(4,128)S(1)} %get-tuple-element.41), channel_id=1, source_target_pairs={{4,0},{8,4},{12,8},{16,12},{20,16},{24,20},{28,24},{0,28},{5,1},{9... | collective-permute-start | bytes 4616 | tf_op jit(solution)/shard_map/ppermute | solution.py:28
  42.4 0.7 %collective-permute-done.13.c2 = f32[3,128]{1,0:T(4,128)S(1)} collective-permute-done((f32[3,128]{1,0:T(4,128)S(1)}, f32[3,128]{1,0:T(4,128)S(1)}, u32[]{:S(2)}, u32[]{:S(2)}) %collective-permute-start.13) | collective-permute-done | bytes 1568 | tf_op jit(solution)/shard_map/ppermute | solution.py:28
  43.1 2.7 %collective-permute-start.14 = (f32[3,128]{1,0:T(4,128)S(1)}, f32[3,128]{1,0:T(4,128)S(1)}, u32[]{:S(2)}, u32[]{:S(2)}) collective-permute-start(f32[3,128]{1,0:T(4,128)S(1)} %get-tuple-element.42), channel_id=1, source_target_pairs={{0,1},{1,2},{2,3},{3,0},{4,5},{5,6},{6,7},{7,4},{8,9},{9,10},{10,1... | collective-permute-start | bytes 4616 | tf_op jit(solution)/shard_map/ppermute | solution.py:28
  45.8 0.7 %collective-permute-done.14.c3 = f32[3,128]{1,0:T(4,128)S(1)} collective-permute-done((f32[3,128]{1,0:T(4,128)S(1)}, f32[3,128]{1,0:T(4,128)S(1)}, u32[]{:S(2)}, u32[]{:S(2)}) %collective-permute-start.14) | collective-permute-done | bytes 1568 | tf_op jit(solution)/shard_map/ppermute | solution.py:28
  46.6 1.4 %collective-permute-start.15 = (f32[3,128]{1,0:T(4,128)S(1)}, f32[3,128]{1,0:T(4,128)S(1)}, u32[]{:S(2)}, u32[]{:S(2)}) collective-permute-start(f32[3,128]{1,0:T(4,128)S(1)} %get-tuple-element.43), channel_id=1, source_target_pairs={{1,0},{2,1},{3,2},{0,3},{5,4},{6,5},{7,6},{4,7},{9,8},{10,9},{11,1... | collective-permute-start | bytes 4616 | tf_op jit(solution)/shard_map/ppermute | solution.py:28
  48.0 2.1 %collective-permute-done.15.c4 = f32[3,128]{1,0:T(4,128)S(1)} collective-permute-done((f32[3,128]{1,0:T(4,128)S(1)}, f32[3,128]{1,0:T(4,128)S(1)}, u32[]{:S(2)}, u32[]{:S(2)}) %collective-permute-start.15) | collective-permute-done | bytes 1568 | tf_op jit(solution)/shard_map/ppermute | solution.py:28
  50.1 0.0 collective-permute-done.8.one
  50.1 0.0 collective-permute-done.9.two
  50.1 0.0 collective-permute-done.10.three
  50.1 0.0 collective-permute-done.11.four
  50.1 0.0 copy-start.6
  50.1 0.6 %copy-done.6 = s32[1,1,128]{2,1,0:T(1,128)S(1)} copy-done((s32[1,1,128]{2,1,0:T(1,128)S(1)}, s32[1,1,128]{2,1,0:T(1,128)}, u32[]{:S(2)}) %copy-start.6) | copy-done | bytes 536
  50.8 1.7 %shard_map.81 = (f32[2,1,1,5,128,128]{5,4,3,2,1,0:T(8,128)}, f32[1,1,3,64]{3,2,1,0:T(4,128)S(1)}) custom-call(f32[2,1,1,5,128,128]{5,4,3,2,1,0:T(8,128)S(1)} %copy-done.1, f32[3,1,1,5,128,128]{5,4,3,2,1,0:T(8,128)S(1)} %copy-done.2, s32[1,1,128]{2,1,0:T(1,128)S(1)} %copy-done.6, f32[2,128,640]{2,1,0:T(8,128)S(1)} %get-tuple-element.30.base, ...), custom_call_target="tpu_custom_call" | custom-call | flops 201326592 | bytes 3932160 | tf_op jit(solution)/shard_map/pallas_call | solution.py:162
  52.4 0.6 %copy.8 = f32[1,1,3,64]{3,1,2,0:T(1,128)} copy(f32[1,1,3,64]{3,2,1,0:T(4,128)S(1)} %get-tuple-element.45) | data formatting | bytes 1536 | tf_op jit(solution)/shard_map/pallas_call | solution.py:162
Async XLA Ops:
  0.6 7.4 %copy-start.3 = (f32[1,1,5,128,128]{4,3,2,1,0:T(8,128)S(1)}, f32[1,1,5,128,128]{4,3,2,1,0:T(8,128)}, u32[]{:S(2)}) copy-start(f32[1,1,5,128,128]{4,3,2,1,0:T(8,128)} %inv_ref.3) | copy-start | bytes 983044
  0.6 1.0 %copy-start.4 = (f32[1,1,5,128,128]{4,3,2,1,0:T(8,128)S(1)}, f32[1,1,5,128,128]{4,3,2,1,0:T(8,128)}, u32[]{:S(2)}) copy-start(f32[1,1,5,128,128]{4,3,2,1,0:T(8,128)} %ham_ref.3) | copy-start | bytes 983044
  1.7 0.7 %copy-start.5 = (s32[1,1,5]{2,1,0:T(1,128)S(1)}, s32[1,1,5]{2,1,0:T(1,128)}, u32[]{:S(2)}) copy-start(s32[1,1,5]{2,1,0:T(1,128)} %cutoff_ref.7) | copy-start | bytes 64
  2.9 9.9 %collective-permute-start = (f32[2,128,128]{2,1,0:T(8,128)S(1)}, f32[2,128,128]{2,1,0:T(8,128)S(1)}, u32[]{:S(2)}, u32[]{:S(2)}) collective-permute-start(f32[2,128,128]{2,1,0:T(8,128)S(1)} %get-tuple-element.26), channel_id=1, source_target_pairs={{4,0},{8,4},{12,8},{16,12},{20,16},{24,20},{28,24},{0,28},{5,1},{9... | collective-permute-start | bytes 393224 | tf_op jit(solution)/shard_map/ppermute | solution.py:28
  8.1 6.5 %collective-permute-start.1 = (f32[2,128,128]{2,1,0:T(8,128)S(1)}, f32[2,128,128]{2,1,0:T(8,128)S(1)}, u32[]{:S(2)}, u32[]{:S(2)}) collective-permute-start(f32[2,128,128]{2,1,0:T(8,128)S(1)} %get-tuple-element.27), channel_id=1, source_target_pairs={{0,4},{4,8},{8,12},{12,16},{16,20},{20,24},{24,28},{28,0},{1,5},{5... | collective-permute-start | bytes 393224 | tf_op jit(solution)/shard_map/ppermute | solution.py:28
  8.1 1.1 %copy-start = (f32[2,1,1,5,128,128]{5,4,3,2,1,0:T(8,128)S(1)}, f32[2,1,1,5,128,128]{5,4,3,2,1,0:T(8,128)}, u32[]{:S(2)}) copy-start(f32[2,1,1,5,128,128]{5,4,3,2,1,0:T(8,128)} %rho_ref.7) | copy-start | bytes 1966084
  9.2 16.3 %copy-start.1 = (f32[2,1,1,5,128,128]{5,4,3,2,1,0:T(8,128)S(1)}, f32[2,1,1,5,128,128]{5,4,3,2,1,0:T(8,128)}, u32[]{:S(2)}) copy-start(f32[2,1,1,5,128,128]{5,4,3,2,1,0:T(8,128)} %rho_ref.7) | copy-start | bytes 1966084
  10.7 16.8 %collective-permute-start.7 = (f32[3,128,128]{2,1,0:T(8,128)S(1)}, f32[3,128,128]{2,1,0:T(8,128)S(1)}, u32[]{:S(2)}, u32[]{:S(2)}) collective-permute-start(f32[3,128,128]{2,1,0:T(8,128)S(1)} %get-tuple-element.33), channel_id=1, source_target_pairs={{0,1},{1,2},{2,3},{3,0},{4,5},{5,6},{6,7},{7,4},{8,9},{9,10},{10,1... | collective-permute-start | bytes 589832 | tf_op jit(solution)/shard_map/ppermute | solution.py:28
  12.8 16.2 %collective-permute-start.6 = (f32[3,128,128]{2,1,0:T(8,128)S(1)}, f32[3,128,128]{2,1,0:T(8,128)S(1)}, u32[]{:S(2)}, u32[]{:S(2)}) collective-permute-start(f32[3,128,128]{2,1,0:T(8,128)S(1)} %get-tuple-element.33), channel_id=1, source_target_pairs={{1,0},{2,1},{3,2},{0,3},{5,4},{6,5},{7,6},{4,7},{9,8},{10,9},{11,1... | collective-permute-start | bytes 589832 | tf_op jit(solution)/shard_map/ppermute | solution.py:28
  12.8 16.7 %collective-permute-start.5 = (f32[3,128,128]{2,1,0:T(8,128)S(1)}, f32[3,128,128]{2,1,0:T(8,128)S(1)}, u32[]{:S(2)}, u32[]{:S(2)}) collective-permute-start(f32[3,128,128]{2,1,0:T(8,128)S(1)} %get-tuple-element.33), channel_id=1, source_target_pairs={{0,4},{4,8},{8,12},{12,16},{16,20},{20,24},{24,28},{28,0},{1,5},{5... | collective-permute-start | bytes 589832 | tf_op jit(solution)/shard_map/ppermute | solution.py:28
  12.8 7.7 %collective-permute-start.2 = (f32[2,128,128]{2,1,0:T(8,128)S(1)}, f32[2,128,128]{2,1,0:T(8,128)S(1)}, u32[]{:S(2)}, u32[]{:S(2)}) collective-permute-start(f32[2,128,128]{2,1,0:T(8,128)S(1)} %get-tuple-element.28), channel_id=1, source_target_pairs={{1,0},{2,1},{3,2},{0,3},{5,4},{6,5},{7,6},{4,7},{9,8},{10,9},{11,1... | collective-permute-start | bytes 393224 | tf_op jit(solution)/shard_map/ppermute | solution.py:28
  14.6 10.9 %collective-permute-start.3 = (f32[2,128,128]{2,1,0:T(8,128)S(1)}, f32[2,128,128]{2,1,0:T(8,128)S(1)}, u32[]{:S(2)}, u32[]{:S(2)}) collective-permute-start(f32[2,128,128]{2,1,0:T(8,128)S(1)} %get-tuple-element.29), channel_id=1, source_target_pairs={{0,1},{1,2},{2,3},{3,0},{4,5},{5,6},{6,7},{7,4},{8,9},{9,10},{10,1... | collective-permute-start | bytes 393224 | tf_op jit(solution)/shard_map/ppermute | solution.py:28
  20.4 10.2 %collective-permute-start.4 = (f32[3,128,128]{2,1,0:T(8,128)S(1)}, f32[3,128,128]{2,1,0:T(8,128)S(1)}, u32[]{:S(2)}, u32[]{:S(2)}) collective-permute-start(f32[3,128,128]{2,1,0:T(8,128)S(1)} %get-tuple-element.33), channel_id=1, source_target_pairs={{4,0},{8,4},{12,8},{16,12},{20,16},{24,20},{28,24},{0,28},{5,1},{9... | collective-permute-start | bytes 589832 | tf_op jit(solution)/shard_map/ppermute | solution.py:28
  25.5 5.2 %copy-start.2 = (f32[3,1,1,5,128,128]{5,4,3,2,1,0:T(8,128)S(1)}, f32[3,1,1,5,128,128]{5,4,3,2,1,0:T(8,128)}, u32[]{:S(2)}) copy-start(f32[3,1,1,5,128,128]{5,4,3,2,1,0:T(8,128)} %der_ref.3) | copy-start | bytes 2949124
  27.4 22.7 %collective-permute-start.8 = (f32[3,128,128]{2,1,0:T(8,128)S(1)}, f32[3,128,128]{2,1,0:T(8,128)S(1)}, u32[]{:S(2)}, u32[]{:S(2)}) collective-permute-start(f32[3,128,128]{2,1,0:T(8,128)S(1)} %get-tuple-element.36), channel_id=1, source_target_pairs={{4,0},{8,4},{12,8},{16,12},{20,16},{24,20},{28,24},{0,28},{5,1},{9... | collective-permute-start | bytes 589832 | tf_op jit(solution)/shard_map/ppermute | solution.py:28
  27.5 22.6 %collective-permute-start.9 = (f32[3,128,128]{2,1,0:T(8,128)S(1)}, f32[3,128,128]{2,1,0:T(8,128)S(1)}, u32[]{:S(2)}, u32[]{:S(2)}) collective-permute-start(f32[3,128,128]{2,1,0:T(8,128)S(1)} %get-tuple-element.37), channel_id=1, source_target_pairs={{0,4},{4,8},{8,12},{12,16},{16,20},{20,24},{24,28},{28,0},{1,5},{5... | collective-permute-start | bytes 589832 | tf_op jit(solution)/shard_map/ppermute | solution.py:28
  28.9 21.2 %collective-permute-start.10 = (f32[3,128,128]{2,1,0:T(8,128)S(1)}, f32[3,128,128]{2,1,0:T(8,128)S(1)}, u32[]{:S(2)}, u32[]{:S(2)}) collective-permute-start(f32[3,128,128]{2,1,0:T(8,128)S(1)} %get-tuple-element.38), channel_id=1, source_target_pairs={{1,0},{2,1},{3,2},{0,3},{5,4},{6,5},{7,6},{4,7},{9,8},{10,9},{11,1... | collective-permute-start | bytes 589832 | tf_op jit(solution)/shard_map/ppermute | solution.py:28
  29.5 20.6 %collective-permute-start.11 = (f32[3,128,128]{2,1,0:T(8,128)S(1)}, f32[3,128,128]{2,1,0:T(8,128)S(1)}, u32[]{:S(2)}, u32[]{:S(2)}) collective-permute-start(f32[3,128,128]{2,1,0:T(8,128)S(1)} %get-tuple-element.39), channel_id=1, source_target_pairs={{0,1},{1,2},{2,3},{3,0},{4,5},{5,6},{6,7},{7,4},{8,9},{9,10},{10,1... | collective-permute-start | bytes 589832 | tf_op jit(solution)/shard_map/ppermute | solution.py:28
  31.9 5.3 %collective-permute-start.12 = (f32[3,128]{1,0:T(4,128)S(1)}, f32[3,128]{1,0:T(4,128)S(1)}, u32[]{:S(2)}, u32[]{:S(2)}) collective-permute-start(f32[3,128]{1,0:T(4,128)S(1)} %get-tuple-element.40), channel_id=1, source_target_pairs={{0,4},{4,8},{8,12},{12,16},{16,20},{20,24},{24,28},{28,0},{1,5},{5... | collective-permute-start | bytes 4616 | tf_op jit(solution)/shard_map/ppermute | solution.py:28
  37.2 5.9 %collective-permute-start.13 = (f32[3,128]{1,0:T(4,128)S(1)}, f32[3,128]{1,0:T(4,128)S(1)}, u32[]{:S(2)}, u32[]{:S(2)}) collective-permute-start(f32[3,128]{1,0:T(4,128)S(1)} %get-tuple-element.41), channel_id=1, source_target_pairs={{4,0},{8,4},{12,8},{16,12},{20,16},{24,20},{28,24},{0,28},{5,1},{9... | collective-permute-start | bytes 4616 | tf_op jit(solution)/shard_map/ppermute | solution.py:28
  43.1 3.5 %collective-permute-start.14 = (f32[3,128]{1,0:T(4,128)S(1)}, f32[3,128]{1,0:T(4,128)S(1)}, u32[]{:S(2)}, u32[]{:S(2)}) collective-permute-start(f32[3,128]{1,0:T(4,128)S(1)} %get-tuple-element.42), channel_id=1, source_target_pairs={{0,1},{1,2},{2,3},{3,0},{4,5},{5,6},{6,7},{7,4},{8,9},{9,10},{10,1... | collective-permute-start | bytes 4616 | tf_op jit(solution)/shard_map/ppermute | solution.py:28
  46.6 3.5 %collective-permute-start.15 = (f32[3,128]{1,0:T(4,128)S(1)}, f32[3,128]{1,0:T(4,128)S(1)}, u32[]{:S(2)}, u32[]{:S(2)}) collective-permute-start(f32[3,128]{1,0:T(4,128)S(1)} %get-tuple-element.43), channel_id=1, source_target_pairs={{1,0},{2,1},{3,2},{0,3},{5,4},{6,5},{7,6},{4,7},{9,8},{10,9},{11,1... | collective-permute-start | bytes 4616 | tf_op jit(solution)/shard_map/ppermute | solution.py:28
  50.1 0.7 %copy-start.6 = (s32[1,1,128]{2,1,0:T(1,128)S(1)}, s32[1,1,128]{2,1,0:T(1,128)}, u32[]{:S(2)}) copy-start(s32[1,1,128]{2,1,0:T(1,128)} %atom_ref.1) | copy-start | bytes 1540

commit v2 on v1

v2 whole, which is shorter than its diff:
```python
import jax
import jax.numpy as jnp
from jax import lax
from jax.experimental import pallas as pl
from jax.experimental.pallas import tpu as pltpu
from jax.sharding import PartitionSpec as P

B = 128
ATOMS = 64

opposite = (0, 2, 1, 4, 3)
time_step = 0.25
vmem = pl.BlockSpec(memory_space=pltpu.VMEM)
smem = pl.BlockSpec(memory_space=pltpu.SMEM)
hbm = pl.BlockSpec(memory_space=pltpu.HBM)
f32 = jnp.float32
bf16 = jnp.bfloat16


def shifted(cells, offset):
    axis = "gx" if offset < 3 else "gy"
    count = lax.axis_size(axis)
    if offset in (1, 3):
        pairs = [((i + 1) % count, i) for i in range(count)]
    else:
        pairs = [(i, (i + 1) % count) for i in range(count)]
    return lax.ppermute(cells, axis, pairs)


def cols(offset, count=1):
    return slice(offset * B, (offset + count) * B)


def split(values):
    high = values.astype(bf16)
    return high, (values - high.astype(f32)).astype(bf16)


def dot(left, right):
    def one(a, b):
        return jnp.dot(a, b, preferred_element_type=f32)

    return one(left[0], right[0]) + (one(left[0], right[1]) + one(left[1], right[0]))


def part(pair, rows, columns):
    return pair[0][rows, columns], pair[1][rows, columns]


def keep_of(cutoff_ref, offset):
    return cutoff_ref[0, 0, offset].astype(f32)


def first_kernel(cutoff_ref, ham_ref, one, two, ham):
    ham[0] = ham_ref[0, 0, 0]
    for offset in range(1, 5):
        ham[offset] = ham_ref[0, 0, offset] * keep_of(cutoff_ref, offset)
    for offset, out in ((1, one), (2, two)):
        out[0] = ham[0]
        out[1] = ham[opposite[offset]]


def second_kernel(
    cutoff_ref, inv_ref, rho_ref, atom_ref, ham_ref, send, three, four, left_high, left_low, start, members, ham_high, ham_low
):
    for offset in range(5):
        here = cols(offset)
        blocks = (inv_ref[0, 0, offset], rho_ref[0, 0, 0, offset], rho_ref[1, 0, 0, offset])
        if offset > 0:
            blocks = [block * keep_of(cutoff_ref, offset) for block in blocks]
        for place, block in enumerate((*blocks, ham_ref[offset])):
            if offset == 0:
                if place < 3:
                    send[place] = block
                three[place] = block
                four[place] = block
            elif offset > 2:
                (four if offset == 3 else three)[4 + place] = block
            if place < 3:
                rows = slice(place * B, (place + 1) * B)
                left_high[rows, here], left_low[rows, here] = split(block)
            else:
                ham_high[:, here], ham_low[:, here] = split(block)
    left = (left_high, left_low)
    ham = (ham_high, ham_low)
    start[...] = dot(part(left, slice(0, 3 * B), cols(0)), part(ham, slice(0, B), slice(0, 5 * B)))
    atoms = jnp.broadcast_to(atom_ref[0], (ATOMS, B))
    members[...] = -(lax.broadcasted_iota(jnp.int32, (ATOMS, B), 0) == atoms).astype(f32)


def mixed_kernel(offsets, left_high, left_low, start, near_zero, near_back, mixed_high, mixed_low):
    left = (left_high, left_low)
    every = slice(0, 3 * B)
    diagonal = start[:, cols(0)]
    for offset, zero, back in zip(offsets, near_zero, near_back):
        here = part(left, every, cols(offset))
        diagonal = diagonal + dot(here, split(back))
        other = start[:, cols(offset)] + dot(here, split(zero))
        at = cols(offset - offsets[0])
        mixed_high[:, at], mixed_low[:, at] = split(other)
    return diagonal


def third_kernel(left_high, left_low, start, one, two, mixed_high, mixed_low, diagonal):
    diagonal[...] = mixed_kernel(
        (1, 2), left_high, left_low, start, (one[0], two[0]), (one[1], two[1]), mixed_high, mixed_low
    )


def fourth_kernel(
    cutoff_ref, inv_ref, rho_ref, left_high, left_low, start, diagonal, three, four, send_one, send_two, mixed_high, mixed_low, base
):
    for offset, send in ((1, send_one), (2, send_two)):
        back = opposite[offset]
        keep = keep_of(cutoff_ref, back)
        send[0] = inv_ref[0, 0, back] * keep
        send[1] = rho_ref[0, 0, 0, back] * keep
        send[2] = rho_ref[1, 0, 0, back] * keep
    left = (left_high, left_low)
    total = mixed_kernel(
        (3, 4), left_high, left_low, start, (three[3], four[3]), (three[7], four[7]), mixed_high, mixed_low
    )
    mixed = split(total - start[:, cols(0)] + diagonal[...])
    top = slice(0, B)
    whole = slice(0, 5 * B)
    prop = (mixed[0][top], mixed[1][top])
    rest = (mixed[0][B:], mixed[1][B:])
    inner = dot(rest, part(left, top, whole))
    base[0] = dot(prop, part(left, slice(B, 2 * B), whole)) - inner[:B]
    base[1] = dot(prop, part(left, slice(2 * B, 3 * B), whole)) - inner[B:]


def fifth_kernel(
    cutoff_ref, rho_ref, der_ref, base, high_x, low_x, high_y, low_y, one, two, three, four, out_hbm, row_part, *refs
):
    columns, (new, sems) = refs[:4], refs[4:]
    weighted = [jnp.zeros((B, B), f32) for _ in range(3)]
    copies = []
    for offset, near in enumerate((one, two, three, four), 1):
        keep = keep_of(cutoff_ref, offset)
        here = cols(offset)
        mixed = (high_x, low_x) if offset < 3 else (high_y, low_y)
        at = cols((offset - 1) % 2)
        prop = part(mixed, slice(0, B), at)
        inner = dot(part(mixed, slice(B, 3 * B), at), split(near[0]))
        imag_comm = base[1, :, here] + dot(prop, split(near[2])) - inner[B:]
        real_new = rho_ref[0, 0, 0, offset] * keep + time_step * imag_comm
        new[0, offset - 1] = real_new
        for direction in range(3):
            product = real_new * der_ref[direction, 0, 0, offset]
            weighted[direction] = weighted[direction] + product
            columns[offset - 1][direction : direction + 1, :] = jnp.sum(product, axis=0, keepdims=True)
        real_comm = base[0, :, here] + dot(prop, split(near[1])) - inner[:B]
        new[1, offset - 1] = rho_ref[1, 0, 0, offset] * keep - time_step * real_comm
        for place in range(2):
            copy = pltpu.make_async_copy(
                new.at[place, offset - 1], out_hbm.at[place, 0, 0, offset], sems.at[place, offset - 1]
            )
            copy.start()
            copies.append(copy)
    for direction in range(3):
        row_part[direction : direction + 1, :] = jnp.sum(weighted[direction].T, axis=0, keepdims=True)
    for copy in copies:
        copy.wait()


def sixth_kernel(
    rho_ref, der_ref, members, base, high_x, low_x, high_y, low_y, row_part, one, two, three, four, c1, c2, c3, c4, old_hbm,
    out_hbm, forces_ref, new, sems
):
    real_comm = base[0, :, cols(0)]
    imag_comm = base[1, :, cols(0)]
    for offset, near in enumerate((one, two, three, four), 1):
        mixed = (high_x, low_x) if offset < 3 else (high_y, low_y)
        at = cols((offset - 1) % 2)
        first = 0 if offset < 3 else 4
        prop = part(mixed, slice(0, B), at)
        inner = dot(part(mixed, slice(B, 3 * B), at), split(near[first]))
        imag_comm = imag_comm + dot(prop, split(near[first + 2])) - inner[B:]
        real_comm = real_comm + dot(prop, split(near[first + 1])) - inner[:B]
    real_new = rho_ref[0, 0, 0, 0] + time_step * imag_comm
    new[0] = real_new
    new[1] = rho_ref[1, 0, 0, 0] - time_step * real_comm
    copies = [pltpu.make_async_copy(new.at[place], out_hbm.at[place, 0, 0, 0], sems.at[place]) for place in range(2)]
    for copy in copies:
        copy.start()
    parts = []
    for direction in range(3):
        product = real_new * der_ref[direction, 0, 0, 0]
        parts.append(jnp.sum(product + product.T, axis=0, keepdims=True))
    orbital = jnp.concatenate(parts, axis=0) + row_part[...] + ((c1[...] + c2[...]) + (c3[...] + c4[...]))
    forces = lax.dot_general(
        orbital, members[...], (((1,), (1,)), ((), ())), precision=lax.Precision.HIGHEST, preferred_element_type=f32
    )
    for direction in range(3):
        forces_ref[direction] = forces[direction : direction + 1]
    for copy in copies:
        copy.wait()


def call(kernel, shapes, in_specs, products, args, out_specs=None, scratch=(), aliases={}):
    moved = sum(4 * x.size for x in args) + sum(4 * x.size for x in shapes)
    return pl.pallas_call(
        kernel,
        out_shape=shapes,
        in_specs=in_specs,
        out_specs=out_specs or [vmem] * len(shapes),
        scratch_shapes=scratch,
        input_output_aliases=aliases,
        compiler_params=pltpu.CompilerParams(vmem_limit_bytes=32 * 2**20),
        cost_estimate=pl.CostEstimate(flops=products * 6 * B**3, bytes_accessed=moved, transcendentals=0),
    )(*args)


def local(hamiltonian, inverse_margin, density, cutoff, derivative, atom_of):
    def shape(*dims, kind=f32):
        return jax.ShapeDtypeStruct(dims, kind)

    dma = pltpu.SemaphoreType.DMA
    first = call(
        first_kernel,
        [shape(2, B, B)] * 2 + [shape(5, B, B)],
        [smem, vmem],
        0,
        (cutoff, hamiltonian),
    )
    ham_x = [shifted(first[offset - 1], offset) for offset in (1, 2)]
    send, send_three, send_four, left_high, left_low, start, members = call(
        second_kernel,
        [shape(3, B, B), shape(8, B, B), shape(8, B, B)]
        + [shape(3 * B, 5 * B, kind=bf16)] * 2
        + [shape(3 * B, 5 * B), shape(ATOMS, B)],
        [smem] + [vmem] * 4,
        15,
        (cutoff, inverse_margin, density, atom_of, first[2]),
        scratch=[pltpu.VMEM((B, 5 * B), bf16)] * 2,
    )
    near_y = [shifted(send_three, 3), shifted(send_four, 4)]
    zero_x = [shifted(send, offset) for offset in (1, 2)]
    pair = [shape(3 * B, 2 * B, kind=bf16)] * 2
    high_x, low_x, diagonal = call(
        third_kernel, pair + [shape(3 * B, B)], [vmem] * 5, 6000, (left_high, left_low, start, *ham_x)
    )
    send_one, send_two, high_y, low_y, base = call(
        fourth_kernel,
        [shape(3, B, B)] * 2 + pair + [shape(2, B, 5 * B)],
        [smem] + [vmem] * 8,
        32,
        (cutoff, inverse_margin, density, left_high, left_low, start, diagonal, *near_y),
    )
    back_x = [shifted(send_one, 1), shifted(send_two, 2)]
    fifth = call(
        fifth_kernel,
        [shape(*density.shape), shape(3, B)] + [shape(3, B)] * 4,
        [smem] + [vmem] * 11,
        16,
        (cutoff, density, derivative, base, high_x, low_x, high_y, low_y, *zero_x, *near_y),
        out_specs=[hbm] + [vmem] * 5,
        scratch=[pltpu.VMEM((2, 4, B, B), f32), dma((2, 4))],
    )
    columns = [shifted(fifth[offset + 1], opposite[offset]) for offset in range(1, 5)]
    args = (density, derivative, members, base, high_x, low_x, high_y, low_y, fifth[1], *back_x, *near_y, *columns, fifth[0])
    new_density, forces = call(
        sixth_kernel,
        [shape(*density.shape), shape(3, 1, ATOMS)],
        [vmem] * 17 + [hbm],
        16,
        args,
        out_specs=[hbm, vmem],
        scratch=[pltpu.VMEM((2, B, B), f32), dma((2,))],
        aliases={17: 0},
    )
    return new_density, forces.reshape(1, 1, 3, ATOMS)


def solution(mesh):
    placed = (
        P("gx", "gy", None, None, None),
        P("gx", "gy", None, None, None),
        P(None, "gx", "gy", None, None, None),
        P("gx", "gy", None),
        P(None, "gx", "gy", None, None, None),
        P("gx", "gy", None),
    )
    return jax.shard_map(
        local,
        mesh=mesh,
        in_specs=placed,
        out_specs=(P(None, "gx", "gy", None, None, None), P("gx", "gy", None, None)),
        check_vma=False,
    )
```

time: 53.2 us -> 49.9 us (0.938)
  the two profiles are of different devices: /device:TPU:1 before, /device:TPU:0 now
where the time goes in v2:
time: 49.9 us; the launch traced here: 49.7 us
  starting transfers between devices  21.9 us (44%)
  waiting for transfers between devices  15.9 us (32%)
  Pallas kernels  7.79 us (16%)
  local copies, waits for them, and re-layouts  3.41 us (7%)
  between operations  0.72 us (1%)
    ppermute x12, starting transfers between devices, shifted(): return lax.ppermute(cells, axis, pairs)  21.9 us
    ppermute x12, waiting for transfers between devices, shifted(): return lax.ppermute(cells, axis, pairs)  15.9 us
    pallas_call x6, Pallas kernels, call(): pl.pallas_call(kernel, out_shape=shapes, in_specs=in_specs, out_specs=out...  7.79 us
    unnamed x14, local copies, waits for them, and re-layouts  3.41 us
  transfers between devices with their start and end apart: 12, of which 6 were waited for; matrix products, arithmetic and copies ran while one was open for 0% of the time, Pallas kernels for 11%

profile of v2, /device:TPU:0, one launch (start us, length us, event | category | flops | bytes accessed | tf_op | source)
XLA Modules:
  0.0 49.7 jit_solution(5860175780337339410)
XLA Ops:
  0.6 0.0 copy-start.3
  0.6 0.0 copy-start.4
  0.6 1.0 %copy-done.4 = f32[1,1,5,128,128]{4,3,2,1,0:T(8,128)S(1)} copy-done((f32[1,1,5,128,128]{4,3,2,1,0:T(8,128)S(1)}, f32[1,1,5,128,128]{4,3,2,1,0:T(8,128)}, u32[]{:S(2)}) %copy-start.4) | copy-done | bytes 327704
  1.7 0.0 copy-start.5
  1.7 0.7 %copy-done.5 = s32[1,1,5]{2,1,0:T(1,128)S(1)} copy-done((s32[1,1,5]{2,1,0:T(1,128)S(1)}, s32[1,1,5]{2,1,0:T(1,128)}, u32[]{:S(2)}) %copy-start.5) | copy-done | bytes 44
  2.3 0.6 %shard_map.77 = (f32[2,128,128]{2,1,0:T(8,128)S(1)}, f32[2,128,128]{2,1,0:T(8,128)S(1)}, f32[5,128,128]{2,1,0:T(8,128)S(1)}) custom-call(s32[1,1,5]{2,1,0:T(1,128)S(1)} %copy-done.5, f32[1,1,5,128,128]{4,3,2,1,0:T(8,128)S(1)} %copy-done.4), custom_call_target="tpu_custom_call" | custom-call | bytes 917524 | tf_op jit(solution)/shard_map/pallas_call | solution.py:203
  2.9 6.1 %collective-permute-start = (f32[2,128,128]{2,1,0:T(8,128)S(1)}, f32[2,128,128]{2,1,0:T(8,128)S(1)}, u32[]{:S(2)}, u32[]{:S(2)}) collective-permute-start(f32[2,128,128]{2,1,0:T(8,128)S(1)} %get-tuple-element.33), channel_id=1, source_target_pairs={{4,0},{8,4},{12,8},{16,12},{20,16},{24,20},{28,24},{0,28},{5,1},{9... | collective-permute-start | bytes 393224 | tf_op jit(solution)/shard_map/ppermute | solution.py:27
  9.0 0.0 copy-start.6
  9.0 0.0 collective-permute-start.1
  9.0 0.0 copy-done.3
  9.0 0.6 %copy-done.6 = s32[1,1,128]{2,1,0:T(1,128)S(1)} copy-done((s32[1,1,128]{2,1,0:T(1,128)S(1)}, s32[1,1,128]{2,1,0:T(1,128)}, u32[]{:S(2)}) %copy-start.6) | copy-done | bytes 536
  9.6 0.0 copy-start
  9.6 1.1 %copy-done = f32[2,1,1,5,128,128]{5,4,3,2,1,0:T(8,128)S(1)} copy-done((f32[2,1,1,5,128,128]{5,4,3,2,1,0:T(8,128)S(1)}, f32[2,1,1,5,128,128]{5,4,3,2,1,0:T(8,128)}, u32[]{:S(2)}) %copy-start) | copy-done | bytes 655384
  10.7 1.3 %shard_map.78 = (f32[3,128,128]{2,1,0:T(8,128)S(1)}, f32[8,128,128]{2,1,0:T(8,128)S(1)}, f32[8,128,128]{2,1,0:T(8,128)S(1)}, bf16[384,640]{1,0:T(8,128)(2,1)S(1)...) custom-call(s32[1,1,5]{2,1,0:T(1,128)S(1)} %copy-done.5, ...), custom_call_target="tpu_custom_call" | custom-call | flops 188743680 | bytes 5538324 | tf_op jit(solution)/shard_map/pallas_call | solution.py:203
  12.0 4.1 %collective-permute-start.4 = (f32[3,128,128]{2,1,0:T(8,128)S(1)}, f32[3,128,128]{2,1,0:T(8,128)S(1)}, u32[]{:S(2)}, u32[]{:S(2)}) collective-permute-start(f32[3,128,128]{2,1,0:T(8,128)S(1)} %get-tuple-element.43), channel_id=1, source_target_pairs={{4,0},{8,4},{12,8},{16,12},{20,16},{24,20},{28,24},{0,28},{5,1},{9... | collective-permute-start | bytes 589832 | tf_op jit(solution)/shard_map/ppermute | solution.py:27
  16.2 0.0 collective-permute-start.5
  16.2 0.1 collective-permute-start.2
  16.3 0.0 collective-permute-done.one
  16.3 0.4 collective-permute-start.3
  16.7 0.4 collective-permute-done.1.two
  17.1 0.0 copy-start.1
  17.1 0.5 shard_map.79
  17.6 10.1 %collective-permute-done.2.three = f32[8,128,128]{2,1,0:T(8,128)S(1)} collective-permute-done((f32[8,128,128]{2,1,0:T(8,128)S(1)}, f32[8,128,128]{2,1,0:T(8,128)S(1)}, u32[]{:S(2)}, u32[]{:S(2)}) %collective-permute-start.2) | collective-permute-done | bytes 524320 | tf_op jit(solution)/shard_map/ppermute | solution.py:27
  27.7 2.7 %collective-permute-done.3.four = f32[8,128,128]{2,1,0:T(8,128)S(1)} collective-permute-done((f32[8,128,128]{2,1,0:T(8,128)S(1)}, f32[8,128,128]{2,1,0:T(8,128)S(1)}, u32[]{:S(2)}, u32[]{:S(2)}) %collective-permute-start.3) | collective-permute-done | bytes 524320 | tf_op jit(solution)/shard_map/ppermute | solution.py:27
  30.4 0.0 copy-done.1
  30.4 0.0 copy-start.2
  30.4 1.6 %shard_map.80 = (f32[3,128,128]{2,1,0:T(8,128)S(1)}, f32[3,128,128]{2,1,0:T(8,128)S(1)}, bf16[384,256]{1,0:T(8,128)(2,1)S(1)}, bf16[384,256]{1,0:T(8,128)(2,1)S(1)}, f32[2,128,640]{2,1,0:T(8,128)S(1)}) custom-call(s32[1,1,5]{2,1,0:T(1,128)S(1)} %copy-done.5, f32[1,1,5,128,128]{4,3,2,1,0:T(8,128)S(1)} %copy-done.3, f32[2,1,1,5,128,128]{5,4,3,2,1,0:T(8,128)S(1)} %copy-done.1, ...), custom_call_target="tpu_custom_call" | custom-call | flops 402653184 | bytes 7012372 | tf_op jit(solution)/shard_map/pallas_call | solution.py:203
  32.1 4.7 %collective-permute-start.6 = (f32[3,128,128]{2,1,0:T(8,128)S(1)}, f32[3,128,128]{2,1,0:T(8,128)S(1)}, u32[]{:S(2)}, u32[]{:S(2)}) collective-permute-start(f32[3,128,128]{2,1,0:T(8,128)S(1)} %get-tuple-element.45), channel_id=1, source_target_pairs={{4,0},{8,4},{12,8},{16,12},{20,16},{24,20},{28,24},{0,28},{5,1},{9... | collective-permute-start | bytes 589832 | tf_op jit(solution)/shard_map/ppermute | solution.py:27
  36.8 0.0 collective-permute-start.7
  36.8 0.0 collective-permute-done.4.one
  36.8 0.0 collective-permute-done.5.two
  36.8 0.0 copy-done.2
  36.8 1.9 %shard_map.81 = (f32[2,1,1,5,128,128]{5,4,3,2,1,0:T(8,128)}, f32[3,128]{1,0:T(4,128)S(1)}, f32[3,128]{1,0:T(4,128)S(1)}, f32[3,128]{1,0:T(4,128)S(1)}, f32[3,128]{1,0:T(4,128)S(1)}, /*index=5*/f32[3,128]{1,0:T(4,128)S(1)}) custom-call(s32[1,1,5]{2,1,0:T(1,128)S(1)} %copy-done.5, f32[2,1,1,5,128,128]{5,4,3,2,1,0:T(8,128)S(1)} %copy-done.1, ...), custom_call_target="tpu_custom_call" | custom-call | flops 201326592 | bytes 5971476 | tf_op jit(solution)/shard_map/pallas_call | solution.py:203
  38.7 0.1 collective-permute-start.10
  38.8 1.7 %collective-permute-start.11 = (f32[3,128]{1,0:T(4,128)S(1)}, f32[3,128]{1,0:T(4,128)S(1)}, u32[]{:S(2)}, u32[]{:S(2)}) collective-permute-start(f32[3,128]{1,0:T(4,128)S(1)} %get-tuple-element.50), channel_id=1, source_target_pairs={{1,0},{2,1},{3,2},{0,3},{5,4},{6,5},{7,6},{4,7},{9,8},{10,9},{11,1... | collective-permute-start | bytes 4616 | tf_op jit(solution)/shard_map/ppermute | solution.py:27
  40.5 0.0 collective-permute-start.8
  40.5 1.3 %collective-permute-done.10.c3 = f32[3,128]{1,0:T(4,128)S(1)} collective-permute-done((f32[3,128]{1,0:T(4,128)S(1)}, f32[3,128]{1,0:T(4,128)S(1)}, u32[]{:S(2)}, u32[]{:S(2)}) %collective-permute-start.10) | collective-permute-done | bytes 1568 | tf_op jit(solution)/shard_map/ppermute | solution.py:27
  41.8 4.7 %collective-permute-start.9 = (f32[3,128]{1,0:T(4,128)S(1)}, f32[3,128]{1,0:T(4,128)S(1)}, u32[]{:S(2)}, u32[]{:S(2)}) collective-permute-start(f32[3,128]{1,0:T(4,128)S(1)} %get-tuple-element.48), channel_id=1, source_target_pairs={{4,0},{8,4},{12,8},{16,12},{20,16},{24,20},{28,24},{0,28},{5,1},{9... | collective-permute-start | bytes 4616 | tf_op jit(solution)/shard_map/ppermute | solution.py:27
  46.5 0.0 collective-permute-done.11.c4
  46.5 0.3 collective-permute-done.8.c1
  46.8 1.0 %collective-permute-done.9.c2 = f32[3,128]{1,0:T(4,128)S(1)} collective-permute-done((f32[3,128]{1,0:T(4,128)S(1)}, f32[3,128]{1,0:T(4,128)S(1)}, u32[]{:S(2)}, u32[]{:S(2)}) %collective-permute-start.9) | collective-permute-done | bytes 1568 | tf_op jit(solution)/shard_map/ppermute | solution.py:27
  47.8 0.0 collective-permute-done.6.one
  47.8 0.0 collective-permute-done.7.two
  47.8 1.9 %shard_map.82 = (f32[2,1,1,5,128,128]{5,4,3,2,1,0:T(8,128)}, f32[3,1,64]{2,1,0:T(1,128)}) custom-call(f32[2,1,1,5,128,128]{5,4,3,2,1,0:T(8,128)S(1)} %copy-done.1, f32[3,1,1,5,128,128]{5,4,3,2,1,0:T(8,128)S(1)} %copy-done.2, f32[64,128]{1,0:T(8,128)S(1)} %get-tuple-element.29.members, ...), custom_call_target="tpu_custom_call", output_to_operand_aliasing={{0}: (17, {})} | custom-call | flops 201326592 | bytes 6660352 | tf_op jit(solution)/shard_map/pallas_call | solution.py:203
Async XLA Ops:
  0.6 8.3 %copy-start.3 = (f32[1,1,5,128,128]{4,3,2,1,0:T(8,128)S(1)}, f32[1,1,5,128,128]{4,3,2,1,0:T(8,128)}, u32[]{:S(2)}) copy-start(f32[1,1,5,128,128]{4,3,2,1,0:T(8,128)} %inv_ref.3) | copy-start | bytes 983044
  0.6 1.0 %copy-start.4 = (f32[1,1,5,128,128]{4,3,2,1,0:T(8,128)S(1)}, f32[1,1,5,128,128]{4,3,2,1,0:T(8,128)}, u32[]{:S(2)}) copy-start(f32[1,1,5,128,128]{4,3,2,1,0:T(8,128)} %ham_ref.1) | copy-start | bytes 983044
  1.7 0.7 %copy-start.5 = (s32[1,1,5]{2,1,0:T(1,128)S(1)}, s32[1,1,5]{2,1,0:T(1,128)}, u32[]{:S(2)}) copy-start(s32[1,1,5]{2,1,0:T(1,128)} %cutoff_ref.7) | copy-start | bytes 64
  2.9 13.4 %collective-permute-start = (f32[2,128,128]{2,1,0:T(8,128)S(1)}, f32[2,128,128]{2,1,0:T(8,128)S(1)}, u32[]{:S(2)}, u32[]{:S(2)}) collective-permute-start(f32[2,128,128]{2,1,0:T(8,128)S(1)} %get-tuple-element.33), channel_id=1, source_target_pairs={{4,0},{8,4},{12,8},{16,12},{20,16},{24,20},{28,24},{0,28},{5,1},{9... | collective-permute-start | bytes 393224 | tf_op jit(solution)/shard_map/ppermute | solution.py:27
  9.0 0.7 %copy-start.6 = (s32[1,1,128]{2,1,0:T(1,128)S(1)}, s32[1,1,128]{2,1,0:T(1,128)}, u32[]{:S(2)}) copy-start(s32[1,1,128]{2,1,0:T(1,128)} %atom_ref.1) | copy-start | bytes 1540
  9.0 8.1 %collective-permute-start.1 = (f32[2,128,128]{2,1,0:T(8,128)S(1)}, f32[2,128,128]{2,1,0:T(8,128)S(1)}, u32[]{:S(2)}, u32[]{:S(2)}) collective-permute-start(f32[2,128,128]{2,1,0:T(8,128)S(1)} %get-tuple-element.34), channel_id=1, source_target_pairs={{0,4},{4,8},{8,12},{12,16},{16,20},{20,24},{24,28},{28,0},{1,5},{5... | collective-permute-start | bytes 393224 | tf_op jit(solution)/shard_map/ppermute | solution.py:27
  9.6 1.1 %copy-start = (f32[2,1,1,5,128,128]{5,4,3,2,1,0:T(8,128)S(1)}, f32[2,1,1,5,128,128]{5,4,3,2,1,0:T(8,128)}, u32[]{:S(2)}) copy-start(f32[2,1,1,5,128,128]{5,4,3,2,1,0:T(8,128)} %rho_ref.7) | copy-start | bytes 1966084
  12.0 24.8 %collective-permute-start.4 = (f32[3,128,128]{2,1,0:T(8,128)S(1)}, f32[3,128,128]{2,1,0:T(8,128)S(1)}, u32[]{:S(2)}, u32[]{:S(2)}) collective-permute-start(f32[3,128,128]{2,1,0:T(8,128)S(1)} %get-tuple-element.43), channel_id=1, source_target_pairs={{4,0},{8,4},{12,8},{16,12},{20,16},{24,20},{28,24},{0,28},{5,1},{9... | collective-permute-start | bytes 589832 | tf_op jit(solution)/shard_map/ppermute | solution.py:27
  16.2 20.6 %collective-permute-start.5 = (f32[3,128,128]{2,1,0:T(8,128)S(1)}, f32[3,128,128]{2,1,0:T(8,128)S(1)}, u32[]{:S(2)}, u32[]{:S(2)}) collective-permute-start(f32[3,128,128]{2,1,0:T(8,128)S(1)} %get-tuple-element.43), channel_id=1, source_target_pairs={{0,4},{4,8},{8,12},{12,16},{16,20},{20,24},{24,28},{28,0},{1,5},{5... | collective-permute-start | bytes 589832 | tf_op jit(solution)/shard_map/ppermute | solution.py:27
  16.2 11.5 %collective-permute-start.2 = (f32[8,128,128]{2,1,0:T(8,128)S(1)}, f32[8,128,128]{2,1,0:T(8,128)S(1)}, u32[]{:S(2)}, u32[]{:S(2)}) collective-permute-start(f32[8,128,128]{2,1,0:T(8,128)S(1)} %get-tuple-element.36), channel_id=1, source_target_pairs={{1,0},{2,1},{3,2},{0,3},{5,4},{6,5},{7,6},{4,7},{9,8},{10,9},{11,1... | collective-permute-start | bytes 1572872 | tf_op jit(solution)/shard_map/ppermute | solution.py:27
  16.3 14.2 %collective-permute-start.3 = (f32[8,128,128]{2,1,0:T(8,128)S(1)}, f32[8,128,128]{2,1,0:T(8,128)S(1)}, u32[]{:S(2)}, u32[]{:S(2)}) collective-permute-start(f32[8,128,128]{2,1,0:T(8,128)S(1)} %get-tuple-element.37), channel_id=1, source_target_pairs={{0,1},{1,2},{2,3},{3,0},{4,5},{5,6},{6,7},{7,4},{8,9},{9,10},{10,1... | collective-permute-start | bytes 1572872 | tf_op jit(solution)/shard_map/ppermute | solution.py:27
  17.1 13.4 %copy-start.1 = (f32[2,1,1,5,128,128]{5,4,3,2,1,0:T(8,128)S(1)}, f32[2,1,1,5,128,128]{5,4,3,2,1,0:T(8,128)}, u32[]{:S(2)}) copy-start(f32[2,1,1,5,128,128]{5,4,3,2,1,0:T(8,128)} %rho_ref.7) | copy-start | bytes 1966084
  30.4 6.4 %copy-start.2 = (f32[3,1,1,5,128,128]{5,4,3,2,1,0:T(8,128)S(1)}, f32[3,1,1,5,128,128]{5,4,3,2,1,0:T(8,128)}, u32[]{:S(2)}) copy-start(f32[3,1,1,5,128,128]{5,4,3,2,1,0:T(8,128)} %der_ref.3) | copy-start | bytes 2949124
  32.1 15.7 %collective-permute-start.6 = (f32[3,128,128]{2,1,0:T(8,128)S(1)}, f32[3,128,128]{2,1,0:T(8,128)S(1)}, u32[]{:S(2)}, u32[]{:S(2)}) collective-permute-start(f32[3,128,128]{2,1,0:T(8,128)S(1)} %get-tuple-element.45), channel_id=1, source_target_pairs={{4,0},{8,4},{12,8},{16,12},{20,16},{24,20},{28,24},{0,28},{5,1},{9... | collective-permute-start | bytes 589832 | tf_op jit(solution)/shard_map/ppermute | solution.py:27
  36.8 11.0 %collective-permute-start.7 = (f32[3,128,128]{2,1,0:T(8,128)S(1)}, f32[3,128,128]{2,1,0:T(8,128)S(1)}, u32[]{:S(2)}, u32[]{:S(2)}) collective-permute-start(f32[3,128,128]{2,1,0:T(8,128)S(1)} %get-tuple-element.46), channel_id=1, source_target_pairs={{0,4},{4,8},{8,12},{12,16},{16,20},{20,24},{24,28},{28,0},{1,5},{5... | collective-permute-start | bytes 589832 | tf_op jit(solution)/shard_map/ppermute | solution.py:27
  38.7 3.1 %collective-permute-start.10 = (f32[3,128]{1,0:T(4,128)S(1)}, f32[3,128]{1,0:T(4,128)S(1)}, u32[]{:S(2)}, u32[]{:S(2)}) collective-permute-start(f32[3,128]{1,0:T(4,128)S(1)} %get-tuple-element.49), channel_id=1, source_target_pairs={{0,1},{1,2},{2,3},{3,0},{4,5},{5,6},{6,7},{7,4},{8,9},{9,10},{10,1... | collective-permute-start | bytes 4616 | tf_op jit(solution)/shard_map/ppermute | solution.py:27
  38.8 7.7 %collective-permute-start.11 = (f32[3,128]{1,0:T(4,128)S(1)}, f32[3,128]{1,0:T(4,128)S(1)}, u32[]{:S(2)}, u32[]{:S(2)}) collective-permute-start(f32[3,128]{1,0:T(4,128)S(1)} %get-tuple-element.50), channel_id=1, source_target_pairs={{1,0},{2,1},{3,2},{0,3},{5,4},{6,5},{7,6},{4,7},{9,8},{10,9},{11,1... | collective-permute-start | bytes 4616 | tf_op jit(solution)/shard_map/ppermute | solution.py:27
  40.5 6.3 %collective-permute-start.8 = (f32[3,128]{1,0:T(4,128)S(1)}, f32[3,128]{1,0:T(4,128)S(1)}, u32[]{:S(2)}, u32[]{:S(2)}) collective-permute-start(f32[3,128]{1,0:T(4,128)S(1)} %get-tuple-element.47), channel_id=1, source_target_pairs={{0,4},{4,8},{8,12},{12,16},{16,20},{20,24},{24,28},{28,0},{1,5},{5... | collective-permute-start | bytes 4616 | tf_op jit(solution)/shard_map/ppermute | solution.py:27
  41.8 6.0 %collective-permute-start.9 = (f32[3,128]{1,0:T(4,128)S(1)}, f32[3,128]{1,0:T(4,128)S(1)}, u32[]{:S(2)}, u32[]{:S(2)}) collective-permute-start(f32[3,128]{1,0:T(4,128)S(1)} %get-tuple-element.48), channel_id=1, source_target_pairs={{4,0},{8,4},{12,8},{16,12},{20,16},{24,20},{28,24},{0,28},{5,1},{9... | collective-permute-start | bytes 4616 | tf_op jit(solution)/shard_map/ppermute | solution.py:27

commit v3 on v2

v3 whole, which is shorter than its diff:
```python
import jax
import jax.numpy as jnp
from jax import lax
from jax.experimental import pallas as pl
from jax.experimental.pallas import tpu as pltpu
from jax.sharding import PartitionSpec as P

B = 128
ATOMS = 64

time_step = 0.25
vmem = pl.BlockSpec(memory_space=pltpu.VMEM)
hbm = pl.BlockSpec(memory_space=pltpu.HBM)
f32 = jnp.float32
bf16 = jnp.bfloat16
dma = pltpu.SemaphoreType.DMA


def swapped(cells, edge):
    axis = "gx" if edge < 3 else "gy"
    count = lax.axis_size(axis)
    assert count % 2 == 0
    first = 0 if edge in (1, 3) else 1
    pairs = []
    for i in range(first, count, 2):
        j = (i + 1) % count
        pairs += [(i, j), (j, i)]
    return lax.ppermute(cells, axis, pairs)


def order_of():
    odd_x = lax.rem(lax.axis_index("gx"), 2)
    odd_y = lax.rem(lax.axis_index("gy"), 2)
    return 0, 1 + odd_x, 2 - odd_x, 3 + odd_y, 4 - odd_y


def cols(place, count=1):
    return slice(place * B, (place + count) * B)


def split(values):
    high = values.astype(bf16)
    return high, (values - high.astype(f32)).astype(bf16)


def beside(*pairs):
    return tuple(jnp.concatenate(parts, axis=1) for parts in zip(*pairs))


def dot(left, right):
    def one(a, b):
        return jnp.dot(a, b, preferred_element_type=f32)

    return one(left[0], right[0]) + (one(left[0], right[1]) + one(left[1], right[0]))


def part(pair, rows, columns):
    return pair[0][rows, columns], pair[1][rows, columns]


def rows_of(pair):
    return (pair[0][:B], pair[1][:B]), (pair[0][B:], pair[1][B:])


def store(pair, columns, values):
    pair[0][:, columns], pair[1][:, columns] = values


def start_all(copies):
    for copy in copies:
        copy.start()
    return copies


def first_kernel(cutoff_hbm, ham_hbm, inv_hbm, rho_hbm, one, cutoff_ref, cutoff_sem, sems):
    flags = pltpu.make_async_copy(cutoff_hbm, cutoff_ref, cutoff_sem)
    flags.start()
    offset = order_of()[1]
    sources = (ham_hbm.at[0, 0, offset], ham_hbm.at[0, 0, 0], inv_hbm.at[0, 0, 0], rho_hbm.at[0, 0, 0, 0], rho_hbm.at[1, 0, 0, 0])
    copies = start_all(
        [pltpu.make_async_copy(source, one.at[(at + 4) % 5], sems.at[at]) for at, source in enumerate(sources)]
    )
    flags.wait()
    copies[0].wait()
    one[4] = one[4] * cutoff_ref[0, 0, offset].astype(f32)
    for copy in copies[1:]:
        copy.wait()


def second_kernel(
    cutoff_hbm, ham_hbm, inv_hbm, rho_hbm, atom_hbm, after, two, three, four, held, left_high, left_low, ham_high, ham_low, members,
    raw, cutoff_ref, atom_ref, cutoff_sem, atom_sem, sems
):
    flags = pltpu.make_async_copy(cutoff_hbm, cutoff_ref, cutoff_sem)
    flags.start()
    sources = (ham_hbm.at[0, 0], inv_hbm.at[0, 0], rho_hbm.at[0, 0, 0], rho_hbm.at[1, 0, 0])
    copies = start_all([pltpu.make_async_copy(source, raw.at[at], sems.at[at]) for at, source in enumerate(sources)])
    owners = pltpu.make_async_copy(atom_hbm, atom_ref, atom_sem)
    owners.start()
    order = order_of()
    flags.wait()
    keeps = [cutoff_ref[0, 0, offset].astype(f32) for offset in order]
    for kind, copy in enumerate(copies):
        copy.wait()
        for place, offset in enumerate(order):
            block = raw[kind, offset]
            if place == 0:
                for message in (two, three, four):
                    message[kind] = block
            else:
                block = block * keeps[place]
                if place > 2 or (place == 2 and kind == 0):
                    (two, three, four)[place - 2][4 + kind] = block
            if kind == 0:
                store((ham_high, ham_low), cols(place), split(block))
            else:
                held[kind - 1, place] = block
                rows = slice((kind - 1) * B, kind * B)
                left_high[rows, cols(place)], left_low[rows, cols(place)] = split(block)
    owners.wait()
    atoms = jnp.broadcast_to(atom_ref[0], (ATOMS, B))
    members[...] = -(lax.broadcasted_iota(jnp.int32, (ATOMS, B), 0) == atoms).astype(f32)


def edge(left, begun, near_zero, near_back):
    both = dot(left, beside(split(near_zero), split(near_back)))
    return split(begun + both[:, :B]), both[:, B:]


def commutators(mixed, invs, reals, imags):
    prop, inner = rows_of(mixed)
    count = len(reals)
    ahead = dot(prop, beside(*[split(x) for x in (*reals, *imags)]))
    behind = dot(inner, beside(*[split(x) for x in invs]))
    real = [ahead[:, cols(at)] - behind[:B, cols(at)] for at in range(count)]
    imag = [ahead[:, cols(count + at)] - behind[B:, cols(at)] for at in range(count)]
    return real, imag


def third_kernel(left_high, left_low, ham_high, ham_low, one, start, mixed_high, mixed_low, diagonal, other):
    left = (left_high, left_low)
    every = slice(0, 3 * B)
    begun = dot(part(left, every, cols(0)), part((ham_high, ham_low), slice(0, B), cols(0, 5)))
    start[...] = begun
    mixed, added = edge(part(left, every, cols(1)), begun[:, cols(1)], one[0], one[4])
    diagonal[...] = begun[:, cols(0)] + added
    mixed_high[...], mixed_low[...] = mixed
    (real,), (imag,) = commutators(mixed, (one[1],), (one[2],), (one[3],))
    other[0], other[1] = real, imag


def fourth_kernel(left_high, left_low, start, diagonal, held, three, four, one_more, two_more, diagonal_out, other):
    for kind in range(3):
        one_more[kind] = held[kind, 1]
        two_more[kind] = held[kind, 2]
    total = diagonal[...]
    for place, near in ((3, three), (4, four)):
        here = part((left_high, left_low), slice(0, 3 * B), cols(place))
        mixed, added = edge(here, start[:, cols(place)], near[0], near[4])
        total = total + added
        real, imag = commutators(mixed, (near[1], near[5]), (near[2], near[6]), (near[3], near[7]))
        other[0, place - 3], other[1, place - 3] = real[0], imag[0]
        if place == 3:
            other[0, 2], other[1, 2] = real[1], imag[1]
        else:
            other[0, 2] = other[0, 2] + real[1]
            other[1, 2] = other[1, 2] + imag[1]
    diagonal_out[...] = total


def fifth_kernel(
    left_high, left_low, start, diagonal, held, der_ref, other_one, other_y, two,
    out_hbm, mixed_high, mixed_low, comm, row_part, c1, c2, c3, c4, new, sems
):
    order = order_of()
    left = (left_high, left_low)
    mixed, added = edge(part(left, slice(0, 3 * B), cols(2)), start[:, cols(2)], two[0], two[4])
    mixed_high[...], mixed_low[...] = mixed
    (real_two,), (imag_two,) = commutators(mixed, (two[1],), (two[2],), (two[3],))
    total = diagonal[...] + added
    prop, inner = rows_of(split(total))
    whole = cols(0, 5)
    behind = dot(inner, part(left, slice(0, B), whole))
    imag_comm = dot(prop, part(left, slice(2 * B, 3 * B), whole)) - behind[B:]
    real_comm = dot(prop, part(left, slice(B, 2 * B), whole)) - behind[:B]
    others = [(other_one[0], other_one[1]), (real_two, imag_two)]
    others += [(other_y[0, at], other_y[1, at]) for at in range(2)]
    comm[0] = real_comm[:, cols(0)] + other_y[0, 2]
    comm[1] = imag_comm[:, cols(0)] + other_y[1, 2]
    weighted = [jnp.zeros((B, B), f32) for _ in range(3)]
    copies = []
    for place, column in enumerate((c1, c2, c3, c4), 1):
        real, imag = others[place - 1]
        real_new = held[1, place] + time_step * (imag_comm[:, cols(place)] + imag)
        new[0, place - 1] = real_new
        new[1, place - 1] = held[2, place] - time_step * (real_comm[:, cols(place)] + real)
        copies += start_all(
            [
                pltpu.make_async_copy(new.at[at, place - 1], out_hbm.at[at, 0, 0, order[place]], sems.at[at, place - 1])
                for at in range(2)
            ]
        )
        for direction in range(3):
            product = real_new * der_ref[direction, 0, 0, order[place]]
            weighted[direction] = weighted[direction] + product
            column[direction : direction + 1, :] = jnp.sum(product, axis=0, keepdims=True)
    for direction in range(3):
        row_part[direction : direction + 1, :] = jnp.sum(weighted[direction].T, axis=0, keepdims=True)
    for copy in copies:
        copy.wait()


def sixth_kernel(
    held, der_ref, members, high_one, low_one, high_two, low_two, comm, row_part, one, two, c1, c2, c3, c4, old_hbm, out_hbm, forces_ref, new, sems
):
    prop, inner = rows_of(beside((high_one[...], low_one[...]), (high_two[...], low_two[...])))
    near = [tuple(jnp.concatenate(x, axis=0) for x in zip(split(one[kind]), split(two[kind]))) for kind in range(3)]
    behind = dot(inner, near[0])
    ahead = dot(prop, beside(near[2], near[1]))
    real_new = held[1, 0] + time_step * (comm[1] + ahead[:, :B] - behind[B:])
    new[0] = real_new
    new[1] = held[2, 0] - time_step * (comm[0] + ahead[:, B:] - behind[:B])
    copies = start_all([pltpu.make_async_copy(new.at[at], out_hbm.at[at, 0, 0, 0], sems.at[at]) for at in range(2)])
    parts = []
    for direction in range(3):
        product = real_new * der_ref[direction, 0, 0, 0]
        parts.append(jnp.sum(product + product.T, axis=0, keepdims=True))
    orbital = jnp.concatenate(parts, axis=0) + row_part[...] + ((c1[...] + c2[...]) + (c3[...] + c4[...]))
    forces = lax.dot_general(
        orbital, members[...], (((1,), (1,)), ((), ())), precision=lax.Precision.HIGHEST, preferred_element_type=f32
    )
    for direction in range(3):
        forces_ref[direction] = forces[direction : direction + 1]
    for copy in copies:
        copy.wait()


def call(kernel, shapes, in_specs, products, args, out_specs=None, scratch=(), aliases={}):
    moved = sum(4 * x.size for x in args) + sum(4 * x.size for x in shapes)
    return pl.pallas_call(
        kernel,
        out_shape=shapes,
        in_specs=in_specs,
        out_specs=out_specs or [vmem] * len(shapes),
        scratch_shapes=scratch,
        input_output_aliases=aliases,
        compiler_params=pltpu.CompilerParams(vmem_limit_bytes=32 * 2**20),
        cost_estimate=pl.CostEstimate(flops=products * 6 * B**3, bytes_accessed=moved, transcendentals=0),
    )(*args)


def local(hamiltonian, inverse_margin, density, cutoff, derivative, atom_of):
    def shape(*dims, kind=f32):
        return jax.ShapeDtypeStruct(dims, kind)

    hamiltonian, inverse_margin, density, cutoff, atom_of = (
        pltpu.with_memory_space_constraint(x, pltpu.HBM) for x in (hamiltonian, inverse_margin, density, cutoff, atom_of)
    )
    flags = pltpu.SMEM((1, 1, 5), jnp.int32)
    (first,) = call(
        first_kernel,
        [shape(5, B, B)],
        [hbm] * 4,
        0,
        (cutoff, hamiltonian, inverse_margin, density),
        scratch=[flags, dma(()), dma((5,))],
    )
    near_one = swapped(first, 1)
    left = [shape(3 * B, 5 * B, kind=bf16)] * 2
    ham = [shape(B, 5 * B, kind=bf16)] * 2
    send_two, send_three, send_four, held, left_high, left_low, ham_high, ham_low, members = call(
        second_kernel,
        [shape(5, B, B), shape(8, B, B), shape(8, B, B), shape(3, 5, B, B)] + left + ham + [shape(ATOMS, B)],
        [hbm] * 6,
        0,
        (cutoff, hamiltonian, inverse_margin, density, atom_of, first),
        scratch=[pltpu.VMEM((4, 5, B, B), f32), flags, pltpu.VMEM((1, 1, B), jnp.int32), dma(()), dma(()), dma((4,))],
    )
    near_four = swapped(send_four, 4)
    near_three = swapped(send_three, 3)
    near_two = swapped(send_two, 2)
    mixed = [shape(3 * B, B, kind=bf16)] * 2
    start, high_one, low_one, diagonal, other_one = call(
        third_kernel,
        [shape(3 * B, 5 * B)] + mixed + [shape(3 * B, B), shape(2, B, B)],
        [vmem] * 5,
        8000,
        (left_high, left_low, ham_high, ham_low, near_one),
    )
    one_more, two_more, diagonal, other_y = call(
        fourth_kernel,
        [shape(3, B, B)] * 2 + [shape(3 * B, B), shape(2, 3, B, B)],
        [vmem] * 7,
        28,
        (left_high, left_low, start, diagonal, held, near_three, near_four),
    )
    near_one_more = swapped(one_more, 1)
    near_two_more = swapped(two_more, 2)
    args = (left_high, left_low, start, diagonal, held, derivative, other_one, other_y, near_two)
    out, high_two, low_two, comm, row_part, *columns = call(
        fifth_kernel,
        [shape(*density.shape)] + mixed + [shape(2, B, B)] + [shape(3, B)] * 5,
        [vmem] * 9,
        30,
        args,
        out_specs=[hbm] + [vmem] * 8,
        scratch=[pltpu.VMEM((2, 4, B, B), f32), dma((2, 4))],
    )
    columns = [swapped(column, at) for at, column in enumerate(columns, 1)]
    args = (held, derivative, members, high_one, low_one, high_two, low_two, comm, row_part)
    args += (near_one_more, near_two_more, *columns, out)
    new_density, forces = call(
        sixth_kernel,
        [shape(*density.shape), shape(3, 1, ATOMS)],
        [vmem] * 15 + [hbm],
        8,
        args,
        out_specs=[hbm, vmem],
        scratch=[pltpu.VMEM((2, B, B), f32), dma((2,))],
        aliases={15: 0},
    )
    return new_density, forces.reshape(1, 1, 3, ATOMS)


def solution(mesh):
    placed = (
        P("gx", "gy", None, None, None),
        P("gx", "gy", None, None, None),
        P(None, "gx", "gy", None, None, None),
        P("gx", "gy", None),
        P(None, "gx", "gy", None, None, None),
        P("gx", "gy", None),
    )
    return jax.shard_map(
        local,
        mesh=mesh,
        in_specs=placed,
        out_specs=(P(None, "gx", "gy", None, None, None), P("gx", "gy", None, None)),
        check_vma=False,
    )
```

time: 49.9 us -> 40.9 us (0.82)
  starting transfers between devices: 21.9 us -> 14 us
  local copies, waits for them, and re-layouts: 3.41 us -> 0.01 us
  waiting for transfers between devices: 15.9 us -> 17.7 us
    ppermute x12 -> x10, starting transfers between devices: 21.9 us -> 14 us  [swapped(): return lax.ppermute(cells, axis, pairs)]
    unnamed x14 -> x2, local copies, waits for them, and re-layouts: 3.41 us -> 0.01 us
    ppermute x12 -> x10, waiting for transfers between devices: 15.9 us -> 17.7 us  [swapped(): return lax.ppermute(cells, axis, pairs)]
  transfers between devices with their start and end apart: 12 -> 10, of which waited for: 6 -> 4; matrix products, arithmetic and copies ran while one was open for 0% -> 0% of each run, Pallas kernels for 11% -> 14%
where the time goes in v3:
time: 40.9 us; the launch traced here: 40.7 us
  waiting for transfers between devices  17.7 us (43%)
  starting transfers between devices  14 us (34%)
  Pallas kernels  8.23 us (20%)
  between operations  0.69 us (2%)
    ppermute x10, waiting for transfers between devices, swapped(): return lax.ppermute(cells, axis, pairs)  17.7 us
    ppermute x10, starting transfers between devices, swapped(): return lax.ppermute(cells, axis, pairs)  14 us
    pallas_call x6, Pallas kernels, call(): pl.pallas_call(kernel, out_shape=shapes, in_specs=in_specs, out_specs=out...  8.23 us
  transfers between devices with their start and end apart: 10, of which 4 were waited for; matrix products, arithmetic and copies ran while one was open for 0% of the time, Pallas kernels for 14%

profile of v3, /device:TPU:0, one launch (start us, length us, event | category | flops | bytes accessed | tf_op | source)
XLA Modules:
  0.0 40.7 jit_solution(1380218981404977910)
XLA Ops:
  0.6 1.0 %shard_map.77.after = f32[5,128,128]{2,1,0:T(8,128)S(1)} custom-call(s32[1,1,5]{2,1,0:T(1,128)} %cutoff_hbm.3, f32[1,1,5,128,128]{4,3,2,1,0:T(8,128)} %ham_hbm.3, f32[1,1,5,128,128]{4,3,2,1,0:T(8,128)} %inv_hbm.3, f32[2,1,1,5,128,128]{5,4,3,2,1,0:T(8,128)} %rho_hbm.3), custom_call_target="tpu_custom_call" | custom-call | bytes 1638420 | tf_op jit(solution)/shard_map/pallas_call | solution.py:240
  1.7 3.0 %collective-permute-start = (f32[5,128,128]{2,1,0:T(8,128)S(1)}, f32[5,128,128]{2,1,0:T(8,128)S(1)}, u32[]{:S(2)}, u32[]{:S(2)}) collective-permute-start(f32[5,128,128]{2,1,0:T(8,128)S(1)} %shard_map.77.after), channel_id=1, source_target_pairs={{0,4},{4,0},{8,12},{12,8},{16,20},{20,16},{24,28},{28,24},{1,5},{5... | collective-permute-start | bytes 983048 | tf_op jit(solution)/shard_map/ppermute | solution.py:28
  4.7 1.4 %shard_map.78 = (f32[5,128,128]{2,1,0:T(8,128)S(1)}, f32[8,128,128]{2,1,0:T(8,128)S(1)}, f32[8,128,128]{2,1,0:T(8,128)S(1)}, f32[3,5,128,128]{3,2,1,0:T(8,128)S(...) custom-call(s32[1,1,5]{2,1,0:T(1,128)} %cutoff_hbm.3, ...), custom_call_target="tpu_custom_call" | custom-call | bytes 6652436 | tf_op jit(solution)/shard_map/pallas_call | solution.py:240
  6.1 3.6 %collective-permute-start.3 = (f32[5,128,128]{2,1,0:T(8,128)S(1)}, f32[5,128,128]{2,1,0:T(8,128)S(1)}, u32[]{:S(2)}, u32[]{:S(2)}) collective-permute-start(f32[5,128,128]{2,1,0:T(8,128)S(1)} %get-tuple-element.46), channel_id=1, source_target_pairs={{4,8},{8,4},{12,16},{16,12},{20,24},{24,20},{28,0},{0,28},{5,9},{9... | collective-permute-start | bytes 983048 | tf_op jit(solution)/shard_map/ppermute | solution.py:28
  9.7 0.0 collective-permute-start.1
  9.7 1.6 %collective-permute-start.2 = (f32[8,128,128]{2,1,0:T(8,128)S(1)}, f32[8,128,128]{2,1,0:T(8,128)S(1)}, u32[]{:S(2)}, u32[]{:S(2)}) collective-permute-start(f32[8,128,128]{2,1,0:T(8,128)S(1)} %get-tuple-element.42), channel_id=1, source_target_pairs={{1,2},{2,1},{3,0},{0,3},{5,6},{6,5},{7,4},{4,7},{9,10},{10,9},{11,... | collective-permute-start | bytes 1572872 | tf_op jit(solution)/shard_map/ppermute | solution.py:28
  11.3 8.1 %collective-permute-done.one = f32[5,128,128]{2,1,0:T(8,128)S(1)} collective-permute-done((f32[5,128,128]{2,1,0:T(8,128)S(1)}, f32[5,128,128]{2,1,0:T(8,128)S(1)}, u32[]{:S(2)}, u32[]{:S(2)}) %collective-permute-start) | collective-permute-done | bytes 327712 | tf_op jit(solution)/shard_map/ppermute | solution.py:28
  19.4 1.0 %shard_map.79 = (f32[384,640]{1,0:T(8,128)S(1)}, bf16[384,128]{1,0:T(8,128)(2,1)S(1)}, bf16[384,128]{1,0:T(8,128)(2,1)S(1)}, f32[384,128]{1,0:T(8,128)S(1)}, f32[2,128,128]{2,1,0:T(8,128)S(1)}) custom-call(bf16[384,640]{1,0:T(8,128)(2,1)S(1)} %get-tuple-element.33.left_high, bf16[384,640]{1,0:T(8,128)(2,1)S(1)} %get-tuple-element.34.left_low, ...), custom_call_target="tpu_custom_call" | custom-call | flops 100663296000 | bytes 4653056 | tf_op jit(solution)/shard_map/pallas_call | solution.py:240
  20.5 0.0 collective-permute-done.1.three
  20.5 2.9 %collective-permute-done.2.four = f32[8,128,128]{2,1,0:T(8,128)S(1)} collective-permute-done((f32[8,128,128]{2,1,0:T(8,128)S(1)}, f32[8,128,128]{2,1,0:T(8,128)S(1)}, u32[]{:S(2)}, u32[]{:S(2)}) %collective-permute-start.2) | collective-permute-done | bytes 524320 | tf_op jit(solution)/shard_map/ppermute | solution.py:28
  23.3 0.0 copy-start
  23.3 1.0 %shard_map.80 = (f32[3,128,128]{2,1,0:T(8,128)S(1)}, f32[3,128,128]{2,1,0:T(8,128)S(1)}, f32[384,128]{1,0:T(8,128)S(1)}, f32[2,3,128,128]{3,2,1,0:T(8,128)S(1)}) custom-call(bf16[384,640]{1,0:T(8,128)(2,1)S(1)} %get-tuple-element.33.left_high, bf16[384,640]{1,0:T(8,128)(2,1)S(1)} %get-tuple-element.34.left_low, f32[384,640]{1,0:T(8,128)S(1)} %get-tuple-element.39.start, ...), custom_call_target="tpu_custom_call" | custom-call | flops 352321536 | bytes 6160384 | tf_op jit(solution)/shard_map/pallas_call | solution.py:240
  24.3 0.1 collective-permute-start.4
  24.4 2.4 %collective-permute-start.5 = (f32[3,128,128]{2,1,0:T(8,128)S(1)}, f32[3,128,128]{2,1,0:T(8,128)S(1)}, u32[]{:S(2)}, u32[]{:S(2)}) collective-permute-start(f32[3,128,128]{2,1,0:T(8,128)S(1)} %get-tuple-element.52), channel_id=1, source_target_pairs={{4,8},{8,4},{12,16},{16,12},{20,24},{24,20},{28,0},{0,28},{5,9},{9... | collective-permute-start | bytes 589832 | tf_op jit(solution)/shard_map/ppermute | solution.py:28
  26.9 0.0 collective-permute-done.3.two
  26.9 0.0 copy-done
  26.9 2.1 %shard_map.81 = (f32[2,1,1,5,128,128]{5,4,3,2,1,0:T(8,128)}, bf16[384,128]{1,0:T(8,128)(2,1)S(1)}, bf16[384,128]{1,0:T(8,128)(2,1)S(1)}, f32[2,128,128]{2,1,0:T(...) custom-call(bf16[384,640]{1,0:T(8,128)(2,1)S(1)} %get-tuple-element., ...), custom_call_target="tpu_custom_call" | custom-call | flops 377487360 | bytes 7151104 | tf_op jit(solution)/shard_map/pallas_call | solution.py:240
  29.0 0.1 collective-permute-start.6
  29.1 2.3 %collective-permute-start.7 = (f32[3,128]{1,0:T(4,128)S(1)}, f32[3,128]{1,0:T(4,128)S(1)}, u32[]{:S(2)}, u32[]{:S(2)}) collective-permute-start(f32[3,128]{1,0:T(4,128)S(1)} %get-tuple-element.54), channel_id=1, source_target_pairs={{4,8},{8,4},{12,16},{16,12},{20,24},{24,20},{28,0},{0,28},{5,9},{9... | collective-permute-start | bytes 4616 | tf_op jit(solution)/shard_map/ppermute | solution.py:28
  31.5 0.0 collective-permute-start.8
  31.5 4.5 %collective-permute-done.6.c1 = f32[3,128]{1,0:T(4,128)S(1)} collective-permute-done((f32[3,128]{1,0:T(4,128)S(1)}, f32[3,128]{1,0:T(4,128)S(1)}, u32[]{:S(2)}, u32[]{:S(2)}) %collective-permute-start.6) | collective-permute-done | bytes 1568 | tf_op jit(solution)/shard_map/ppermute | solution.py:28
  36.0 0.8 %collective-permute-start.9 = (f32[3,128]{1,0:T(4,128)S(1)}, f32[3,128]{1,0:T(4,128)S(1)}, u32[]{:S(2)}, u32[]{:S(2)}) collective-permute-start(f32[3,128]{1,0:T(4,128)S(1)} %get-tuple-element.56), channel_id=1, source_target_pairs={{1,2},{2,1},{3,0},{0,3},{5,6},{6,5},{7,4},{4,7},{9,10},{10,9},{11,... | collective-permute-start | bytes 4616 | tf_op jit(solution)/shard_map/ppermute | solution.py:28
  36.7 0.0 collective-permute-done.7.c2
  36.7 0.0 collective-permute-done.8.c3
  36.8 2.2 %collective-permute-done.9.c4 = f32[3,128]{1,0:T(4,128)S(1)} collective-permute-done((f32[3,128]{1,0:T(4,128)S(1)}, f32[3,128]{1,0:T(4,128)S(1)}, u32[]{:S(2)}, u32[]{:S(2)}) %collective-permute-start.9) | collective-permute-done | bytes 1568 | tf_op jit(solution)/shard_map/ppermute | solution.py:28
  39.0 0.0 collective-permute-done.4.one
  39.0 0.0 collective-permute-done.5.two
  39.0 1.7 %shard_map.82 = (f32[2,1,1,5,128,128]{5,4,3,2,1,0:T(8,128)}, f32[3,1,64]{2,1,0:T(1,128)}) custom-call(f32[3,5,128,128]{3,2,1,0:T(8,128)S(1)} %get-tuple-element.31.held, f32[3,1,1,5,128,128]{5,4,3,2,1,0:T(8,128)S(1)} %copy-done, f32[64,128]{1,0:T(8,128)S(1)} %get-tuple-element.32.members, ...), custom_call_target="tpu_custom_call", output_to_operand_aliasing={{0}: (15, {})} | custom-call | flops 100663296 | bytes 4628736 | tf_op jit(solution)/shard_map/pallas_call | solution.py:240
Async XLA Ops:
  1.7 17.8 %collective-permute-start = (f32[5,128,128]{2,1,0:T(8,128)S(1)}, f32[5,128,128]{2,1,0:T(8,128)S(1)}, u32[]{:S(2)}, u32[]{:S(2)}) collective-permute-start(f32[5,128,128]{2,1,0:T(8,128)S(1)} %shard_map.77.after), channel_id=1, source_target_pairs={{0,4},{4,0},{8,12},{12,8},{16,20},{20,16},{24,28},{28,24},{1,5},{5... | collective-permute-start | bytes 983048 | tf_op jit(solution)/shard_map/ppermute | solution.py:28
  6.1 20.7 %collective-permute-start.3 = (f32[5,128,128]{2,1,0:T(8,128)S(1)}, f32[5,128,128]{2,1,0:T(8,128)S(1)}, u32[]{:S(2)}, u32[]{:S(2)}) collective-permute-start(f32[5,128,128]{2,1,0:T(8,128)S(1)} %get-tuple-element.46), channel_id=1, source_target_pairs={{4,8},{8,4},{12,16},{16,12},{20,24},{24,20},{28,0},{0,28},{5,9},{9... | collective-permute-start | bytes 983048 | tf_op jit(solution)/shard_map/ppermute | solution.py:28
  9.7 10.7 %collective-permute-start.1 = (f32[8,128,128]{2,1,0:T(8,128)S(1)}, f32[8,128,128]{2,1,0:T(8,128)S(1)}, u32[]{:S(2)}, u32[]{:S(2)}) collective-permute-start(f32[8,128,128]{2,1,0:T(8,128)S(1)} %get-tuple-element.41), channel_id=1, source_target_pairs={{0,1},{1,0},{2,3},{3,2},{4,5},{5,4},{6,7},{7,6},{8,9},{9,8},{10,11... | collective-permute-start | bytes 1572872 | tf_op jit(solution)/shard_map/ppermute | solution.py:28
  9.7 13.6 %collective-permute-start.2 = (f32[8,128,128]{2,1,0:T(8,128)S(1)}, f32[8,128,128]{2,1,0:T(8,128)S(1)}, u32[]{:S(2)}, u32[]{:S(2)}) collective-permute-start(f32[8,128,128]{2,1,0:T(8,128)S(1)} %get-tuple-element.42), channel_id=1, source_target_pairs={{1,2},{2,1},{3,0},{0,3},{5,6},{6,5},{7,4},{4,7},{9,10},{10,9},{11,... | collective-permute-start | bytes 1572872 | tf_op jit(solution)/shard_map/ppermute | solution.py:28
  23.3 3.5 %copy-start = (f32[3,1,1,5,128,128]{5,4,3,2,1,0:T(8,128)S(1)}, f32[3,1,1,5,128,128]{5,4,3,2,1,0:T(8,128)}, u32[]{:S(2)}) copy-start(f32[3,1,1,5,128,128]{5,4,3,2,1,0:T(8,128)} %der_ref.3) | copy-start | bytes 2949124
  24.3 14.7 %collective-permute-start.4 = (f32[3,128,128]{2,1,0:T(8,128)S(1)}, f32[3,128,128]{2,1,0:T(8,128)S(1)}, u32[]{:S(2)}, u32[]{:S(2)}) collective-permute-start(f32[3,128,128]{2,1,0:T(8,128)S(1)} %get-tuple-element.51), channel_id=1, source_target_pairs={{0,4},{4,0},{8,12},{12,8},{16,20},{20,16},{24,28},{28,24},{1,5},{5... | collective-permute-start | bytes 589832 | tf_op jit(solution)/shard_map/ppermute | solution.py:28
  24.4 14.6 %collective-permute-start.5 = (f32[3,128,128]{2,1,0:T(8,128)S(1)}, f32[3,128,128]{2,1,0:T(8,128)S(1)}, u32[]{:S(2)}, u32[]{:S(2)}) collective-permute-start(f32[3,128,128]{2,1,0:T(8,128)S(1)} %get-tuple-element.52), channel_id=1, source_target_pairs={{4,8},{8,4},{12,16},{16,12},{20,24},{24,20},{28,0},{0,28},{5,9},{9... | collective-permute-start | bytes 589832 | tf_op jit(solution)/shard_map/ppermute | solution.py:28
  29.0 7.0 %collective-permute-start.6 = (f32[3,128]{1,0:T(4,128)S(1)}, f32[3,128]{1,0:T(4,128)S(1)}, u32[]{:S(2)}, u32[]{:S(2)}) collective-permute-start(f32[3,128]{1,0:T(4,128)S(1)} %get-tuple-element.53), channel_id=1, source_target_pairs={{0,4},{4,0},{8,12},{12,8},{16,20},{20,16},{24,28},{28,24},{1,5},{5... | collective-permute-start | bytes 4616 | tf_op jit(solution)/shard_map/ppermute | solution.py:28
  29.1 7.6 %collective-permute-start.7 = (f32[3,128]{1,0:T(4,128)S(1)}, f32[3,128]{1,0:T(4,128)S(1)}, u32[]{:S(2)}, u32[]{:S(2)}) collective-permute-start(f32[3,128]{1,0:T(4,128)S(1)} %get-tuple-element.54), channel_id=1, source_target_pairs={{4,8},{8,4},{12,16},{16,12},{20,24},{24,20},{28,0},{0,28},{5,9},{9... | collective-permute-start | bytes 4616 | tf_op jit(solution)/shard_map/ppermute | solution.py:28
  31.5 5.3 %collective-permute-start.8 = (f32[3,128]{1,0:T(4,128)S(1)}, f32[3,128]{1,0:T(4,128)S(1)}, u32[]{:S(2)}, u32[]{:S(2)}) collective-permute-start(f32[3,128]{1,0:T(4,128)S(1)} %get-tuple-element.55), channel_id=1, source_target_pairs={{0,1},{1,0},{2,3},{3,2},{4,5},{5,4},{6,7},{7,6},{8,9},{9,8},{10,11... | collective-permute-start | bytes 4616 | tf_op jit(solution)/shard_map/ppermute | solution.py:28
  36.0 3.0 %collective-permute-start.9 = (f32[3,128]{1,0:T(4,128)S(1)}, f32[3,128]{1,0:T(4,128)S(1)}, u32[]{:S(2)}, u32[]{:S(2)}) collective-permute-start(f32[3,128]{1,0:T(4,128)S(1)} %get-tuple-element.56), channel_id=1, source_target_pairs={{1,2},{2,1},{3,0},{0,3},{5,6},{6,5},{7,4},{4,7},{9,10},{10,9},{11,... | collective-permute-start | bytes 4616 | tf_op jit(solution)/shard_map/ppermute | solution.py:28

commit v4 on v3

--- a/solution.py
+++ b/solution.py
@@ -28,6 +28,11 @@
     return lax.ppermute(cells, axis, pairs)
 
 
+def relayed(cells):
+    count = lax.axis_size("gx")
+    return lax.ppermute(cells, "gx", [(i, (i + (2 if i % 2 == 0 else count - 2)) % count) for i in range(count)])
+
+
 def order_of():
     odd_x = lax.rem(lax.axis_index("gx"), 2)
     odd_y = lax.rem(lax.axis_index("gy"), 2)
@@ -75,20 +80,18 @@
 def first_kernel(cutoff_hbm, ham_hbm, inv_hbm, rho_hbm, one, cutoff_ref, cutoff_sem, sems):
     flags = pltpu.make_async_copy(cutoff_hbm, cutoff_ref, cutoff_sem)
     flags.start()
-    offset = order_of()[1]
-    sources = (ham_hbm.at[0, 0, offset], ham_hbm.at[0, 0, 0], inv_hbm.at[0, 0, 0], rho_hbm.at[0, 0, 0, 0], rho_hbm.at[1, 0, 0, 0])
-    copies = start_all(
-        [pltpu.make_async_copy(source, one.at[(at + 4) % 5], sems.at[at]) for at, source in enumerate(sources)]
-    )
+    order = order_of()
+    sources = (ham_hbm.at[0, 0, 0], inv_hbm.at[0, 0, 0], rho_hbm.at[1, 0, 0, 0], ham_hbm.at[0, 0, order[2]], ham_hbm.at[0, 0, order[1]])
+    copies = start_all([pltpu.make_async_copy(source, one.at[at], sems.at[at]) for at, source in enumerate(sources)])
     flags.wait()
-    copies[0].wait()
-    one[4] = one[4] * cutoff_ref[0, 0, offset].astype(f32)
-    for copy in copies[1:]:
+    for copy in copies:
         copy.wait()
+    for at, place in ((3, 2), (4, 1)):
+        one[at] = one[at] * cutoff_ref[0, 0, order[place]].astype(f32)
 
 
 def second_kernel(
-    cutoff_hbm, ham_hbm, inv_hbm, rho_hbm, atom_hbm, after, two, three, four, held, left_high, left_low, ham_high, ham_low, members,
+    cutoff_hbm, ham_hbm, inv_hbm, rho_hbm, atom_hbm, after, three, four, held, left_high, left_low, ham_high, ham_low, members,
     raw, cutoff_ref, atom_ref, cutoff_sem, atom_sem, sems
 ):
     flags = pltpu.make_async_copy(cutoff_hbm, cutoff_ref, cutoff_sem)
@@ -105,12 +108,12 @@
         for place, offset in enumerate(order):
             block = raw[kind, offset]
             if place == 0:
-                for message in (two, three, four):
-                    message[kind] = block
+                three[kind] = block
+                four[kind] = block
             else:
                 block = block * keeps[place]
-                if place > 2 or (place == 2 and kind == 0):
-                    (two, three, four)[place - 2][4 + kind] = block
+                if place > 2:
+                    (three, four)[place - 3][4 + kind] = block
             if kind == 0:
                 store((ham_high, ham_low), cols(place), split(block))
             else:
@@ -129,12 +132,22 @@
 
 def commutators(mixed, invs, reals, imags):
     prop, inner = rows_of(mixed)
-    count = len(reals)
-    ahead = dot(prop, beside(*[split(x) for x in (*reals, *imags)]))
+    count = len(invs)
+    ahead = dot(prop, beside(*[split(x) for x in (*imags, *reals)]))
     behind = dot(inner, beside(*[split(x) for x in invs]))
-    real = [ahead[:, cols(at)] - behind[:B, cols(at)] for at in range(count)]
-    imag = [ahead[:, cols(count + at)] - behind[B:, cols(at)] for at in range(count)]
+    imag = [ahead[:, cols(at)] - behind[B:, cols(at)] for at in range(count)]
+    real = [-behind[:B, cols(at)] for at in range(count)]
+    if len(reals) > 0:
+        real = [ahead[:, cols(count + at)] + real[at] for at in range(count)]
     return real, imag
+
+
+def more_kernel(near, held, relay, one_more, two_more):
+    relay[...] = near[:4]
+    for more, place in ((one_more, 1), (two_more, 2)):
+        more[0] = held[1, 0]
+        for kind in range(3):
+            more[1 + kind] = held[kind, place]
 
 
 def third_kernel(left_high, left_low, ham_high, ham_low, one, start, mixed_high, mixed_low, diagonal, other):
@@ -145,14 +158,11 @@
     mixed, added = edge(part(left, every, cols(1)), begun[:, cols(1)], one[0], one[4])
     diagonal[...] = begun[:, cols(0)] + added
     mixed_high[...], mixed_low[...] = mixed
-    (real,), (imag,) = commutators(mixed, (one[1],), (one[2],), (one[3],))
+    (real,), (imag,) = commutators(mixed, (one[1],), (), (one[2],))
     other[0], other[1] = real, imag
 
 
-def fourth_kernel(left_high, left_low, start, diagonal, held, three, four, one_more, two_more, diagonal_out, other):
-    for kind in range(3):
-        one_more[kind] = held[kind, 1]
-        two_more[kind] = held[kind, 2]
+def fourth_kernel(left_high, left_low, start, diagonal, three, four, diagonal_out, other):
     total = diagonal[...]
     for place, near in ((3, three), (4, four)):
         here = part((left_high, left_low), slice(0, 3 * B), cols(place))
@@ -170,57 +180,72 @@
 
 def fifth_kernel(
     left_high, left_low, start, diagonal, held, der_ref, other_one, other_y, two,
-    out_hbm, mixed_high, mixed_low, comm, row_part, c1, c2, c3, c4, new, sems
+    out_hbm, mixed_high, mixed_low, self_high, self_low, real_two, comm, weighted, c1, c2, c3, c4, new, sems
 ):
     order = order_of()
     left = (left_high, left_low)
-    mixed, added = edge(part(left, slice(0, 3 * B), cols(2)), start[:, cols(2)], two[0], two[4])
+    mixed, added = edge(part(left, slice(0, 3 * B), cols(2)), start[:, cols(2)], two[0], two[3])
     mixed_high[...], mixed_low[...] = mixed
-    (real_two,), (imag_two,) = commutators(mixed, (two[1],), (two[2],), (two[3],))
-    total = diagonal[...] + added
-    prop, inner = rows_of(split(total))
+    (real_two[...],), (imag_two,) = commutators(mixed, (two[1],), (), (two[2],))
+    at_self = split(diagonal[...] + added)
+    self_high[...], self_low[...] = at_self
     whole = cols(0, 5)
-    behind = dot(inner, part(left, slice(0, B), whole))
-    imag_comm = dot(prop, part(left, slice(2 * B, 3 * B), whole)) - behind[B:]
-    real_comm = dot(prop, part(left, slice(B, 2 * B), whole)) - behind[:B]
-    others = [(other_one[0], other_one[1]), (real_two, imag_two)]
-    others += [(other_y[0, at], other_y[1, at]) for at in range(2)]
-    comm[0] = real_comm[:, cols(0)] + other_y[0, 2]
-    comm[1] = imag_comm[:, cols(0)] + other_y[1, 2]
-    weighted = [jnp.zeros((B, B), f32) for _ in range(3)]
+    ahead = dot(part(at_self, slice(0, B), cols(0)), part(left, slice(2 * B, 3 * B), whole))
+    behind = dot(part(at_self, slice(2 * B, 3 * B), cols(0)), part(left, slice(0, B), whole))
+    imag_comm = ahead - behind
+    comm[...] = imag_comm[:, cols(0)] + other_y[1, 2]
+    sums = [None] * 3
     copies = []
     for place, column in enumerate((c1, c2, c3, c4), 1):
-        real, imag = others[place - 1]
+        imag = (other_one[1], imag_two, other_y[1, 0], other_y[1, 1])[place - 1]
         real_new = held[1, place] + time_step * (imag_comm[:, cols(place)] + imag)
-        new[0, place - 1] = real_new
-        new[1, place - 1] = held[2, place] - time_step * (real_comm[:, cols(place)] + real)
+        new[place - 1] = real_new
         copies += start_all(
-            [
-                pltpu.make_async_copy(new.at[at, place - 1], out_hbm.at[at, 0, 0, order[place]], sems.at[at, place - 1])
-                for at in range(2)
-            ]
+            [pltpu.make_async_copy(new.at[place - 1], out_hbm.at[0, 0, 0, order[place]], sems.at[place - 1])]
         )
         for direction in range(3):
             product = real_new * der_ref[direction, 0, 0, order[place]]
-            weighted[direction] = weighted[direction] + product
+            sums[direction] = product if place == 1 else sums[direction] + product
             column[direction : direction + 1, :] = jnp.sum(product, axis=0, keepdims=True)
     for direction in range(3):
-        row_part[direction : direction + 1, :] = jnp.sum(weighted[direction].T, axis=0, keepdims=True)
+        weighted[direction] = sums[direction]
     for copy in copies:
         copy.wait()
 
 
+def real_kernel(left_high, left_low, self_high, self_low, other_one, real_two, other_y, weighted, comm, row_part):
+    left = (left_high, left_low)
+    whole = cols(0, 5)
+    at_self = (self_high, self_low)
+    ahead = dot(part(at_self, slice(0, B), cols(0)), part(left, slice(B, 2 * B), whole))
+    behind = dot(part(at_self, slice(B, 2 * B), cols(0)), part(left, slice(0, B), whole))
+    real_comm = ahead - behind
+    for place, other in enumerate((other_y[0, 2], other_one[0], real_two[...], other_y[0, 0], other_y[0, 1])):
+        comm[place] = real_comm[:, cols(place)] + other
+    for direction in range(3):
+        row_part[direction : direction + 1, :] = jnp.sum(weighted[direction].T, axis=0, keepdims=True)
+
+
 def sixth_kernel(
-    held, der_ref, members, high_one, low_one, high_two, low_two, comm, row_part, one, two, c1, c2, c3, c4, old_hbm, out_hbm, forces_ref, new, sems
+    held, der_ref, members, high_one, low_one, high_two, low_two, imag_part, real_part, row_part, one, two, c1, c2, c3, c4, old_hbm,
+    out_hbm, forces_ref, new, sems
 ):
-    prop, inner = rows_of(beside((high_one[...], low_one[...]), (high_two[...], low_two[...])))
-    near = [tuple(jnp.concatenate(x, axis=0) for x in zip(split(one[kind]), split(two[kind]))) for kind in range(3)]
-    behind = dot(inner, near[0])
-    ahead = dot(prop, beside(near[2], near[1]))
-    real_new = held[1, 0] + time_step * (comm[1] + ahead[:, :B] - behind[B:])
-    new[0] = real_new
-    new[1] = held[2, 0] - time_step * (comm[0] + ahead[:, B:] - behind[:B])
-    copies = start_all([pltpu.make_async_copy(new.at[at], out_hbm.at[at, 0, 0, 0], sems.at[at]) for at in range(2)])
+    order = order_of()
+    real_comm = [real_part[place] for place in range(5)]
+    imag_comm = imag_part[...]
+    for place, mixed, near in ((1, (high_one, low_one), one), (2, (high_two, low_two), two)):
+        prop, inner = rows_of(mixed)
+        ahead = dot(prop, beside(split(near[3]), split(near[2]), split(near[0])))
+        behind = dot(inner, split(near[1]))
+        imag_comm = imag_comm + ahead[:, cols(0)] - behind[B:]
+        real_comm[0] = real_comm[0] + ahead[:, cols(1)] - behind[:B]
+        real_comm[place] = real_comm[place] + ahead[:, cols(2)]
+    real_new = held[1, 0] + time_step * imag_comm
+    new[5] = real_new
+    copies = start_all([pltpu.make_async_copy(new.at[5], out_hbm.at[0, 0, 0, 0], sems.at[5])])
+    for place in range(5):
+        new[place] = held[2, place] - time_step * real_comm[place]
+        copies += start_all([pltpu.make_async_copy(new.at[place], out_hbm.at[1, 0, 0, order[place]], sems.at[place])])
     parts = []
     for direction in range(3):
         product = real_new * der_ref[direction, 0, 0, 0]
@@ -268,9 +293,9 @@
     near_one = swapped(first, 1)
     left = [shape(3 * B, 5 * B, kind=bf16)] * 2
     ham = [shape(B, 5 * B, kind=bf16)] * 2
-    send_two, send_three, send_four, held, left_high, left_low, ham_high, ham_low, members = call(
+    send_three, send_four, held, left_high, left_low, ham_high, ham_low, members = call(
         second_kernel,
-        [shape(5, B, B), shape(8, B, B), shape(8, B, B), shape(3, 5, B, B)] + left + ham + [shape(ATOMS, B)],
+        [shape(8, B, B), shape(8, B, B), shape(3, 5, B, B)] + left + ham + [shape(ATOMS, B)],
         [hbm] * 6,
         0,
         (cutoff, hamiltonian, inverse_margin, density, atom_of, first),
@@ -278,7 +303,10 @@
     )
     near_four = swapped(send_four, 4)
     near_three = swapped(send_three, 3)
-    near_two = swapped(send_two, 2)
+    relay, one_more, two_more = call(more_kernel, [shape(4, B, B)] * 3, [vmem] * 2, 0, (near_one, held))
+    near_two = relayed(relay)
+    near_one_more = swapped(one_more, 1)
+    near_two_more = swapped(two_more, 2)
     mixed = [shape(3 * B, B, kind=bf16)] * 2
     start, high_one, low_one, diagonal, other_one = call(
         third_kernel,
@@ -287,37 +315,41 @@
         8000,
         (left_high, left_low, ham_high, ham_low, near_one),
     )
-    one_more, two_more, diagonal, other_y = call(
+    diagonal, other_y = call(
         fourth_kernel,
-        [shape(3, B, B)] * 2 + [shape(3 * B, B), shape(2, 3, B, B)],
-        [vmem] * 7,
+        [shape(3 * B, B), shape(2, 3, B, B)],
+        [vmem] * 6,
         28,
-        (left_high, left_low, start, diagonal, held, near_three, near_four),
-    )
-    near_one_more = swapped(one_more, 1)
-    near_two_more = swapped(two_more, 2)
-    args = (left_high, left_low, start, diagonal, held, derivative, other_one, other_y, near_two)
-    out, high_two, low_two, comm, row_part, *columns = call(
+        (left_high, left_low, start, diagonal, near_three, near_four),
+    )
+    out, high_two, low_two, self_high, self_low, real_two, imag_part, weighted, *columns = call(
         fifth_kernel,
-        [shape(*density.shape)] + mixed + [shape(2, B, B)] + [shape(3, B)] * 5,
+        [shape(*density.shape)] + mixed * 2 + [shape(B, B), shape(B, B), shape(3, B, B)] + [shape(3, B)] * 4,
         [vmem] * 9,
-        30,
-        args,
-        out_specs=[hbm] + [vmem] * 8,
-        scratch=[pltpu.VMEM((2, 4, B, B), f32), dma((2, 4))],
+        22,
+        (left_high, left_low, start, diagonal, held, derivative, other_one, other_y, near_two),
+        out_specs=[hbm] + [vmem] * 11,
+        scratch=[pltpu.VMEM((4, B, B), f32), dma((4,))],
     )
     columns = [swapped(column, at) for at, column in enumerate(columns, 1)]
-    args = (held, derivative, members, high_one, low_one, high_two, low_two, comm, row_part)
+    real_part, row_part = call(
+        real_kernel,
+        [shape(5, B, B), shape(3, B)],
+        [vmem] * 8,
+        10,
+        (left_high, left_low, self_high, self_low, other_one, real_two, other_y, weighted),
+    )
+    args = (held, derivative, members, high_one, low_one, high_two, low_two, imag_part, real_part, row_part)
     args += (near_one_more, near_two_more, *columns, out)
     new_density, forces = call(
         sixth_kernel,
         [shape(*density.shape), shape(3, 1, ATOMS)],
-        [vmem] * 15 + [hbm],
-        8,
+        [vmem] * 16 + [hbm],
+        10,
         args,
         out_specs=[hbm, vmem],
-        scratch=[pltpu.VMEM((2, B, B), f32), dma((2,))],
-        aliases={15: 0},
+        scratch=[pltpu.VMEM((6, B, B), f32), dma((6,))],
+        aliases={16: 0},
     )
     return new_density, forces.reshape(1, 1, 3, ATOMS)
 

time: 40.9 us -> 37.4 us (0.914)
  waiting for transfers between devices: 17.7 us -> 9.34 us
  starting transfers between devices: 14 us -> 18.8 us
    ppermute x10 -> x9, waiting for transfers between devices: 17.7 us -> 6.65 us  [swapped(): return lax.ppermute(cells, axis, pairs)]
    ppermute x10 -> x9, starting transfers between devices: 14 us -> 16.9 us  [swapped(): return lax.ppermute(cells, axis, pairs)]
    ppermute x0 -> x1, waiting for transfers between devices: none -> 2.69 us  [relayed(): lax.ppermute(cells, 'gx', [(i, (i + (2 if i % 2 == 0 else count - 2)) % c...]
    ppermute x0 -> x1, starting transfers between devices: none -> 1.85 us  [relayed(): lax.ppermute(cells, 'gx', [(i, (i + (2 if i % 2 == 0 else count - 2)) % c...]
    pallas_call x6 -> x8, Pallas kernels: 8.23 us -> 8.27 us  [call(): pl.pallas_call(kernel, out_shape=shapes, in_specs=in_specs, out_specs=out...]
where the time goes in v4:
time: 37.4 us; the launch traced here: 37.1 us
  starting transfers between devices  18.8 us (50%)
  waiting for transfers between devices  9.34 us (25%)
  Pallas kernels  8.27 us (22%)
  between operations  0.73 us (2%)
    ppermute x9, starting transfers between devices, swapped(): return lax.ppermute(cells, axis, pairs)  16.9 us
    pallas_call x8, Pallas kernels, call(): pl.pallas_call(kernel, out_shape=shapes, in_specs=in_specs, out_specs=out...  8.27 us
    ppermute x9, waiting for transfers between devices, swapped(): return lax.ppermute(cells, axis, pairs)  6.65 us
    ppermute x1, waiting for transfers between devices, relayed(): lax.ppermute(cells, 'gx', [(i, (i + (2 if i % 2 == 0 else count - 2)) % c...  2.69 us
    ppermute x1, starting transfers between devices, relayed(): lax.ppermute(cells, 'gx', [(i, (i + (2 if i % 2 == 0 else count - 2)) % c...  1.85 us
  transfers between devices with their start and end apart: 10, of which 4 were waited for; matrix products, arithmetic and copies ran while one was open for 0% of the time, Pallas kernels for 14%

profile of v4, /device:TPU:0, one launch (start us, length us, event | category | flops | bytes accessed | tf_op | source)
XLA Modules:
  0.0 37.1 jit_solution(17233155668370068431)
XLA Ops:
  0.6 1.0 %shard_map.77.after = f32[5,128,128]{2,1,0:T(8,128)S(1)} custom-call(s32[1,1,5]{2,1,0:T(1,128)} %cutoff_hbm.3, f32[1,1,5,128,128]{4,3,2,1,0:T(8,128)} %ham_hbm.3, f32[1,1,5,128,128]{4,3,2,1,0:T(8,128)} %inv_hbm.3, f32[2,1,1,5,128,128]{5,4,3,2,1,0:T(8,128)} %rho_hbm.3), custom_call_target="tpu_custom_call" | custom-call | bytes 1638420 | tf_op jit(solution)/shard_map/pallas_call | solution.py:265
  1.7 3.0 %collective-permute-start = (f32[5,128,128]{2,1,0:T(8,128)S(1)}, f32[5,128,128]{2,1,0:T(8,128)S(1)}, u32[]{:S(2)}, u32[]{:S(2)}) collective-permute-start(f32[5,128,128]{2,1,0:T(8,128)S(1)} %shard_map.77.after), channel_id=1, source_target_pairs={{0,4},{4,0},{8,12},{12,8},{16,20},{20,16},{24,28},{28,24},{1,5},{5... | collective-permute-start | bytes 983048 | tf_op jit(solution)/shard_map/ppermute | solution.py:28
  4.7 1.4 %shard_map.78 = (f32[8,128,128]{2,1,0:T(8,128)S(1)}, f32[8,128,128]{2,1,0:T(8,128)S(1)}, f32[3,5,128,128]{3,2,1,0:T(8,128)S(1)}, bf16[384,640]{1,0:T(8,128)(2,1)...) custom-call(s32[1,1,5]{2,1,0:T(1,128)} %cutoff_hbm.3, ...), custom_call_target="tpu_custom_call" | custom-call | bytes 6324756 | tf_op jit(solution)/shard_map/pallas_call | solution.py:265
  6.1 0.1 collective-permute-start.1
  6.2 1.6 %collective-permute-start.2 = (f32[8,128,128]{2,1,0:T(8,128)S(1)}, f32[8,128,128]{2,1,0:T(8,128)S(1)}, u32[]{:S(2)}, u32[]{:S(2)}) collective-permute-start(f32[8,128,128]{2,1,0:T(8,128)S(1)} %get-tuple-element.47), channel_id=1, source_target_pairs={{1,2},{2,1},{3,0},{0,3},{5,6},{6,5},{7,4},{4,7},{9,10},{10,9},{11,... | collective-permute-start | bytes 1572872 | tf_op jit(solution)/shard_map/ppermute | solution.py:28
  7.8 4.6 %collective-permute-done.one.near = f32[5,128,128]{2,1,0:T(8,128)S(1)} collective-permute-done((f32[5,128,128]{2,1,0:T(8,128)S(1)}, f32[5,128,128]{2,1,0:T(8,128)S(1)}, u32[]{:S(2)}, u32[]{:S(2)}) %collective-permute-start) | collective-permute-done | bytes 327712 | tf_op jit(solution)/shard_map/ppermute | solution.py:28
  12.4 0.1 shard_map.81
  12.5 1.8 %collective-permute-start.3 = (f32[4,128,128]{2,1,0:T(8,128)S(1)}, f32[4,128,128]{2,1,0:T(8,128)S(1)}, u32[]{:S(2)}, u32[]{:S(2)}) collective-permute-start(f32[4,128,128]{2,1,0:T(8,128)S(1)} %get-tuple-element.51), channel_id=1, source_target_pairs={{0,8},{4,28},{8,16},{12,4},{16,24},{20,12},{24,0},{28,20},{1,9},{5... | collective-permute-start | bytes 786440 | tf_op jit(solution)/shard_map/ppermute | solution.py:33
  14.3 3.5 %collective-permute-start.4 = (f32[4,128,128]{2,1,0:T(8,128)S(1)}, f32[4,128,128]{2,1,0:T(8,128)S(1)}, u32[]{:S(2)}, u32[]{:S(2)}) collective-permute-start(f32[4,128,128]{2,1,0:T(8,128)S(1)} %get-tuple-element.61), channel_id=1, source_target_pairs={{0,4},{4,0},{8,12},{12,8},{16,20},{20,16},{24,28},{28,24},{1,5},{5... | collective-permute-start | bytes 786440 | tf_op jit(solution)/shard_map/ppermute | solution.py:28
  17.9 0.0 collective-permute-start.5
  17.9 0.9 %shard_map.79 = (f32[384,640]{1,0:T(8,128)S(1)}, bf16[384,128]{1,0:T(8,128)(2,1)S(1)}, bf16[384,128]{1,0:T(8,128)(2,1)S(1)}, f32[384,128]{1,0:T(8,128)S(1)}, f32[2,128,128]{2,1,0:T(8,128)S(1)}) custom-call(bf16[384,640]{1,0:T(8,128)(2,1)S(1)} %get-tuple-element.38.left_high, bf16[384,640]{1,0:T(8,128)(2,1)S(1)} %get-tuple-element.39.left_low, ...), custom_call_target="tpu_custom_call" | custom-call | flops 100663296000 | bytes 4653056 | tf_op jit(solution)/shard_map/pallas_call | solution.py:265
  18.8 0.0 collective-permute-done.1.three
  18.8 1.1 %collective-permute-done.2.four = f32[8,128,128]{2,1,0:T(8,128)S(1)} collective-permute-done((f32[8,128,128]{2,1,0:T(8,128)S(1)}, f32[8,128,128]{2,1,0:T(8,128)S(1)}, u32[]{:S(2)}, u32[]{:S(2)}) %collective-permute-start.2) | collective-permute-done | bytes 524320 | tf_op jit(solution)/shard_map/ppermute | solution.py:28
  19.9 0.0 copy-start
  19.9 1.0 %shard_map.80 = (f32[384,128]{1,0:T(8,128)S(1)}, f32[2,3,128,128]{3,2,1,0:T(8,128)S(1)}) custom-call(bf16[384,640]{1,0:T(8,128)(2,1)S(1)} %get-tuple-element.38.left_high, bf16[384,640]{1,0:T(8,128)(2,1)S(1)} %get-tuple-element.39.left_low, f32[384,640]{1,0:T(8,128)S(1)} %get-tuple-element.44.start, f32[384,128]{1,0:T(8,128)S(1)} %get-tuple-element.45.diagonal, ...), custom_call_target="tpu_custom_call" | custom-call | flops 352321536 | bytes 4784128 | tf_op jit(solution)/shard_map/pallas_call | solution.py:265
  20.9 2.7 %collective-permute-done.3.two = f32[4,128,128]{2,1,0:T(8,128)S(1)} collective-permute-done((f32[4,128,128]{2,1,0:T(8,128)S(1)}, f32[4,128,128]{2,1,0:T(8,128)S(1)}, u32[]{:S(2)}, u32[]{:S(2)}) %collective-permute-start.3) | collective-permute-done | bytes 262176 | tf_op jit(solution)/shard_map/ppermute | solution.py:33
  23.6 0.0 copy-done
  23.6 1.5 %shard_map.82 = (f32[2,1,1,5,128,128]{5,4,3,2,1,0:T(8,128)}, bf16[384,128]{1,0:T(8,128)(2,1)S(1)}, bf16[384,128]{1,0:T(8,128)(2,1)S(1)}, bf16[384,128]{1,0:T(8,1...) custom-call(bf16[384,640]{1,0:T(8,128)(2,1)S(1)} %get-tuple-element., ...), custom_call_target="tpu_custom_call" | custom-call | flops 276824064 | bytes 7673856 | tf_op jit(solution)/shard_map/pallas_call | solution.py:265
  25.2 1.1 %collective-permute-start.6 = (f32[3,128]{1,0:T(4,128)S(1)}, f32[3,128]{1,0:T(4,128)S(1)}, u32[]{:S(2)}, u32[]{:S(2)}) collective-permute-start(f32[3,128]{1,0:T(4,128)S(1)} %get-tuple-element.63), channel_id=1, source_target_pairs={{0,4},{4,0},{8,12},{12,8},{16,20},{20,16},{24,28},{28,24},{1,5},{5... | collective-permute-start | bytes 4616 | tf_op jit(solution)/shard_map/ppermute | solution.py:28
  26.2 6.0 %collective-permute-start.7 = (f32[3,128]{1,0:T(4,128)S(1)}, f32[3,128]{1,0:T(4,128)S(1)}, u32[]{:S(2)}, u32[]{:S(2)}) collective-permute-start(f32[3,128]{1,0:T(4,128)S(1)} %get-tuple-element.64), channel_id=1, source_target_pairs={{4,8},{8,4},{12,16},{16,12},{20,24},{24,20},{28,0},{0,28},{5,9},{9... | collective-permute-start | bytes 4616 | tf_op jit(solution)/shard_map/ppermute | solution.py:28
  32.2 0.0 collective-permute-start.8
  32.2 0.0 collective-permute-done.4.one
  32.2 1.6 %collective-permute-start.9 = (f32[3,128]{1,0:T(4,128)S(1)}, f32[3,128]{1,0:T(4,128)S(1)}, u32[]{:S(2)}, u32[]{:S(2)}) collective-permute-start(f32[3,128]{1,0:T(4,128)S(1)} %get-tuple-element.66), channel_id=1, source_target_pairs={{1,2},{2,1},{3,0},{0,3},{5,6},{6,5},{7,4},{4,7},{9,10},{10,9},{11,... | collective-permute-start | bytes 4616 | tf_op jit(solution)/shard_map/ppermute | solution.py:28
  33.8 0.4 %shard_map.83 = (f32[5,128,128]{2,1,0:T(8,128)S(1)}, f32[3,128]{1,0:T(4,128)S(1)}) custom-call(bf16[384,640]{1,0:T(8,128)(2,1)S(1)} %get-tuple-element.38.left_high, bf16[384,640]{1,0:T(8,128)(2,1)S(1)} %get-tuple-element.39.left_low, bf16[384,128]{1,0:T(8,128)(2,1)S(1)} %get-tuple-element.55.self_high, bf16[384,128]{1,0:T(8,128)(2,1)S(1)} %get-tuple-element.56.self_low, ...), custom_call_target="tpu_custom_call" | custom-call | flops 125829120 | bytes 3474944 | tf_op jit(solution)/shard_map/pallas_call | solution.py:265
  34.2 0.0 collective-permute-done.5.two
  34.2 0.0 collective-permute-done.6.c1
  34.3 0.0 collective-permute-done.7.c2
  34.3 0.0 collective-permute-done.8.c3
  34.3 1.0 %collective-permute-done.9.c4 = f32[3,128]{1,0:T(4,128)S(1)} collective-permute-done((f32[3,128]{1,0:T(4,128)S(1)}, f32[3,128]{1,0:T(4,128)S(1)}, u32[]{:S(2)}, u32[]{:S(2)}) %collective-permute-start.9) | collective-permute-done | bytes 1568 | tf_op jit(solution)/shard_map/ppermute | solution.py:28
  35.2 1.9 %shard_map.84 = (f32[2,1,1,5,128,128]{5,4,3,2,1,0:T(8,128)}, f32[3,1,64]{2,1,0:T(1,128)}) custom-call(f32[3,5,128,128]{3,2,1,0:T(8,128)S(1)} %get-tuple-element.36.held, f32[3,1,1,5,128,128]{5,4,3,2,1,0:T(8,128)S(1)} %copy-done, f32[64,128]{1,0:T(8,128)S(1)} %get-tuple-element.37.members, ...), custom_call_target="tpu_custom_call", output_to_operand_aliasing={{0}: (16, {})} | custom-call | flops 125829120 | bytes 5021952 | tf_op jit(solution)/shard_map/pallas_call | solution.py:265
Async XLA Ops:
  1.7 10.7 %collective-permute-start = (f32[5,128,128]{2,1,0:T(8,128)S(1)}, f32[5,128,128]{2,1,0:T(8,128)S(1)}, u32[]{:S(2)}, u32[]{:S(2)}) collective-permute-start(f32[5,128,128]{2,1,0:T(8,128)S(1)} %shard_map.77.after), channel_id=1, source_target_pairs={{0,4},{4,0},{8,12},{12,8},{16,20},{20,16},{24,28},{28,24},{1,5},{5... | collective-permute-start | bytes 983048 | tf_op jit(solution)/shard_map/ppermute | solution.py:28
  6.1 12.7 %collective-permute-start.1 = (f32[8,128,128]{2,1,0:T(8,128)S(1)}, f32[8,128,128]{2,1,0:T(8,128)S(1)}, u32[]{:S(2)}, u32[]{:S(2)}) collective-permute-start(f32[8,128,128]{2,1,0:T(8,128)S(1)} %get-tuple-element.46), channel_id=1, source_target_pairs={{0,1},{1,0},{2,3},{3,2},{4,5},{5,4},{6,7},{7,6},{8,9},{9,8},{10,11... | collective-permute-start | bytes 1572872 | tf_op jit(solution)/shard_map/ppermute | solution.py:28
  6.2 13.7 %collective-permute-start.2 = (f32[8,128,128]{2,1,0:T(8,128)S(1)}, f32[8,128,128]{2,1,0:T(8,128)S(1)}, u32[]{:S(2)}, u32[]{:S(2)}) collective-permute-start(f32[8,128,128]{2,1,0:T(8,128)S(1)} %get-tuple-element.47), channel_id=1, source_target_pairs={{1,2},{2,1},{3,0},{0,3},{5,6},{6,5},{7,4},{4,7},{9,10},{10,9},{11,... | collective-permute-start | bytes 1572872 | tf_op jit(solution)/shard_map/ppermute | solution.py:28
  12.5 11.1 %collective-permute-start.3 = (f32[4,128,128]{2,1,0:T(8,128)S(1)}, f32[4,128,128]{2,1,0:T(8,128)S(1)}, u32[]{:S(2)}, u32[]{:S(2)}) collective-permute-start(f32[4,128,128]{2,1,0:T(8,128)S(1)} %get-tuple-element.51), channel_id=1, source_target_pairs={{0,8},{4,28},{8,16},{12,4},{16,24},{20,12},{24,0},{28,20},{1,9},{5... | collective-permute-start | bytes 786440 | tf_op jit(solution)/shard_map/ppermute | solution.py:33
  14.3 17.9 %collective-permute-start.4 = (f32[4,128,128]{2,1,0:T(8,128)S(1)}, f32[4,128,128]{2,1,0:T(8,128)S(1)}, u32[]{:S(2)}, u32[]{:S(2)}) collective-permute-start(f32[4,128,128]{2,1,0:T(8,128)S(1)} %get-tuple-element.61), channel_id=1, source_target_pairs={{0,4},{4,0},{8,12},{12,8},{16,20},{20,16},{24,28},{28,24},{1,5},{5... | collective-permute-start | bytes 786440 | tf_op jit(solution)/shard_map/ppermute | solution.py:28
  17.9 16.4 %collective-permute-start.5 = (f32[4,128,128]{2,1,0:T(8,128)S(1)}, f32[4,128,128]{2,1,0:T(8,128)S(1)}, u32[]{:S(2)}, u32[]{:S(2)}) collective-permute-start(f32[4,128,128]{2,1,0:T(8,128)S(1)} %get-tuple-element.62), channel_id=1, source_target_pairs={{4,8},{8,4},{12,16},{16,12},{20,24},{24,20},{28,0},{0,28},{5,9},{9... | collective-permute-start | bytes 786440 | tf_op jit(solution)/shard_map/ppermute | solution.py:28
  19.9 3.7 %copy-start = (f32[3,1,1,5,128,128]{5,4,3,2,1,0:T(8,128)S(1)}, f32[3,1,1,5,128,128]{5,4,3,2,1,0:T(8,128)}, u32[]{:S(2)}) copy-start(f32[3,1,1,5,128,128]{5,4,3,2,1,0:T(8,128)} %der_ref.3) | copy-start | bytes 2949124
  25.2 9.1 %collective-permute-start.6 = (f32[3,128]{1,0:T(4,128)S(1)}, f32[3,128]{1,0:T(4,128)S(1)}, u32[]{:S(2)}, u32[]{:S(2)}) collective-permute-start(f32[3,128]{1,0:T(4,128)S(1)} %get-tuple-element.63), channel_id=1, source_target_pairs={{0,4},{4,0},{8,12},{12,8},{16,20},{20,16},{24,28},{28,24},{1,5},{5... | collective-permute-start | bytes 4616 | tf_op jit(solution)/shard_map/ppermute | solution.py:28
  26.2 8.0 %collective-permute-start.7 = (f32[3,128]{1,0:T(4,128)S(1)}, f32[3,128]{1,0:T(4,128)S(1)}, u32[]{:S(2)}, u32[]{:S(2)}) collective-permute-start(f32[3,128]{1,0:T(4,128)S(1)} %get-tuple-element.64), channel_id=1, source_target_pairs={{4,8},{8,4},{12,16},{16,12},{20,24},{24,20},{28,0},{0,28},{5,9},{9... | collective-permute-start | bytes 4616 | tf_op jit(solution)/shard_map/ppermute | solution.py:28
  32.2 2.1 %collective-permute-start.8 = (f32[3,128]{1,0:T(4,128)S(1)}, f32[3,128]{1,0:T(4,128)S(1)}, u32[]{:S(2)}, u32[]{:S(2)}) collective-permute-start(f32[3,128]{1,0:T(4,128)S(1)} %get-tuple-element.65), channel_id=1, source_target_pairs={{0,1},{1,0},{2,3},{3,2},{4,5},{5,4},{6,7},{7,6},{8,9},{9,8},{10,11... | collective-permute-start | bytes 4616 | tf_op jit(solution)/shard_map/ppermute | solution.py:28
  32.2 3.0 %collective-permute-start.9 = (f32[3,128]{1,0:T(4,128)S(1)}, f32[3,128]{1,0:T(4,128)S(1)}, u32[]{:S(2)}, u32[]{:S(2)}) collective-permute-start(f32[3,128]{1,0:T(4,128)S(1)} %get-tuple-element.66), channel_id=1, source_target_pairs={{1,2},{2,1},{3,0},{0,3},{5,6},{6,5},{7,4},{4,7},{9,10},{10,9},{11,... | collective-permute-start | bytes 4616 | tf_op jit(solution)/shard_map/ppermute | solution.py:28

commit v5 on v4

v5 whole, which is shorter than its diff:
```python
import jax
import jax.numpy as jnp
from jax import lax
from jax.experimental import pallas as pl
from jax.experimental.pallas import tpu as pltpu
from jax.sharding import PartitionSpec as P

B = 128
ATOMS = 64

time_step = 0.25
vmem = pl.BlockSpec(memory_space=pltpu.VMEM)
hbm = pl.BlockSpec(memory_space=pltpu.HBM)
f32 = jnp.float32
bf16 = jnp.bfloat16
dma = pltpu.SemaphoreType.DMA


def swapped(cells, edge):
    axis = "gx" if edge < 3 else "gy"
    count = lax.axis_size(axis)
    assert count % 2 == 0
    first = 0 if edge in (1, 3) else 1
    pairs = []
    for i in range(first, count, 2):
        j = (i + 1) % count
        pairs += [(i, j), (j, i)]
    return lax.ppermute(cells, axis, pairs)


def order_of():
    odd_x = lax.rem(lax.axis_index("gx"), 2)
    odd_y = lax.rem(lax.axis_index("gy"), 2)
    return 0, 1 + odd_x, 2 - odd_x, 3 + odd_y, 4 - odd_y


def cols(place, count=1):
    return slice(place * B, (place + count) * B)


def split(values):
    high = values.astype(bf16)
    return high, (values - high.astype(f32)).astype(bf16)


def beside(*pairs):
    return tuple(jnp.concatenate(parts, axis=1) for parts in zip(*pairs))


def dot(left, right):
    def one(a, b):
        return jnp.dot(a, b, preferred_element_type=f32)

    return one(left[0], right[0]) + (one(left[0], right[1]) + one(left[1], right[0]))


def part(pair, rows, columns):
    return pair[0][rows, columns], pair[1][rows, columns]


def rows_of(pair):
    return (pair[0][:B], pair[1][:B]), (pair[0][B:], pair[1][B:])


def store(pair, columns, values):
    pair[0][:, columns], pair[1][:, columns] = values


def start_all(copies):
    for copy in copies:
        copy.start()
    return copies


def first_kernel(cutoff_hbm, ham_hbm, inv_hbm, rho_hbm, one, two, cutoff_ref, cutoff_sem, sems):
    flags = pltpu.make_async_copy(cutoff_hbm, cutoff_ref, cutoff_sem)
    flags.start()
    order = order_of()
    copies = []
    for at, message in enumerate((one, two)):
        sources = (ham_hbm.at[0, 0, 0], inv_hbm.at[0, 0, 0], rho_hbm.at[1, 0, 0, 0], ham_hbm.at[0, 0, order[1 + at]])
        copies += start_all(
            [pltpu.make_async_copy(source, message.at[kind], sems.at[at, kind]) for kind, source in enumerate(sources)]
        )
    flags.wait()
    for copy in copies:
        copy.wait()
    for at, message in enumerate((one, two)):
        message[3] = message[3] * cutoff_ref[0, 0, order[1 + at]].astype(f32)


def second_kernel(
    cutoff_hbm, ham_hbm, inv_hbm, rho_hbm, atom_hbm, after, three, four, held, left_high, left_low, ham_high, ham_low, members,
    raw, cutoff_ref, atom_ref, cutoff_sem, atom_sem, sems
):
    flags = pltpu.make_async_copy(cutoff_hbm, cutoff_ref, cutoff_sem)
    flags.start()
    sources = (ham_hbm.at[0, 0], inv_hbm.at[0, 0], rho_hbm.at[0, 0, 0], rho_hbm.at[1, 0, 0])
    copies = start_all([pltpu.make_async_copy(source, raw.at[at], sems.at[at]) for at, source in enumerate(sources)])
    owners = pltpu.make_async_copy(atom_hbm, atom_ref, atom_sem)
    owners.start()
    order = order_of()
    flags.wait()
    keeps = [cutoff_ref[0, 0, offset].astype(f32) for offset in order]
    for kind, copy in enumerate(copies):
        copy.wait()
        for place, offset in enumerate(order):
            block = raw[kind, offset]
            if place == 0:
                three[(0, 1, 4, 2)[kind]] = block
                if kind != 2:
                    four[(0, 1, None, 2)[kind]] = block
            else:
                block = block * keeps[place]
                if place == 3:
                    three[(3, 5, 6, 7)[kind]] = block
                elif place == 4 and kind == 0:
                    four[3] = block
            if kind == 0:
                store((ham_high, ham_low), cols(place), split(block))
            else:
                held[kind - 1, place] = block
                rows = slice((kind - 1) * B, kind * B)
                left_high[rows, cols(place)], left_low[rows, cols(place)] = split(block)
    owners.wait()
    atoms = jnp.broadcast_to(atom_ref[0], (ATOMS, B))
    members[...] = -(lax.broadcasted_iota(jnp.int32, (ATOMS, B), 0) == atoms).astype(f32)


def first_half(left, place, start, near, diagonal):
    both = dot(part(left, slice(0, 3 * B), cols(place)), beside(split(near[0]), split(near[3])))
    mixed = split(start[:, cols(place)] + both[:, :B])
    prop, inner = rows_of(mixed)
    behind = dot(inner, split(near[1]))
    imag = dot(prop, split(near[2])) - behind[B:]
    return mixed, diagonal + both[:, B:], -behind[:B], imag


def second_half(mixed, near):
    prop, inner = rows_of(mixed)
    ahead = dot(prop, beside(split(near[0]), split(near[2]), split(near[3])))
    behind = dot(inner, split(near[1]))
    return ahead[:, cols(0)], ahead[:, cols(1)] - behind[:B], ahead[:, cols(2)] - behind[B:]


def send_more(more, held, place):
    more[0] = held[1, 0]
    for kind in range(3):
        more[1 + kind] = held[kind, place]


def third_kernel(
    left_high, left_low, ham_high, ham_low, held, one, one_more, two_more, start, mixed_high, mixed_low, diagonal, other
):
    send_more(one_more, held, 1)
    send_more(two_more, held, 2)
    left = (left_high, left_low)
    start[...] = dot(part(left, slice(0, 3 * B), cols(0)), part((ham_high, ham_low), slice(0, B), cols(0, 5)))
    mixed, diagonal[...], other[0], other[1] = first_half(left, 1, start, one, start[:, cols(0)])
    mixed_high[...], mixed_low[...] = mixed


def fourth_kernel(
    left_high, left_low, start, held, diagonal, three, four, four_more, mixed_high, mixed_low, diagonal_out, other
):
    send_more(four_more, held, 4)
    left = (left_high, left_low)
    mixed, total, real, other[1, 0] = first_half(left, 3, start, three, diagonal[...])
    added, other[0, 2], other[1, 2] = second_half(mixed, three[4:])
    other[0, 0] = real + added
    mixed, diagonal_out[...], other[0, 1], other[1, 1] = first_half(left, 4, start, four, total)
    mixed_high[...], mixed_low[...] = mixed


def fifth_kernel(
    left_high, left_low, start, diagonal, held, der_ref, other_one, other_y, two,
    out_hbm, mixed_high, mixed_low, self_high, self_low, real_two, comm, weighted, c1, c2, c3, c4, new, sems
):
    order = order_of()
    left = (left_high, left_low)
    mixed, total, real_two[...], imag_two = first_half(left, 2, start, two, diagonal[...])
    mixed_high[...], mixed_low[...] = mixed
    at_self = split(total)
    self_high[...], self_low[...] = at_self
    whole = cols(0, 5)
    ahead = dot(part(at_self, slice(0, B), cols(0)), part(left, slice(2 * B, 3 * B), whole))
    behind = dot(part(at_self, slice(2 * B, 3 * B), cols(0)), part(left, slice(0, B), whole))
    imag_comm = ahead - behind
    comm[...] = imag_comm[:, cols(0)] + other_y[1, 2]
    sums = [None] * 3
    copies = []
    for place, column in enumerate((c1, c2, c3, c4), 1):
        imag = (other_one[1], imag_two, other_y[1, 0], other_y[1, 1])[place - 1]
        real_new = held[1, place] + time_step * (imag_comm[:, cols(place)] + imag)
        new[place - 1] = real_new
        copies += start_all(
            [pltpu.make_async_copy(new.at[place - 1], out_hbm.at[0, 0, 0, order[place]], sems.at[place - 1])]
        )
        for direction in range(3):
            product = real_new * der_ref[direction, 0, 0, order[place]]
            sums[direction] = product if place == 1 else sums[direction] + product
            column[direction : direction + 1, :] = jnp.sum(product, axis=0, keepdims=True)
    for direction in range(3):
        weighted[direction] = sums[direction]
    for copy in copies:
        copy.wait()


def real_kernel(
    left_high, left_low, self_high, self_low, other_one, real_two, other_y, weighted, high_one, low_one, high_four, low_four,
    imag_part, one, four, comm, imag_out, row_part
):
    left = (left_high, left_low)
    whole = cols(0, 5)
    at_self = (self_high, self_low)
    ahead = dot(part(at_self, slice(0, B), cols(0)), part(left, slice(B, 2 * B), whole))
    behind = dot(part(at_self, slice(B, 2 * B), cols(0)), part(left, slice(0, B), whole))
    real_comm = ahead - behind
    added_one, real_one, imag_one = second_half((high_one[...], low_one[...]), one)
    added_four, real_four, imag_four = second_half((high_four[...], low_four[...]), four)
    comm[0] = real_comm[:, cols(0)] + other_y[0, 2] + real_one + real_four
    comm[1] = real_comm[:, cols(1)] + other_one[0] + added_one
    comm[2] = real_comm[:, cols(2)] + real_two[...]
    comm[3] = real_comm[:, cols(3)] + other_y[0, 0]
    comm[4] = real_comm[:, cols(4)] + other_y[0, 1] + added_four
    imag_out[...] = imag_part[...] + imag_one + imag_four
    for direction in range(3):
        row_part[direction : direction + 1, :] = jnp.sum(weighted[direction].T, axis=0, keepdims=True)


def sixth_kernel(
    held, der_ref, members, high_two, low_two, imag_part, real_part, row_part, two, c1, c2, c3, c4, old_hbm,
    out_hbm, forces_ref, new, sems
):
    order = order_of()
    added, real_two, imag_two = second_half((high_two[...], low_two[...]), two)
    real_new = held[1, 0] + time_step * (imag_part[...] + imag_two)
    new[5] = real_new
    copies = start_all([pltpu.make_async_copy(new.at[5], out_hbm.at[0, 0, 0, 0], sems.at[5])])
    for place in range(5):
        comm = real_part[place]
        if place in (0, 2):
            comm = comm + (real_two if place == 0 else added)
        new[place] = held[2, place] - time_step * comm
        copies += start_all([pltpu.make_async_copy(new.at[place], out_hbm.at[1, 0, 0, order[place]], sems.at[place])])
    parts = []
    for direction in range(3):
        product = real_new * der_ref[direction, 0, 0, 0]
        parts.append(jnp.sum(product + product.T, axis=0, keepdims=True))
    orbital = jnp.concatenate(parts, axis=0) + row_part[...] + ((c1[...] + c2[...]) + (c3[...] + c4[...]))
    forces = lax.dot_general(
        orbital, members[...], (((1,), (1,)), ((), ())), precision=lax.Precision.HIGHEST, preferred_element_type=f32
    )
    for direction in range(3):
        forces_ref[direction] = forces[direction : direction + 1]
    for copy in copies:
        copy.wait()


def call(kernel, shapes, in_specs, products, args, out_specs=None, scratch=(), aliases={}):
    moved = sum(4 * x.size for x in args) + sum(4 * x.size for x in shapes)
    return pl.pallas_call(
        kernel,
        out_shape=shapes,
        in_specs=in_specs,
        out_specs=out_specs or [vmem] * len(shapes),
        scratch_shapes=scratch,
        input_output_aliases=aliases,
        compiler_params=pltpu.CompilerParams(vmem_limit_bytes=32 * 2**20),
        cost_estimate=pl.CostEstimate(flops=products * 6 * B**3, bytes_accessed=moved, transcendentals=0),
    )(*args)


def local(hamiltonian, inverse_margin, density, cutoff, derivative, atom_of):
    def shape(*dims, kind=f32):
        return jax.ShapeDtypeStruct(dims, kind)

    hamiltonian, inverse_margin, density, cutoff, atom_of = (
        pltpu.with_memory_space_constraint(x, pltpu.HBM) for x in (hamiltonian, inverse_margin, density, cutoff, atom_of)
    )
    flags = pltpu.SMEM((1, 1, 5), jnp.int32)
    message = shape(4, B, B)
    first_one, first_two = call(
        first_kernel,
        [message] * 2,
        [hbm] * 4,
        0,
        (cutoff, hamiltonian, inverse_margin, density),
        scratch=[flags, dma(()), dma((2, 4))],
    )
    near_one = swapped(first_one, 1)
    near_two = swapped(first_two, 2)
    left = [shape(3 * B, 5 * B, kind=bf16)] * 2
    ham = [shape(B, 5 * B, kind=bf16)] * 2
    send_three, send_four, held, left_high, left_low, ham_high, ham_low, members = call(
        second_kernel,
        [shape(8, B, B), message, shape(3, 5, B, B)] + left + ham + [shape(ATOMS, B)],
        [hbm] * 6,
        0,
        (cutoff, hamiltonian, inverse_margin, density, atom_of, first_one),
        scratch=[pltpu.VMEM((4, 5, B, B), f32), flags, pltpu.VMEM((1, 1, B), jnp.int32), dma(()), dma(()), dma((4,))],
    )
    near_four = swapped(send_four, 4)
    near_three = swapped(send_three, 3)
    mixed = [shape(3 * B, B, kind=bf16)] * 2
    one_more, two_more, start, high_one, low_one, diagonal, other_one = call(
        third_kernel,
        [message] * 2 + [shape(3 * B, 5 * B)] + mixed + [shape(3 * B, B), shape(2, B, B)],
        [vmem] * 6,
        8000,
        (left_high, left_low, ham_high, ham_low, held, near_one),
    )
    near_one_more = swapped(one_more, 1)
    near_two_more = swapped(two_more, 2)
    four_more, high_four, low_four, diagonal, other_y = call(
        fourth_kernel,
        [message] + mixed + [shape(3 * B, B), shape(2, 3, B, B)],
        [vmem] * 7,
        28,
        (left_high, left_low, start, held, diagonal, near_three, near_four),
    )
    near_four_more = swapped(four_more, 4)
    out, high_two, low_two, self_high, self_low, real_two, imag_part, weighted, *columns = call(
        fifth_kernel,
        [shape(*density.shape)] + mixed * 2 + [shape(B, B), shape(B, B), shape(3, B, B)] + [shape(3, B)] * 4,
        [vmem] * 9,
        22,
        (left_high, left_low, start, diagonal, held, derivative, other_one, other_y, near_two),
        out_specs=[hbm] + [vmem] * 11,
        scratch=[pltpu.VMEM((4, B, B), f32), dma((4,))],
    )
    columns = [swapped(column, at) for at, column in enumerate(columns, 1)]
    args = (left_high, left_low, self_high, self_low, other_one, real_two, other_y, weighted, high_one, low_one)
    args += (high_four, low_four, imag_part, near_one_more, near_four_more)
    real_part, imag_part, row_part = call(
        real_kernel, [shape(5, B, B), shape(B, B), shape(3, B)], [vmem] * 15, 20, args
    )
    args = (held, derivative, members, high_two, low_two, imag_part, real_part, row_part, near_two_more, *columns, out)
    new_density, forces = call(
        sixth_kernel,
        [shape(*density.shape), shape(3, 1, ATOMS)],
        [vmem] * 13 + [hbm],
        10,
        args,
        out_specs=[hbm, vmem],
        scratch=[pltpu.VMEM((6, B, B), f32), dma((6,))],
        aliases={13: 0},
    )
    return new_density, forces.reshape(1, 1, 3, ATOMS)


def solution(mesh):
    placed = (
        P("gx", "gy", None, None, None),
        P("gx", "gy", None, None, None),
        P(None, "gx", "gy", None, None, None),
        P("gx", "gy", None),
        P(None, "gx", "gy", None, None, None),
        P("gx", "gy", None),
    )
    return jax.shard_map(
        local,
        mesh=mesh,
        in_specs=placed,
        out_specs=(P(None, "gx", "gy", None, None, None), P("gx", "gy", None, None)),
        check_vma=False,
    )
```

time: 37.4 us -> 35.1 us (0.939)
  waiting for transfers between devices: 9.34 us -> 7.65 us
  starting transfers between devices: 18.8 us -> 17.4 us
  Pallas kernels: 8.27 us -> 9 us
    ppermute x1 -> x0, waiting for transfers between devices: 2.69 us -> none  [relayed(): lax.ppermute(cells, 'gx', [(i, (i + (2 if i % 2 == 0 else count - 2)) % c...]
    ppermute x1 -> x0, starting transfers between devices: 1.85 us -> none  [relayed(): lax.ppermute(cells, 'gx', [(i, (i + (2 if i % 2 == 0 else count - 2)) % c...]
    ppermute x9 -> x11, waiting for transfers between devices: 6.65 us -> 7.65 us  [swapped(): return lax.ppermute(cells, axis, pairs)]
    pallas_call x8 -> x7, Pallas kernels: 8.27 us -> 9 us  [call(): pl.pallas_call(kernel, out_shape=shapes, in_specs=in_specs, out_specs=out...]
    ppermute x9 -> x11, starting transfers between devices: 16.9 us -> 17.4 us  [swapped(): return lax.ppermute(cells, axis, pairs)]
  transfers between devices with their start and end apart: 10 -> 11, of which waited for: 4 -> 5; matrix products, arithmetic and copies ran while one was open for 0% -> 0% of each run, Pallas kernels for 14% -> 18%
where the time goes in v5:
time: 35.1 us; the launch traced here: 34.7 us
  starting transfers between devices  17.4 us (50%)
  Pallas kernels  9 us (26%)
  waiting for transfers between devices  7.65 us (22%)
  between operations  0.71 us (2%)
    ppermute x11, starting transfers between devices, swapped(): return lax.ppermute(cells, axis, pairs)  17.4 us
    pallas_call x7, Pallas kernels, call(): pl.pallas_call(kernel, out_shape=shapes, in_specs=in_specs, out_specs=out...  9 us
    ppermute x11, waiting for transfers between devices, swapped(): return lax.ppermute(cells, axis, pairs)  7.65 us
  transfers between devices with their start and end apart: 11, of which 5 were waited for; matrix products, arithmetic and copies ran while one was open for 0% of the time, Pallas kernels for 18%

profile of v5, /device:TPU:0, one launch (start us, length us, event | category | flops | bytes accessed | tf_op | source)
XLA Modules:
  0.0 34.7 jit_solution(638976892954430531)
XLA Ops:
  0.6 1.2 %shard_map.77 = (f32[4,128,128]{2,1,0:T(8,128)S(1)}, f32[4,128,128]{2,1,0:T(8,128)S(1)}) custom-call(s32[1,1,5]{2,1,0:T(1,128)} %cutoff_hbm.3, f32[1,1,5,128,128]{4,3,2,1,0:T(8,128)} %ham_hbm.3, f32[1,1,5,128,128]{4,3,2,1,0:T(8,128)} %inv_hbm.3, f32[2,1,1,5,128,128]{5,4,3,2,1,0:T(8,128)} %rho_hbm.3), custom_call_target="tpu_custom_call" | custom-call | bytes 1835028 | tf_op jit(solution)/shard_map/pallas_call | solution.py:262
  1.8 3.0 %collective-permute-start = (f32[4,128,128]{2,1,0:T(8,128)S(1)}, f32[4,128,128]{2,1,0:T(8,128)S(1)}, u32[]{:S(2)}, u32[]{:S(2)}) collective-permute-start(f32[4,128,128]{2,1,0:T(8,128)S(1)} %get-tuple-element.41.after), channel_id=1, source_target_pairs={{0,4},{4,0},{8,12},{12,8},{16,20},{20,16},{24,28},{28,24},{1,5},{5... | collective-permute-start | bytes 786440 | tf_op jit(solution)/shard_map/ppermute | solution.py:28
  4.8 3.5 %collective-permute-start.3 = (f32[4,128,128]{2,1,0:T(8,128)S(1)}, f32[4,128,128]{2,1,0:T(8,128)S(1)}, u32[]{:S(2)}, u32[]{:S(2)}) collective-permute-start(f32[4,128,128]{2,1,0:T(8,128)S(1)} %get-tuple-element.55), channel_id=1, source_target_pairs={{4,8},{8,4},{12,16},{16,12},{20,24},{24,20},{28,0},{0,28},{5,9},{9... | collective-permute-start | bytes 786440 | tf_op jit(solution)/shard_map/ppermute | solution.py:28
  8.4 1.4 %shard_map.78 = (f32[8,128,128]{2,1,0:T(8,128)S(1)}, f32[4,128,128]{2,1,0:T(8,128)S(1)}, f32[3,5,128,128]{3,2,1,0:T(8,128)S(1)}, bf16[384,640]{1,0:T(8,128)(2,1)...) custom-call(s32[1,1,5]{2,1,0:T(1,128)} %cutoff_hbm.3, ...), custom_call_target="tpu_custom_call" | custom-call | bytes 5997076 | tf_op jit(solution)/shard_map/pallas_call | solution.py:262
  9.8 0.4 %collective-permute-start.2 = (f32[4,128,128]{2,1,0:T(8,128)S(1)}, f32[4,128,128]{2,1,0:T(8,128)S(1)}, u32[]{:S(2)}, u32[]{:S(2)}) collective-permute-start(f32[4,128,128]{2,1,0:T(8,128)S(1)} %get-tuple-element.51), channel_id=1, source_target_pairs={{1,2},{2,1},{3,0},{0,3},{5,6},{6,5},{7,4},{4,7},{9,10},{10,9},{11,... | collective-permute-start | bytes 786440 | tf_op jit(solution)/shard_map/ppermute | solution.py:28
  10.2 1.2 %collective-permute-start.1 = (f32[8,128,128]{2,1,0:T(8,128)S(1)}, f32[8,128,128]{2,1,0:T(8,128)S(1)}, u32[]{:S(2)}, u32[]{:S(2)}) collective-permute-start(f32[8,128,128]{2,1,0:T(8,128)S(1)} %get-tuple-element.50), channel_id=1, source_target_pairs={{0,1},{1,0},{2,3},{3,2},{4,5},{5,4},{6,7},{7,6},{8,9},{9,8},{10,11... | collective-permute-start | bytes 1572872 | tf_op jit(solution)/shard_map/ppermute | solution.py:28
  11.5 5.3 %collective-permute-done.one = f32[4,128,128]{2,1,0:T(8,128)S(1)} collective-permute-done((f32[4,128,128]{2,1,0:T(8,128)S(1)}, f32[4,128,128]{2,1,0:T(8,128)S(1)}, u32[]{:S(2)}, u32[]{:S(2)}) %collective-permute-start) | collective-permute-done | bytes 262176 | tf_op jit(solution)/shard_map/ppermute | solution.py:28
  16.8 1.0 %shard_map.79 = (f32[4,128,128]{2,1,0:T(8,128)S(1)}, f32[4,128,128]{2,1,0:T(8,128)S(1)}, f32[384,640]{1,0:T(8,128)S(1)}, bf16[384,128]{1,0:T(8,128)(2,1)S(1)}, b...) custom-call(bf16[384,640]{1,0:T(8,128)(2,1)S(1)} %get-tuple-element.44.left_high, ...), custom_call_target="tpu_custom_call" | custom-call | flops 100663296000 | bytes 6094848 | tf_op jit(solution)/shard_map/pallas_call | solution.py:262
  17.8 1.8 %collective-permute-start.4 = (f32[4,128,128]{2,1,0:T(8,128)S(1)}, f32[4,128,128]{2,1,0:T(8,128)S(1)}, u32[]{:S(2)}, u32[]{:S(2)}) collective-permute-start(f32[4,128,128]{2,1,0:T(8,128)S(1)} %get-tuple-element.67), channel_id=1, source_target_pairs={{0,4},{4,0},{8,12},{12,8},{16,20},{20,16},{24,28},{28,24},{1,5},{5... | collective-permute-start | bytes 786440 | tf_op jit(solution)/shard_map/ppermute | solution.py:28
  19.6 0.0 collective-permute-done.2.four
  19.6 0.0 collective-permute-done.1.three
  19.6 0.0 copy-start
  19.6 1.4 %shard_map.80 = (f32[4,128,128]{2,1,0:T(8,128)S(1)}, bf16[384,128]{1,0:T(8,128)(2,1)S(1)}, bf16[384,128]{1,0:T(8,128)(2,1)S(1)}, f32[384,128]{1,0:T(8,128)S(1)}, f32[2,3,128,128]{3,2,1,0:T(8,128)S(1)}) custom-call(bf16[384,640]{1,0:T(8,128)(2,1)S(1)} %get-tuple-element.44.left_high, bf16[384,640]{1,0:T(8,128)(2,1)S(1)} %get-tuple-element.45.left_low, ...), custom_call_target="tpu_custom_call" | custom-call | flops 352321536 | bytes 6160384 | tf_op jit(solution)/shard_map/pallas_call | solution.py:262
  21.0 0.1 collective-permute-start.5
  21.1 3.6 %collective-permute-start.6 = (f32[4,128,128]{2,1,0:T(8,128)S(1)}, f32[4,128,128]{2,1,0:T(8,128)S(1)}, u32[]{:S(2)}, u32[]{:S(2)}) collective-permute-start(f32[4,128,128]{2,1,0:T(8,128)S(1)} %get-tuple-element.72), channel_id=1, source_target_pairs={{4,8},{8,4},{12,16},{16,12},{20,24},{24,20},{28,0},{0,28},{5,9},{9... | collective-permute-start | bytes 786440 | tf_op jit(solution)/shard_map/ppermute | solution.py:28
  24.7 0.0 collective-permute-done.3.two
  24.7 0.0 copy-done
  24.7 1.6 %shard_map.81 = (f32[2,1,1,5,128,128]{5,4,3,2,1,0:T(8,128)}, bf16[384,128]{1,0:T(8,128)(2,1)S(1)}, bf16[384,128]{1,0:T(8,128)(2,1)S(1)}, bf16[384,128]{1,0:T(8,1...) custom-call(bf16[384,640]{1,0:T(8,128)(2,1)S(1)} %get-tuple-element., ...), custom_call_target="tpu_custom_call" | custom-call | flops 276824064 | bytes 7673856 | tf_op jit(solution)/shard_map/pallas_call | solution.py:262
  26.3 0.1 collective-permute-start.7
  26.4 1.9 %collective-permute-start.8 = (f32[3,128]{1,0:T(4,128)S(1)}, f32[3,128]{1,0:T(4,128)S(1)}, u32[]{:S(2)}, u32[]{:S(2)}) collective-permute-start(f32[3,128]{1,0:T(4,128)S(1)} %get-tuple-element.74), channel_id=1, source_target_pairs={{4,8},{8,4},{12,16},{16,12},{20,24},{24,20},{28,0},{0,28},{5,9},{9... | collective-permute-start | bytes 4616 | tf_op jit(solution)/shard_map/ppermute | solution.py:28
  28.3 1.7 %collective-permute-done.4.one = f32[4,128,128]{2,1,0:T(8,128)S(1)} collective-permute-done((f32[4,128,128]{2,1,0:T(8,128)S(1)}, f32[4,128,128]{2,1,0:T(8,128)S(1)}, u32[]{:S(2)}, u32[]{:S(2)}) %collective-permute-start.4) | collective-permute-done | bytes 262176 | tf_op jit(solution)/shard_map/ppermute | solution.py:28
  29.9 0.0 collective-permute-start.9
  29.9 0.0 collective-permute-done.5.four
  29.9 1.6 %collective-permute-start.10 = (f32[3,128]{1,0:T(4,128)S(1)}, f32[3,128]{1,0:T(4,128)S(1)}, u32[]{:S(2)}, u32[]{:S(2)}) collective-permute-start(f32[3,128]{1,0:T(4,128)S(1)} %get-tuple-element.76), channel_id=1, source_target_pairs={{1,2},{2,1},{3,0},{0,3},{5,6},{6,5},{7,4},{4,7},{9,10},{10,9},{11,... | collective-permute-start | bytes 4616 | tf_op jit(solution)/shard_map/ppermute | solution.py:28
  31.6 0.7 %shard_map.82 = (f32[5,128,128]{2,1,0:T(8,128)S(1)}, f32[128,128]{1,0:T(8,128)S(1)}, f32[3,128]{1,0:T(4,128)S(1)}) custom-call(bf16[384,640]{1,0:T(8,128)(2,1)S(1)} %get-tuple-element.44.left_high, bf16[384,640]{1,0:T(8,128)(2,1)S(1)} %get-tuple-element.45.left_low, bf16[384,128]{1,0:T(8,128)(2,1)S(1)} %get-tuple-element.58.self_high, ...), custom_call_target="tpu_custom_call" | custom-call | flops 251658240 | bytes 4916736 | tf_op jit(solution)/shard_map/pallas_call | solution.py:262
  32.3 0.3 collective-permute-done.6.two
  32.6 0.0 collective-permute-done.7.c1
  32.6 0.3 collective-permute-done.8.c2
  32.8 0.0 collective-permute-done.9.c3
  32.8 0.1 collective-permute-done.10.c4
  33.0 1.8 %shard_map.83 = (f32[2,1,1,5,128,128]{5,4,3,2,1,0:T(8,128)}, f32[3,1,64]{2,1,0:T(1,128)}) custom-call(f32[3,5,128,128]{3,2,1,0:T(8,128)S(1)} %get-tuple-element.42.held, f32[3,1,1,5,128,128]{5,4,3,2,1,0:T(8,128)S(1)} %copy-done, f32[64,128]{1,0:T(8,128)S(1)} %get-tuple-element.43.members, ...), custom_call_target="tpu_custom_call", output_to_operand_aliasing={{0}: (13, {})} | custom-call | flops 125829120 | bytes 4366592 | tf_op jit(solution)/shard_map/pallas_call | solution.py:262
Async XLA Ops:
  1.8 15.0 %collective-permute-start = (f32[4,128,128]{2,1,0:T(8,128)S(1)}, f32[4,128,128]{2,1,0:T(8,128)S(1)}, u32[]{:S(2)}, u32[]{:S(2)}) collective-permute-start(f32[4,128,128]{2,1,0:T(8,128)S(1)} %get-tuple-element.41.after), channel_id=1, source_target_pairs={{0,4},{4,0},{8,12},{12,8},{16,20},{20,16},{24,28},{28,24},{1,5},{5... | collective-permute-start | bytes 786440 | tf_op jit(solution)/shard_map/ppermute | solution.py:28
  4.8 19.9 %collective-permute-start.3 = (f32[4,128,128]{2,1,0:T(8,128)S(1)}, f32[4,128,128]{2,1,0:T(8,128)S(1)}, u32[]{:S(2)}, u32[]{:S(2)}) collective-permute-start(f32[4,128,128]{2,1,0:T(8,128)S(1)} %get-tuple-element.55), channel_id=1, source_target_pairs={{4,8},{8,4},{12,16},{16,12},{20,24},{24,20},{28,0},{0,28},{5,9},{9... | collective-permute-start | bytes 786440 | tf_op jit(solution)/shard_map/ppermute | solution.py:28
  9.8 9.8 %collective-permute-start.2 = (f32[4,128,128]{2,1,0:T(8,128)S(1)}, f32[4,128,128]{2,1,0:T(8,128)S(1)}, u32[]{:S(2)}, u32[]{:S(2)}) collective-permute-start(f32[4,128,128]{2,1,0:T(8,128)S(1)} %get-tuple-element.51), channel_id=1, source_target_pairs={{1,2},{2,1},{3,0},{0,3},{5,6},{6,5},{7,4},{4,7},{9,10},{10,9},{11,... | collective-permute-start | bytes 786440 | tf_op jit(solution)/shard_map/ppermute | solution.py:28
  10.2 9.4 %collective-permute-start.1 = (f32[8,128,128]{2,1,0:T(8,128)S(1)}, f32[8,128,128]{2,1,0:T(8,128)S(1)}, u32[]{:S(2)}, u32[]{:S(2)}) collective-permute-start(f32[8,128,128]{2,1,0:T(8,128)S(1)} %get-tuple-element.50), channel_id=1, source_target_pairs={{0,1},{1,0},{2,3},{3,2},{4,5},{5,4},{6,7},{7,6},{8,9},{9,8},{10,11... | collective-permute-start | bytes 1572872 | tf_op jit(solution)/shard_map/ppermute | solution.py:28
  17.8 12.2 %collective-permute-start.4 = (f32[4,128,128]{2,1,0:T(8,128)S(1)}, f32[4,128,128]{2,1,0:T(8,128)S(1)}, u32[]{:S(2)}, u32[]{:S(2)}) collective-permute-start(f32[4,128,128]{2,1,0:T(8,128)S(1)} %get-tuple-element.67), channel_id=1, source_target_pairs={{0,4},{4,0},{8,12},{12,8},{16,20},{20,16},{24,28},{28,24},{1,5},{5... | collective-permute-start | bytes 786440 | tf_op jit(solution)/shard_map/ppermute | solution.py:28
  19.6 5.1 %copy-start = (f32[3,1,1,5,128,128]{5,4,3,2,1,0:T(8,128)S(1)}, f32[3,1,1,5,128,128]{5,4,3,2,1,0:T(8,128)}, u32[]{:S(2)}) copy-start(f32[3,1,1,5,128,128]{5,4,3,2,1,0:T(8,128)} %der_ref.3) | copy-start | bytes 2949124
  21.0 8.9 %collective-permute-start.5 = (f32[4,128,128]{2,1,0:T(8,128)S(1)}, f32[4,128,128]{2,1,0:T(8,128)S(1)}, u32[]{:S(2)}, u32[]{:S(2)}) collective-permute-start(f32[4,128,128]{2,1,0:T(8,128)S(1)} %get-tuple-element.68), channel_id=1, source_target_pairs={{1,2},{2,1},{3,0},{0,3},{5,6},{6,5},{7,4},{4,7},{9,10},{10,9},{11,... | collective-permute-start | bytes 786440 | tf_op jit(solution)/shard_map/ppermute | solution.py:28
  21.1 11.5 %collective-permute-start.6 = (f32[4,128,128]{2,1,0:T(8,128)S(1)}, f32[4,128,128]{2,1,0:T(8,128)S(1)}, u32[]{:S(2)}, u32[]{:S(2)}) collective-permute-start(f32[4,128,128]{2,1,0:T(8,128)S(1)} %get-tuple-element.72), channel_id=1, source_target_pairs={{4,8},{8,4},{12,16},{16,12},{20,24},{24,20},{28,0},{0,28},{5,9},{9... | collective-permute-start | bytes 786440 | tf_op jit(solution)/shard_map/ppermute | solution.py:28
  26.3 6.3 %collective-permute-start.7 = (f32[3,128]{1,0:T(4,128)S(1)}, f32[3,128]{1,0:T(4,128)S(1)}, u32[]{:S(2)}, u32[]{:S(2)}) collective-permute-start(f32[3,128]{1,0:T(4,128)S(1)} %get-tuple-element.73), channel_id=1, source_target_pairs={{0,4},{4,0},{8,12},{12,8},{16,20},{20,16},{24,28},{28,24},{1,5},{5... | collective-permute-start | bytes 4616 | tf_op jit(solution)/shard_map/ppermute | solution.py:28
  26.4 6.5 %collective-permute-start.8 = (f32[3,128]{1,0:T(4,128)S(1)}, f32[3,128]{1,0:T(4,128)S(1)}, u32[]{:S(2)}, u32[]{:S(2)}) collective-permute-start(f32[3,128]{1,0:T(4,128)S(1)} %get-tuple-element.74), channel_id=1, source_target_pairs={{4,8},{8,4},{12,16},{16,12},{20,24},{24,20},{28,0},{0,28},{5,9},{9... | collective-permute-start | bytes 4616 | tf_op jit(solution)/shard_map/ppermute | solution.py:28
  29.9 2.9 %collective-permute-start.9 = (f32[3,128]{1,0:T(4,128)S(1)}, f32[3,128]{1,0:T(4,128)S(1)}, u32[]{:S(2)}, u32[]{:S(2)}) collective-permute-start(f32[3,128]{1,0:T(4,128)S(1)} %get-tuple-element.75), channel_id=1, source_target_pairs={{0,1},{1,0},{2,3},{3,2},{4,5},{5,4},{6,7},{7,6},{8,9},{9,8},{10,11... | collective-permute-start | bytes 4616 | tf_op jit(solution)/shard_map/ppermute | solution.py:28
  29.9 3.0 %collective-permute-start.10 = (f32[3,128]{1,0:T(4,128)S(1)}, f32[3,128]{1,0:T(4,128)S(1)}, u32[]{:S(2)}, u32[]{:S(2)}) collective-permute-start(f32[3,128]{1,0:T(4,128)S(1)} %get-tuple-element.76), channel_id=1, source_target_pairs={{1,2},{2,1},{3,0},{0,3},{5,6},{6,5},{7,4},{4,7},{9,10},{10,9},{11,... | collective-permute-start | bytes 4616 | tf_op jit(solution)/shard_map/ppermute | solution.py:28

commit v6 on v5

--- a/solution.py
+++ b/solution.py
@@ -1,3 +1,5 @@
+import functools
+
 import jax
 import jax.numpy as jnp
 from jax import lax
@@ -72,25 +74,31 @@
     return copies
 
 
-def first_kernel(cutoff_hbm, ham_hbm, inv_hbm, rho_hbm, one, two, cutoff_ref, cutoff_sem, sems):
+def first_kernel(cutoff_hbm, ham_hbm, inv_hbm, rho_hbm, one, rest, cutoff_ref, cutoff_sem, sems):
     flags = pltpu.make_async_copy(cutoff_hbm, cutoff_ref, cutoff_sem)
     flags.start()
     order = order_of()
-    copies = []
-    for at, message in enumerate((one, two)):
-        sources = (ham_hbm.at[0, 0, 0], inv_hbm.at[0, 0, 0], rho_hbm.at[1, 0, 0, 0], ham_hbm.at[0, 0, order[1 + at]])
-        copies += start_all(
-            [pltpu.make_async_copy(source, message.at[kind], sems.at[at, kind]) for kind, source in enumerate(sources)]
-        )
+    sources = (ham_hbm.at[0, 0, 0], inv_hbm.at[0, 0, 0], rho_hbm.at[1, 0, 0, 0], ham_hbm.at[0, 0, order[1]])
+    copies = [pltpu.make_async_copy(source, one.at[at], sems.at[at]) for at, source in enumerate(sources)]
+    copies += [
+        pltpu.make_async_copy(ham_hbm.at[0, 0, order[place]], rest.at[at], sems.at[4 + at]) for at, place in enumerate((4, 2))
+    ]
+    start_all(copies)
     flags.wait()
     for copy in copies:
         copy.wait()
-    for at, message in enumerate((one, two)):
-        message[3] = message[3] * cutoff_ref[0, 0, order[1 + at]].astype(f32)
+    one[3] = one[3] * cutoff_ref[0, 0, order[1]].astype(f32)
+    for at, place in enumerate((4, 2)):
+        rest[at] = rest[at] * cutoff_ref[0, 0, order[place]].astype(f32)
+
+
+def next_kernel(at, message, rest, out):
+    out[:3] = message[:3]
+    out[3] = rest[at]
 
 
 def second_kernel(
-    cutoff_hbm, ham_hbm, inv_hbm, rho_hbm, atom_hbm, after, three, four, held, left_high, left_low, ham_high, ham_low, members,
+    cutoff_hbm, ham_hbm, inv_hbm, rho_hbm, atom_hbm, after, three, held, left_high, left_low, ham_high, ham_low, members,
     raw, cutoff_ref, atom_ref, cutoff_sem, atom_sem, sems
 ):
     flags = pltpu.make_async_copy(cutoff_hbm, cutoff_ref, cutoff_sem)
@@ -108,14 +116,10 @@
             block = raw[kind, offset]
             if place == 0:
                 three[(0, 1, 4, 2)[kind]] = block
-                if kind != 2:
-                    four[(0, 1, None, 2)[kind]] = block
             else:
                 block = block * keeps[place]
                 if place == 3:
                     three[(3, 5, 6, 7)[kind]] = block
-                elif place == 4 and kind == 0:
-                    four[3] = block
             if kind == 0:
                 store((ham_high, ham_low), cols(place), split(block))
             else:
@@ -150,30 +154,30 @@
 
 
 def third_kernel(
-    left_high, left_low, ham_high, ham_low, held, one, one_more, two_more, start, mixed_high, mixed_low, diagonal, other
+    left_high, left_low, ham_high, ham_low, held, four, one_more, four_more, start, mixed_high, mixed_low, diagonal, other
 ):
     send_more(one_more, held, 1)
+    send_more(four_more, held, 4)
+    left = (left_high, left_low)
+    start[...] = dot(part(left, slice(0, 3 * B), cols(0)), part((ham_high, ham_low), slice(0, B), cols(0, 5)))
+    mixed, diagonal[...], other[0], other[1] = first_half(left, 4, start, four, start[:, cols(0)])
+    mixed_high[...], mixed_low[...] = mixed
+
+
+def fourth_kernel(
+    left_high, left_low, start, held, diagonal, one, three, two_more, mixed_high, mixed_low, diagonal_out, other
+):
     send_more(two_more, held, 2)
     left = (left_high, left_low)
-    start[...] = dot(part(left, slice(0, 3 * B), cols(0)), part((ham_high, ham_low), slice(0, B), cols(0, 5)))
-    mixed, diagonal[...], other[0], other[1] = first_half(left, 1, start, one, start[:, cols(0)])
+    mixed, total, real, other[1, 1] = first_half(left, 3, start, three, diagonal[...])
+    added, other[0, 2], other[1, 2] = second_half(mixed, three[4:])
+    other[0, 1] = real + added
+    mixed, diagonal_out[...], other[0, 0], other[1, 0] = first_half(left, 1, start, one, total)
     mixed_high[...], mixed_low[...] = mixed
 
 
-def fourth_kernel(
-    left_high, left_low, start, held, diagonal, three, four, four_more, mixed_high, mixed_low, diagonal_out, other
-):
-    send_more(four_more, held, 4)
-    left = (left_high, left_low)
-    mixed, total, real, other[1, 0] = first_half(left, 3, start, three, diagonal[...])
-    added, other[0, 2], other[1, 2] = second_half(mixed, three[4:])
-    other[0, 0] = real + added
-    mixed, diagonal_out[...], other[0, 1], other[1, 1] = first_half(left, 4, start, four, total)
-    mixed_high[...], mixed_low[...] = mixed
-
-
 def fifth_kernel(
-    left_high, left_low, start, diagonal, held, der_ref, other_one, other_y, two,
+    left_high, left_low, start, diagonal, held, der_ref, other, other_four, two,
     out_hbm, mixed_high, mixed_low, self_high, self_low, real_two, comm, weighted, c1, c2, c3, c4, new, sems
 ):
     order = order_of()
@@ -186,11 +190,11 @@
     ahead = dot(part(at_self, slice(0, B), cols(0)), part(left, slice(2 * B, 3 * B), whole))
     behind = dot(part(at_self, slice(2 * B, 3 * B), cols(0)), part(left, slice(0, B), whole))
     imag_comm = ahead - behind
-    comm[...] = imag_comm[:, cols(0)] + other_y[1, 2]
+    comm[...] = imag_comm[:, cols(0)] + other[1, 2]
     sums = [None] * 3
     copies = []
     for place, column in enumerate((c1, c2, c3, c4), 1):
-        imag = (other_one[1], imag_two, other_y[1, 0], other_y[1, 1])[place - 1]
+        imag = (other[1, 0], imag_two, other[1, 1], other_four[1])[place - 1]
         real_new = held[1, place] + time_step * (imag_comm[:, cols(place)] + imag)
         new[place - 1] = real_new
         copies += start_all(
@@ -207,7 +211,7 @@
 
 
 def real_kernel(
-    left_high, left_low, self_high, self_low, other_one, real_two, other_y, weighted, high_one, low_one, high_four, low_four,
+    left_high, left_low, self_high, self_low, other, real_two, other_four, weighted, high_one, low_one, high_four, low_four,
     imag_part, one, four, comm, imag_out, row_part
 ):
     left = (left_high, left_low)
@@ -218,11 +222,11 @@
     real_comm = ahead - behind
     added_one, real_one, imag_one = second_half((high_one[...], low_one[...]), one)
     added_four, real_four, imag_four = second_half((high_four[...], low_four[...]), four)
-    comm[0] = real_comm[:, cols(0)] + other_y[0, 2] + real_one + real_four
-    comm[1] = real_comm[:, cols(1)] + other_one[0] + added_one
+    comm[0] = real_comm[:, cols(0)] + other[0, 2] + real_one + real_four
+    comm[1] = real_comm[:, cols(1)] + other[0, 0] + added_one
     comm[2] = real_comm[:, cols(2)] + real_two[...]
-    comm[3] = real_comm[:, cols(3)] + other_y[0, 0]
-    comm[4] = real_comm[:, cols(4)] + other_y[0, 1] + added_four
+    comm[3] = real_comm[:, cols(3)] + other[0, 1]
+    comm[4] = real_comm[:, cols(4)] + other_four[0] + added_four
     imag_out[...] = imag_part[...] + imag_one + imag_four
     for direction in range(3):
         row_part[direction : direction + 1, :] = jnp.sum(weighted[direction].T, axis=0, keepdims=True)
@@ -280,57 +284,59 @@
     )
     flags = pltpu.SMEM((1, 1, 5), jnp.int32)
     message = shape(4, B, B)
-    first_one, first_two = call(
+    first_one, rest = call(
         first_kernel,
-        [message] * 2,
+        [message, shape(2, B, B)],
         [hbm] * 4,
         0,
         (cutoff, hamiltonian, inverse_margin, density),
-        scratch=[flags, dma(()), dma((2, 4))],
+        scratch=[flags, dma(()), dma((6,))],
     )
     near_one = swapped(first_one, 1)
+    (first_four,) = call(functools.partial(next_kernel, 0), [message], [vmem] * 2, 0, (first_one, rest))
+    near_four = swapped(first_four, 4)
+    (first_two,) = call(functools.partial(next_kernel, 1), [message], [vmem] * 2, 0, (first_four, rest))
     near_two = swapped(first_two, 2)
     left = [shape(3 * B, 5 * B, kind=bf16)] * 2
     ham = [shape(B, 5 * B, kind=bf16)] * 2
-    send_three, send_four, held, left_high, left_low, ham_high, ham_low, members = call(
+    send_three, held, left_high, left_low, ham_high, ham_low, members = call(
         second_kernel,
-        [shape(8, B, B), message, shape(3, 5, B, B)] + left + ham + [shape(ATOMS, B)],
+        [shape(8, B, B), shape(3, 5, B, B)] + left + ham + [shape(ATOMS, B)],
         [hbm] * 6,
         0,
-        (cutoff, hamiltonian, inverse_margin, density, atom_of, first_one),
+        (cutoff, hamiltonian, inverse_margin, density, atom_of, first_two),
         scratch=[pltpu.VMEM((4, 5, B, B), f32), flags, pltpu.VMEM((1, 1, B), jnp.int32), dma(()), dma(()), dma((4,))],
     )
-    near_four = swapped(send_four, 4)
     near_three = swapped(send_three, 3)
     mixed = [shape(3 * B, B, kind=bf16)] * 2
-    one_more, two_more, start, high_one, low_one, diagonal, other_one = call(
+    one_more, four_more, start, high_four, low_four, diagonal, other_four = call(
         third_kernel,
         [message] * 2 + [shape(3 * B, 5 * B)] + mixed + [shape(3 * B, B), shape(2, B, B)],
         [vmem] * 6,
         8000,
-        (left_high, left_low, ham_high, ham_low, held, near_one),
+        (left_high, left_low, ham_high, ham_low, held, near_four),
     )
     near_one_more = swapped(one_more, 1)
-    near_two_more = swapped(two_more, 2)
-    four_more, high_four, low_four, diagonal, other_y = call(
+    near_four_more = swapped(four_more, 4)
+    two_more, high_one, low_one, diagonal, other = call(
         fourth_kernel,
         [message] + mixed + [shape(3 * B, B), shape(2, 3, B, B)],
         [vmem] * 7,
-        28,
-        (left_high, left_low, start, held, diagonal, near_three, near_four),
-    )
-    near_four_more = swapped(four_more, 4)
+        24,
+        (left_high, left_low, start, held, diagonal, near_one, near_three),
+    )
+    near_two_more = swapped(two_more, 2)
     out, high_two, low_two, self_high, self_low, real_two, imag_part, weighted, *columns = call(
         fifth_kernel,
         [shape(*density.shape)] + mixed * 2 + [shape(B, B), shape(B, B), shape(3, B, B)] + [shape(3, B)] * 4,
         [vmem] * 9,
         22,
-        (left_high, left_low, start, diagonal, held, derivative, other_one, other_y, near_two),
+        (left_high, left_low, start, diagonal, held, derivative, other, other_four, near_two),
         out_specs=[hbm] + [vmem] * 11,
         scratch=[pltpu.VMEM((4, B, B), f32), dma((4,))],
     )
     columns = [swapped(column, at) for at, column in enumerate(columns, 1)]
-    args = (left_high, left_low, self_high, self_low, other_one, real_two, other_y, weighted, high_one, low_one)
+    args = (left_high, left_low, self_high, self_low, other, real_two, other_four, weighted, high_one, low_one)
     args += (high_four, low_four, imag_part, near_one_more, near_four_more)
     real_part, imag_part, row_part = call(
         real_kernel, [shape(5, B, B), shape(B, B), shape(3, B)], [vmem] * 15, 20, args

time: 35.1 us -> 35 us (level)
  starting transfers between devices: 17.4 us -> 18.4 us
  waiting for transfers between devices: 7.65 us -> 6.71 us
    ppermute x11, starting transfers between devices: 17.4 us -> 18.4 us  [swapped(): return lax.ppermute(cells, axis, pairs)]
    ppermute x11, waiting for transfers between devices: 7.65 us -> 6.71 us  [swapped(): return lax.ppermute(cells, axis, pairs)]
    pallas_call x7 -> x9, Pallas kernels: 9 us -> 8.95 us  [call(): pl.pallas_call(kernel, out_shape=shapes, in_specs=in_specs, out_specs=out...]
  transfers between devices with their start and end apart: 11 -> 11, of which waited for: 5 -> 3; matrix products, arithmetic and copies ran while one was open for 0% -> 0% of each run, Pallas kernels for 18% -> 17%
where the time goes in v6:
time: 35 us; the launch traced here: 34.8 us
  starting transfers between devices  18.4 us (53%)
  Pallas kernels  8.95 us (26%)
  waiting for transfers between devices  6.71 us (19%)
  between operations  0.71 us (2%)
    ppermute x11, starting transfers between devices, swapped(): return lax.ppermute(cells, axis, pairs)  18.4 us
    pallas_call x9, Pallas kernels, call(): pl.pallas_call(kernel, out_shape=shapes, in_specs=in_specs, out_specs=out...  8.95 us
    ppermute x11, waiting for transfers between devices, swapped(): return lax.ppermute(cells, axis, pairs)  6.71 us
  transfers between devices with their start and end apart: 11, of which 3 were waited for; matrix products, arithmetic and copies ran while one was open for 0% of the time, Pallas kernels for 17%

profile of v6, /device:TPU:0, one launch (start us, length us, event | category | flops | bytes accessed | tf_op | source)
XLA Modules:
  0.0 34.8 jit_solution(9492358445626458136)
XLA Ops:
  0.6 1.1 %shard_map.77 = (f32[4,128,128]{2,1,0:T(8,128)S(1)}, f32[2,128,128]{2,1,0:T(8,128)S(1)}) custom-call(s32[1,1,5]{2,1,0:T(1,128)} %cutoff_hbm.3, f32[1,1,5,128,128]{4,3,2,1,0:T(8,128)} %ham_hbm.3, f32[1,1,5,128,128]{4,3,2,1,0:T(8,128)} %inv_hbm.3, f32[2,1,1,5,128,128]{5,4,3,2,1,0:T(8,128)} %rho_hbm.3), custom_call_target="tpu_custom_call" | custom-call | bytes 1703956 | tf_op jit(solution)/shard_map/pallas_call | solution.py:266
  1.7 2.4 %collective-permute-start = (f32[4,128,128]{2,1,0:T(8,128)S(1)}, f32[4,128,128]{2,1,0:T(8,128)S(1)}, u32[]{:S(2)}, u32[]{:S(2)}) collective-permute-start(f32[4,128,128]{2,1,0:T(8,128)S(1)} %shard_map.78.message), channel_id=1, source_target_pairs={{1,2},{2,1},{3,0},{0,3},{5,6},{6,5},{7,4},{4,7},{9,10},{10,9},{11,... | collective-permute-start | bytes 786440 | tf_op jit(solution)/shard_map/ppermute | solution.py:30
  4.2 1.5 %collective-permute-start.1 = (f32[4,128,128]{2,1,0:T(8,128)S(1)}, f32[4,128,128]{2,1,0:T(8,128)S(1)}, u32[]{:S(2)}, u32[]{:S(2)}) collective-permute-start(f32[4,128,128]{2,1,0:T(8,128)S(1)} %get-tuple-element.40.message), channel_id=1, source_target_pairs={{0,4},{4,0},{8,12},{12,8},{16,20},{20,16},{24,28},{28,24},{1,5},{5... | collective-permute-start | bytes 786440 | tf_op jit(solution)/shard_map/ppermute | solution.py:30
  5.7 3.6 %collective-permute-start.3 = (f32[4,128,128]{2,1,0:T(8,128)S(1)}, f32[4,128,128]{2,1,0:T(8,128)S(1)}, u32[]{:S(2)}, u32[]{:S(2)}) collective-permute-start(f32[4,128,128]{2,1,0:T(8,128)S(1)} %shard_map.79.after), channel_id=1, source_target_pairs={{4,8},{8,4},{12,16},{16,12},{20,24},{24,20},{28,0},{0,28},{5,9},{9... | collective-permute-start | bytes 786440 | tf_op jit(solution)/shard_map/ppermute | solution.py:30
  9.3 1.4 %shard_map.80 = (f32[8,128,128]{2,1,0:T(8,128)S(1)}, f32[3,5,128,128]{3,2,1,0:T(8,128)S(1)}, bf16[384,640]{1,0:T(8,128)(2,1)S(1)}, bf16[384,640]{1,0:T(8,128)(2,...) custom-call(s32[1,1,5]{2,1,0:T(1,128)} %cutoff_hbm.3, ...), custom_call_target="tpu_custom_call" | custom-call | bytes 5734932 | tf_op jit(solution)/shard_map/pallas_call | solution.py:266
  10.7 0.2 collective-permute-start.2
  11.0 0.0 collective-permute-done.four
  11.0 1.0 %shard_map.81 = (f32[4,128,128]{2,1,0:T(8,128)S(1)}, f32[4,128,128]{2,1,0:T(8,128)S(1)}, f32[384,640]{1,0:T(8,128)S(1)}, bf16[384,128]{1,0:T(8,128)(2,1)S(1)}, b...) custom-call(bf16[384,640]{1,0:T(8,128)(2,1)S(1)} %get-tuple-element.44.left_high, ...), custom_call_target="tpu_custom_call" | custom-call | flops 100663296000 | bytes 6094848 | tf_op jit(solution)/shard_map/pallas_call | solution.py:266
  12.0 2.4 %collective-permute-start.4 = (f32[4,128,128]{2,1,0:T(8,128)S(1)}, f32[4,128,128]{2,1,0:T(8,128)S(1)}, u32[]{:S(2)}, u32[]{:S(2)}) collective-permute-start(f32[4,128,128]{2,1,0:T(8,128)S(1)} %get-tuple-element.65), channel_id=1, source_target_pairs={{0,4},{4,0},{8,12},{12,8},{16,20},{20,16},{24,28},{28,24},{1,5},{5... | collective-permute-start | bytes 786440 | tf_op jit(solution)/shard_map/ppermute | solution.py:30
  14.4 1.0 %collective-permute-start.5 = (f32[4,128,128]{2,1,0:T(8,128)S(1)}, f32[4,128,128]{2,1,0:T(8,128)S(1)}, u32[]{:S(2)}, u32[]{:S(2)}) collective-permute-start(f32[4,128,128]{2,1,0:T(8,128)S(1)} %get-tuple-element.66), channel_id=1, source_target_pairs={{1,2},{2,1},{3,0},{0,3},{5,6},{6,5},{7,4},{4,7},{9,10},{10,9},{11,... | collective-permute-start | bytes 786440 | tf_op jit(solution)/shard_map/ppermute | solution.py:30
  15.4 3.6 %collective-permute-done.1.one = f32[4,128,128]{2,1,0:T(8,128)S(1)} collective-permute-done((f32[4,128,128]{2,1,0:T(8,128)S(1)}, f32[4,128,128]{2,1,0:T(8,128)S(1)}, u32[]{:S(2)}, u32[]{:S(2)}) %collective-permute-start.1) | collective-permute-done | bytes 262176 | tf_op jit(solution)/shard_map/ppermute | solution.py:30
  19.0 0.0 collective-permute-done.2.three
  19.0 0.0 copy-start
  19.0 1.4 %shard_map.82 = (f32[4,128,128]{2,1,0:T(8,128)S(1)}, bf16[384,128]{1,0:T(8,128)(2,1)S(1)}, bf16[384,128]{1,0:T(8,128)(2,1)S(1)}, f32[384,128]{1,0:T(8,128)S(1)}, f32[2,3,128,128]{3,2,1,0:T(8,128)S(1)}) custom-call(bf16[384,640]{1,0:T(8,128)(2,1)S(1)} %get-tuple-element.44.left_high, bf16[384,640]{1,0:T(8,128)(2,1)S(1)} %get-tuple-element.45.left_low, ...), custom_call_target="tpu_custom_call" | custom-call | flops 301989888 | bytes 6160384 | tf_op jit(solution)/shard_map/pallas_call | solution.py:266
  20.4 4.6 %collective-permute-start.6 = (f32[4,128,128]{2,1,0:T(8,128)S(1)}, f32[4,128,128]{2,1,0:T(8,128)S(1)}, u32[]{:S(2)}, u32[]{:S(2)}) collective-permute-start(f32[4,128,128]{2,1,0:T(8,128)S(1)} %get-tuple-element.70), channel_id=1, source_target_pairs={{4,8},{8,4},{12,16},{16,12},{20,24},{24,20},{28,0},{0,28},{5,9},{9... | collective-permute-start | bytes 786440 | tf_op jit(solution)/shard_map/ppermute | solution.py:30
  25.0 0.0 collective-permute-done.3.two
  25.0 0.0 copy-done
  25.0 1.6 %shard_map.83 = (f32[2,1,1,5,128,128]{5,4,3,2,1,0:T(8,128)}, bf16[384,128]{1,0:T(8,128)(2,1)S(1)}, bf16[384,128]{1,0:T(8,128)(2,1)S(1)}, bf16[384,128]{1,0:T(8,1...) custom-call(bf16[384,640]{1,0:T(8,128)(2,1)S(1)} %get-tuple-element., ...), custom_call_target="tpu_custom_call" | custom-call | flops 276824064 | bytes 7673856 | tf_op jit(solution)/shard_map/pallas_call | solution.py:266
  26.6 0.1 collective-permute-start.7
  26.7 1.9 %collective-permute-start.8 = (f32[3,128]{1,0:T(4,128)S(1)}, f32[3,128]{1,0:T(4,128)S(1)}, u32[]{:S(2)}, u32[]{:S(2)}) collective-permute-start(f32[3,128]{1,0:T(4,128)S(1)} %get-tuple-element.72), channel_id=1, source_target_pairs={{4,8},{8,4},{12,16},{16,12},{20,24},{24,20},{28,0},{0,28},{5,9},{9... | collective-permute-start | bytes 4616 | tf_op jit(solution)/shard_map/ppermute | solution.py:30
  28.6 0.5 %collective-permute-done.4.one = f32[4,128,128]{2,1,0:T(8,128)S(1)} collective-permute-done((f32[4,128,128]{2,1,0:T(8,128)S(1)}, f32[4,128,128]{2,1,0:T(8,128)S(1)}, u32[]{:S(2)}, u32[]{:S(2)}) %collective-permute-start.4) | collective-permute-done | bytes 262176 | tf_op jit(solution)/shard_map/ppermute | solution.py:30
  29.0 0.0 collective-permute-start.9
  29.0 0.0 collective-permute-done.5.four
  29.1 0.6 %collective-permute-start.10 = (f32[3,128]{1,0:T(4,128)S(1)}, f32[3,128]{1,0:T(4,128)S(1)}, u32[]{:S(2)}, u32[]{:S(2)}) collective-permute-start(f32[3,128]{1,0:T(4,128)S(1)} %get-tuple-element.74), channel_id=1, source_target_pairs={{1,2},{2,1},{3,0},{0,3},{5,6},{6,5},{7,4},{4,7},{9,10},{10,9},{11,... | collective-permute-start | bytes 4616 | tf_op jit(solution)/shard_map/ppermute | solution.py:30
  29.7 0.7 %shard_map.84 = (f32[5,128,128]{2,1,0:T(8,128)S(1)}, f32[128,128]{1,0:T(8,128)S(1)}, f32[3,128]{1,0:T(4,128)S(1)}) custom-call(bf16[384,640]{1,0:T(8,128)(2,1)S(1)} %get-tuple-element.44.left_high, bf16[384,640]{1,0:T(8,128)(2,1)S(1)} %get-tuple-element.45.left_low, bf16[384,128]{1,0:T(8,128)(2,1)S(1)} %get-tuple-element.56.self_high, ...), custom_call_target="tpu_custom_call" | custom-call | flops 251658240 | bytes 4916736 | tf_op jit(solution)/shard_map/pallas_call | solution.py:266
  30.4 0.0 collective-permute-done.7.c1
  30.4 2.6 %collective-permute-done.8.c2 = f32[3,128]{1,0:T(4,128)S(1)} collective-permute-done((f32[3,128]{1,0:T(4,128)S(1)}, f32[3,128]{1,0:T(4,128)S(1)}, u32[]{:S(2)}, u32[]{:S(2)}) %collective-permute-start.8) | collective-permute-done | bytes 1568 | tf_op jit(solution)/shard_map/ppermute | solution.py:30
  33.0 0.0 collective-permute-done.9.c3
  33.0 0.0 collective-permute-done.10.c4
  33.0 0.0 collective-permute-done.6.two
  33.0 1.8 %shard_map.85 = (f32[2,1,1,5,128,128]{5,4,3,2,1,0:T(8,128)}, f32[3,1,64]{2,1,0:T(1,128)}) custom-call(f32[3,5,128,128]{3,2,1,0:T(8,128)S(1)} %get-tuple-element.42.held, f32[3,1,1,5,128,128]{5,4,3,2,1,0:T(8,128)S(1)} %copy-done, f32[64,128]{1,0:T(8,128)S(1)} %get-tuple-element.43.members, ...), custom_call_target="tpu_custom_call", output_to_operand_aliasing={{0}: (13, {})} | custom-call | flops 125829120 | bytes 4366592 | tf_op jit(solution)/shard_map/pallas_call | solution.py:266
  (2 shorter events, 0.0 us)
Async XLA Ops:
  1.7 9.2 %collective-permute-start = (f32[4,128,128]{2,1,0:T(8,128)S(1)}, f32[4,128,128]{2,1,0:T(8,128)S(1)}, u32[]{:S(2)}, u32[]{:S(2)}) collective-permute-start(f32[4,128,128]{2,1,0:T(8,128)S(1)} %shard_map.78.message), channel_id=1, source_target_pairs={{1,2},{2,1},{3,0},{0,3},{5,6},{6,5},{7,4},{4,7},{9,10},{10,9},{11,... | collective-permute-start | bytes 786440 | tf_op jit(solution)/shard_map/ppermute | solution.py:30
  4.2 14.8 %collective-permute-start.1 = (f32[4,128,128]{2,1,0:T(8,128)S(1)}, f32[4,128,128]{2,1,0:T(8,128)S(1)}, u32[]{:S(2)}, u32[]{:S(2)}) collective-permute-start(f32[4,128,128]{2,1,0:T(8,128)S(1)} %get-tuple-element.40.message), channel_id=1, source_target_pairs={{0,4},{4,0},{8,12},{12,8},{16,20},{20,16},{24,28},{28,24},{1,5},{5... | collective-permute-start | bytes 786440 | tf_op jit(solution)/shard_map/ppermute | solution.py:30
  5.7 19.3 %collective-permute-start.3 = (f32[4,128,128]{2,1,0:T(8,128)S(1)}, f32[4,128,128]{2,1,0:T(8,128)S(1)}, u32[]{:S(2)}, u32[]{:S(2)}) collective-permute-start(f32[4,128,128]{2,1,0:T(8,128)S(1)} %shard_map.79.after), channel_id=1, source_target_pairs={{4,8},{8,4},{12,16},{16,12},{20,24},{24,20},{28,0},{0,28},{5,9},{9... | collective-permute-start | bytes 786440 | tf_op jit(solution)/shard_map/ppermute | solution.py:30
  10.7 8.2 %collective-permute-start.2 = (f32[8,128,128]{2,1,0:T(8,128)S(1)}, f32[8,128,128]{2,1,0:T(8,128)S(1)}, u32[]{:S(2)}, u32[]{:S(2)}) collective-permute-start(f32[8,128,128]{2,1,0:T(8,128)S(1)} %get-tuple-element.50), channel_id=1, source_target_pairs={{0,1},{1,0},{2,3},{3,2},{4,5},{5,4},{6,7},{7,6},{8,9},{9,8},{10,11... | collective-permute-start | bytes 1572872 | tf_op jit(solution)/shard_map/ppermute | solution.py:30
  12.0 17.0 %collective-permute-start.4 = (f32[4,128,128]{2,1,0:T(8,128)S(1)}, f32[4,128,128]{2,1,0:T(8,128)S(1)}, u32[]{:S(2)}, u32[]{:S(2)}) collective-permute-start(f32[4,128,128]{2,1,0:T(8,128)S(1)} %get-tuple-element.65), channel_id=1, source_target_pairs={{0,4},{4,0},{8,12},{12,8},{16,20},{20,16},{24,28},{28,24},{1,5},{5... | collective-permute-start | bytes 786440 | tf_op jit(solution)/shard_map/ppermute | solution.py:30
  14.4 14.6 %collective-permute-start.5 = (f32[4,128,128]{2,1,0:T(8,128)S(1)}, f32[4,128,128]{2,1,0:T(8,128)S(1)}, u32[]{:S(2)}, u32[]{:S(2)}) collective-permute-start(f32[4,128,128]{2,1,0:T(8,128)S(1)} %get-tuple-element.66), channel_id=1, source_target_pairs={{1,2},{2,1},{3,0},{0,3},{5,6},{6,5},{7,4},{4,7},{9,10},{10,9},{11,... | collective-permute-start | bytes 786440 | tf_op jit(solution)/shard_map/ppermute | solution.py:30
  19.0 6.0 %copy-start = (f32[3,1,1,5,128,128]{5,4,3,2,1,0:T(8,128)S(1)}, f32[3,1,1,5,128,128]{5,4,3,2,1,0:T(8,128)}, u32[]{:S(2)}) copy-start(f32[3,1,1,5,128,128]{5,4,3,2,1,0:T(8,128)} %der_ref.3) | copy-start | bytes 2949124
  20.4 12.7 %collective-permute-start.6 = (f32[4,128,128]{2,1,0:T(8,128)S(1)}, f32[4,128,128]{2,1,0:T(8,128)S(1)}, u32[]{:S(2)}, u32[]{:S(2)}) collective-permute-start(f32[4,128,128]{2,1,0:T(8,128)S(1)} %get-tuple-element.70), channel_id=1, source_target_pairs={{4,8},{8,4},{12,16},{16,12},{20,24},{24,20},{28,0},{0,28},{5,9},{9... | collective-permute-start | bytes 786440 | tf_op jit(solution)/shard_map/ppermute | solution.py:30
  26.6 3.8 %collective-permute-start.7 = (f32[3,128]{1,0:T(4,128)S(1)}, f32[3,128]{1,0:T(4,128)S(1)}, u32[]{:S(2)}, u32[]{:S(2)}) collective-permute-start(f32[3,128]{1,0:T(4,128)S(1)} %get-tuple-element.71), channel_id=1, source_target_pairs={{0,4},{4,0},{8,12},{12,8},{16,20},{20,16},{24,28},{28,24},{1,5},{5... | collective-permute-start | bytes 4616 | tf_op jit(solution)/shard_map/ppermute | solution.py:30
  26.7 6.3 %collective-permute-start.8 = (f32[3,128]{1,0:T(4,128)S(1)}, f32[3,128]{1,0:T(4,128)S(1)}, u32[]{:S(2)}, u32[]{:S(2)}) collective-permute-start(f32[3,128]{1,0:T(4,128)S(1)} %get-tuple-element.72), channel_id=1, source_target_pairs={{4,8},{8,4},{12,16},{16,12},{20,24},{24,20},{28,0},{0,28},{5,9},{9... | collective-permute-start | bytes 4616 | tf_op jit(solution)/shard_map/ppermute | solution.py:30
  29.0 4.0 %collective-permute-start.9 = (f32[3,128]{1,0:T(4,128)S(1)}, f32[3,128]{1,0:T(4,128)S(1)}, u32[]{:S(2)}, u32[]{:S(2)}) collective-permute-start(f32[3,128]{1,0:T(4,128)S(1)} %get-tuple-element.73), channel_id=1, source_target_pairs={{0,1},{1,0},{2,3},{3,2},{4,5},{5,4},{6,7},{7,6},{8,9},{9,8},{10,11... | collective-permute-start | bytes 4616 | tf_op jit(solution)/shard_map/ppermute | solution.py:30
  29.1 4.0 %collective-permute-start.10 = (f32[3,128]{1,0:T(4,128)S(1)}, f32[3,128]{1,0:T(4,128)S(1)}, u32[]{:S(2)}, u32[]{:S(2)}) collective-permute-start(f32[3,128]{1,0:T(4,128)S(1)} %get-tuple-element.74), channel_id=1, source_target_pairs={{1,2},{2,1},{3,0},{0,3},{5,6},{6,5},{7,4},{4,7},{9,10},{10,9},{11,... | collective-permute-start | bytes 4616 | tf_op jit(solution)/shard_map/ppermute | solution.py:30

commit v7 on v6

--- a/solution.py
+++ b/solution.py
@@ -153,10 +153,7 @@
         more[1 + kind] = held[kind, place]
 
 
-def third_kernel(
-    left_high, left_low, ham_high, ham_low, held, four, one_more, four_more, start, mixed_high, mixed_low, diagonal, other
-):
-    send_more(one_more, held, 1)
+def third_kernel(left_high, left_low, ham_high, ham_low, held, four, four_more, start, mixed_high, mixed_low, diagonal, other):
     send_more(four_more, held, 4)
     left = (left_high, left_low)
     start[...] = dot(part(left, slice(0, 3 * B), cols(0)), part((ham_high, ham_low), slice(0, B), cols(0, 5)))
@@ -164,22 +161,23 @@
     mixed_high[...], mixed_low[...] = mixed
 
 
-def fourth_kernel(
-    left_high, left_low, start, held, diagonal, one, three, two_more, mixed_high, mixed_low, diagonal_out, other
+def whole_kernel(left_high, left_low, start, held, diagonal, three, one_more, diagonal_out, other):
+    send_more(one_more, held, 1)
+    mixed, diagonal_out[...], real, other[1, 0] = first_half((left_high, left_low), 3, start, three, diagonal[...])
+    added, other[0, 1], other[1, 1] = second_half(mixed, three[4:])
+    other[0, 0] = real + added
+
+
+def fourth_kernel(left_high, left_low, start, diagonal, one, mixed_high, mixed_low, diagonal_out, other):
+    mixed, diagonal_out[...], other[0], other[1] = first_half((left_high, left_low), 1, start, one, diagonal[...])
+    mixed_high[...], mixed_low[...] = mixed
+
+
+def fifth_kernel(
+    left_high, left_low, start, diagonal, held, der_ref, other_one, other_three, other_four, two,
+    two_more, new, mixed_high, mixed_low, self_high, self_low, real_two, comm, weighted, c1, c2, c3, c4
 ):
     send_more(two_more, held, 2)
-    left = (left_high, left_low)
-    mixed, total, real, other[1, 1] = first_half(left, 3, start, three, diagonal[...])
-    added, other[0, 2], other[1, 2] = second_half(mixed, three[4:])
-    other[0, 1] = real + added
-    mixed, diagonal_out[...], other[0, 0], other[1, 0] = first_half(left, 1, start, one, total)
-    mixed_high[...], mixed_low[...] = mixed
-
-
-def fifth_kernel(
-    left_high, left_low, start, diagonal, held, der_ref, other, other_four, two,
-    out_hbm, mixed_high, mixed_low, self_high, self_low, real_two, comm, weighted, c1, c2, c3, c4, new, sems
-):
     order = order_of()
     left = (left_high, left_low)
     mixed, total, real_two[...], imag_two = first_half(left, 2, start, two, diagonal[...])
@@ -190,30 +188,34 @@
     ahead = dot(part(at_self, slice(0, B), cols(0)), part(left, slice(2 * B, 3 * B), whole))
     behind = dot(part(at_self, slice(2 * B, 3 * B), cols(0)), part(left, slice(0, B), whole))
     imag_comm = ahead - behind
-    comm[...] = imag_comm[:, cols(0)] + other[1, 2]
+    comm[...] = imag_comm[:, cols(0)] + other_three[1, 1]
     sums = [None] * 3
-    copies = []
     for place, column in enumerate((c1, c2, c3, c4), 1):
-        imag = (other[1, 0], imag_two, other[1, 1], other_four[1])[place - 1]
+        imag = (other_one[1], imag_two, other_three[1, 0], other_four[1])[place - 1]
         real_new = held[1, place] + time_step * (imag_comm[:, cols(place)] + imag)
         new[place - 1] = real_new
-        copies += start_all(
-            [pltpu.make_async_copy(new.at[place - 1], out_hbm.at[0, 0, 0, order[place]], sems.at[place - 1])]
-        )
         for direction in range(3):
             product = real_new * der_ref[direction, 0, 0, order[place]]
             sums[direction] = product if place == 1 else sums[direction] + product
             column[direction : direction + 1, :] = jnp.sum(product, axis=0, keepdims=True)
     for direction in range(3):
         weighted[direction] = sums[direction]
-    for copy in copies:
-        copy.wait()
+
+
+def four_kernel(mixed_high, mixed_low, four, c3, c4, c3_out, c4_out, other):
+    c3_out[...] = c3[...]
+    c4_out[...] = c4[...]
+    other[0], other[1], other[2] = second_half((mixed_high[...], mixed_low[...]), four)
 
 
 def real_kernel(
-    left_high, left_low, self_high, self_low, other, real_two, other_four, weighted, high_one, low_one, high_four, low_four,
-    imag_part, one, four, comm, imag_out, row_part
+    held, new, left_high, left_low, self_high, self_low, other_one, real_two, other_three, other_four, more_four, weighted,
+    high_one, low_one, imag_part, one, out_hbm, comm, row_part, imag_new, sems
 ):
+    order = order_of()
+    copies = start_all(
+        [pltpu.make_async_copy(new.at[at], out_hbm.at[0, 0, 0, order[1 + at]], sems.at[0, at]) for at in range(4)]
+    )
     left = (left_high, left_low)
     whole = cols(0, 5)
     at_self = (self_high, self_low)
@@ -221,32 +223,30 @@
     behind = dot(part(at_self, slice(B, 2 * B), cols(0)), part(left, slice(0, B), whole))
     real_comm = ahead - behind
     added_one, real_one, imag_one = second_half((high_one[...], low_one[...]), one)
-    added_four, real_four, imag_four = second_half((high_four[...], low_four[...]), four)
-    comm[0] = real_comm[:, cols(0)] + other[0, 2] + real_one + real_four
-    comm[1] = real_comm[:, cols(1)] + other[0, 0] + added_one
+    others = ((1, other_one[0] + added_one), (3, other_three[0, 0]), (4, other_four[0] + more_four[0]))
+    for at, (place, other) in enumerate(others):
+        imag_new[at] = held[2, place] - time_step * (real_comm[:, cols(place)] + other)
+        copies += start_all(
+            [pltpu.make_async_copy(imag_new.at[at], out_hbm.at[1, 0, 0, order[place]], sems.at[1, at])]
+        )
+    comm[0] = real_comm[:, cols(0)] + other_three[0, 1] + real_one + more_four[1]
+    comm[1] = imag_part[...] + imag_one + more_four[2]
     comm[2] = real_comm[:, cols(2)] + real_two[...]
-    comm[3] = real_comm[:, cols(3)] + other[0, 1]
-    comm[4] = real_comm[:, cols(4)] + other_four[0] + added_four
-    imag_out[...] = imag_part[...] + imag_one + imag_four
     for direction in range(3):
         row_part[direction : direction + 1, :] = jnp.sum(weighted[direction].T, axis=0, keepdims=True)
+    for copy in copies:
+        copy.wait()
 
 
 def sixth_kernel(
-    held, der_ref, members, high_two, low_two, imag_part, real_part, row_part, two, c1, c2, c3, c4, old_hbm,
-    out_hbm, forces_ref, new, sems
+    held, der_ref, members, high_two, low_two, comm, row_part, two, c1, c2, c3, c4, old_hbm, out_hbm, forces_hbm, new, forces_ref, sems
 ):
     order = order_of()
-    added, real_two, imag_two = second_half((high_two[...], low_two[...]), two)
-    real_new = held[1, 0] + time_step * (imag_part[...] + imag_two)
-    new[5] = real_new
-    copies = start_all([pltpu.make_async_copy(new.at[5], out_hbm.at[0, 0, 0, 0], sems.at[5])])
-    for place in range(5):
-        comm = real_part[place]
-        if place in (0, 2):
-            comm = comm + (real_two if place == 0 else added)
-        new[place] = held[2, place] - time_step * comm
-        copies += start_all([pltpu.make_async_copy(new.at[place], out_hbm.at[1, 0, 0, order[place]], sems.at[place])])
+    prop, inner = rows_of((high_two[...], low_two[...]))
+    behind = dot(inner, split(two[1]))
+    real_new = held[1, 0] + time_step * (comm[1] + dot(prop, split(two[3])) - behind[B:])
+    new[0] = real_new
+    copies = start_all([pltpu.make_async_copy(new.at[0], out_hbm.at[0, 0, 0, 0], sems.at[0])])
     parts = []
     for direction in range(3):
         product = real_new * der_ref[direction, 0, 0, 0]
@@ -257,6 +257,13 @@
     )
     for direction in range(3):
         forces_ref[direction] = forces[direction : direction + 1]
+    copies += start_all([pltpu.make_async_copy(forces_ref, forces_hbm, sems.at[3])])
+    ahead = dot(prop, beside(split(two[2]), split(two[0])))
+    new[1] = held[2, 0] - time_step * (comm[0] + ahead[:, cols(0)] - behind[:B])
+    new[2] = held[2, 2] - time_step * (comm[2] + ahead[:, cols(1)])
+    copies += start_all(
+        [pltpu.make_async_copy(new.at[1 + at], out_hbm.at[1, 0, 0, order[2 * at]], sems.at[1 + at]) for at in range(2)]
+    )
     for copy in copies:
         copy.wait()
 
@@ -309,48 +316,67 @@
     )
     near_three = swapped(send_three, 3)
     mixed = [shape(3 * B, B, kind=bf16)] * 2
-    one_more, four_more, start, high_four, low_four, diagonal, other_four = call(
+    four_more, start, high_four, low_four, diagonal, other_four = call(
         third_kernel,
-        [message] * 2 + [shape(3 * B, 5 * B)] + mixed + [shape(3 * B, B), shape(2, B, B)],
+        [message, shape(3 * B, 5 * B)] + mixed + [shape(3 * B, B), shape(2, B, B)],
         [vmem] * 6,
         8000,
         (left_high, left_low, ham_high, ham_low, held, near_four),
     )
+    near_four_more = swapped(four_more, 4)
+    one_more, diagonal, other_three = call(
+        whole_kernel,
+        [message, shape(3 * B, B), shape(2, 2, B, B)],
+        [vmem] * 6,
+        14,
+        (left_high, left_low, start, held, diagonal, near_three),
+    )
     near_one_more = swapped(one_more, 1)
-    near_four_more = swapped(four_more, 4)
-    two_more, high_one, low_one, diagonal, other = call(
+    high_one, low_one, diagonal, other_one = call(
         fourth_kernel,
-        [message] + mixed + [shape(3 * B, B), shape(2, 3, B, B)],
-        [vmem] * 7,
-        24,
-        (left_high, left_low, start, held, diagonal, near_one, near_three),
+        mixed + [shape(3 * B, B), shape(2, B, B)],
+        [vmem] * 5,
+        10,
+        (left_high, left_low, start, diagonal, near_one),
+    )
+    block = shape(B, B)
+    two_more, new, high_two, low_two, self_high, self_low, real_two, imag_part, weighted, *columns = call(
+        fifth_kernel,
+        [message, message] + mixed * 2 + [block, block, shape(3, B, B)] + [shape(3, B)] * 4,
+        [vmem] * 10,
+        22,
+        (left_high, left_low, start, diagonal, held, derivative, other_one, other_three, other_four, near_two),
     )
     near_two_more = swapped(two_more, 2)
-    out, high_two, low_two, self_high, self_low, real_two, imag_part, weighted, *columns = call(
-        fifth_kernel,
-        [shape(*density.shape)] + mixed * 2 + [shape(B, B), shape(B, B), shape(3, B, B)] + [shape(3, B)] * 4,
-        [vmem] * 9,
-        22,
-        (left_high, left_low, start, diagonal, held, derivative, other, other_four, near_two),
-        out_specs=[hbm] + [vmem] * 11,
-        scratch=[pltpu.VMEM((4, B, B), f32), dma((4,))],
-    )
-    columns = [swapped(column, at) for at, column in enumerate(columns, 1)]
-    args = (left_high, left_low, self_high, self_low, other, real_two, other_four, weighted, high_one, low_one)
-    args += (high_four, low_four, imag_part, near_one_more, near_four_more)
-    real_part, imag_part, row_part = call(
-        real_kernel, [shape(5, B, B), shape(B, B), shape(3, B)], [vmem] * 15, 20, args
-    )
-    args = (held, derivative, members, high_two, low_two, imag_part, real_part, row_part, near_two_more, *columns, out)
+    c3, c4, more_four = call(
+        four_kernel,
+        [shape(3, B)] * 2 + [shape(3, B, B)],
+        [vmem] * 5,
+        5,
+        (high_four, low_four, near_four_more, *columns[2:]),
+    )
+    columns = [swapped(column, at) for at, column in enumerate((*columns[:2], c3, c4), 1)]
+    args = (held, new, left_high, left_low, self_high, self_low, other_one, real_two, other_three, other_four, more_four, weighted)
+    args += (high_one, low_one, imag_part, near_one_more)
+    out, comm, row_part = call(
+        real_kernel,
+        [shape(*density.shape), shape(3, B, B), shape(3, B)],
+        [vmem] * 16,
+        15,
+        args,
+        out_specs=[hbm] + [vmem] * 2,
+        scratch=[pltpu.VMEM((3, B, B), f32), dma((2, 4))],
+    )
+    args = (held, derivative, members, high_two, low_two, comm, row_part, near_two_more, *columns, out)
     new_density, forces = call(
         sixth_kernel,
         [shape(*density.shape), shape(3, 1, ATOMS)],
-        [vmem] * 13 + [hbm],
+        [vmem] * 12 + [hbm],
         10,
         args,
-        out_specs=[hbm, vmem],
-        scratch=[pltpu.VMEM((6, B, B), f32), dma((6,))],
-        aliases={13: 0},
+        out_specs=[hbm, hbm],
+        scratch=[pltpu.VMEM((3, B, B), f32), pltpu.VMEM((3, 1, ATOMS), f32), dma((4,))],
+        aliases={12: 0},
     )
     return new_density, forces.reshape(1, 1, 3, ATOMS)
 

time: 35 us -> 33.6 us (0.960)
  waiting for transfers between devices: 6.71 us -> 4.47 us
  local copies, waits for them, and re-layouts: 0.01 us -> 0.59 us
  starting transfers between devices: 18.4 us -> 18.8 us
    ppermute x11, waiting for transfers between devices: 6.71 us -> 4.47 us  [swapped(): return lax.ppermute(cells, axis, pairs)]
    unnamed x2, local copies, waits for them, and re-layouts: 0.01 us -> 0.59 us
    ppermute x11, starting transfers between devices: 18.4 us -> 18.8 us  [swapped(): return lax.ppermute(cells, axis, pairs)]
    pallas_call x9 -> x11, Pallas kernels: 8.95 us -> 8.69 us  [call(): pl.pallas_call(kernel, out_shape=shapes, in_specs=in_specs, out_specs=out...]
  transfers between devices with their start and end apart: 11 -> 11, of which waited for: 3 -> 2; matrix products, arithmetic and copies ran while one was open for 0% -> 0% of each run, Pallas kernels for 17% -> 19%
where the time goes in v7:
time: 33.6 us; the launch traced here: 33.3 us
  starting transfers between devices  18.8 us (56%)
  Pallas kernels  8.69 us (26%)
  waiting for transfers between devices  4.47 us (13%)
  between operations  0.74 us (2%)
  local copies, waits for them, and re-layouts  0.59 us (2%)
    ppermute x11, starting transfers between devices, swapped(): return lax.ppermute(cells, axis, pairs)  18.8 us
    pallas_call x11, Pallas kernels, call(): pl.pallas_call(kernel, out_shape=shapes, in_specs=in_specs, out_specs=out...  8.69 us
    ppermute x11, waiting for transfers between devices, swapped(): return lax.ppermute(cells, axis, pairs)  4.47 us
  transfers between devices with their start and end apart: 11, of which 2 were waited for; matrix products, arithmetic and copies ran while one was open for 0% of the time, Pallas kernels for 19%

profile of v7, /device:TPU:0, one launch (start us, length us, event | category | flops | bytes accessed | tf_op | source)
XLA Modules:
  0.0 33.3 jit_solution(12752516340185129924)
XLA Ops:
  0.6 1.1 %shard_map.77 = (f32[4,128,128]{2,1,0:T(8,128)S(1)}, f32[2,128,128]{2,1,0:T(8,128)S(1)}) custom-call(s32[1,1,5]{2,1,0:T(1,128)} %cutoff_hbm.3, f32[1,1,5,128,128]{4,3,2,1,0:T(8,128)} %ham_hbm.3, f32[1,1,5,128,128]{4,3,2,1,0:T(8,128)} %inv_hbm.3, f32[2,1,1,5,128,128]{5,4,3,2,1,0:T(8,128)} %rho_hbm.3), custom_call_target="tpu_custom_call" | custom-call | bytes 1703956 | tf_op jit(solution)/shard_map/pallas_call | solution.py:273
  1.7 2.4 %collective-permute-start = (f32[4,128,128]{2,1,0:T(8,128)S(1)}, f32[4,128,128]{2,1,0:T(8,128)S(1)}, u32[]{:S(2)}, u32[]{:S(2)}) collective-permute-start(f32[4,128,128]{2,1,0:T(8,128)S(1)} %shard_map.78.message), channel_id=1, source_target_pairs={{1,2},{2,1},{3,0},{0,3},{5,6},{6,5},{7,4},{4,7},{9,10},{10,9},{11,... | collective-permute-start | bytes 786440 | tf_op jit(solution)/shard_map/ppermute | solution.py:30
  4.2 1.5 %collective-permute-start.2 = (f32[4,128,128]{2,1,0:T(8,128)S(1)}, f32[4,128,128]{2,1,0:T(8,128)S(1)}, u32[]{:S(2)}, u32[]{:S(2)}) collective-permute-start(f32[4,128,128]{2,1,0:T(8,128)S(1)} %get-tuple-element.45.message), channel_id=1, source_target_pairs={{0,4},{4,0},{8,12},{12,8},{16,20},{20,16},{24,28},{28,24},{1,5},{5... | collective-permute-start | bytes 786440 | tf_op jit(solution)/shard_map/ppermute | solution.py:30
  5.7 3.6 %collective-permute-start.3 = (f32[4,128,128]{2,1,0:T(8,128)S(1)}, f32[4,128,128]{2,1,0:T(8,128)S(1)}, u32[]{:S(2)}, u32[]{:S(2)}) collective-permute-start(f32[4,128,128]{2,1,0:T(8,128)S(1)} %shard_map.79.after), channel_id=1, source_target_pairs={{4,8},{8,4},{12,16},{16,12},{20,24},{24,20},{28,0},{0,28},{5,9},{9... | collective-permute-start | bytes 786440 | tf_op jit(solution)/shard_map/ppermute | solution.py:30
  9.3 1.4 %shard_map.80 = (f32[8,128,128]{2,1,0:T(8,128)S(1)}, f32[3,5,128,128]{3,2,1,0:T(8,128)S(1)}, bf16[384,640]{1,0:T(8,128)(2,1)S(1)}, bf16[384,640]{1,0:T(8,128)(2,...) custom-call(s32[1,1,5]{2,1,0:T(1,128)} %cutoff_hbm.3, ...), custom_call_target="tpu_custom_call" | custom-call | bytes 5734932 | tf_op jit(solution)/shard_map/pallas_call | solution.py:273
  10.7 0.2 collective-permute-start.1
  11.0 0.0 collective-permute-done.four
  11.0 1.0 %shard_map.81 = (f32[4,128,128]{2,1,0:T(8,128)S(1)}, f32[384,640]{1,0:T(8,128)S(1)}, bf16[384,128]{1,0:T(8,128)(2,1)S(1)}, bf16[384,128]{1,0:T(8,128)(2,1)S(1)},...) custom-call(bf16[384,640]{1,0:T(8,128)(2,1)S(1)} %get-tuple-element.49.left_high, ...), custom_call_target="tpu_custom_call" | custom-call | flops 100663296000 | bytes 5832704 | tf_op jit(solution)/shard_map/pallas_call | solution.py:273
  12.0 2.2 %collective-permute-start.4 = (f32[4,128,128]{2,1,0:T(8,128)S(1)}, f32[4,128,128]{2,1,0:T(8,128)S(1)}, u32[]{:S(2)}, u32[]{:S(2)}) collective-permute-start(f32[4,128,128]{2,1,0:T(8,128)S(1)} %get-tuple-element.69), channel_id=1, source_target_pairs={{1,2},{2,1},{3,0},{0,3},{5,6},{6,5},{7,4},{4,7},{9,10},{10,9},{11,... | collective-permute-start | bytes 786440 | tf_op jit(solution)/shard_map/ppermute | solution.py:30
  14.2 0.0 collective-permute-done.1.three
  14.2 0.8 %shard_map.82 = (f32[4,128,128]{2,1,0:T(8,128)S(1)}, f32[384,128]{1,0:T(8,128)S(1)}, f32[2,2,128,128]{3,2,1,0:T(8,128)S(1)}) custom-call(bf16[384,640]{1,0:T(8,128)(2,1)S(1)} %get-tuple-element.49.left_high, bf16[384,640]{1,0:T(8,128)(2,1)S(1)} %get-tuple-element.50.left_low, f32[384,640]{1,0:T(8,128)S(1)} %get-tuple-element.53.start, ...), custom_call_target="tpu_custom_call" | custom-call | flops 176160768 | bytes 5373952 | tf_op jit(solution)/shard_map/pallas_call | solution.py:273
  15.0 1.6 %collective-permute-start.5 = (f32[4,128,128]{2,1,0:T(8,128)S(1)}, f32[4,128,128]{2,1,0:T(8,128)S(1)}, u32[]{:S(2)}, u32[]{:S(2)}) collective-permute-start(f32[4,128,128]{2,1,0:T(8,128)S(1)} %get-tuple-element.77), channel_id=1, source_target_pairs={{0,4},{4,0},{8,12},{12,8},{16,20},{20,16},{24,28},{28,24},{1,5},{5... | collective-permute-start | bytes 786440 | tf_op jit(solution)/shard_map/ppermute | solution.py:30
  16.6 2.4 %collective-permute-done.2.one = f32[4,128,128]{2,1,0:T(8,128)S(1)} collective-permute-done((f32[4,128,128]{2,1,0:T(8,128)S(1)}, f32[4,128,128]{2,1,0:T(8,128)S(1)}, u32[]{:S(2)}, u32[]{:S(2)}) %collective-permute-start.2) | collective-permute-done | bytes 262176 | tf_op jit(solution)/shard_map/ppermute | solution.py:30
  19.0 0.0 copy-start
  19.0 0.6 %shard_map.83 = (bf16[384,128]{1,0:T(8,128)(2,1)S(1)}, bf16[384,128]{1,0:T(8,128)(2,1)S(1)}, f32[384,128]{1,0:T(8,128)S(1)}, f32[2,128,128]{2,1,0:T(8,128)S(1)}) custom-call(bf16[384,640]{1,0:T(8,128)(2,1)S(1)} %get-tuple-element.49.left_high, bf16[384,640]{1,0:T(8,128)(2,1)S(1)} %get-tuple-element.50.left_low, f32[384,640]{1,0:T(8,128)S(1)} %get-tuple-element.53.start, ...), custom_call_target="tpu_custom_call" | custom-call | flops 125829120 | bytes 4128768 | tf_op jit(solution)/shard_map/pallas_call | solution.py:273
  19.6 0.0 collective-permute-done.3.two
  19.6 0.6 %copy-done = f32[3,1,1,5,128,128]{5,4,3,2,1,0:T(8,128)S(1)} copy-done((f32[3,1,1,5,128,128]{5,4,3,2,1,0:T(8,128)S(1)}, f32[3,1,1,5,128,128]{5,4,3,2,1,0:T(8,128)}, u32[]{:S(2)}) %copy-start) | copy-done | bytes 983064
  20.2 0.9 %shard_map.84 = (f32[4,128,128]{2,1,0:T(8,128)S(1)}, f32[4,128,128]{2,1,0:T(8,128)S(1)}, bf16[384,128]{1,0:T(8,128)(2,1)S(1)}, bf16[384,128]{1,0:T(8,128)(2,1)S(...) custom-call(bf16[384,640]{1,0:T(8,128)(2,1)S(1)} %get-tuple-element., ...), custom_call_target="tpu_custom_call" | custom-call | flops 276824064 | bytes 7542784 | tf_op jit(solution)/shard_map/pallas_call | solution.py:273
  21.1 4.6 %collective-permute-start.6 = (f32[4,128,128]{2,1,0:T(8,128)S(1)}, f32[4,128,128]{2,1,0:T(8,128)S(1)}, u32[]{:S(2)}, u32[]{:S(2)}) collective-permute-start(f32[4,128,128]{2,1,0:T(8,128)S(1)} %get-tuple-element.80), channel_id=1, source_target_pairs={{4,8},{8,4},{12,16},{16,12},{20,24},{24,20},{28,0},{0,28},{5,9},{9... | collective-permute-start | bytes 786440 | tf_op jit(solution)/shard_map/ppermute | solution.py:30
  25.7 0.0 collective-permute-start.7
  25.7 1.9 %collective-permute-start.8 = (f32[3,128]{1,0:T(4,128)S(1)}, f32[3,128]{1,0:T(4,128)S(1)}, u32[]{:S(2)}, u32[]{:S(2)}) collective-permute-start(f32[3,128]{1,0:T(4,128)S(1)} %get-tuple-element.82), channel_id=1, source_target_pairs={{4,8},{8,4},{12,16},{16,12},{20,24},{24,20},{28,0},{0,28},{5,9},{9... | collective-permute-start | bytes 4616 | tf_op jit(solution)/shard_map/ppermute | solution.py:30
  27.7 0.0 collective-permute-done.4.four
  27.7 0.3 shard_map.85
  27.9 0.1 collective-permute-start.9
  28.0 0.0 collective-permute-done.5.one
  28.0 0.7 %collective-permute-start.10 = (f32[3,128]{1,0:T(4,128)S(1)}, f32[3,128]{1,0:T(4,128)S(1)}, u32[]{:S(2)}, u32[]{:S(2)}) collective-permute-start(f32[3,128]{1,0:T(4,128)S(1)} %get-tuple-element.84), channel_id=1, source_target_pairs={{1,2},{2,1},{3,0},{0,3},{5,6},{6,5},{7,4},{4,7},{9,10},{10,9},{11,... | collective-permute-start | bytes 4616 | tf_op jit(solution)/shard_map/ppermute | solution.py:30
  28.7 1.2 %shard_map.86 = (f32[2,1,1,5,128,128]{5,4,3,2,1,0:T(8,128)}, f32[3,128,128]{2,1,0:T(8,128)S(1)}, f32[3,128]{1,0:T(4,128)S(1)}) custom-call(f32[3,5,128,128]{3,2,1,0:T(8,128)S(1)} %get-tuple-element.47.held, f32[4,128,128]{2,1,0:T(8,128)S(1)} %get-tuple-element.63.new, bf16[384,640]{1,0:T(8,128)(2,1)S(1)} %get-tuple-element.49.left_high, ...), custom_call_target="tpu_custom_call" | custom-call | flops 188743680 | bytes 6161920 | tf_op jit(solution)/shard_map/pallas_call | solution.py:273
  30.0 0.0 collective-permute-done.7.c1
  30.0 2.1 %collective-permute-done.8.c2 = f32[3,128]{1,0:T(4,128)S(1)} collective-permute-done((f32[3,128]{1,0:T(4,128)S(1)}, f32[3,128]{1,0:T(4,128)S(1)}, u32[]{:S(2)}, u32[]{:S(2)}) %collective-permute-start.8) | collective-permute-done | bytes 1568 | tf_op jit(solution)/shard_map/ppermute | solution.py:30
  32.0 0.0 collective-permute-done.9.c3
  32.0 0.0 collective-permute-done.10.c4
  32.0 0.0 collective-permute-done.6.two
  32.0 1.3 %shard_map.87 = (f32[2,1,1,5,128,128]{5,4,3,2,1,0:T(8,128)}, f32[3,1,64]{2,1,0:T(1,128)}) custom-call(f32[3,5,128,128]{3,2,1,0:T(8,128)S(1)} %get-tuple-element.47.held, f32[3,1,1,5,128,128]{5,4,3,2,1,0:T(8,128)S(1)} %copy-done, f32[64,128]{1,0:T(8,128)S(1)} %get-tuple-element.48.members, ...), custom_call_target="tpu_custom_call", output_to_operand_aliasing={{0}: (12, {})} | custom-call | flops 125829120 | bytes 4169984 | tf_op jit(solution)/shard_map/pallas_call | solution.py:273
  (2 shorter events, 0.0 us)
Async XLA Ops:
  1.7 9.2 %collective-permute-start = (f32[4,128,128]{2,1,0:T(8,128)S(1)}, f32[4,128,128]{2,1,0:T(8,128)S(1)}, u32[]{:S(2)}, u32[]{:S(2)}) collective-permute-start(f32[4,128,128]{2,1,0:T(8,128)S(1)} %shard_map.78.message), channel_id=1, source_target_pairs={{1,2},{2,1},{3,0},{0,3},{5,6},{6,5},{7,4},{4,7},{9,10},{10,9},{11,... | collective-permute-start | bytes 786440 | tf_op jit(solution)/shard_map/ppermute | solution.py:30
  4.2 14.8 %collective-permute-start.2 = (f32[4,128,128]{2,1,0:T(8,128)S(1)}, f32[4,128,128]{2,1,0:T(8,128)S(1)}, u32[]{:S(2)}, u32[]{:S(2)}) collective-permute-start(f32[4,128,128]{2,1,0:T(8,128)S(1)} %get-tuple-element.45.message), channel_id=1, source_target_pairs={{0,4},{4,0},{8,12},{12,8},{16,20},{20,16},{24,28},{28,24},{1,5},{5... | collective-permute-start | bytes 786440 | tf_op jit(solution)/shard_map/ppermute | solution.py:30
  5.7 13.9 %collective-permute-start.3 = (f32[4,128,128]{2,1,0:T(8,128)S(1)}, f32[4,128,128]{2,1,0:T(8,128)S(1)}, u32[]{:S(2)}, u32[]{:S(2)}) collective-permute-start(f32[4,128,128]{2,1,0:T(8,128)S(1)} %shard_map.79.after), channel_id=1, source_target_pairs={{4,8},{8,4},{12,16},{16,12},{20,24},{24,20},{28,0},{0,28},{5,9},{9... | collective-permute-start | bytes 786440 | tf_op jit(solution)/shard_map/ppermute | solution.py:30
  10.7 3.4 %collective-permute-start.1 = (f32[8,128,128]{2,1,0:T(8,128)S(1)}, f32[8,128,128]{2,1,0:T(8,128)S(1)}, u32[]{:S(2)}, u32[]{:S(2)}) collective-permute-start(f32[8,128,128]{2,1,0:T(8,128)S(1)} %get-tuple-element.55), channel_id=1, source_target_pairs={{0,1},{1,0},{2,3},{3,2},{4,5},{5,4},{6,7},{7,6},{8,9},{9,8},{10,11... | collective-permute-start | bytes 1572872 | tf_op jit(solution)/shard_map/ppermute | solution.py:30
  12.0 15.7 %collective-permute-start.4 = (f32[4,128,128]{2,1,0:T(8,128)S(1)}, f32[4,128,128]{2,1,0:T(8,128)S(1)}, u32[]{:S(2)}, u32[]{:S(2)}) collective-permute-start(f32[4,128,128]{2,1,0:T(8,128)S(1)} %get-tuple-element.69), channel_id=1, source_target_pairs={{1,2},{2,1},{3,0},{0,3},{5,6},{6,5},{7,4},{4,7},{9,10},{10,9},{11,... | collective-permute-start | bytes 786440 | tf_op jit(solution)/shard_map/ppermute | solution.py:30
  15.0 13.0 %collective-permute-start.5 = (f32[4,128,128]{2,1,0:T(8,128)S(1)}, f32[4,128,128]{2,1,0:T(8,128)S(1)}, u32[]{:S(2)}, u32[]{:S(2)}) collective-permute-start(f32[4,128,128]{2,1,0:T(8,128)S(1)} %get-tuple-element.77), channel_id=1, source_target_pairs={{0,4},{4,0},{8,12},{12,8},{16,20},{20,16},{24,28},{28,24},{1,5},{5... | collective-permute-start | bytes 786440 | tf_op jit(solution)/shard_map/ppermute | solution.py:30
  19.0 1.2 %copy-start = (f32[3,1,1,5,128,128]{5,4,3,2,1,0:T(8,128)S(1)}, f32[3,1,1,5,128,128]{5,4,3,2,1,0:T(8,128)}, u32[]{:S(2)}) copy-start(f32[3,1,1,5,128,128]{5,4,3,2,1,0:T(8,128)} %der_ref.3) | copy-start | bytes 2949124
  21.1 10.9 %collective-permute-start.6 = (f32[4,128,128]{2,1,0:T(8,128)S(1)}, f32[4,128,128]{2,1,0:T(8,128)S(1)}, u32[]{:S(2)}, u32[]{:S(2)}) collective-permute-start(f32[4,128,128]{2,1,0:T(8,128)S(1)} %get-tuple-element.80), channel_id=1, source_target_pairs={{4,8},{8,4},{12,16},{16,12},{20,24},{24,20},{28,0},{0,28},{5,9},{9... | collective-permute-start | bytes 786440 | tf_op jit(solution)/shard_map/ppermute | solution.py:30
  25.7 4.2 %collective-permute-start.7 = (f32[3,128]{1,0:T(4,128)S(1)}, f32[3,128]{1,0:T(4,128)S(1)}, u32[]{:S(2)}, u32[]{:S(2)}) collective-permute-start(f32[3,128]{1,0:T(4,128)S(1)} %get-tuple-element.81), channel_id=1, source_target_pairs={{0,4},{4,0},{8,12},{12,8},{16,20},{20,16},{24,28},{28,24},{1,5},{5... | collective-permute-start | bytes 4616 | tf_op jit(solution)/shard_map/ppermute | solution.py:30
  25.7 6.3 %collective-permute-start.8 = (f32[3,128]{1,0:T(4,128)S(1)}, f32[3,128]{1,0:T(4,128)S(1)}, u32[]{:S(2)}, u32[]{:S(2)}) collective-permute-start(f32[3,128]{1,0:T(4,128)S(1)} %get-tuple-element.82), channel_id=1, source_target_pairs={{4,8},{8,4},{12,16},{16,12},{20,24},{24,20},{28,0},{0,28},{5,9},{9... | collective-permute-start | bytes 4616 | tf_op jit(solution)/shard_map/ppermute | solution.py:30
  27.9 4.1 %collective-permute-start.9 = (f32[3,128]{1,0:T(4,128)S(1)}, f32[3,128]{1,0:T(4,128)S(1)}, u32[]{:S(2)}, u32[]{:S(2)}) collective-permute-start(f32[3,128]{1,0:T(4,128)S(1)} %get-tuple-element.83), channel_id=1, source_target_pairs={{0,1},{1,0},{2,3},{3,2},{4,5},{5,4},{6,7},{7,6},{8,9},{9,8},{10,11... | collective-permute-start | bytes 4616 | tf_op jit(solution)/shard_map/ppermute | solution.py:30
  28.0 4.0 %collective-permute-start.10 = (f32[3,128]{1,0:T(4,128)S(1)}, f32[3,128]{1,0:T(4,128)S(1)}, u32[]{:S(2)}, u32[]{:S(2)}) collective-permute-start(f32[3,128]{1,0:T(4,128)S(1)} %get-tuple-element.84), channel_id=1, source_target_pairs={{1,2},{2,1},{3,0},{0,3},{5,6},{6,5},{7,4},{4,7},{9,10},{10,9},{11,... | collective-permute-start | bytes 4616 | tf_op jit(solution)/shard_map/ppermute | solution.py:30

commit v8 on v7

--- a/solution.py
+++ b/solution.py
@@ -161,11 +161,14 @@
     mixed_high[...], mixed_low[...] = mixed
 
 
-def whole_kernel(left_high, left_low, start, held, diagonal, three, one_more, diagonal_out, other):
-    send_more(one_more, held, 1)
+def whole_kernel(left_high, left_low, start, held, diagonal, three, der_hbm, two_more, diagonal_out, other, der, sem):
+    copy = pltpu.make_async_copy(der_hbm, der, sem)
+    copy.start()
+    send_more(two_more, held, 2)
     mixed, diagonal_out[...], real, other[1, 0] = first_half((left_high, left_low), 3, start, three, diagonal[...])
     added, other[0, 1], other[1, 1] = second_half(mixed, three[4:])
     other[0, 0] = real + added
+    copy.wait()
 
 
 def fourth_kernel(left_high, left_low, start, diagonal, one, mixed_high, mixed_low, diagonal_out, other):
@@ -175,9 +178,9 @@
 
 def fifth_kernel(
     left_high, left_low, start, diagonal, held, der_ref, other_one, other_three, other_four, two,
-    two_more, new, mixed_high, mixed_low, self_high, self_low, real_two, comm, weighted, c1, c2, c3, c4
+    one_more, new, mixed_high, mixed_low, self_high, self_low, real_two, comm, weighted, c1, c2, c3, c4
 ):
-    send_more(two_more, held, 2)
+    send_more(one_more, held, 1)
     order = order_of()
     left = (left_high, left_low)
     mixed, total, real_two[...], imag_two = first_half(left, 2, start, two, diagonal[...])
@@ -202,15 +205,18 @@
         weighted[direction] = sums[direction]
 
 
-def four_kernel(mixed_high, mixed_low, four, c3, c4, c3_out, c4_out, other):
-    c3_out[...] = c3[...]
-    c4_out[...] = c4[...]
+def pass_kernel(arrived, column, out):
+    out[...] = column[...]
+
+
+def four_kernel(mixed_high, mixed_low, four, column, out, other):
+    out[...] = column[...]
     other[0], other[1], other[2] = second_half((mixed_high[...], mixed_low[...]), four)
 
 
 def real_kernel(
     held, new, left_high, left_low, self_high, self_low, other_one, real_two, other_three, other_four, more_four, weighted,
-    high_one, low_one, imag_part, one, out_hbm, comm, row_part, imag_new, sems
+    high_two, low_two, imag_part, two, out_hbm, comm, row_part, imag_new, sems
 ):
     order = order_of()
     copies = start_all(
@@ -222,16 +228,16 @@
     ahead = dot(part(at_self, slice(0, B), cols(0)), part(left, slice(B, 2 * B), whole))
     behind = dot(part(at_self, slice(B, 2 * B), cols(0)), part(left, slice(0, B), whole))
     real_comm = ahead - behind
-    added_one, real_one, imag_one = second_half((high_one[...], low_one[...]), one)
-    others = ((1, other_one[0] + added_one), (3, other_three[0, 0]), (4, other_four[0] + more_four[0]))
+    added_two, real_self, imag_self = second_half((high_two[...], low_two[...]), two)
+    others = ((2, real_two[...] + added_two), (3, other_three[0, 0]), (4, other_four[0] + more_four[0]))
     for at, (place, other) in enumerate(others):
         imag_new[at] = held[2, place] - time_step * (real_comm[:, cols(place)] + other)
         copies += start_all(
             [pltpu.make_async_copy(imag_new.at[at], out_hbm.at[1, 0, 0, order[place]], sems.at[1, at])]
         )
-    comm[0] = real_comm[:, cols(0)] + other_three[0, 1] + real_one + more_four[1]
-    comm[1] = imag_part[...] + imag_one + more_four[2]
-    comm[2] = real_comm[:, cols(2)] + real_two[...]
+    comm[0] = real_comm[:, cols(0)] + other_three[0, 1] + real_self + more_four[1]
+    comm[1] = imag_part[...] + imag_self + more_four[2]
+    comm[2] = real_comm[:, cols(1)] + other_one[0]
     for direction in range(3):
         row_part[direction : direction + 1, :] = jnp.sum(weighted[direction].T, axis=0, keepdims=True)
     for copy in copies:
@@ -239,12 +245,12 @@
 
 
 def sixth_kernel(
-    held, der_ref, members, high_two, low_two, comm, row_part, two, c1, c2, c3, c4, old_hbm, out_hbm, forces_hbm, new, forces_ref, sems
+    held, der_ref, members, high_one, low_one, comm, row_part, one, c1, c2, c3, c4, old_hbm, out_hbm, forces_hbm, new, forces_ref, sems
 ):
     order = order_of()
-    prop, inner = rows_of((high_two[...], low_two[...]))
-    behind = dot(inner, split(two[1]))
-    real_new = held[1, 0] + time_step * (comm[1] + dot(prop, split(two[3])) - behind[B:])
+    prop, inner = rows_of((high_one[...], low_one[...]))
+    behind = dot(inner, split(one[1]))
+    real_new = held[1, 0] + time_step * (comm[1] + dot(prop, split(one[3])) - behind[B:])
     new[0] = real_new
     copies = start_all([pltpu.make_async_copy(new.at[0], out_hbm.at[0, 0, 0, 0], sems.at[0])])
     parts = []
@@ -258,11 +264,11 @@
     for direction in range(3):
         forces_ref[direction] = forces[direction : direction + 1]
     copies += start_all([pltpu.make_async_copy(forces_ref, forces_hbm, sems.at[3])])
-    ahead = dot(prop, beside(split(two[2]), split(two[0])))
+    ahead = dot(prop, beside(split(one[2]), split(one[0])))
     new[1] = held[2, 0] - time_step * (comm[0] + ahead[:, cols(0)] - behind[:B])
-    new[2] = held[2, 2] - time_step * (comm[2] + ahead[:, cols(1)])
+    new[2] = held[2, 1] - time_step * (comm[2] + ahead[:, cols(1)])
     copies += start_all(
-        [pltpu.make_async_copy(new.at[1 + at], out_hbm.at[1, 0, 0, order[2 * at]], sems.at[1 + at]) for at in range(2)]
+        [pltpu.make_async_copy(new.at[1 + at], out_hbm.at[1, 0, 0, order[at]], sems.at[1 + at]) for at in range(2)]
     )
     for copy in copies:
         copy.wait()
@@ -286,8 +292,9 @@
     def shape(*dims, kind=f32):
         return jax.ShapeDtypeStruct(dims, kind)
 
-    hamiltonian, inverse_margin, density, cutoff, atom_of = (
-        pltpu.with_memory_space_constraint(x, pltpu.HBM) for x in (hamiltonian, inverse_margin, density, cutoff, atom_of)
+    args = (hamiltonian, inverse_margin, density, cutoff, derivative, atom_of)
+    hamiltonian, inverse_margin, density, cutoff, derivative, atom_of = (
+        pltpu.with_memory_space_constraint(x, pltpu.HBM) for x in args
     )
     flags = pltpu.SMEM((1, 1, 5), jnp.int32)
     message = shape(4, B, B)
@@ -324,14 +331,15 @@
         (left_high, left_low, ham_high, ham_low, held, near_four),
     )
     near_four_more = swapped(four_more, 4)
-    one_more, diagonal, other_three = call(
+    two_more, diagonal, other_three, derivative = call(
         whole_kernel,
-        [message, shape(3 * B, B), shape(2, 2, B, B)],
-        [vmem] * 6,
+        [message, shape(3 * B, B), shape(2, 2, B, B), shape(*derivative.shape)],
+        [vmem] * 6 + [hbm],
         14,
-        (left_high, left_low, start, held, diagonal, near_three),
-    )
-    near_one_more = swapped(one_more, 1)
+        (left_high, left_low, start, held, diagonal, near_three, derivative),
+        scratch=[dma(())],
+    )
+    near_two_more = swapped(two_more, 2)
     high_one, low_one, diagonal, other_one = call(
         fourth_kernel,
         mixed + [shape(3 * B, B), shape(2, B, B)],
@@ -340,24 +348,29 @@
         (left_high, left_low, start, diagonal, near_one),
     )
     block = shape(B, B)
-    two_more, new, high_two, low_two, self_high, self_low, real_two, imag_part, weighted, *columns = call(
+    one_more, new, high_two, low_two, self_high, self_low, real_two, imag_part, weighted, *columns = call(
         fifth_kernel,
         [message, message] + mixed * 2 + [block, block, shape(3, B, B)] + [shape(3, B)] * 4,
         [vmem] * 10,
         22,
         (left_high, left_low, start, diagonal, held, derivative, other_one, other_three, other_four, near_two),
     )
-    near_two_more = swapped(two_more, 2)
-    c3, c4, more_four = call(
+    near_one_more = swapped(one_more, 1)
+    c4, more_four = call(
         four_kernel,
-        [shape(3, B)] * 2 + [shape(3, B, B)],
-        [vmem] * 5,
+        [shape(3, B), shape(3, B, B)],
+        [vmem] * 4,
         5,
-        (high_four, low_four, near_four_more, *columns[2:]),
-    )
-    columns = [swapped(column, at) for at, column in enumerate((*columns[:2], c3, c4), 1)]
+        (high_four, low_four, near_four_more, columns[3]),
+    )
+    c1, c2, c3, _ = columns
+    c2 = swapped(c2, 2)
+    c1 = swapped(c1, 1)
+    c4 = swapped(c4, 4)
+    (c3,) = call(pass_kernel, [shape(3, B)], [vmem] * 2, 0, (c1, c3))
+    columns = (c1, c2, swapped(c3, 3), c4)
     args = (held, new, left_high, left_low, self_high, self_low, other_one, real_two, other_three, other_four, more_four, weighted)
-    args += (high_one, low_one, imag_part, near_one_more)
+    args += (high_two, low_two, imag_part, near_two_more)
     out, comm, row_part = call(
         real_kernel,
         [shape(*density.shape), shape(3, B, B), shape(3, B)],
@@ -367,7 +380,7 @@
         out_specs=[hbm] + [vmem] * 2,
         scratch=[pltpu.VMEM((3, B, B), f32), dma((2, 4))],
     )
-    args = (held, derivative, members, high_two, low_two, comm, row_part, near_two_more, *columns, out)
+    args = (held, derivative, members, high_one, low_one, comm, row_part, near_one_more, *columns, out)
     new_density, forces = call(
         sixth_kernel,
         [shape(*density.shape), shape(3, 1, ATOMS)],

time: 33.6 us -> 35.4 us (1.054)
  starting transfers between devices: 18.8 us -> 20.4 us
  local copies, waits for them, and re-layouts: 0.59 us -> 0 us
  waiting for transfers between devices: 4.47 us -> 4.92 us
  Pallas kernels: 8.69 us -> 9.1 us
    ppermute x11, starting transfers between devices: 18.8 us -> 20.4 us  [swapped(): return lax.ppermute(cells, axis, pairs)]
    unnamed x2 -> x0, local copies, waits for them, and re-layouts: 0.59 us -> none
    ppermute x11, waiting for transfers between devices: 4.47 us -> 4.92 us  [swapped(): return lax.ppermute(cells, axis, pairs)]
    pallas_call x11 -> x12, Pallas kernels: 8.69 us -> 9.1 us  [call(): pl.pallas_call(kernel, out_shape=shapes, in_specs=in_specs, out_specs=out...]
  transfers between devices with their start and end apart: 11 -> 11, of which waited for: 2 -> 1; matrix products, arithmetic and copies ran while one was open for 0% -> 0% of each run, Pallas kernels for 19% -> 19%
where the time goes in v8:
time: 35.4 us; the launch traced here: 35.2 us
  starting transfers between devices  20.4 us (58%)
  Pallas kernels  9.1 us (26%)
  waiting for transfers between devices  4.92 us (14%)
  between operations  0.76 us (2%)
    ppermute x11, starting transfers between devices, swapped(): return lax.ppermute(cells, axis, pairs)  20.4 us
    pallas_call x12, Pallas kernels, call(): pl.pallas_call(kernel, out_shape=shapes, in_specs=in_specs, out_specs=out...  9.1 us
    ppermute x11, waiting for transfers between devices, swapped(): return lax.ppermute(cells, axis, pairs)  4.92 us
  transfers between devices with their start and end apart: 11, of which 1 were waited for; matrix products, arithmetic and copies ran while one was open for 0% of the time, Pallas kernels for 19%

profile of v8, /device:TPU:0, one launch (start us, length us, event | category | flops | bytes accessed | tf_op | source)
XLA Modules:
  0.0 35.2 jit_solution(8956894363496187926)
XLA Ops:
  0.6 1.1 %shard_map.77 = (f32[4,128,128]{2,1,0:T(8,128)S(1)}, f32[2,128,128]{2,1,0:T(8,128)S(1)}) custom-call(s32[1,1,5]{2,1,0:T(1,128)} %cutoff_hbm.3, f32[1,1,5,128,128]{4,3,2,1,0:T(8,128)} %ham_hbm.3, f32[1,1,5,128,128]{4,3,2,1,0:T(8,128)} %inv_hbm.3, f32[2,1,1,5,128,128]{5,4,3,2,1,0:T(8,128)} %rho_hbm.3), custom_call_target="tpu_custom_call" | custom-call | bytes 1703956 | tf_op jit(solution)/shard_map/pallas_call | solution.py:279
  1.7 2.4 %collective-permute-start = (f32[4,128,128]{2,1,0:T(8,128)S(1)}, f32[4,128,128]{2,1,0:T(8,128)S(1)}, u32[]{:S(2)}, u32[]{:S(2)}) collective-permute-start(f32[4,128,128]{2,1,0:T(8,128)S(1)} %shard_map.78.message), channel_id=1, source_target_pairs={{1,2},{2,1},{3,0},{0,3},{5,6},{6,5},{7,4},{4,7},{9,10},{10,9},{11,... | collective-permute-start | bytes 786440 | tf_op jit(solution)/shard_map/ppermute | solution.py:30
  4.2 1.5 %collective-permute-start.2 = (f32[4,128,128]{2,1,0:T(8,128)S(1)}, f32[4,128,128]{2,1,0:T(8,128)S(1)}, u32[]{:S(2)}, u32[]{:S(2)}) collective-permute-start(f32[4,128,128]{2,1,0:T(8,128)S(1)} %get-tuple-element.45.message), channel_id=1, source_target_pairs={{0,4},{4,0},{8,12},{12,8},{16,20},{20,16},{24,28},{28,24},{1,5},{5... | collective-permute-start | bytes 786440 | tf_op jit(solution)/shard_map/ppermute | solution.py:30
  5.7 3.6 %collective-permute-start.3 = (f32[4,128,128]{2,1,0:T(8,128)S(1)}, f32[4,128,128]{2,1,0:T(8,128)S(1)}, u32[]{:S(2)}, u32[]{:S(2)}) collective-permute-start(f32[4,128,128]{2,1,0:T(8,128)S(1)} %shard_map.79.after), channel_id=1, source_target_pairs={{4,8},{8,4},{12,16},{16,12},{20,24},{24,20},{28,0},{0,28},{5,9},{9... | collective-permute-start | bytes 786440 | tf_op jit(solution)/shard_map/ppermute | solution.py:30
  9.3 1.4 %shard_map.80 = (f32[8,128,128]{2,1,0:T(8,128)S(1)}, f32[3,5,128,128]{3,2,1,0:T(8,128)S(1)}, bf16[384,640]{1,0:T(8,128)(2,1)S(1)}, bf16[384,640]{1,0:T(8,128)(2,...) custom-call(s32[1,1,5]{2,1,0:T(1,128)} %cutoff_hbm.3, ...), custom_call_target="tpu_custom_call" | custom-call | bytes 5734932 | tf_op jit(solution)/shard_map/pallas_call | solution.py:279
  10.7 0.2 collective-permute-start.1
  11.0 0.0 collective-permute-done.four
  11.0 1.0 %shard_map.81 = (f32[4,128,128]{2,1,0:T(8,128)S(1)}, f32[384,640]{1,0:T(8,128)S(1)}, bf16[384,128]{1,0:T(8,128)(2,1)S(1)}, bf16[384,128]{1,0:T(8,128)(2,1)S(1)},...) custom-call(bf16[384,640]{1,0:T(8,128)(2,1)S(1)} %get-tuple-element.48.left_high, ...), custom_call_target="tpu_custom_call" | custom-call | flops 100663296000 | bytes 5832704 | tf_op jit(solution)/shard_map/pallas_call | solution.py:279
  12.0 2.2 %collective-permute-start.4 = (f32[4,128,128]{2,1,0:T(8,128)S(1)}, f32[4,128,128]{2,1,0:T(8,128)S(1)}, u32[]{:S(2)}, u32[]{:S(2)}) collective-permute-start(f32[4,128,128]{2,1,0:T(8,128)S(1)} %get-tuple-element.70), channel_id=1, source_target_pairs={{1,2},{2,1},{3,0},{0,3},{5,6},{6,5},{7,4},{4,7},{9,10},{10,9},{11,... | collective-permute-start | bytes 786440 | tf_op jit(solution)/shard_map/ppermute | solution.py:30
  14.2 0.0 collective-permute-done.1.three
  14.2 1.2 %shard_map.82 = (f32[4,128,128]{2,1,0:T(8,128)S(1)}, f32[384,128]{1,0:T(8,128)S(1)}, f32[2,2,128,128]{3,2,1,0:T(8,128)S(1)}, f32[3,1,1,5,128,128]{5,4,3,2,1,0:T(8,128)S(1)}) custom-call(bf16[384,640]{1,0:T(8,128)(2,1)S(1)} %get-tuple-element.48.left_high, bf16[384,640]{1,0:T(8,128)(2,1)S(1)} %get-tuple-element.49.left_low, ...), custom_call_target="tpu_custom_call" | custom-call | flops 176160768 | bytes 7340032 | tf_op jit(solution)/shard_map/pallas_call | solution.py:279
  15.4 4.6 %collective-permute-start.5 = (f32[4,128,128]{2,1,0:T(8,128)S(1)}, f32[4,128,128]{2,1,0:T(8,128)S(1)}, u32[]{:S(2)}, u32[]{:S(2)}) collective-permute-start(f32[4,128,128]{2,1,0:T(8,128)S(1)} %get-tuple-element.77), channel_id=1, source_target_pairs={{4,8},{8,4},{12,16},{16,12},{20,24},{24,20},{28,0},{0,28},{5,9},{9... | collective-permute-start | bytes 786440 | tf_op jit(solution)/shard_map/ppermute | solution.py:30
  20.0 0.0 collective-permute-done.2.one
  20.0 0.6 %shard_map.83 = (bf16[384,128]{1,0:T(8,128)(2,1)S(1)}, bf16[384,128]{1,0:T(8,128)(2,1)S(1)}, f32[384,128]{1,0:T(8,128)S(1)}, f32[2,128,128]{2,1,0:T(8,128)S(1)}) custom-call(bf16[384,640]{1,0:T(8,128)(2,1)S(1)} %get-tuple-element.48.left_high, bf16[384,640]{1,0:T(8,128)(2,1)S(1)} %get-tuple-element.49.left_low, f32[384,640]{1,0:T(8,128)S(1)} %get-tuple-element.52.start, ...), custom_call_target="tpu_custom_call" | custom-call | flops 125829120 | bytes 4128768 | tf_op jit(solution)/shard_map/pallas_call | solution.py:279
  20.6 0.0 collective-permute-done.3.two
  20.6 0.9 %shard_map.84 = (f32[4,128,128]{2,1,0:T(8,128)S(1)}, f32[4,128,128]{2,1,0:T(8,128)S(1)}, bf16[384,128]{1,0:T(8,128)(2,1)S(1)}, bf16[384,128]{1,0:T(8,128)(2,1)S(...) custom-call(bf16[384,640]{1,0:T(8,128)(2,1)S(1)} %get-tuple-element., ...), custom_call_target="tpu_custom_call" | custom-call | flops 276824064 | bytes 7542784 | tf_op jit(solution)/shard_map/pallas_call | solution.py:279
  21.6 0.3 collective-permute-start.6
  21.8 1.8 %collective-permute-start.7 = (f32[3,128]{1,0:T(4,128)S(1)}, f32[3,128]{1,0:T(4,128)S(1)}, u32[]{:S(2)}, u32[]{:S(2)}) collective-permute-start(f32[3,128]{1,0:T(4,128)S(1)} %get-tuple-element.81), channel_id=1, source_target_pairs={{0,4},{4,0},{8,12},{12,8},{16,20},{20,16},{24,28},{28,24},{1,5},{5... | collective-permute-start | bytes 4616 | tf_op jit(solution)/shard_map/ppermute | solution.py:30
  23.7 0.0 collective-permute-done.4.four
  23.7 0.3 shard_map.85
  24.0 0.1 collective-permute-start.10
  24.1 3.6 %collective-permute-start.8 = (f32[3,128]{1,0:T(4,128)S(1)}, f32[3,128]{1,0:T(4,128)S(1)}, u32[]{:S(2)}, u32[]{:S(2)}) collective-permute-start(f32[3,128]{1,0:T(4,128)S(1)} %get-tuple-element.82), channel_id=1, source_target_pairs={{4,8},{8,4},{12,16},{16,12},{20,24},{24,20},{28,0},{0,28},{5,9},{9... | collective-permute-start | bytes 4616 | tf_op jit(solution)/shard_map/ppermute | solution.py:30
  27.7 4.9 %collective-permute-done.7.arrived.c1 = f32[3,128]{1,0:T(4,128)S(1)} collective-permute-done((f32[3,128]{1,0:T(4,128)S(1)}, f32[3,128]{1,0:T(4,128)S(1)}, u32[]{:S(2)}, u32[]{:S(2)}) %collective-permute-start.7) | collective-permute-done | bytes 1568 | tf_op jit(solution)/shard_map/ppermute | solution.py:30
  32.6 0.0 collective-permute-start.9
  32.6 0.0 collective-permute-done.5.two
  32.6 1.3 %shard_map.86 = (f32[2,1,1,5,128,128]{5,4,3,2,1,0:T(8,128)}, f32[3,128,128]{2,1,0:T(8,128)S(1)}, f32[3,128]{1,0:T(4,128)S(1)}) custom-call(f32[3,5,128,128]{3,2,1,0:T(8,128)S(1)} %get-tuple-element.47.held, f32[4,128,128]{2,1,0:T(8,128)S(1)} %get-tuple-element.64.new, bf16[384,640]{1,0:T(8,128)(2,1)S(1)} %get-tuple-element.48.left_high, ...), custom_call_target="tpu_custom_call" | custom-call | flops 188743680 | bytes 6161920 | tf_op jit(solution)/shard_map/pallas_call | solution.py:279
  33.9 0.0 collective-permute-done.10.c4
  33.9 0.0 collective-permute-done.8.c2
  33.9 0.0 collective-permute-done.9.c3
  33.9 0.0 collective-permute-done.6.one
  33.9 1.3 %shard_map.88 = (f32[2,1,1,5,128,128]{5,4,3,2,1,0:T(8,128)}, f32[3,1,64]{2,1,0:T(1,128)}) custom-call(f32[3,5,128,128]{3,2,1,0:T(8,128)S(1)} %get-tuple-element.47.held, f32[3,1,1,5,128,128]{5,4,3,2,1,0:T(8,128)S(1)} %get-tuple-element.55.der_ref, f32[64,128]{1,0:T(8,128)S(1)} %get-tuple-element.56.members, ...), custom_call_target="tpu_custom_call", output_to_operand_aliasing={{0}: (12, {})} | custom-call | flops 125829120 | bytes 4169984 | tf_op jit(solution)/shard_map/pallas_call | solution.py:279
  (3 shorter events, 0.0 us)
Async XLA Ops:
  1.7 9.2 %collective-permute-start = (f32[4,128,128]{2,1,0:T(8,128)S(1)}, f32[4,128,128]{2,1,0:T(8,128)S(1)}, u32[]{:S(2)}, u32[]{:S(2)}) collective-permute-start(f32[4,128,128]{2,1,0:T(8,128)S(1)} %shard_map.78.message), channel_id=1, source_target_pairs={{1,2},{2,1},{3,0},{0,3},{5,6},{6,5},{7,4},{4,7},{9,10},{10,9},{11,... | collective-permute-start | bytes 786440 | tf_op jit(solution)/shard_map/ppermute | solution.py:30
  4.2 15.8 %collective-permute-start.2 = (f32[4,128,128]{2,1,0:T(8,128)S(1)}, f32[4,128,128]{2,1,0:T(8,128)S(1)}, u32[]{:S(2)}, u32[]{:S(2)}) collective-permute-start(f32[4,128,128]{2,1,0:T(8,128)S(1)} %get-tuple-element.45.message), channel_id=1, source_target_pairs={{0,4},{4,0},{8,12},{12,8},{16,20},{20,16},{24,28},{28,24},{1,5},{5... | collective-permute-start | bytes 786440 | tf_op jit(solution)/shard_map/ppermute | solution.py:30
  5.7 14.9 %collective-permute-start.3 = (f32[4,128,128]{2,1,0:T(8,128)S(1)}, f32[4,128,128]{2,1,0:T(8,128)S(1)}, u32[]{:S(2)}, u32[]{:S(2)}) collective-permute-start(f32[4,128,128]{2,1,0:T(8,128)S(1)} %shard_map.79.after), channel_id=1, source_target_pairs={{4,8},{8,4},{12,16},{16,12},{20,24},{24,20},{28,0},{0,28},{5,9},{9... | collective-permute-start | bytes 786440 | tf_op jit(solution)/shard_map/ppermute | solution.py:30
  10.7 3.4 %collective-permute-start.1 = (f32[8,128,128]{2,1,0:T(8,128)S(1)}, f32[8,128,128]{2,1,0:T(8,128)S(1)}, u32[]{:S(2)}, u32[]{:S(2)}) collective-permute-start(f32[8,128,128]{2,1,0:T(8,128)S(1)} %get-tuple-element.54), channel_id=1, source_target_pairs={{0,1},{1,0},{2,3},{3,2},{4,5},{5,4},{6,7},{7,6},{8,9},{9,8},{10,11... | collective-permute-start | bytes 1572872 | tf_op jit(solution)/shard_map/ppermute | solution.py:30
  12.0 11.7 %collective-permute-start.4 = (f32[4,128,128]{2,1,0:T(8,128)S(1)}, f32[4,128,128]{2,1,0:T(8,128)S(1)}, u32[]{:S(2)}, u32[]{:S(2)}) collective-permute-start(f32[4,128,128]{2,1,0:T(8,128)S(1)} %get-tuple-element.70), channel_id=1, source_target_pairs={{1,2},{2,1},{3,0},{0,3},{5,6},{6,5},{7,4},{4,7},{9,10},{10,9},{11,... | collective-permute-start | bytes 786440 | tf_op jit(solution)/shard_map/ppermute | solution.py:30
  15.4 17.2 %collective-permute-start.5 = (f32[4,128,128]{2,1,0:T(8,128)S(1)}, f32[4,128,128]{2,1,0:T(8,128)S(1)}, u32[]{:S(2)}, u32[]{:S(2)}) collective-permute-start(f32[4,128,128]{2,1,0:T(8,128)S(1)} %get-tuple-element.77), channel_id=1, source_target_pairs={{4,8},{8,4},{12,16},{16,12},{20,24},{24,20},{28,0},{0,28},{5,9},{9... | collective-permute-start | bytes 786440 | tf_op jit(solution)/shard_map/ppermute | solution.py:30
  21.6 12.3 %collective-permute-start.6 = (f32[4,128,128]{2,1,0:T(8,128)S(1)}, f32[4,128,128]{2,1,0:T(8,128)S(1)}, u32[]{:S(2)}, u32[]{:S(2)}) collective-permute-start(f32[4,128,128]{2,1,0:T(8,128)S(1)} %get-tuple-element.80), channel_id=1, source_target_pairs={{0,4},{4,0},{8,12},{12,8},{16,20},{20,16},{24,28},{28,24},{1,5},{5... | collective-permute-start | bytes 786440 | tf_op jit(solution)/shard_map/ppermute | solution.py:30
  21.8 10.7 %collective-permute-start.7 = (f32[3,128]{1,0:T(4,128)S(1)}, f32[3,128]{1,0:T(4,128)S(1)}, u32[]{:S(2)}, u32[]{:S(2)}) collective-permute-start(f32[3,128]{1,0:T(4,128)S(1)} %get-tuple-element.81), channel_id=1, source_target_pairs={{0,4},{4,0},{8,12},{12,8},{16,20},{20,16},{24,28},{28,24},{1,5},{5... | collective-permute-start | bytes 4616 | tf_op jit(solution)/shard_map/ppermute | solution.py:30
  24.0 9.9 %collective-permute-start.10 = (f32[3,128]{1,0:T(4,128)S(1)}, f32[3,128]{1,0:T(4,128)S(1)}, u32[]{:S(2)}, u32[]{:S(2)}) collective-permute-start(f32[3,128]{1,0:T(4,128)S(1)} %get-tuple-element.84), channel_id=1, source_target_pairs={{1,2},{2,1},{3,0},{0,3},{5,6},{6,5},{7,4},{4,7},{9,10},{10,9},{11,... | collective-permute-start | bytes 4616 | tf_op jit(solution)/shard_map/ppermute | solution.py:30
  24.1 9.8 %collective-permute-start.8 = (f32[3,128]{1,0:T(4,128)S(1)}, f32[3,128]{1,0:T(4,128)S(1)}, u32[]{:S(2)}, u32[]{:S(2)}) collective-permute-start(f32[3,128]{1,0:T(4,128)S(1)} %get-tuple-element.82), channel_id=1, source_target_pairs={{4,8},{8,4},{12,16},{16,12},{20,24},{24,20},{28,0},{0,28},{5,9},{9... | collective-permute-start | bytes 4616 | tf_op jit(solution)/shard_map/ppermute | solution.py:30
  32.6 1.3 %collective-permute-start.9 = (f32[3,128]{1,0:T(4,128)S(1)}, f32[3,128]{1,0:T(4,128)S(1)}, u32[]{:S(2)}, u32[]{:S(2)}) collective-permute-start(f32[3,128]{1,0:T(4,128)S(1)} %shard_map.87), channel_id=1, source_target_pairs={{0,1},{1,0},{2,3},{3,2},{4,5},{5,4},{6,7},{7,6},{8,9},{9,8},{10,11... | collective-permute-start | bytes 4616 | tf_op jit(solution)/shard_map/ppermute | solution.py:30

commit v9 on v8

--- a/solution.py
+++ b/solution.py
@@ -178,9 +178,8 @@
 
 def fifth_kernel(
     left_high, left_low, start, diagonal, held, der_ref, other_one, other_three, other_four, two,
-    one_more, new, mixed_high, mixed_low, self_high, self_low, real_two, comm, weighted, c1, c2, c3, c4
+    new, mixed_high, mixed_low, self_high, self_low, real_two, comm, weighted, c1, c2, c3, c4
 ):
-    send_more(one_more, held, 1)
     order = order_of()
     left = (left_high, left_low)
     mixed, total, real_two[...], imag_two = first_half(left, 2, start, two, diagonal[...])
@@ -205,7 +204,8 @@
         weighted[direction] = sums[direction]
 
 
-def pass_kernel(arrived, column, out):
+def more_kernel(held, arrived, column, one_more, out):
+    send_more(one_more, held, 1)
     out[...] = column[...]
 
 
@@ -309,7 +309,7 @@
     near_one = swapped(first_one, 1)
     (first_four,) = call(functools.partial(next_kernel, 0), [message], [vmem] * 2, 0, (first_one, rest))
     near_four = swapped(first_four, 4)
-    (first_two,) = call(functools.partial(next_kernel, 1), [message], [vmem] * 2, 0, (first_four, rest))
+    (first_two,) = call(functools.partial(next_kernel, 1), [message], [vmem] * 2, 500, (first_four, rest))
     near_two = swapped(first_two, 2)
     left = [shape(3 * B, 5 * B, kind=bf16)] * 2
     ham = [shape(B, 5 * B, kind=bf16)] * 2
@@ -348,27 +348,26 @@
         (left_high, left_low, start, diagonal, near_one),
     )
     block = shape(B, B)
-    one_more, new, high_two, low_two, self_high, self_low, real_two, imag_part, weighted, *columns = call(
+    new, high_two, low_two, self_high, self_low, real_two, imag_part, weighted, *columns = call(
         fifth_kernel,
-        [message, message] + mixed * 2 + [block, block, shape(3, B, B)] + [shape(3, B)] * 4,
+        [message] + mixed * 2 + [block, block, shape(3, B, B)] + [shape(3, B)] * 4,
         [vmem] * 10,
         22,
         (left_high, left_low, start, diagonal, held, derivative, other_one, other_three, other_four, near_two),
     )
+    c1, c2, c3, c4 = columns
+    c1 = swapped(c1, 1)
+    c2 = swapped(c2, 2)
+    one_more, c3 = call(more_kernel, [message, shape(3, B)], [vmem] * 3, 0, (held, c1, c3))
     near_one_more = swapped(one_more, 1)
     c4, more_four = call(
         four_kernel,
         [shape(3, B), shape(3, B, B)],
         [vmem] * 4,
         5,
-        (high_four, low_four, near_four_more, columns[3]),
-    )
-    c1, c2, c3, _ = columns
-    c2 = swapped(c2, 2)
-    c1 = swapped(c1, 1)
-    c4 = swapped(c4, 4)
-    (c3,) = call(pass_kernel, [shape(3, B)], [vmem] * 2, 0, (c1, c3))
-    columns = (c1, c2, swapped(c3, 3), c4)
+        (high_four, low_four, near_four_more, c4),
+    )
+    columns = (c1, c2, swapped(c3, 3), swapped(c4, 4))
     args = (held, new, left_high, left_low, self_high, self_low, other_one, real_two, other_three, other_four, more_four, weighted)
     args += (high_two, low_two, imag_part, near_two_more)
     out, comm, row_part = call(

time: 35.4 us -> 35.3 us (level)
  starting transfers between devices: 20.4 us -> 15.9 us
  waiting for transfers between devices: 4.92 us -> 9.26 us
    ppermute x11, starting transfers between devices: 20.4 us -> 15.9 us  [swapped(): return lax.ppermute(cells, axis, pairs)]
    ppermute x11, waiting for transfers between devices: 4.92 us -> 9.26 us  [swapped(): return lax.ppermute(cells, axis, pairs)]
  transfers between devices with their start and end apart: 11 -> 11, of which waited for: 1 -> 4; matrix products, arithmetic and copies ran while one was open for 0% -> 0% of each run, Pallas kernels for 19% -> 19%
where the time goes in v9:
time: 35.3 us; the launch traced here: 35 us
  starting transfers between devices  15.9 us (45%)
  waiting for transfers between devices  9.26 us (26%)
  Pallas kernels  9.11 us (26%)
  between operations  0.75 us (2%)
    ppermute x11, starting transfers between devices, swapped(): return lax.ppermute(cells, axis, pairs)  15.9 us
    ppermute x11, waiting for transfers between devices, swapped(): return lax.ppermute(cells, axis, pairs)  9.26 us
    pallas_call x12, Pallas kernels, call(): pl.pallas_call(kernel, out_shape=shapes, in_specs=in_specs, out_specs=out...  9.11 us
  transfers between devices with their start and end apart: 11, of which 4 were waited for; matrix products, arithmetic and copies ran while one was open for 0% of the time, Pallas kernels for 19%

profile of v9, /device:TPU:0, one launch (start us, length us, event | category | flops | bytes accessed | tf_op | source)
XLA Modules:
  0.0 35.0 jit_solution(4614651323165891530)
XLA Ops:
  0.6 1.1 %shard_map.77 = (f32[4,128,128]{2,1,0:T(8,128)S(1)}, f32[2,128,128]{2,1,0:T(8,128)S(1)}) custom-call(s32[1,1,5]{2,1,0:T(1,128)} %cutoff_hbm.3, f32[1,1,5,128,128]{4,3,2,1,0:T(8,128)} %ham_hbm.3, f32[1,1,5,128,128]{4,3,2,1,0:T(8,128)} %inv_hbm.3, f32[2,1,1,5,128,128]{5,4,3,2,1,0:T(8,128)} %rho_hbm.3), custom_call_target="tpu_custom_call" | custom-call | bytes 1703956 | tf_op jit(solution)/shard_map/pallas_call | solution.py:279
  1.7 3.0 %collective-permute-start.2 = (f32[4,128,128]{2,1,0:T(8,128)S(1)}, f32[4,128,128]{2,1,0:T(8,128)S(1)}, u32[]{:S(2)}, u32[]{:S(2)}) collective-permute-start(f32[4,128,128]{2,1,0:T(8,128)S(1)} %get-tuple-element.46.message), channel_id=1, source_target_pairs={{0,4},{4,0},{8,12},{12,8},{16,20},{20,16},{24,28},{28,24},{1,5},{5... | collective-permute-start | bytes 786440 | tf_op jit(solution)/shard_map/ppermute | solution.py:30
  4.8 0.7 %collective-permute-start = (f32[4,128,128]{2,1,0:T(8,128)S(1)}, f32[4,128,128]{2,1,0:T(8,128)S(1)}, u32[]{:S(2)}, u32[]{:S(2)}) collective-permute-start(f32[4,128,128]{2,1,0:T(8,128)S(1)} %shard_map.78.message), channel_id=1, source_target_pairs={{1,2},{2,1},{3,0},{0,3},{5,6},{6,5},{7,4},{4,7},{9,10},{10,9},{11,... | collective-permute-start | bytes 786440 | tf_op jit(solution)/shard_map/ppermute | solution.py:30
  5.5 3.6 %collective-permute-start.3 = (f32[4,128,128]{2,1,0:T(8,128)S(1)}, f32[4,128,128]{2,1,0:T(8,128)S(1)}, u32[]{:S(2)}, u32[]{:S(2)}) collective-permute-start(f32[4,128,128]{2,1,0:T(8,128)S(1)} %shard_map.79.after), channel_id=1, source_target_pairs={{4,8},{8,4},{12,16},{16,12},{20,24},{24,20},{28,0},{0,28},{5,9},{9... | collective-permute-start | bytes 786440 | tf_op jit(solution)/shard_map/ppermute | solution.py:30
  9.1 1.4 %shard_map.80 = (f32[8,128,128]{2,1,0:T(8,128)S(1)}, f32[3,5,128,128]{3,2,1,0:T(8,128)S(1)}, bf16[384,640]{1,0:T(8,128)(2,1)S(1)}, bf16[384,640]{1,0:T(8,128)(2,...) custom-call(s32[1,1,5]{2,1,0:T(1,128)} %cutoff_hbm.3, ...), custom_call_target="tpu_custom_call" | custom-call | bytes 5734932 | tf_op jit(solution)/shard_map/pallas_call | solution.py:279
  10.5 0.7 %collective-permute-start.1 = (f32[8,128,128]{2,1,0:T(8,128)S(1)}, f32[8,128,128]{2,1,0:T(8,128)S(1)}, u32[]{:S(2)}, u32[]{:S(2)}) collective-permute-start(f32[8,128,128]{2,1,0:T(8,128)S(1)} %get-tuple-element.55), channel_id=1, source_target_pairs={{0,1},{1,0},{2,3},{3,2},{4,5},{5,4},{6,7},{7,6},{8,9},{9,8},{10,11... | collective-permute-start | bytes 1572872 | tf_op jit(solution)/shard_map/ppermute | solution.py:30
  11.3 2.1 %collective-permute-done.four = f32[4,128,128]{2,1,0:T(8,128)S(1)} collective-permute-done((f32[4,128,128]{2,1,0:T(8,128)S(1)}, f32[4,128,128]{2,1,0:T(8,128)S(1)}, u32[]{:S(2)}, u32[]{:S(2)}) %collective-permute-start) | collective-permute-done | bytes 262176 | tf_op jit(solution)/shard_map/ppermute | solution.py:30
  13.4 1.0 %shard_map.81 = (f32[4,128,128]{2,1,0:T(8,128)S(1)}, f32[384,640]{1,0:T(8,128)S(1)}, bf16[384,128]{1,0:T(8,128)(2,1)S(1)}, bf16[384,128]{1,0:T(8,128)(2,1)S(1)},...) custom-call(bf16[384,640]{1,0:T(8,128)(2,1)S(1)} %get-tuple-element.49.left_high, ...), custom_call_target="tpu_custom_call" | custom-call | flops 100663296000 | bytes 5832704 | tf_op jit(solution)/shard_map/pallas_call | solution.py:279
  14.4 0.8 %collective-permute-start.4 = (f32[4,128,128]{2,1,0:T(8,128)S(1)}, f32[4,128,128]{2,1,0:T(8,128)S(1)}, u32[]{:S(2)}, u32[]{:S(2)}) collective-permute-start(f32[4,128,128]{2,1,0:T(8,128)S(1)} %get-tuple-element.71), channel_id=1, source_target_pairs={{1,2},{2,1},{3,0},{0,3},{5,6},{6,5},{7,4},{4,7},{9,10},{10,9},{11,... | collective-permute-start | bytes 786440 | tf_op jit(solution)/shard_map/ppermute | solution.py:30
  15.2 0.0 collective-permute-done.1.three
  15.2 1.2 %shard_map.82 = (f32[4,128,128]{2,1,0:T(8,128)S(1)}, f32[384,128]{1,0:T(8,128)S(1)}, f32[2,2,128,128]{3,2,1,0:T(8,128)S(1)}, f32[3,1,1,5,128,128]{5,4,3,2,1,0:T(8,128)S(1)}) custom-call(bf16[384,640]{1,0:T(8,128)(2,1)S(1)} %get-tuple-element.49.left_high, bf16[384,640]{1,0:T(8,128)(2,1)S(1)} %get-tuple-element.50.left_low, ...), custom_call_target="tpu_custom_call" | custom-call | flops 176160768 | bytes 7340032 | tf_op jit(solution)/shard_map/pallas_call | solution.py:279
  16.4 3.6 %collective-permute-start.5 = (f32[4,128,128]{2,1,0:T(8,128)S(1)}, f32[4,128,128]{2,1,0:T(8,128)S(1)}, u32[]{:S(2)}, u32[]{:S(2)}) collective-permute-start(f32[4,128,128]{2,1,0:T(8,128)S(1)} %get-tuple-element.78), channel_id=1, source_target_pairs={{4,8},{8,4},{12,16},{16,12},{20,24},{24,20},{28,0},{0,28},{5,9},{9... | collective-permute-start | bytes 786440 | tf_op jit(solution)/shard_map/ppermute | solution.py:30
  20.0 0.0 collective-permute-done.2.one
  20.0 0.6 %shard_map.83 = (bf16[384,128]{1,0:T(8,128)(2,1)S(1)}, bf16[384,128]{1,0:T(8,128)(2,1)S(1)}, f32[384,128]{1,0:T(8,128)S(1)}, f32[2,128,128]{2,1,0:T(8,128)S(1)}) custom-call(bf16[384,640]{1,0:T(8,128)(2,1)S(1)} %get-tuple-element.49.left_high, bf16[384,640]{1,0:T(8,128)(2,1)S(1)} %get-tuple-element.50.left_low, f32[384,640]{1,0:T(8,128)S(1)} %get-tuple-element.53.start, ...), custom_call_target="tpu_custom_call" | custom-call | flops 125829120 | bytes 4128768 | tf_op jit(solution)/shard_map/pallas_call | solution.py:279
  20.6 0.0 collective-permute-done.3.two
  20.7 0.9 %shard_map.84 = (f32[4,128,128]{2,1,0:T(8,128)S(1)}, bf16[384,128]{1,0:T(8,128)(2,1)S(1)}, bf16[384,128]{1,0:T(8,128)(2,1)S(1)}, bf16[384,128]{1,0:T(8,128)(2,1)...) custom-call(bf16[384,640]{1,0:T(8,128)(2,1)S(1)} %get-tuple-element., ...), custom_call_target="tpu_custom_call" | custom-call | flops 276824064 | bytes 7280640 | tf_op jit(solution)/shard_map/pallas_call | solution.py:279
  21.6 0.1 collective-permute-start.6
  21.7 3.7 %collective-permute-done.6.arrived.c1 = f32[3,128]{1,0:T(4,128)S(1)} collective-permute-done((f32[3,128]{1,0:T(4,128)S(1)}, f32[3,128]{1,0:T(4,128)S(1)}, u32[]{:S(2)}, u32[]{:S(2)}) %collective-permute-start.6) | collective-permute-done | bytes 1568 | tf_op jit(solution)/shard_map/ppermute | solution.py:30
  25.4 0.1 collective-permute-start.7
  25.5 0.0 collective-permute-done.4.four
  25.5 0.3 shard_map.85
  25.8 0.1 collective-permute-start.10
  25.9 2.1 %collective-permute-start.8 = (f32[3,128]{1,0:T(4,128)S(1)}, f32[3,128]{1,0:T(4,128)S(1)}, u32[]{:S(2)}, u32[]{:S(2)}) collective-permute-start(f32[3,128]{1,0:T(4,128)S(1)} %get-tuple-element.84), channel_id=1, source_target_pairs={{4,8},{8,4},{12,16},{16,12},{20,24},{24,20},{28,0},{0,28},{5,9},{9... | collective-permute-start | bytes 4616 | tf_op jit(solution)/shard_map/ppermute | solution.py:30
  28.0 1.1 %collective-permute-start.9 = (f32[3,128]{1,0:T(4,128)S(1)}, f32[3,128]{1,0:T(4,128)S(1)}, u32[]{:S(2)}, u32[]{:S(2)}) collective-permute-start(f32[3,128]{1,0:T(4,128)S(1)} %get-tuple-element.85), channel_id=1, source_target_pairs={{0,1},{1,0},{2,3},{3,2},{4,5},{5,4},{6,7},{7,6},{8,9},{9,8},{10,11... | collective-permute-start | bytes 4616 | tf_op jit(solution)/shard_map/ppermute | solution.py:30
  29.1 0.0 collective-permute-done.5.two
  29.1 1.3 %shard_map.86 = (f32[2,1,1,5,128,128]{5,4,3,2,1,0:T(8,128)}, f32[3,128,128]{2,1,0:T(8,128)S(1)}, f32[3,128]{1,0:T(4,128)S(1)}) custom-call(f32[3,5,128,128]{3,2,1,0:T(8,128)S(1)} %get-tuple-element.48.held, f32[4,128,128]{2,1,0:T(8,128)S(1)} %get-tuple-element.65.new, bf16[384,640]{1,0:T(8,128)(2,1)S(1)} %get-tuple-element.49.left_high, ...), custom_call_target="tpu_custom_call" | custom-call | flops 188743680 | bytes 6161920 | tf_op jit(solution)/shard_map/pallas_call | solution.py:279
  30.4 0.0 collective-permute-done.10.c4
  30.4 2.0 %collective-permute-done.8.c2 = f32[3,128]{1,0:T(4,128)S(1)} collective-permute-done((f32[3,128]{1,0:T(4,128)S(1)}, f32[3,128]{1,0:T(4,128)S(1)}, u32[]{:S(2)}, u32[]{:S(2)}) %collective-permute-start.8) | collective-permute-done | bytes 1568 | tf_op jit(solution)/shard_map/ppermute | solution.py:30
  32.3 0.0 collective-permute-done.9.c3
  32.3 1.4 %collective-permute-done.7.one = f32[4,128,128]{2,1,0:T(8,128)S(1)} collective-permute-done((f32[4,128,128]{2,1,0:T(8,128)S(1)}, f32[4,128,128]{2,1,0:T(8,128)S(1)}, u32[]{:S(2)}, u32[]{:S(2)}) %collective-permute-start.7) | collective-permute-done | bytes 262176 | tf_op jit(solution)/shard_map/ppermute | solution.py:30
  33.8 1.3 %shard_map.88 = (f32[2,1,1,5,128,128]{5,4,3,2,1,0:T(8,128)}, f32[3,1,64]{2,1,0:T(1,128)}) custom-call(f32[3,5,128,128]{3,2,1,0:T(8,128)S(1)} %get-tuple-element.48.held, f32[3,1,1,5,128,128]{5,4,3,2,1,0:T(8,128)S(1)} %get-tuple-element.56.der_ref, f32[64,128]{1,0:T(8,128)S(1)} %get-tuple-element.57.members, ...), custom_call_target="tpu_custom_call", output_to_operand_aliasing={{0}: (12, {})} | custom-call | flops 125829120 | bytes 4169984 | tf_op jit(solution)/shard_map/pallas_call | solution.py:279
  (3 shorter events, 0.1 us)
Async XLA Ops:
  1.7 18.3 %collective-permute-start.2 = (f32[4,128,128]{2,1,0:T(8,128)S(1)}, f32[4,128,128]{2,1,0:T(8,128)S(1)}, u32[]{:S(2)}, u32[]{:S(2)}) collective-permute-start(f32[4,128,128]{2,1,0:T(8,128)S(1)} %get-tuple-element.46.message), channel_id=1, source_target_pairs={{0,4},{4,0},{8,12},{12,8},{16,20},{20,16},{24,28},{28,24},{1,5},{5... | collective-permute-start | bytes 786440 | tf_op jit(solution)/shard_map/ppermute | solution.py:30
  4.8 8.6 %collective-permute-start = (f32[4,128,128]{2,1,0:T(8,128)S(1)}, f32[4,128,128]{2,1,0:T(8,128)S(1)}, u32[]{:S(2)}, u32[]{:S(2)}) collective-permute-start(f32[4,128,128]{2,1,0:T(8,128)S(1)} %shard_map.78.message), channel_id=1, source_target_pairs={{1,2},{2,1},{3,0},{0,3},{5,6},{6,5},{7,4},{4,7},{9,10},{10,9},{11,... | collective-permute-start | bytes 786440 | tf_op jit(solution)/shard_map/ppermute | solution.py:30
  5.5 15.1 %collective-permute-start.3 = (f32[4,128,128]{2,1,0:T(8,128)S(1)}, f32[4,128,128]{2,1,0:T(8,128)S(1)}, u32[]{:S(2)}, u32[]{:S(2)}) collective-permute-start(f32[4,128,128]{2,1,0:T(8,128)S(1)} %shard_map.79.after), channel_id=1, source_target_pairs={{4,8},{8,4},{12,16},{16,12},{20,24},{24,20},{28,0},{0,28},{5,9},{9... | collective-permute-start | bytes 786440 | tf_op jit(solution)/shard_map/ppermute | solution.py:30
  10.5 4.7 %collective-permute-start.1 = (f32[8,128,128]{2,1,0:T(8,128)S(1)}, f32[8,128,128]{2,1,0:T(8,128)S(1)}, u32[]{:S(2)}, u32[]{:S(2)}) collective-permute-start(f32[8,128,128]{2,1,0:T(8,128)S(1)} %get-tuple-element.55), channel_id=1, source_target_pairs={{0,1},{1,0},{2,3},{3,2},{4,5},{5,4},{6,7},{7,6},{8,9},{9,8},{10,11... | collective-permute-start | bytes 1572872 | tf_op jit(solution)/shard_map/ppermute | solution.py:30
  14.4 11.1 %collective-permute-start.4 = (f32[4,128,128]{2,1,0:T(8,128)S(1)}, f32[4,128,128]{2,1,0:T(8,128)S(1)}, u32[]{:S(2)}, u32[]{:S(2)}) collective-permute-start(f32[4,128,128]{2,1,0:T(8,128)S(1)} %get-tuple-element.71), channel_id=1, source_target_pairs={{1,2},{2,1},{3,0},{0,3},{5,6},{6,5},{7,4},{4,7},{9,10},{10,9},{11,... | collective-permute-start | bytes 786440 | tf_op jit(solution)/shard_map/ppermute | solution.py:30
  16.4 12.7 %collective-permute-start.5 = (f32[4,128,128]{2,1,0:T(8,128)S(1)}, f32[4,128,128]{2,1,0:T(8,128)S(1)}, u32[]{:S(2)}, u32[]{:S(2)}) collective-permute-start(f32[4,128,128]{2,1,0:T(8,128)S(1)} %get-tuple-element.78), channel_id=1, source_target_pairs={{4,8},{8,4},{12,16},{16,12},{20,24},{24,20},{28,0},{0,28},{5,9},{9... | collective-permute-start | bytes 786440 | tf_op jit(solution)/shard_map/ppermute | solution.py:30
  21.6 3.8 %collective-permute-start.6 = (f32[3,128]{1,0:T(4,128)S(1)}, f32[3,128]{1,0:T(4,128)S(1)}, u32[]{:S(2)}, u32[]{:S(2)}) collective-permute-start(f32[3,128]{1,0:T(4,128)S(1)} %get-tuple-element.81), channel_id=1, source_target_pairs={{0,4},{4,0},{8,12},{12,8},{16,20},{20,16},{24,28},{28,24},{1,5},{5... | collective-permute-start | bytes 4616 | tf_op jit(solution)/shard_map/ppermute | solution.py:30
  25.4 8.3 %collective-permute-start.7 = (f32[4,128,128]{2,1,0:T(8,128)S(1)}, f32[4,128,128]{2,1,0:T(8,128)S(1)}, u32[]{:S(2)}, u32[]{:S(2)}) collective-permute-start(f32[4,128,128]{2,1,0:T(8,128)S(1)} %get-tuple-element.83), channel_id=1, source_target_pairs={{0,4},{4,0},{8,12},{12,8},{16,20},{20,16},{24,28},{28,24},{1,5},{5... | collective-permute-start | bytes 786440 | tf_op jit(solution)/shard_map/ppermute | solution.py:30
  25.8 4.6 %collective-permute-start.10 = (f32[3,128]{1,0:T(4,128)S(1)}, f32[3,128]{1,0:T(4,128)S(1)}, u32[]{:S(2)}, u32[]{:S(2)}) collective-permute-start(f32[3,128]{1,0:T(4,128)S(1)} %get-tuple-element.86), channel_id=1, source_target_pairs={{1,2},{2,1},{3,0},{0,3},{5,6},{6,5},{7,4},{4,7},{9,10},{10,9},{11,... | collective-permute-start | bytes 4616 | tf_op jit(solution)/shard_map/ppermute | solution.py:30
  25.9 6.4 %collective-permute-start.8 = (f32[3,128]{1,0:T(4,128)S(1)}, f32[3,128]{1,0:T(4,128)S(1)}, u32[]{:S(2)}, u32[]{:S(2)}) collective-permute-start(f32[3,128]{1,0:T(4,128)S(1)} %get-tuple-element.84), channel_id=1, source_target_pairs={{4,8},{8,4},{12,16},{16,12},{20,24},{24,20},{28,0},{0,28},{5,9},{9... | collective-permute-start | bytes 4616 | tf_op jit(solution)/shard_map/ppermute | solution.py:30
  28.0 4.4 %collective-permute-start.9 = (f32[3,128]{1,0:T(4,128)S(1)}, f32[3,128]{1,0:T(4,128)S(1)}, u32[]{:S(2)}, u32[]{:S(2)}) collective-permute-start(f32[3,128]{1,0:T(4,128)S(1)} %get-tuple-element.85), channel_id=1, source_target_pairs={{0,1},{1,0},{2,3},{3,2},{4,5},{5,4},{6,7},{7,6},{8,9},{9,8},{10,11... | collective-permute-start | bytes 4616 | tf_op jit(solution)/shard_map/ppermute | solution.py:30

commit v10 on v9

--- a/solution.py
+++ b/solution.py
@@ -161,9 +161,10 @@
     mixed_high[...], mixed_low[...] = mixed
 
 
-def whole_kernel(left_high, left_low, start, held, diagonal, three, der_hbm, two_more, diagonal_out, other, der, sem):
+def whole_kernel(left_high, left_low, start, held, diagonal, three, der_hbm, one_more, two_more, diagonal_out, other, der, sem):
     copy = pltpu.make_async_copy(der_hbm, der, sem)
     copy.start()
+    send_more(one_more, held, 1)
     send_more(two_more, held, 2)
     mixed, diagonal_out[...], real, other[1, 0] = first_half((left_high, left_low), 3, start, three, diagonal[...])
     added, other[0, 1], other[1, 1] = second_half(mixed, three[4:])
@@ -204,8 +205,7 @@
         weighted[direction] = sums[direction]
 
 
-def more_kernel(held, arrived, column, one_more, out):
-    send_more(one_more, held, 1)
+def pass_kernel(arrived, column, out):
     out[...] = column[...]
 
 
@@ -216,7 +216,7 @@
 
 def real_kernel(
     held, new, left_high, left_low, self_high, self_low, other_one, real_two, other_three, other_four, more_four, weighted,
-    high_two, low_two, imag_part, two, out_hbm, comm, row_part, imag_new, sems
+    high_one, low_one, imag_part, one, out_hbm, comm, row_part, imag_new, sems
 ):
     order = order_of()
     copies = start_all(
@@ -228,16 +228,16 @@
     ahead = dot(part(at_self, slice(0, B), cols(0)), part(left, slice(B, 2 * B), whole))
     behind = dot(part(at_self, slice(B, 2 * B), cols(0)), part(left, slice(0, B), whole))
     real_comm = ahead - behind
-    added_two, real_self, imag_self = second_half((high_two[...], low_two[...]), two)
-    others = ((2, real_two[...] + added_two), (3, other_three[0, 0]), (4, other_four[0] + more_four[0]))
+    added_one, real_one, imag_one = second_half((high_one[...], low_one[...]), one)
+    others = ((1, other_one[0] + added_one), (3, other_three[0, 0]), (4, other_four[0] + more_four[0]))
     for at, (place, other) in enumerate(others):
         imag_new[at] = held[2, place] - time_step * (real_comm[:, cols(place)] + other)
         copies += start_all(
             [pltpu.make_async_copy(imag_new.at[at], out_hbm.at[1, 0, 0, order[place]], sems.at[1, at])]
         )
-    comm[0] = real_comm[:, cols(0)] + other_three[0, 1] + real_self + more_four[1]
-    comm[1] = imag_part[...] + imag_self + more_four[2]
-    comm[2] = real_comm[:, cols(1)] + other_one[0]
+    comm[0] = real_comm[:, cols(0)] + other_three[0, 1] + real_one + more_four[1]
+    comm[1] = imag_part[...] + imag_one + more_four[2]
+    comm[2] = real_comm[:, cols(2)] + real_two[...]
     for direction in range(3):
         row_part[direction : direction + 1, :] = jnp.sum(weighted[direction].T, axis=0, keepdims=True)
     for copy in copies:
@@ -245,12 +245,12 @@
 
 
 def sixth_kernel(
-    held, der_ref, members, high_one, low_one, comm, row_part, one, c1, c2, c3, c4, old_hbm, out_hbm, forces_hbm, new, forces_ref, sems
+    held, der_ref, members, high_two, low_two, comm, row_part, two, c1, c2, c3, c4, old_hbm, out_hbm, forces_hbm, new, forces_ref, sems
 ):
     order = order_of()
-    prop, inner = rows_of((high_one[...], low_one[...]))
-    behind = dot(inner, split(one[1]))
-    real_new = held[1, 0] + time_step * (comm[1] + dot(prop, split(one[3])) - behind[B:])
+    prop, inner = rows_of((high_two[...], low_two[...]))
+    behind = dot(inner, split(two[1]))
+    real_new = held[1, 0] + time_step * (comm[1] + dot(prop, split(two[3])) - behind[B:])
     new[0] = real_new
     copies = start_all([pltpu.make_async_copy(new.at[0], out_hbm.at[0, 0, 0, 0], sems.at[0])])
     parts = []
@@ -264,11 +264,11 @@
     for direction in range(3):
         forces_ref[direction] = forces[direction : direction + 1]
     copies += start_all([pltpu.make_async_copy(forces_ref, forces_hbm, sems.at[3])])
-    ahead = dot(prop, beside(split(one[2]), split(one[0])))
+    ahead = dot(prop, beside(split(two[2]), split(two[0])))
     new[1] = held[2, 0] - time_step * (comm[0] + ahead[:, cols(0)] - behind[:B])
-    new[2] = held[2, 1] - time_step * (comm[2] + ahead[:, cols(1)])
+    new[2] = held[2, 2] - time_step * (comm[2] + ahead[:, cols(1)])
     copies += start_all(
-        [pltpu.make_async_copy(new.at[1 + at], out_hbm.at[1, 0, 0, order[at]], sems.at[1 + at]) for at in range(2)]
+        [pltpu.make_async_copy(new.at[1 + at], out_hbm.at[1, 0, 0, order[2 * at]], sems.at[1 + at]) for at in range(2)]
     )
     for copy in copies:
         copy.wait()
@@ -331,14 +331,15 @@
         (left_high, left_low, ham_high, ham_low, held, near_four),
     )
     near_four_more = swapped(four_more, 4)
-    two_more, diagonal, other_three, derivative = call(
+    one_more, two_more, diagonal, other_three, derivative = call(
         whole_kernel,
-        [message, shape(3 * B, B), shape(2, 2, B, B), shape(*derivative.shape)],
+        [message, message, shape(3 * B, B), shape(2, 2, B, B), shape(*derivative.shape)],
         [vmem] * 6 + [hbm],
         14,
         (left_high, left_low, start, held, diagonal, near_three, derivative),
         scratch=[dma(())],
     )
+    near_one_more = swapped(one_more, 1)
     near_two_more = swapped(two_more, 2)
     high_one, low_one, diagonal, other_one = call(
         fourth_kernel,
@@ -356,10 +357,6 @@
         (left_high, left_low, start, diagonal, held, derivative, other_one, other_three, other_four, near_two),
     )
     c1, c2, c3, c4 = columns
-    c1 = swapped(c1, 1)
-    c2 = swapped(c2, 2)
-    one_more, c3 = call(more_kernel, [message, shape(3, B)], [vmem] * 3, 0, (held, c1, c3))
-    near_one_more = swapped(one_more, 1)
     c4, more_four = call(
         four_kernel,
         [shape(3, B), shape(3, B, B)],
@@ -367,9 +364,10 @@
         5,
         (high_four, low_four, near_four_more, c4),
     )
-    columns = (c1, c2, swapped(c3, 3), swapped(c4, 4))
+    (c3,) = call(pass_kernel, [shape(3, B)], [vmem] * 2, 0, (near_one_more, c3))
+    columns = [swapped(column, at) for at, column in enumerate((c1, c2, c3, c4), 1)]
     args = (held, new, left_high, left_low, self_high, self_low, other_one, real_two, other_three, other_four, more_four, weighted)
-    args += (high_two, low_two, imag_part, near_two_more)
+    args += (high_one, low_one, imag_part, near_one_more)
     out, comm, row_part = call(
         real_kernel,
         [shape(*density.shape), shape(3, B, B), shape(3, B)],
@@ -379,7 +377,7 @@
         out_specs=[hbm] + [vmem] * 2,
         scratch=[pltpu.VMEM((3, B, B), f32), dma((2, 4))],
     )
-    args = (held, derivative, members, high_one, low_one, comm, row_part, near_one_more, *columns, out)
+    args = (held, derivative, members, high_two, low_two, comm, row_part, near_two_more, *columns, out)
     new_density, forces = call(
         sixth_kernel,
         [shape(*density.shape), shape(3, 1, ATOMS)],

time: 35.3 us -> 33.9 us (0.960)
  waiting for transfers between devices: 9.26 us -> 3.65 us
  starting transfers between devices: 15.9 us -> 20.1 us
    ppermute x11, waiting for transfers between devices: 9.26 us -> 3.65 us  [swapped(): return lax.ppermute(cells, axis, pairs)]
    ppermute x11, starting transfers between devices: 15.9 us -> 20.1 us  [swapped(): return lax.ppermute(cells, axis, pairs)]
  transfers between devices with their start and end apart: 11 -> 11, of which waited for: 4 -> 2; matrix products, arithmetic and copies ran while one was open for 0% -> 0% of each run, Pallas kernels for 19% -> 20%
where the time goes in v10:
time: 33.9 us; the launch traced here: 33.6 us
  starting transfers between devices  20.1 us (59%)
  Pallas kernels  9.09 us (27%)
  waiting for transfers between devices  3.65 us (11%)
  between operations  0.76 us (2%)
    ppermute x11, starting transfers between devices, swapped(): return lax.ppermute(cells, axis, pairs)  20.1 us
    pallas_call x12, Pallas kernels, call(): pl.pallas_call(kernel, out_shape=shapes, in_specs=in_specs, out_specs=out...  9.09 us
    ppermute x11, waiting for transfers between devices, swapped(): return lax.ppermute(cells, axis, pairs)  3.65 us
  transfers between devices with their start and end apart: 11, of which 2 were waited for; matrix products, arithmetic and copies ran while one was open for 0% of the time, Pallas kernels for 20%

profile of v10, /device:TPU:0, one launch (start us, length us, event | category | flops | bytes accessed | tf_op | source)
XLA Modules:
  0.0 33.6 jit_solution(15781811200136801260)
XLA Ops:
  0.6 1.1 %shard_map.77 = (f32[4,128,128]{2,1,0:T(8,128)S(1)}, f32[2,128,128]{2,1,0:T(8,128)S(1)}) custom-call(s32[1,1,5]{2,1,0:T(1,128)} %cutoff_hbm.3, f32[1,1,5,128,128]{4,3,2,1,0:T(8,128)} %ham_hbm.3, f32[1,1,5,128,128]{4,3,2,1,0:T(8,128)} %inv_hbm.3, f32[2,1,1,5,128,128]{5,4,3,2,1,0:T(8,128)} %rho_hbm.3), custom_call_target="tpu_custom_call" | custom-call | bytes 1703956 | tf_op jit(solution)/shard_map/pallas_call | solution.py:279
  1.7 3.0 %collective-permute-start.2 = (f32[4,128,128]{2,1,0:T(8,128)S(1)}, f32[4,128,128]{2,1,0:T(8,128)S(1)}, u32[]{:S(2)}, u32[]{:S(2)}) collective-permute-start(f32[4,128,128]{2,1,0:T(8,128)S(1)} %get-tuple-element.45.message), channel_id=1, source_target_pairs={{0,4},{4,0},{8,12},{12,8},{16,20},{20,16},{24,28},{28,24},{1,5},{5... | collective-permute-start | bytes 786440 | tf_op jit(solution)/shard_map/ppermute | solution.py:30
  4.8 0.7 %collective-permute-start = (f32[4,128,128]{2,1,0:T(8,128)S(1)}, f32[4,128,128]{2,1,0:T(8,128)S(1)}, u32[]{:S(2)}, u32[]{:S(2)}) collective-permute-start(f32[4,128,128]{2,1,0:T(8,128)S(1)} %shard_map.78.message), channel_id=1, source_target_pairs={{1,2},{2,1},{3,0},{0,3},{5,6},{6,5},{7,4},{4,7},{9,10},{10,9},{11,... | collective-permute-start | bytes 786440 | tf_op jit(solution)/shard_map/ppermute | solution.py:30
  5.5 3.6 %collective-permute-start.3 = (f32[4,128,128]{2,1,0:T(8,128)S(1)}, f32[4,128,128]{2,1,0:T(8,128)S(1)}, u32[]{:S(2)}, u32[]{:S(2)}) collective-permute-start(f32[4,128,128]{2,1,0:T(8,128)S(1)} %shard_map.79.after), channel_id=1, source_target_pairs={{4,8},{8,4},{12,16},{16,12},{20,24},{24,20},{28,0},{0,28},{5,9},{9... | collective-permute-start | bytes 786440 | tf_op jit(solution)/shard_map/ppermute | solution.py:30
  9.1 1.4 %shard_map.80 = (f32[8,128,128]{2,1,0:T(8,128)S(1)}, f32[3,5,128,128]{3,2,1,0:T(8,128)S(1)}, bf16[384,640]{1,0:T(8,128)(2,1)S(1)}, bf16[384,640]{1,0:T(8,128)(2,...) custom-call(s32[1,1,5]{2,1,0:T(1,128)} %cutoff_hbm.3, ...), custom_call_target="tpu_custom_call" | custom-call | bytes 5734932 | tf_op jit(solution)/shard_map/pallas_call | solution.py:279
  10.5 0.7 %collective-permute-start.1 = (f32[8,128,128]{2,1,0:T(8,128)S(1)}, f32[8,128,128]{2,1,0:T(8,128)S(1)}, u32[]{:S(2)}, u32[]{:S(2)}) collective-permute-start(f32[8,128,128]{2,1,0:T(8,128)S(1)} %get-tuple-element.54), channel_id=1, source_target_pairs={{0,1},{1,0},{2,3},{3,2},{4,5},{5,4},{6,7},{7,6},{8,9},{9,8},{10,11... | collective-permute-start | bytes 1572872 | tf_op jit(solution)/shard_map/ppermute | solution.py:30
  11.3 2.1 %collective-permute-done.four = f32[4,128,128]{2,1,0:T(8,128)S(1)} collective-permute-done((f32[4,128,128]{2,1,0:T(8,128)S(1)}, f32[4,128,128]{2,1,0:T(8,128)S(1)}, u32[]{:S(2)}, u32[]{:S(2)}) %collective-permute-start) | collective-permute-done | bytes 262176 | tf_op jit(solution)/shard_map/ppermute | solution.py:30
  13.4 1.0 %shard_map.81 = (f32[4,128,128]{2,1,0:T(8,128)S(1)}, f32[384,640]{1,0:T(8,128)S(1)}, bf16[384,128]{1,0:T(8,128)(2,1)S(1)}, bf16[384,128]{1,0:T(8,128)(2,1)S(1)},...) custom-call(bf16[384,640]{1,0:T(8,128)(2,1)S(1)} %get-tuple-element.48.left_high, ...), custom_call_target="tpu_custom_call" | custom-call | flops 100663296000 | bytes 5832704 | tf_op jit(solution)/shard_map/pallas_call | solution.py:279
  14.4 0.8 %collective-permute-start.4 = (f32[4,128,128]{2,1,0:T(8,128)S(1)}, f32[4,128,128]{2,1,0:T(8,128)S(1)}, u32[]{:S(2)}, u32[]{:S(2)}) collective-permute-start(f32[4,128,128]{2,1,0:T(8,128)S(1)} %get-tuple-element.70), channel_id=1, source_target_pairs={{1,2},{2,1},{3,0},{0,3},{5,6},{6,5},{7,4},{4,7},{9,10},{10,9},{11,... | collective-permute-start | bytes 786440 | tf_op jit(solution)/shard_map/ppermute | solution.py:30
  15.2 0.0 collective-permute-done.1.three
  15.2 1.2 %shard_map.82 = (f32[4,128,128]{2,1,0:T(8,128)S(1)}, f32[4,128,128]{2,1,0:T(8,128)S(1)}, f32[384,128]{1,0:T(8,128)S(1)}, f32[2,2,128,128]{3,2,1,0:T(8,128)S(1)}, f32[3,1,1,5,128,128]{5,4,3,2,1,0:T(8,128)S(1)}) custom-call(bf16[384,640]{1,0:T(8,128)(2,1)S(1)} %get-tuple-element.48.left_high, bf16[384,640]{1,0:T(8,128)(2,1)S(1)} %get-tuple-element.49.left_low, ...), custom_call_target="tpu_custom_call" | custom-call | flops 176160768 | bytes 7602176 | tf_op jit(solution)/shard_map/pallas_call | solution.py:279
  16.4 0.6 %collective-permute-start.5 = (f32[4,128,128]{2,1,0:T(8,128)S(1)}, f32[4,128,128]{2,1,0:T(8,128)S(1)}, u32[]{:S(2)}, u32[]{:S(2)}) collective-permute-start(f32[4,128,128]{2,1,0:T(8,128)S(1)} %get-tuple-element.77), channel_id=1, source_target_pairs={{0,4},{4,0},{8,12},{12,8},{16,20},{20,16},{24,28},{28,24},{1,5},{5... | collective-permute-start | bytes 786440 | tf_op jit(solution)/shard_map/ppermute | solution.py:30
  17.0 4.6 %collective-permute-start.6 = (f32[4,128,128]{2,1,0:T(8,128)S(1)}, f32[4,128,128]{2,1,0:T(8,128)S(1)}, u32[]{:S(2)}, u32[]{:S(2)}) collective-permute-start(f32[4,128,128]{2,1,0:T(8,128)S(1)} %get-tuple-element.80), channel_id=1, source_target_pairs={{4,8},{8,4},{12,16},{16,12},{20,24},{24,20},{28,0},{0,28},{5,9},{9... | collective-permute-start | bytes 786440 | tf_op jit(solution)/shard_map/ppermute | solution.py:30
  21.6 0.0 collective-permute-done.2.one
  21.6 0.6 %shard_map.83 = (bf16[384,128]{1,0:T(8,128)(2,1)S(1)}, bf16[384,128]{1,0:T(8,128)(2,1)S(1)}, f32[384,128]{1,0:T(8,128)S(1)}, f32[2,128,128]{2,1,0:T(8,128)S(1)}) custom-call(bf16[384,640]{1,0:T(8,128)(2,1)S(1)} %get-tuple-element.48.left_high, bf16[384,640]{1,0:T(8,128)(2,1)S(1)} %get-tuple-element.49.left_low, f32[384,640]{1,0:T(8,128)S(1)} %get-tuple-element.52.start, ...), custom_call_target="tpu_custom_call" | custom-call | flops 125829120 | bytes 4128768 | tf_op jit(solution)/shard_map/pallas_call | solution.py:279
  22.2 0.0 collective-permute-done.3.two
  22.2 0.9 %shard_map.84 = (f32[4,128,128]{2,1,0:T(8,128)S(1)}, bf16[384,128]{1,0:T(8,128)(2,1)S(1)}, bf16[384,128]{1,0:T(8,128)(2,1)S(1)}, bf16[384,128]{1,0:T(8,128)(2,1)...) custom-call(bf16[384,640]{1,0:T(8,128)(2,1)S(1)} %get-tuple-element., ...), custom_call_target="tpu_custom_call" | custom-call | flops 276824064 | bytes 7280640 | tf_op jit(solution)/shard_map/pallas_call | solution.py:279
  23.1 0.0 collective-permute-done.4.four
  23.2 0.3 shard_map.85
  23.4 1.0 %collective-permute-start.10 = (f32[3,128]{1,0:T(4,128)S(1)}, f32[3,128]{1,0:T(4,128)S(1)}, u32[]{:S(2)}, u32[]{:S(2)}) collective-permute-start(f32[3,128]{1,0:T(4,128)S(1)} %get-tuple-element.84), channel_id=1, source_target_pairs={{1,2},{2,1},{3,0},{0,3},{5,6},{6,5},{7,4},{4,7},{9,10},{10,9},{11,... | collective-permute-start | bytes 4616 | tf_op jit(solution)/shard_map/ppermute | solution.py:30
  24.4 0.5 %collective-permute-start.7 = (f32[3,128]{1,0:T(4,128)S(1)}, f32[3,128]{1,0:T(4,128)S(1)}, u32[]{:S(2)}, u32[]{:S(2)}) collective-permute-start(f32[3,128]{1,0:T(4,128)S(1)} %get-tuple-element.81), channel_id=1, source_target_pairs={{0,4},{4,0},{8,12},{12,8},{16,20},{20,16},{24,28},{28,24},{1,5},{5... | collective-permute-start | bytes 4616 | tf_op jit(solution)/shard_map/ppermute | solution.py:30
  25.0 4.6 %collective-permute-start.8 = (f32[3,128]{1,0:T(4,128)S(1)}, f32[3,128]{1,0:T(4,128)S(1)}, u32[]{:S(2)}, u32[]{:S(2)}) collective-permute-start(f32[3,128]{1,0:T(4,128)S(1)} %get-tuple-element.82), channel_id=1, source_target_pairs={{4,8},{8,4},{12,16},{16,12},{20,24},{24,20},{28,0},{0,28},{5,9},{9... | collective-permute-start | bytes 4616 | tf_op jit(solution)/shard_map/ppermute | solution.py:30
  29.5 1.5 %collective-permute-done.5.one.arrived = f32[4,128,128]{2,1,0:T(8,128)S(1)} collective-permute-done((f32[4,128,128]{2,1,0:T(8,128)S(1)}, f32[4,128,128]{2,1,0:T(8,128)S(1)}, u32[]{:S(2)}, u32[]{:S(2)}) %collective-permute-start.5) | collective-permute-done | bytes 262176 | tf_op jit(solution)/shard_map/ppermute | solution.py:30
  31.0 0.0 collective-permute-start.9
  31.0 1.3 %shard_map.86 = (f32[2,1,1,5,128,128]{5,4,3,2,1,0:T(8,128)}, f32[3,128,128]{2,1,0:T(8,128)S(1)}, f32[3,128]{1,0:T(4,128)S(1)}) custom-call(f32[3,5,128,128]{3,2,1,0:T(8,128)S(1)} %get-tuple-element.47.held, f32[4,128,128]{2,1,0:T(8,128)S(1)} %get-tuple-element.64.new, bf16[384,640]{1,0:T(8,128)(2,1)S(1)} %get-tuple-element.48.left_high, ...), custom_call_target="tpu_custom_call" | custom-call | flops 188743680 | bytes 6161920 | tf_op jit(solution)/shard_map/pallas_call | solution.py:279
  32.3 0.0 collective-permute-done.10.c4
  32.3 0.0 collective-permute-done.7.c1
  32.3 0.0 collective-permute-done.8.c2
  32.3 0.0 collective-permute-done.6.two
  32.3 0.0 collective-permute-done.9.c3
  32.3 1.3 %shard_map.88 = (f32[2,1,1,5,128,128]{5,4,3,2,1,0:T(8,128)}, f32[3,1,64]{2,1,0:T(1,128)}) custom-call(f32[3,5,128,128]{3,2,1,0:T(8,128)S(1)} %get-tuple-element.47.held, f32[3,1,1,5,128,128]{5,4,3,2,1,0:T(8,128)S(1)} %get-tuple-element.55.der_ref, f32[64,128]{1,0:T(8,128)S(1)} %get-tuple-element.56.members, ...), custom_call_target="tpu_custom_call", output_to_operand_aliasing={{0}: (12, {})} | custom-call | flops 125829120 | bytes 4169984 | tf_op jit(solution)/shard_map/pallas_call | solution.py:279
  (3 shorter events, 0.0 us)
Async XLA Ops:
  1.7 19.9 %collective-permute-start.2 = (f32[4,128,128]{2,1,0:T(8,128)S(1)}, f32[4,128,128]{2,1,0:T(8,128)S(1)}, u32[]{:S(2)}, u32[]{:S(2)}) collective-permute-start(f32[4,128,128]{2,1,0:T(8,128)S(1)} %get-tuple-element.45.message), channel_id=1, source_target_pairs={{0,4},{4,0},{8,12},{12,8},{16,20},{20,16},{24,28},{28,24},{1,5},{5... | collective-permute-start | bytes 786440 | tf_op jit(solution)/shard_map/ppermute | solution.py:30
  4.8 8.6 %collective-permute-start = (f32[4,128,128]{2,1,0:T(8,128)S(1)}, f32[4,128,128]{2,1,0:T(8,128)S(1)}, u32[]{:S(2)}, u32[]{:S(2)}) collective-permute-start(f32[4,128,128]{2,1,0:T(8,128)S(1)} %shard_map.78.message), channel_id=1, source_target_pairs={{1,2},{2,1},{3,0},{0,3},{5,6},{6,5},{7,4},{4,7},{9,10},{10,9},{11,... | collective-permute-start | bytes 786440 | tf_op jit(solution)/shard_map/ppermute | solution.py:30
  5.5 16.7 %collective-permute-start.3 = (f32[4,128,128]{2,1,0:T(8,128)S(1)}, f32[4,128,128]{2,1,0:T(8,128)S(1)}, u32[]{:S(2)}, u32[]{:S(2)}) collective-permute-start(f32[4,128,128]{2,1,0:T(8,128)S(1)} %shard_map.79.after), channel_id=1, source_target_pairs={{4,8},{8,4},{12,16},{16,12},{20,24},{24,20},{28,0},{0,28},{5,9},{9... | collective-permute-start | bytes 786440 | tf_op jit(solution)/shard_map/ppermute | solution.py:30
  10.5 4.7 %collective-permute-start.1 = (f32[8,128,128]{2,1,0:T(8,128)S(1)}, f32[8,128,128]{2,1,0:T(8,128)S(1)}, u32[]{:S(2)}, u32[]{:S(2)}) collective-permute-start(f32[8,128,128]{2,1,0:T(8,128)S(1)} %get-tuple-element.54), channel_id=1, source_target_pairs={{0,1},{1,0},{2,3},{3,2},{4,5},{5,4},{6,7},{7,6},{8,9},{9,8},{10,11... | collective-permute-start | bytes 1572872 | tf_op jit(solution)/shard_map/ppermute | solution.py:30
  14.4 8.7 %collective-permute-start.4 = (f32[4,128,128]{2,1,0:T(8,128)S(1)}, f32[4,128,128]{2,1,0:T(8,128)S(1)}, u32[]{:S(2)}, u32[]{:S(2)}) collective-permute-start(f32[4,128,128]{2,1,0:T(8,128)S(1)} %get-tuple-element.70), channel_id=1, source_target_pairs={{1,2},{2,1},{3,0},{0,3},{5,6},{6,5},{7,4},{4,7},{9,10},{10,9},{11,... | collective-permute-start | bytes 786440 | tf_op jit(solution)/shard_map/ppermute | solution.py:30
  16.4 14.6 %collective-permute-start.5 = (f32[4,128,128]{2,1,0:T(8,128)S(1)}, f32[4,128,128]{2,1,0:T(8,128)S(1)}, u32[]{:S(2)}, u32[]{:S(2)}) collective-permute-start(f32[4,128,128]{2,1,0:T(8,128)S(1)} %get-tuple-element.77), channel_id=1, source_target_pairs={{0,4},{4,0},{8,12},{12,8},{16,20},{20,16},{24,28},{28,24},{1,5},{5... | collective-permute-start | bytes 786440 | tf_op jit(solution)/shard_map/ppermute | solution.py:30
  17.0 15.3 %collective-permute-start.6 = (f32[4,128,128]{2,1,0:T(8,128)S(1)}, f32[4,128,128]{2,1,0:T(8,128)S(1)}, u32[]{:S(2)}, u32[]{:S(2)}) collective-permute-start(f32[4,128,128]{2,1,0:T(8,128)S(1)} %get-tuple-element.80), channel_id=1, source_target_pairs={{4,8},{8,4},{12,16},{16,12},{20,24},{24,20},{28,0},{0,28},{5,9},{9... | collective-permute-start | bytes 786440 | tf_op jit(solution)/shard_map/ppermute | solution.py:30
  23.4 8.8 %collective-permute-start.10 = (f32[3,128]{1,0:T(4,128)S(1)}, f32[3,128]{1,0:T(4,128)S(1)}, u32[]{:S(2)}, u32[]{:S(2)}) collective-permute-start(f32[3,128]{1,0:T(4,128)S(1)} %get-tuple-element.84), channel_id=1, source_target_pairs={{1,2},{2,1},{3,0},{0,3},{5,6},{6,5},{7,4},{4,7},{9,10},{10,9},{11,... | collective-permute-start | bytes 4616 | tf_op jit(solution)/shard_map/ppermute | solution.py:30
  24.4 7.9 %collective-permute-start.7 = (f32[3,128]{1,0:T(4,128)S(1)}, f32[3,128]{1,0:T(4,128)S(1)}, u32[]{:S(2)}, u32[]{:S(2)}) collective-permute-start(f32[3,128]{1,0:T(4,128)S(1)} %get-tuple-element.81), channel_id=1, source_target_pairs={{0,4},{4,0},{8,12},{12,8},{16,20},{20,16},{24,28},{28,24},{1,5},{5... | collective-permute-start | bytes 4616 | tf_op jit(solution)/shard_map/ppermute | solution.py:30
  25.0 7.4 %collective-permute-start.8 = (f32[3,128]{1,0:T(4,128)S(1)}, f32[3,128]{1,0:T(4,128)S(1)}, u32[]{:S(2)}, u32[]{:S(2)}) collective-permute-start(f32[3,128]{1,0:T(4,128)S(1)} %get-tuple-element.82), channel_id=1, source_target_pairs={{4,8},{8,4},{12,16},{16,12},{20,24},{24,20},{28,0},{0,28},{5,9},{9... | collective-permute-start | bytes 4616 | tf_op jit(solution)/shard_map/ppermute | solution.py:30
  31.0 1.3 %collective-permute-start.9 = (f32[3,128]{1,0:T(4,128)S(1)}, f32[3,128]{1,0:T(4,128)S(1)}, u32[]{:S(2)}, u32[]{:S(2)}) collective-permute-start(f32[3,128]{1,0:T(4,128)S(1)} %shard_map.87), channel_id=1, source_target_pairs={{0,1},{1,0},{2,3},{3,2},{4,5},{5,4},{6,7},{7,6},{8,9},{9,8},{10,11... | collective-permute-start | bytes 4616 | tf_op jit(solution)/shard_map/ppermute | solution.py:30

commit v11 on v10

--- a/solution.py
+++ b/solution.py
@@ -80,25 +80,37 @@
     order = order_of()
     sources = (ham_hbm.at[0, 0, 0], inv_hbm.at[0, 0, 0], rho_hbm.at[1, 0, 0, 0], ham_hbm.at[0, 0, order[1]])
     copies = [pltpu.make_async_copy(source, one.at[at], sems.at[at]) for at, source in enumerate(sources)]
-    copies += [
-        pltpu.make_async_copy(ham_hbm.at[0, 0, order[place]], rest.at[at], sems.at[4 + at]) for at, place in enumerate((4, 2))
-    ]
+    sources = (ham_hbm.at[0, 0, order[2]], rho_hbm.at[0, 0, 0, 0])
+    for place in (3, 4):
+        sources += (ham_hbm.at[0, 0, order[place]], inv_hbm.at[0, 0, order[place]])
+        sources += (rho_hbm.at[0, 0, 0, order[place]], rho_hbm.at[1, 0, 0, order[place]])
+    copies += [pltpu.make_async_copy(source, rest.at[at], sems.at[4 + at]) for at, source in enumerate(sources)]
     start_all(copies)
     flags.wait()
     for copy in copies:
         copy.wait()
     one[3] = one[3] * cutoff_ref[0, 0, order[1]].astype(f32)
-    for at, place in enumerate((4, 2)):
-        rest[at] = rest[at] * cutoff_ref[0, 0, order[place]].astype(f32)
-
-
-def next_kernel(at, message, rest, out):
+    rest[0] = rest[0] * cutoff_ref[0, 0, order[2]].astype(f32)
+    for place, first in ((3, 2), (4, 6)):
+        keep = cutoff_ref[0, 0, order[place]].astype(f32)
+        for at in range(first, first + 4):
+            rest[at] = rest[at] * keep
+
+
+def whole_first_kernel(first, after, message, rest, out):
     out[:3] = message[:3]
-    out[3] = rest[at]
+    out[3] = rest[first]
+    out[4] = rest[1]
+    out[5:] = rest[first + 1 : first + 4]
+
+
+def two_first_kernel(message, rest, out):
+    out[:3] = message[:3]
+    out[3] = rest[0]
 
 
 def second_kernel(
-    cutoff_hbm, ham_hbm, inv_hbm, rho_hbm, atom_hbm, after, three, held, left_high, left_low, ham_high, ham_low, members,
+    cutoff_hbm, ham_hbm, inv_hbm, rho_hbm, atom_hbm, after, held, left_high, left_low, ham_high, ham_low, members,
     raw, cutoff_ref, atom_ref, cutoff_sem, atom_sem, sems
 ):
     flags = pltpu.make_async_copy(cutoff_hbm, cutoff_ref, cutoff_sem)
@@ -114,12 +126,8 @@
         copy.wait()
         for place, offset in enumerate(order):
             block = raw[kind, offset]
-            if place == 0:
-                three[(0, 1, 4, 2)[kind]] = block
-            else:
+            if place > 0:
                 block = block * keeps[place]
-                if place == 3:
-                    three[(3, 5, 6, 7)[kind]] = block
             if kind == 0:
                 store((ham_high, ham_low), cols(place), split(block))
             else:
@@ -153,23 +161,25 @@
         more[1 + kind] = held[kind, place]
 
 
-def third_kernel(left_high, left_low, ham_high, ham_low, held, four, four_more, start, mixed_high, mixed_low, diagonal, other):
-    send_more(four_more, held, 4)
-    left = (left_high, left_low)
-    start[...] = dot(part(left, slice(0, 3 * B), cols(0)), part((ham_high, ham_low), slice(0, B), cols(0, 5)))
-    mixed, diagonal[...], other[0], other[1] = first_half(left, 4, start, four, start[:, cols(0)])
-    mixed_high[...], mixed_low[...] = mixed
-
-
-def whole_kernel(left_high, left_low, start, held, diagonal, three, der_hbm, one_more, two_more, diagonal_out, other, der, sem):
+def whole_edge(left, place, start, near, diagonal, diagonal_out, other):
+    mixed, diagonal_out[...], real, other[1, 0] = first_half(left, place, start, near, diagonal)
+    added, other[0, 1], other[1, 1] = second_half(mixed, near[4:])
+    other[0, 0] = real + added
+
+
+def third_kernel(left_high, left_low, ham_high, ham_low, held, three, der_hbm, one_more, two_more, start, diagonal, other, der, sem):
     copy = pltpu.make_async_copy(der_hbm, der, sem)
     copy.start()
     send_more(one_more, held, 1)
     send_more(two_more, held, 2)
-    mixed, diagonal_out[...], real, other[1, 0] = first_half((left_high, left_low), 3, start, three, diagonal[...])
-    added, other[0, 1], other[1, 1] = second_half(mixed, three[4:])
-    other[0, 0] = real + added
+    left = (left_high, left_low)
+    start[...] = dot(part(left, slice(0, 3 * B), cols(0)), part((ham_high, ham_low), slice(0, B), cols(0, 5)))
+    whole_edge(left, 3, start, three, start[:, cols(0)], diagonal, other)
     copy.wait()
+
+
+def four_kernel(left_high, left_low, start, diagonal, four, diagonal_out, other):
+    whole_edge((left_high, left_low), 4, start, four, diagonal[...], diagonal_out, other)
 
 
 def fourth_kernel(left_high, left_low, start, diagonal, one, mixed_high, mixed_low, diagonal_out, other):
@@ -191,10 +201,10 @@
     ahead = dot(part(at_self, slice(0, B), cols(0)), part(left, slice(2 * B, 3 * B), whole))
     behind = dot(part(at_self, slice(2 * B, 3 * B), cols(0)), part(left, slice(0, B), whole))
     imag_comm = ahead - behind
-    comm[...] = imag_comm[:, cols(0)] + other_three[1, 1]
+    comm[...] = imag_comm[:, cols(0)] + other_three[1, 1] + other_four[1, 1]
     sums = [None] * 3
     for place, column in enumerate((c1, c2, c3, c4), 1):
-        imag = (other_one[1], imag_two, other_three[1, 0], other_four[1])[place - 1]
+        imag = (other_one[1], imag_two, other_three[1, 0], other_four[1, 0])[place - 1]
         real_new = held[1, place] + time_step * (imag_comm[:, cols(place)] + imag)
         new[place - 1] = real_new
         for direction in range(3):
@@ -209,14 +219,9 @@
     out[...] = column[...]
 
 
-def four_kernel(mixed_high, mixed_low, four, column, out, other):
-    out[...] = column[...]
-    other[0], other[1], other[2] = second_half((mixed_high[...], mixed_low[...]), four)
-
-
 def real_kernel(
-    held, new, left_high, left_low, self_high, self_low, other_one, real_two, other_three, other_four, more_four, weighted,
-    high_one, low_one, imag_part, one, out_hbm, comm, row_part, imag_new, sems
+    held, new, left_high, left_low, self_high, self_low, other_one, real_two, other_three, other_four, weighted,
+    out_hbm, comm, row_part, imag_new, sems
 ):
     order = order_of()
     copies = start_all(
@@ -228,15 +233,13 @@
     ahead = dot(part(at_self, slice(0, B), cols(0)), part(left, slice(B, 2 * B), whole))
     behind = dot(part(at_self, slice(B, 2 * B), cols(0)), part(left, slice(0, B), whole))
     real_comm = ahead - behind
-    added_one, real_one, imag_one = second_half((high_one[...], low_one[...]), one)
-    others = ((1, other_one[0] + added_one), (3, other_three[0, 0]), (4, other_four[0] + more_four[0]))
-    for at, (place, other) in enumerate(others):
-        imag_new[at] = held[2, place] - time_step * (real_comm[:, cols(place)] + other)
+    for at, (place, other) in enumerate(((3, other_three), (4, other_four))):
+        imag_new[at] = held[2, place] - time_step * (real_comm[:, cols(place)] + other[0, 0])
         copies += start_all(
             [pltpu.make_async_copy(imag_new.at[at], out_hbm.at[1, 0, 0, order[place]], sems.at[1, at])]
         )
-    comm[0] = real_comm[:, cols(0)] + other_three[0, 1] + real_one + more_four[1]
-    comm[1] = imag_part[...] + imag_one + more_four[2]
+    comm[0] = real_comm[:, cols(0)] + other_three[0, 1] + other_four[0, 1]
+    comm[1] = real_comm[:, cols(1)] + other_one[0]
     comm[2] = real_comm[:, cols(2)] + real_two[...]
     for direction in range(3):
         row_part[direction : direction + 1, :] = jnp.sum(weighted[direction].T, axis=0, keepdims=True)
@@ -245,14 +248,23 @@
 
 
 def sixth_kernel(
-    held, der_ref, members, high_two, low_two, comm, row_part, two, c1, c2, c3, c4, old_hbm, out_hbm, forces_hbm, new, forces_ref, sems
+    held, der_ref, members, high_one, low_one, high_two, low_two, imag_part, comm, row_part, one, two, c1, c2, c3, c4, old_hbm,
+    out_hbm, forces_hbm, new, forces_ref, sems
 ):
     order = order_of()
-    prop, inner = rows_of((high_two[...], low_two[...]))
-    behind = dot(inner, split(two[1]))
-    real_new = held[1, 0] + time_step * (comm[1] + dot(prop, split(two[3])) - behind[B:])
+    prop, inner = rows_of(beside((high_one[...], low_one[...]), (high_two[...], low_two[...])))
+    near = [tuple(jnp.concatenate(x, axis=0) for x in zip(split(one[1 + kind]), split(two[1 + kind]))) for kind in range(3)]
+    behind = dot(inner, near[0])
+    real_new = held[1, 0] + time_step * (imag_part[...] + dot(prop, near[2]) - behind[B:])
     new[0] = real_new
     copies = start_all([pltpu.make_async_copy(new.at[0], out_hbm.at[0, 0, 0, 0], sems.at[0])])
+    new[1] = held[2, 0] - time_step * (comm[0] + dot(prop, near[1]) - behind[:B])
+    for place, message, mixed in ((1, one, (high_one, low_one)), (2, two, (high_two, low_two))):
+        added = dot(rows_of((mixed[0][...], mixed[1][...]))[0], split(message[0]))
+        new[1 + place] = held[2, place] - time_step * (comm[place] + added)
+    copies += start_all(
+        [pltpu.make_async_copy(new.at[1 + at], out_hbm.at[1, 0, 0, order[at]], sems.at[1 + at]) for at in range(3)]
+    )
     parts = []
     for direction in range(3):
         product = real_new * der_ref[direction, 0, 0, 0]
@@ -263,13 +275,7 @@
     )
     for direction in range(3):
         forces_ref[direction] = forces[direction : direction + 1]
-    copies += start_all([pltpu.make_async_copy(forces_ref, forces_hbm, sems.at[3])])
-    ahead = dot(prop, beside(split(two[2]), split(two[0])))
-    new[1] = held[2, 0] - time_step * (comm[0] + ahead[:, cols(0)] - behind[:B])
-    new[2] = held[2, 2] - time_step * (comm[2] + ahead[:, cols(1)])
-    copies += start_all(
-        [pltpu.make_async_copy(new.at[1 + at], out_hbm.at[1, 0, 0, order[2 * at]], sems.at[1 + at]) for at in range(2)]
-    )
+    copies += start_all([pltpu.make_async_copy(forces_ref, forces_hbm, sems.at[4])])
     for copy in copies:
         copy.wait()
 
@@ -300,47 +306,51 @@
     message = shape(4, B, B)
     first_one, rest = call(
         first_kernel,
-        [message, shape(2, B, B)],
+        [message, shape(10, B, B)],
         [hbm] * 4,
         0,
         (cutoff, hamiltonian, inverse_margin, density),
-        scratch=[flags, dma(()), dma((6,))],
+        scratch=[flags, dma(()), dma((14,))],
     )
     near_one = swapped(first_one, 1)
-    (first_four,) = call(functools.partial(next_kernel, 0), [message], [vmem] * 2, 0, (first_one, rest))
-    near_four = swapped(first_four, 4)
-    (first_two,) = call(functools.partial(next_kernel, 1), [message], [vmem] * 2, 500, (first_four, rest))
+    whole = shape(8, B, B)
+    kernel = functools.partial(whole_first_kernel, 6)
+    (send_four,) = call(kernel, [whole], [vmem] * 3, 0, (first_one, first_one, rest))
+    near_four = swapped(send_four, 4)
+    (first_two,) = call(two_first_kernel, [message], [vmem] * 2, 500, (send_four, rest))
     near_two = swapped(first_two, 2)
+    kernel = functools.partial(whole_first_kernel, 2)
+    (send_three,) = call(kernel, [whole], [vmem] * 3, 500, (first_two, first_one, rest))
+    near_three = swapped(send_three, 3)
     left = [shape(3 * B, 5 * B, kind=bf16)] * 2
     ham = [shape(B, 5 * B, kind=bf16)] * 2
-    send_three, held, left_high, left_low, ham_high, ham_low, members = call(
+    held, left_high, left_low, ham_high, ham_low, members = call(
         second_kernel,
-        [shape(8, B, B), shape(3, 5, B, B)] + left + ham + [shape(ATOMS, B)],
+        [shape(3, 5, B, B)] + left + ham + [shape(ATOMS, B)],
         [hbm] * 6,
-        0,
-        (cutoff, hamiltonian, inverse_margin, density, atom_of, first_two),
+        2000,
+        (cutoff, hamiltonian, inverse_margin, density, atom_of, send_three),
         scratch=[pltpu.VMEM((4, 5, B, B), f32), flags, pltpu.VMEM((1, 1, B), jnp.int32), dma(()), dma(()), dma((4,))],
     )
-    near_three = swapped(send_three, 3)
     mixed = [shape(3 * B, B, kind=bf16)] * 2
-    four_more, start, high_four, low_four, diagonal, other_four = call(
+    both = shape(2, 2, B, B)
+    one_more, two_more, start, diagonal, other_three, derivative = call(
         third_kernel,
-        [message, shape(3 * B, 5 * B)] + mixed + [shape(3 * B, B), shape(2, B, B)],
-        [vmem] * 6,
+        [message, message, shape(3 * B, 5 * B), shape(3 * B, B), both, shape(*derivative.shape)],
+        [vmem] * 6 + [hbm],
         8000,
-        (left_high, left_low, ham_high, ham_low, held, near_four),
-    )
-    near_four_more = swapped(four_more, 4)
-    one_more, two_more, diagonal, other_three, derivative = call(
-        whole_kernel,
-        [message, message, shape(3 * B, B), shape(2, 2, B, B), shape(*derivative.shape)],
-        [vmem] * 6 + [hbm],
+        (left_high, left_low, ham_high, ham_low, held, near_three, derivative),
+        scratch=[dma(())],
+    )
+    near_two_more = swapped(two_more, 2)
+    near_one_more = swapped(one_more, 1)
+    diagonal, other_four = call(
+        four_kernel,
+        [shape(3 * B, B), both],
+        [vmem] * 5,
         14,
-        (left_high, left_low, start, held, diagonal, near_three, derivative),
-        scratch=[dma(())],
-    )
-    near_one_more = swapped(one_more, 1)
-    near_two_more = swapped(two_more, 2)
+        (left_high, left_low, start, diagonal, near_four),
+    )
     high_one, low_one, diagonal, other_one = call(
         fourth_kernel,
         mixed + [shape(3 * B, B), shape(2, B, B)],
@@ -357,36 +367,30 @@
         (left_high, left_low, start, diagonal, held, derivative, other_one, other_three, other_four, near_two),
     )
     c1, c2, c3, c4 = columns
-    c4, more_four = call(
-        four_kernel,
-        [shape(3, B), shape(3, B, B)],
-        [vmem] * 4,
-        5,
-        (high_four, low_four, near_four_more, c4),
-    )
-    (c3,) = call(pass_kernel, [shape(3, B)], [vmem] * 2, 0, (near_one_more, c3))
-    columns = [swapped(column, at) for at, column in enumerate((c1, c2, c3, c4), 1)]
-    args = (held, new, left_high, left_low, self_high, self_low, other_one, real_two, other_three, other_four, more_four, weighted)
-    args += (high_one, low_one, imag_part, near_one_more)
+    c1, c2, c4 = swapped(c1, 1), swapped(c2, 2), swapped(c4, 4)
+    (c3,) = call(pass_kernel, [shape(3, B)], [vmem] * 2, 0, (c4, c3))
+    columns = (c1, c2, swapped(c3, 3), c4)
+    args = (held, new, left_high, left_low, self_high, self_low, other_one, real_two, other_three, other_four, weighted)
     out, comm, row_part = call(
         real_kernel,
         [shape(*density.shape), shape(3, B, B), shape(3, B)],
-        [vmem] * 16,
-        15,
+        [vmem] * 11,
+        10,
         args,
         out_specs=[hbm] + [vmem] * 2,
-        scratch=[pltpu.VMEM((3, B, B), f32), dma((2, 4))],
-    )
-    args = (held, derivative, members, high_two, low_two, comm, row_part, near_two_more, *columns, out)
+        scratch=[pltpu.VMEM((2, B, B), f32), dma((2, 4))],
+    )
+    args = (held, derivative, members, high_one, low_one, high_two, low_two, imag_part, comm, row_part)
+    args += (near_one_more, near_two_more, *columns, out)
     new_density, forces = call(
         sixth_kernel,
         [shape(*density.shape), shape(3, 1, ATOMS)],
-        [vmem] * 12 + [hbm],
+        [vmem] * 16 + [hbm],
         10,
         args,
         out_specs=[hbm, hbm],
-        scratch=[pltpu.VMEM((3, B, B), f32), pltpu.VMEM((3, 1, ATOMS), f32), dma((4,))],
-        aliases={12: 0},
+        scratch=[pltpu.VMEM((4, B, B), f32), pltpu.VMEM((3, 1, ATOMS), f32), dma((5,))],
+        aliases={16: 0},
     )
     return new_density, forces.reshape(1, 1, 3, ATOMS)
 

time: 33.9 us -> 35 us (1.032)
  waiting for transfers between devices: 3.65 us -> 7.95 us
  starting transfers between devices: 20.1 us -> 17.2 us
    ppermute x11 -> x10, waiting for transfers between devices: 3.65 us -> 7.95 us  [swapped(): return lax.ppermute(cells, axis, pairs)]
    ppermute x11 -> x10, starting transfers between devices: 20.1 us -> 17.2 us  [swapped(): return lax.ppermute(cells, axis, pairs)]
  transfers between devices with their start and end apart: 11 -> 10, of which waited for: 2 -> 4; matrix products, arithmetic and copies ran while one was open for 0% -> 0% of each run, Pallas kernels for 20% -> 18%
where the time goes in v11:
time: 35 us; the launch traced here: 34.8 us
  starting transfers between devices  17.2 us (49%)
  Pallas kernels  8.89 us (25%)
  waiting for transfers between devices  7.95 us (23%)
  between operations  0.74 us (2%)
    ppermute x10, starting transfers between devices, swapped(): return lax.ppermute(cells, axis, pairs)  17.2 us
    pallas_call x12, Pallas kernels, call(): pl.pallas_call(kernel, out_shape=shapes, in_specs=in_specs, out_specs=out...  8.89 us
    ppermute x10, waiting for transfers between devices, swapped(): return lax.ppermute(cells, axis, pairs)  7.95 us
  transfers between devices with their start and end apart: 10, of which 4 were waited for; matrix products, arithmetic and copies ran while one was open for 0% of the time, Pallas kernels for 18%

profile of v11, /device:TPU:0, one launch (start us, length us, event | category | flops | bytes accessed | tf_op | source)
XLA Modules:
  0.0 34.8 jit_solution(7807005414471729403)
XLA Ops:
  0.6 1.4 %shard_map.77 = (f32[4,128,128]{2,1,0:T(8,128)S(1)}, f32[10,128,128]{2,1,0:T(8,128)S(1)}) custom-call(s32[1,1,5]{2,1,0:T(1,128)} %cutoff_hbm.3, f32[1,1,5,128,128]{4,3,2,1,0:T(8,128)} %ham_hbm.3, f32[1,1,5,128,128]{4,3,2,1,0:T(8,128)} %inv_hbm.3, f32[2,1,1,5,128,128]{5,4,3,2,1,0:T(8,128)} %rho_hbm.3), custom_call_target="tpu_custom_call" | custom-call | bytes 2228244 | tf_op jit(solution)/shard_map/pallas_call | solution.py:285
  2.0 3.0 %collective-permute-start.2 = (f32[4,128,128]{2,1,0:T(8,128)S(1)}, f32[4,128,128]{2,1,0:T(8,128)S(1)}, u32[]{:S(2)}, u32[]{:S(2)}) collective-permute-start(f32[4,128,128]{2,1,0:T(8,128)S(1)} %get-tuple-element.39.after.message), channel_id=1, source_target_pairs={{0,4},{4,0},{8,12},{12,8},{16,20},{20,16},{24,28},{28,24},{1,5},{5... | collective-permute-start | bytes 786440 | tf_op jit(solution)/shard_map/ppermute | solution.py:30
  5.1 0.7 %collective-permute-start.1 = (f32[8,128,128]{2,1,0:T(8,128)S(1)}, f32[8,128,128]{2,1,0:T(8,128)S(1)}, u32[]{:S(2)}, u32[]{:S(2)}) collective-permute-start(f32[8,128,128]{2,1,0:T(8,128)S(1)} %shard_map.78.message), channel_id=1, source_target_pairs={{1,2},{2,1},{3,0},{0,3},{5,6},{6,5},{7,4},{4,7},{9,10},{10,9},{11,... | collective-permute-start | bytes 1572872 | tf_op jit(solution)/shard_map/ppermute | solution.py:30
  5.8 3.6 %collective-permute-start.3 = (f32[4,128,128]{2,1,0:T(8,128)S(1)}, f32[4,128,128]{2,1,0:T(8,128)S(1)}, u32[]{:S(2)}, u32[]{:S(2)}) collective-permute-start(f32[4,128,128]{2,1,0:T(8,128)S(1)} %shard_map.79.after), channel_id=1, source_target_pairs={{4,8},{8,4},{12,16},{16,12},{20,24},{24,20},{28,0},{0,28},{5,9},{9... | collective-permute-start | bytes 786440 | tf_op jit(solution)/shard_map/ppermute | solution.py:30
  9.5 0.7 %collective-permute-start = (f32[8,128,128]{2,1,0:T(8,128)S(1)}, f32[8,128,128]{2,1,0:T(8,128)S(1)}, u32[]{:S(2)}, u32[]{:S(2)}) collective-permute-start(f32[8,128,128]{2,1,0:T(8,128)S(1)} %shard_map.80.after), channel_id=1, source_target_pairs={{0,1},{1,0},{2,3},{3,2},{4,5},{5,4},{6,7},{7,6},{8,9},{9,8},{10,11... | collective-permute-start | bytes 1572872 | tf_op jit(solution)/shard_map/ppermute | solution.py:30
  10.2 1.4 %shard_map.81 = (f32[3,5,128,128]{3,2,1,0:T(8,128)S(1)}, bf16[384,640]{1,0:T(8,128)(2,1)S(1)}, bf16[384,640]{1,0:T(8,128)(2,1)S(1)}, bf16[128,640]{1,0:T(8,128)(...) custom-call(s32[1,1,5]{2,1,0:T(1,128)} %cutoff_hbm.3, f32[1,1,5,128,128]{4,3,2,1,0:T(8,128)} %ham_hbm.3, ...), custom_call_target="tpu_custom_call" | custom-call | flops 25165824000 | bytes 5472788 | tf_op jit(solution)/shard_map/pallas_call | solution.py:285
  11.6 0.1 collective-permute-done.three
  11.8 1.2 %shard_map.82 = (f32[4,128,128]{2,1,0:T(8,128)S(1)}, f32[4,128,128]{2,1,0:T(8,128)S(1)}, f32[384,640]{1,0:T(8,128)S(1)}, f32[384,128]{1,0:T(8,128)S(1)}, f32[2,2...) custom-call(bf16[384,640]{1,0:T(8,128)(2,1)S(1)} %get-tuple-element.42.left_high, ...), custom_call_target="tpu_custom_call" | custom-call | flops 100663296000 | bytes 8060928 | tf_op jit(solution)/shard_map/pallas_call | solution.py:285
  13.0 0.1 collective-permute-start.4
  13.1 1.9 %collective-permute-start.5 = (f32[4,128,128]{2,1,0:T(8,128)S(1)}, f32[4,128,128]{2,1,0:T(8,128)S(1)}, u32[]{:S(2)}, u32[]{:S(2)}) collective-permute-start(f32[4,128,128]{2,1,0:T(8,128)S(1)} %get-tuple-element.68), channel_id=1, source_target_pairs={{4,8},{8,4},{12,16},{16,12},{20,24},{24,20},{28,0},{0,28},{5,9},{9... | collective-permute-start | bytes 786440 | tf_op jit(solution)/shard_map/ppermute | solution.py:30
  15.0 4.4 %collective-permute-done.1.four = f32[8,128,128]{2,1,0:T(8,128)S(1)} collective-permute-done((f32[8,128,128]{2,1,0:T(8,128)S(1)}, f32[8,128,128]{2,1,0:T(8,128)S(1)}, u32[]{:S(2)}, u32[]{:S(2)}) %collective-permute-start.1) | collective-permute-done | bytes 524320 | tf_op jit(solution)/shard_map/ppermute | solution.py:30
  19.3 0.8 %shard_map.83 = (f32[384,128]{1,0:T(8,128)S(1)}, f32[2,2,128,128]{3,2,1,0:T(8,128)S(1)}) custom-call(bf16[384,640]{1,0:T(8,128)(2,1)S(1)} %get-tuple-element.42.left_high, bf16[384,640]{1,0:T(8,128)(2,1)S(1)} %get-tuple-element.43.left_low, f32[384,640]{1,0:T(8,128)S(1)} %get-tuple-element.48.start, f32[384,128]{1,0:T(8,128)S(1)} %get-tuple-element.49.diagonal, ...), custom_call_target="tpu_custom_call" | custom-call | flops 176160768 | bytes 4128768 | tf_op jit(solution)/shard_map/pallas_call | solution.py:285
  20.2 2.8 %collective-permute-done.2.one = f32[4,128,128]{2,1,0:T(8,128)S(1)} collective-permute-done((f32[4,128,128]{2,1,0:T(8,128)S(1)}, f32[4,128,128]{2,1,0:T(8,128)S(1)}, u32[]{:S(2)}, u32[]{:S(2)}) %collective-permute-start.2) | collective-permute-done | bytes 262176 | tf_op jit(solution)/shard_map/ppermute | solution.py:30
  23.0 0.6 %shard_map.84 = (bf16[384,128]{1,0:T(8,128)(2,1)S(1)}, bf16[384,128]{1,0:T(8,128)(2,1)S(1)}, f32[384,128]{1,0:T(8,128)S(1)}, f32[2,128,128]{2,1,0:T(8,128)S(1)}) custom-call(bf16[384,640]{1,0:T(8,128)(2,1)S(1)} %get-tuple-element.42.left_high, bf16[384,640]{1,0:T(8,128)(2,1)S(1)} %get-tuple-element.43.left_low, f32[384,640]{1,0:T(8,128)S(1)} %get-tuple-element.48.start, ...), custom_call_target="tpu_custom_call" | custom-call | flops 125829120 | bytes 4128768 | tf_op jit(solution)/shard_map/pallas_call | solution.py:285
  23.6 0.0 collective-permute-done.3.two
  23.6 0.9 %shard_map.85 = (f32[4,128,128]{2,1,0:T(8,128)S(1)}, bf16[384,128]{1,0:T(8,128)(2,1)S(1)}, bf16[384,128]{1,0:T(8,128)(2,1)S(1)}, bf16[384,128]{1,0:T(8,128)(2,1)...) custom-call(bf16[384,640]{1,0:T(8,128)(2,1)S(1)} %get-tuple-element., ...), custom_call_target="tpu_custom_call" | custom-call | flops 276824064 | bytes 7411712 | tf_op jit(solution)/shard_map/pallas_call | solution.py:285
  24.6 0.1 collective-permute-start.8
  24.6 2.5 %collective-permute-start.6 = (f32[3,128]{1,0:T(4,128)S(1)}, f32[3,128]{1,0:T(4,128)S(1)}, u32[]{:S(2)}, u32[]{:S(2)}) collective-permute-start(f32[3,128]{1,0:T(4,128)S(1)} %get-tuple-element.69), channel_id=1, source_target_pairs={{0,4},{4,0},{8,12},{12,8},{16,20},{20,16},{24,28},{28,24},{1,5},{5... | collective-permute-start | bytes 4616 | tf_op jit(solution)/shard_map/ppermute | solution.py:30
  27.2 3.5 %collective-permute-start.7 = (f32[3,128]{1,0:T(4,128)S(1)}, f32[3,128]{1,0:T(4,128)S(1)}, u32[]{:S(2)}, u32[]{:S(2)}) collective-permute-start(f32[3,128]{1,0:T(4,128)S(1)} %get-tuple-element.70), channel_id=1, source_target_pairs={{4,8},{8,4},{12,16},{16,12},{20,24},{24,20},{28,0},{0,28},{5,9},{9... | collective-permute-start | bytes 4616 | tf_op jit(solution)/shard_map/ppermute | solution.py:30
  30.7 0.0 collective-permute-done.8.arrived.c4
  30.7 1.0 %collective-permute-start.9 = (f32[3,128]{1,0:T(4,128)S(1)}, f32[3,128]{1,0:T(4,128)S(1)}, u32[]{:S(2)}, u32[]{:S(2)}) collective-permute-start(f32[3,128]{1,0:T(4,128)S(1)} %shard_map.87), channel_id=1, source_target_pairs={{0,1},{1,0},{2,3},{3,2},{4,5},{5,4},{6,7},{7,6},{8,9},{9,8},{10,11... | collective-permute-start | bytes 4616 | tf_op jit(solution)/shard_map/ppermute | solution.py:30
  31.7 1.1 %shard_map.86 = (f32[2,1,1,5,128,128]{5,4,3,2,1,0:T(8,128)}, f32[3,128,128]{2,1,0:T(8,128)S(1)}, f32[3,128]{1,0:T(4,128)S(1)}) custom-call(f32[3,5,128,128]{3,2,1,0:T(8,128)S(1)} %get-tuple-element.41.held, f32[4,128,128]{2,1,0:T(8,128)S(1)} %get-tuple-element.60.new, bf16[384,640]{1,0:T(8,128)(2,1)S(1)} %get-tuple-element.42.left_high, ...), custom_call_target="tpu_custom_call" | custom-call | flops 125829120 | bytes 5375488 | tf_op jit(solution)/shard_map/pallas_call | solution.py:285
  32.9 0.0 collective-permute-done.6.c1
  32.9 0.6 %collective-permute-done.7.c2 = f32[3,128]{1,0:T(4,128)S(1)} collective-permute-done((f32[3,128]{1,0:T(4,128)S(1)}, f32[3,128]{1,0:T(4,128)S(1)}, u32[]{:S(2)}, u32[]{:S(2)}) %collective-permute-start.7) | collective-permute-done | bytes 1568 | tf_op jit(solution)/shard_map/ppermute | solution.py:30
  33.5 0.0 collective-permute-done.9.c3
  33.5 0.0 collective-permute-done.4.one
  33.5 0.0 collective-permute-done.5.two
  33.5 1.3 %shard_map.88 = (f32[2,1,1,5,128,128]{5,4,3,2,1,0:T(8,128)}, f32[3,1,64]{2,1,0:T(1,128)}) custom-call(f32[3,5,128,128]{3,2,1,0:T(8,128)S(1)} %get-tuple-element.41.held, f32[3,1,1,5,128,128]{5,4,3,2,1,0:T(8,128)S(1)} %get-tuple-element.46.der_ref, f32[64,128]{1,0:T(8,128)S(1)} %get-tuple-element.47.members, ...), custom_call_target="tpu_custom_call", output_to_operand_aliasing={{0}: (16, {})} | custom-call | flops 125829120 | bytes 4890880 | tf_op jit(solution)/shard_map/pallas_call | solution.py:285
  (4 shorter events, 0.1 us)
Async XLA Ops:
  2.0 21.0 %collective-permute-start.2 = (f32[4,128,128]{2,1,0:T(8,128)S(1)}, f32[4,128,128]{2,1,0:T(8,128)S(1)}, u32[]{:S(2)}, u32[]{:S(2)}) collective-permute-start(f32[4,128,128]{2,1,0:T(8,128)S(1)} %get-tuple-element.39.after.message), channel_id=1, source_target_pairs={{0,4},{4,0},{8,12},{12,8},{16,20},{20,16},{24,28},{28,24},{1,5},{5... | collective-permute-start | bytes 786440 | tf_op jit(solution)/shard_map/ppermute | solution.py:30
  5.1 14.2 %collective-permute-start.1 = (f32[8,128,128]{2,1,0:T(8,128)S(1)}, f32[8,128,128]{2,1,0:T(8,128)S(1)}, u32[]{:S(2)}, u32[]{:S(2)}) collective-permute-start(f32[8,128,128]{2,1,0:T(8,128)S(1)} %shard_map.78.message), channel_id=1, source_target_pairs={{1,2},{2,1},{3,0},{0,3},{5,6},{6,5},{7,4},{4,7},{9,10},{10,9},{11,... | collective-permute-start | bytes 1572872 | tf_op jit(solution)/shard_map/ppermute | solution.py:30
  5.8 17.8 %collective-permute-start.3 = (f32[4,128,128]{2,1,0:T(8,128)S(1)}, f32[4,128,128]{2,1,0:T(8,128)S(1)}, u32[]{:S(2)}, u32[]{:S(2)}) collective-permute-start(f32[4,128,128]{2,1,0:T(8,128)S(1)} %shard_map.79.after), channel_id=1, source_target_pairs={{4,8},{8,4},{12,16},{16,12},{20,24},{24,20},{28,0},{0,28},{5,9},{9... | collective-permute-start | bytes 786440 | tf_op jit(solution)/shard_map/ppermute | solution.py:30
  9.5 2.3 %collective-permute-start = (f32[8,128,128]{2,1,0:T(8,128)S(1)}, f32[8,128,128]{2,1,0:T(8,128)S(1)}, u32[]{:S(2)}, u32[]{:S(2)}) collective-permute-start(f32[8,128,128]{2,1,0:T(8,128)S(1)} %shard_map.80.after), channel_id=1, source_target_pairs={{0,1},{1,0},{2,3},{3,2},{4,5},{5,4},{6,7},{7,6},{8,9},{9,8},{10,11... | collective-permute-start | bytes 1572872 | tf_op jit(solution)/shard_map/ppermute | solution.py:30
  13.0 20.5 %collective-permute-start.4 = (f32[4,128,128]{2,1,0:T(8,128)S(1)}, f32[4,128,128]{2,1,0:T(8,128)S(1)}, u32[]{:S(2)}, u32[]{:S(2)}) collective-permute-start(f32[4,128,128]{2,1,0:T(8,128)S(1)} %get-tuple-element.67), channel_id=1, source_target_pairs={{0,4},{4,0},{8,12},{12,8},{16,20},{20,16},{24,28},{28,24},{1,5},{5... | collective-permute-start | bytes 786440 | tf_op jit(solution)/shard_map/ppermute | solution.py:30
  13.1 20.4 %collective-permute-start.5 = (f32[4,128,128]{2,1,0:T(8,128)S(1)}, f32[4,128,128]{2,1,0:T(8,128)S(1)}, u32[]{:S(2)}, u32[]{:S(2)}) collective-permute-start(f32[4,128,128]{2,1,0:T(8,128)S(1)} %get-tuple-element.68), channel_id=1, source_target_pairs={{4,8},{8,4},{12,16},{16,12},{20,24},{24,20},{28,0},{0,28},{5,9},{9... | collective-permute-start | bytes 786440 | tf_op jit(solution)/shard_map/ppermute | solution.py:30
  24.6 6.1 %collective-permute-start.8 = (f32[3,128]{1,0:T(4,128)S(1)}, f32[3,128]{1,0:T(4,128)S(1)}, u32[]{:S(2)}, u32[]{:S(2)}) collective-permute-start(f32[3,128]{1,0:T(4,128)S(1)} %get-tuple-element.71), channel_id=1, source_target_pairs={{1,2},{2,1},{3,0},{0,3},{5,6},{6,5},{7,4},{4,7},{9,10},{10,9},{11,... | collective-permute-start | bytes 4616 | tf_op jit(solution)/shard_map/ppermute | solution.py:30
  24.6 8.2 %collective-permute-start.6 = (f32[3,128]{1,0:T(4,128)S(1)}, f32[3,128]{1,0:T(4,128)S(1)}, u32[]{:S(2)}, u32[]{:S(2)}) collective-permute-start(f32[3,128]{1,0:T(4,128)S(1)} %get-tuple-element.69), channel_id=1, source_target_pairs={{0,4},{4,0},{8,12},{12,8},{16,20},{20,16},{24,28},{28,24},{1,5},{5... | collective-permute-start | bytes 4616 | tf_op jit(solution)/shard_map/ppermute | solution.py:30
  27.2 6.3 %collective-permute-start.7 = (f32[3,128]{1,0:T(4,128)S(1)}, f32[3,128]{1,0:T(4,128)S(1)}, u32[]{:S(2)}, u32[]{:S(2)}) collective-permute-start(f32[3,128]{1,0:T(4,128)S(1)} %get-tuple-element.70), channel_id=1, source_target_pairs={{4,8},{8,4},{12,16},{16,12},{20,24},{24,20},{28,0},{0,28},{5,9},{9... | collective-permute-start | bytes 4616 | tf_op jit(solution)/shard_map/ppermute | solution.py:30
  30.7 2.8 %collective-permute-start.9 = (f32[3,128]{1,0:T(4,128)S(1)}, f32[3,128]{1,0:T(4,128)S(1)}, u32[]{:S(2)}, u32[]{:S(2)}) collective-permute-start(f32[3,128]{1,0:T(4,128)S(1)} %shard_map.87), channel_id=1, source_target_pairs={{0,1},{1,0},{2,3},{3,2},{4,5},{5,4},{6,7},{7,6},{8,9},{9,8},{10,11... | collective-permute-start | bytes 4616 | tf_op jit(solution)/shard_map/ppermute | solution.py:30

commit v12 on v11

--- a/solution.py
+++ b/solution.py
@@ -80,33 +80,37 @@
     order = order_of()
     sources = (ham_hbm.at[0, 0, 0], inv_hbm.at[0, 0, 0], rho_hbm.at[1, 0, 0, 0], ham_hbm.at[0, 0, order[1]])
     copies = [pltpu.make_async_copy(source, one.at[at], sems.at[at]) for at, source in enumerate(sources)]
-    sources = (ham_hbm.at[0, 0, order[2]], rho_hbm.at[0, 0, 0, 0])
-    for place in (3, 4):
-        sources += (ham_hbm.at[0, 0, order[place]], inv_hbm.at[0, 0, order[place]])
-        sources += (rho_hbm.at[0, 0, 0, order[place]], rho_hbm.at[1, 0, 0, order[place]])
-    copies += [pltpu.make_async_copy(source, rest.at[at], sems.at[4 + at]) for at, source in enumerate(sources)]
+    copies += [
+        pltpu.make_async_copy(ham_hbm.at[0, 0, order[place]], rest.at[at], sems.at[4 + at]) for at, place in enumerate((4, 2))
+    ]
     start_all(copies)
     flags.wait()
     for copy in copies:
         copy.wait()
     one[3] = one[3] * cutoff_ref[0, 0, order[1]].astype(f32)
-    rest[0] = rest[0] * cutoff_ref[0, 0, order[2]].astype(f32)
-    for place, first in ((3, 2), (4, 6)):
-        keep = cutoff_ref[0, 0, order[place]].astype(f32)
-        for at in range(first, first + 4):
-            rest[at] = rest[at] * keep
-
-
-def whole_first_kernel(first, after, message, rest, out):
+    for at, place in enumerate((4, 2)):
+        rest[at] = rest[at] * cutoff_ref[0, 0, order[place]].astype(f32)
+
+
+def next_kernel(at, message, rest, out):
     out[:3] = message[:3]
-    out[3] = rest[first]
-    out[4] = rest[1]
-    out[5:] = rest[first + 1 : first + 4]
-
-
-def two_first_kernel(message, rest, out):
+    out[3] = rest[at]
+
+
+def whole_first_kernel(cutoff_hbm, ham_hbm, inv_hbm, rho_hbm, message, out, cutoff_ref, cutoff_sem, sems):
+    flags = pltpu.make_async_copy(cutoff_hbm, cutoff_ref, cutoff_sem)
+    flags.start()
+    offset = order_of()[3]
+    sources = (ham_hbm.at[0, 0, offset], rho_hbm.at[0, 0, 0, 0], inv_hbm.at[0, 0, offset], rho_hbm.at[0, 0, 0, offset])
+    sources += (rho_hbm.at[1, 0, 0, offset],)
+    copies = start_all([pltpu.make_async_copy(source, out.at[3 + at], sems.at[at]) for at, source in enumerate(sources)])
     out[:3] = message[:3]
-    out[3] = rest[0]
+    flags.wait()
+    keep = cutoff_ref[0, 0, offset].astype(f32)
+    for copy in copies:
+        copy.wait()
+    for at in (3, 5, 6, 7):
+        out[at] = out[at] * keep
 
 
 def second_kernel(
@@ -161,25 +165,28 @@
         more[1 + kind] = held[kind, place]
 
 
-def whole_edge(left, place, start, near, diagonal, diagonal_out, other):
-    mixed, diagonal_out[...], real, other[1, 0] = first_half(left, place, start, near, diagonal)
-    added, other[0, 1], other[1, 1] = second_half(mixed, near[4:])
-    other[0, 0] = real + added
-
-
-def third_kernel(left_high, left_low, ham_high, ham_low, held, three, der_hbm, one_more, two_more, start, diagonal, other, der, sem):
+def third_kernel(left_high, left_low, ham_high, ham_low, held, three, der_hbm, start, diagonal, other, der, sem):
     copy = pltpu.make_async_copy(der_hbm, der, sem)
     copy.start()
-    send_more(one_more, held, 1)
-    send_more(two_more, held, 2)
     left = (left_high, left_low)
     start[...] = dot(part(left, slice(0, 3 * B), cols(0)), part((ham_high, ham_low), slice(0, B), cols(0, 5)))
-    whole_edge(left, 3, start, three, start[:, cols(0)], diagonal, other)
+    mixed, diagonal[...], real, other[1, 0] = first_half(left, 3, start, three, start[:, cols(0)])
+    added, other[0, 1], other[1, 1] = second_half(mixed, three[4:])
+    other[0, 0] = real + added
     copy.wait()
 
 
-def four_kernel(left_high, left_low, start, diagonal, four, diagonal_out, other):
-    whole_edge((left_high, left_low), 4, start, four, diagonal[...], diagonal_out, other)
+def four_kernel(
+    left_high, left_low, start, held, diagonal, four, one_more, mixed_high, mixed_low, diagonal_out, other
+):
+    send_more(one_more, held, 1)
+    mixed, diagonal_out[...], other[0], other[1] = first_half((left_high, left_low), 4, start, four, diagonal[...])
+    mixed_high[...], mixed_low[...] = mixed
+
+
+def more_kernel(after, held, two_more, four_more):
+    send_more(two_more, held, 2)
+    send_more(four_more, held, 4)
 
 
 def fourth_kernel(left_high, left_low, start, diagonal, one, mixed_high, mixed_low, diagonal_out, other):
@@ -201,10 +208,10 @@
     ahead = dot(part(at_self, slice(0, B), cols(0)), part(left, slice(2 * B, 3 * B), whole))
     behind = dot(part(at_self, slice(2 * B, 3 * B), cols(0)), part(left, slice(0, B), whole))
     imag_comm = ahead - behind
-    comm[...] = imag_comm[:, cols(0)] + other_three[1, 1] + other_four[1, 1]
+    comm[...] = imag_comm[:, cols(0)] + other_three[1, 1]
     sums = [None] * 3
     for place, column in enumerate((c1, c2, c3, c4), 1):
-        imag = (other_one[1], imag_two, other_three[1, 0], other_four[1, 0])[place - 1]
+        imag = (other_one[1], imag_two, other_three[1, 0], other_four[1])[place - 1]
         real_new = held[1, place] + time_step * (imag_comm[:, cols(place)] + imag)
         new[place - 1] = real_new
         for direction in range(3):
@@ -221,7 +228,7 @@
 
 def real_kernel(
     held, new, left_high, left_low, self_high, self_low, other_one, real_two, other_three, other_four, weighted,
-    out_hbm, comm, row_part, imag_new, sems
+    imag_part, high_four, low_four, four, out_hbm, comm, imag_out, row_part, imag_new, sems
 ):
     order = order_of()
     copies = start_all(
@@ -233,12 +240,14 @@
     ahead = dot(part(at_self, slice(0, B), cols(0)), part(left, slice(B, 2 * B), whole))
     behind = dot(part(at_self, slice(B, 2 * B), cols(0)), part(left, slice(0, B), whole))
     real_comm = ahead - behind
-    for at, (place, other) in enumerate(((3, other_three), (4, other_four))):
-        imag_new[at] = held[2, place] - time_step * (real_comm[:, cols(place)] + other[0, 0])
+    added, real_four, imag_four = second_half((high_four[...], low_four[...]), four)
+    imag_out[...] = imag_part[...] + imag_four
+    for at, (place, other) in enumerate(((3, other_three[0, 0]), (4, other_four[0] + added))):
+        imag_new[at] = held[2, place] - time_step * (real_comm[:, cols(place)] + other)
         copies += start_all(
             [pltpu.make_async_copy(imag_new.at[at], out_hbm.at[1, 0, 0, order[place]], sems.at[1, at])]
         )
-    comm[0] = real_comm[:, cols(0)] + other_three[0, 1] + other_four[0, 1]
+    comm[0] = real_comm[:, cols(0)] + other_three[0, 1] + real_four
     comm[1] = real_comm[:, cols(1)] + other_one[0]
     comm[2] = real_comm[:, cols(2)] + real_two[...]
     for direction in range(3):
@@ -306,21 +315,25 @@
     message = shape(4, B, B)
     first_one, rest = call(
         first_kernel,
-        [message, shape(10, B, B)],
+        [message, shape(2, B, B)],
         [hbm] * 4,
         0,
         (cutoff, hamiltonian, inverse_margin, density),
-        scratch=[flags, dma(()), dma((14,))],
+        scratch=[flags, dma(()), dma((6,))],
     )
     near_one = swapped(first_one, 1)
-    whole = shape(8, B, B)
-    kernel = functools.partial(whole_first_kernel, 6)
-    (send_four,) = call(kernel, [whole], [vmem] * 3, 0, (first_one, first_one, rest))
-    near_four = swapped(send_four, 4)
-    (first_two,) = call(two_first_kernel, [message], [vmem] * 2, 500, (send_four, rest))
+    (first_four,) = call(functools.partial(next_kernel, 0), [message], [vmem] * 2, 0, (first_one, rest))
+    near_four = swapped(first_four, 4)
+    (first_two,) = call(functools.partial(next_kernel, 1), [message], [vmem] * 2, 500, (first_four, rest))
     near_two = swapped(first_two, 2)
-    kernel = functools.partial(whole_first_kernel, 2)
-    (send_three,) = call(kernel, [whole], [vmem] * 3, 500, (first_two, first_one, rest))
+    (send_three,) = call(
+        whole_first_kernel,
+        [shape(8, B, B)],
+        [hbm] * 4 + [vmem],
+        500,
+        (cutoff, hamiltonian, inverse_margin, density, first_two),
+        scratch=[flags, dma(()), dma((5,))],
+    )
     near_three = swapped(send_three, 3)
     left = [shape(3 * B, 5 * B, kind=bf16)] * 2
     ham = [shape(B, 5 * B, kind=bf16)] * 2
@@ -334,23 +347,25 @@
     )
     mixed = [shape(3 * B, B, kind=bf16)] * 2
     both = shape(2, 2, B, B)
-    one_more, two_more, start, diagonal, other_three, derivative = call(
+    start, diagonal, other_three, derivative = call(
         third_kernel,
-        [message, message, shape(3 * B, 5 * B), shape(3 * B, B), both, shape(*derivative.shape)],
+        [shape(3 * B, 5 * B), shape(3 * B, B), shape(2, 2, B, B), shape(*derivative.shape)],
         [vmem] * 6 + [hbm],
         8000,
         (left_high, left_low, ham_high, ham_low, held, near_three, derivative),
         scratch=[dma(())],
     )
+    one_more, high_four, low_four, diagonal, other_four = call(
+        four_kernel,
+        [message] + mixed + [shape(3 * B, B), shape(2, B, B)],
+        [vmem] * 6,
+        8,
+        (left_high, left_low, start, held, diagonal, near_four),
+    )
+    near_one_more = swapped(one_more, 1)
+    two_more, four_more = call(more_kernel, [message] * 2, [vmem] * 2, 300, (one_more, held))
+    near_four_more = swapped(four_more, 4)
     near_two_more = swapped(two_more, 2)
-    near_one_more = swapped(one_more, 1)
-    diagonal, other_four = call(
-        four_kernel,
-        [shape(3 * B, B), both],
-        [vmem] * 5,
-        14,
-        (left_high, left_low, start, diagonal, near_four),
-    )
     high_one, low_one, diagonal, other_one = call(
         fourth_kernel,
         mixed + [shape(3 * B, B), shape(2, B, B)],
@@ -367,17 +382,20 @@
         (left_high, left_low, start, diagonal, held, derivative, other_one, other_three, other_four, near_two),
     )
     c1, c2, c3, c4 = columns
-    c1, c2, c4 = swapped(c1, 1), swapped(c2, 2), swapped(c4, 4)
+    c1, c2 = swapped(c1, 1), swapped(c2, 2)
+    (c4,) = call(pass_kernel, [shape(3, B)], [vmem] * 2, 0, (near_four_more, c4))
+    c4 = swapped(c4, 4)
     (c3,) = call(pass_kernel, [shape(3, B)], [vmem] * 2, 0, (c4, c3))
     columns = (c1, c2, swapped(c3, 3), c4)
     args = (held, new, left_high, left_low, self_high, self_low, other_one, real_two, other_three, other_four, weighted)
-    out, comm, row_part = call(
+    args += (imag_part, high_four, low_four, near_four_more)
+    out, comm, imag_part, row_part = call(
         real_kernel,
-        [shape(*density.shape), shape(3, B, B), shape(3, B)],
-        [vmem] * 11,
+        [shape(*density.shape), shape(3, B, B), shape(B, B), shape(3, B)],
+        [vmem] * 15,
         10,
         args,
-        out_specs=[hbm] + [vmem] * 2,
+        out_specs=[hbm] + [vmem] * 3,
         scratch=[pltpu.VMEM((2, B, B), f32), dma((2, 4))],
     )
     args = (held, derivative, members, high_one, low_one, high_two, low_two, imag_part, comm, row_part)

time: 35 us -> 32.1 us (0.917)
  waiting for transfers between devices: 7.95 us -> 1.69 us
  starting transfers between devices: 17.2 us -> 19.9 us
  Pallas kernels: 8.89 us -> 9.5 us
    ppermute x10 -> x11, waiting for transfers between devices: 7.95 us -> 1.69 us  [swapped(): return lax.ppermute(cells, axis, pairs)]
    ppermute x10 -> x11, starting transfers between devices: 17.2 us -> 19.9 us  [swapped(): return lax.ppermute(cells, axis, pairs)]
    pallas_call x12 -> x14, Pallas kernels: 8.89 us -> 9.5 us  [call(): pl.pallas_call(kernel, out_shape=shapes, in_specs=in_specs, out_specs=out...]
  transfers between devices with their start and end apart: 10 -> 11, of which waited for: 4 -> 3; matrix products, arithmetic and copies ran while one was open for 0% -> 0% of each run, Pallas kernels for 18% -> 22%
where the time goes in v12:
time: 32.1 us; the launch traced here: 31.8 us
  starting transfers between devices  19.9 us (62%)
  Pallas kernels  9.5 us (30%)
  waiting for transfers between devices  1.69 us (5%)
  between operations  0.75 us (2%)
    ppermute x11, starting transfers between devices, swapped(): return lax.ppermute(cells, axis, pairs)  19.9 us
    pallas_call x14, Pallas kernels, call(): pl.pallas_call(kernel, out_shape=shapes, in_specs=in_specs, out_specs=out...  9.5 us
    ppermute x11, waiting for transfers between devices, swapped(): return lax.ppermute(cells, axis, pairs)  1.69 us
  transfers between devices with their start and end apart: 11, of which 3 were waited for; matrix products, arithmetic and copies ran while one was open for 0% of the time, Pallas kernels for 22%

profile of v12, /device:TPU:0, one launch (start us, length us, event | category | flops | bytes accessed | tf_op | source)
XLA Modules:
  0.0 31.8 jit_solution(5463079382407056393)
XLA Ops:
  0.6 1.1 %shard_map.77 = (f32[4,128,128]{2,1,0:T(8,128)S(1)}, f32[2,128,128]{2,1,0:T(8,128)S(1)}) custom-call(s32[1,1,5]{2,1,0:T(1,128)} %cutoff_hbm.5, f32[1,1,5,128,128]{4,3,2,1,0:T(8,128)} %ham_hbm.5, f32[1,1,5,128,128]{4,3,2,1,0:T(8,128)} %inv_hbm.5, f32[2,1,1,5,128,128]{5,4,3,2,1,0:T(8,128)} %rho_hbm.5), custom_call_target="tpu_custom_call" | custom-call | bytes 1703956 | tf_op jit(solution)/shard_map/pallas_call | solution.py:294
  1.7 3.0 %collective-permute-start.2 = (f32[4,128,128]{2,1,0:T(8,128)S(1)}, f32[4,128,128]{2,1,0:T(8,128)S(1)}, u32[]{:S(2)}, u32[]{:S(2)}) collective-permute-start(f32[4,128,128]{2,1,0:T(8,128)S(1)} %get-tuple-element.43.message), channel_id=1, source_target_pairs={{0,4},{4,0},{8,12},{12,8},{16,20},{20,16},{24,28},{28,24},{1,5},{5... | collective-permute-start | bytes 786440 | tf_op jit(solution)/shard_map/ppermute | solution.py:30
  4.8 0.7 %collective-permute-start.1 = (f32[4,128,128]{2,1,0:T(8,128)S(1)}, f32[4,128,128]{2,1,0:T(8,128)S(1)}, u32[]{:S(2)}, u32[]{:S(2)}) collective-permute-start(f32[4,128,128]{2,1,0:T(8,128)S(1)} %shard_map.78.message), channel_id=1, source_target_pairs={{1,2},{2,1},{3,0},{0,3},{5,6},{6,5},{7,4},{4,7},{9,10},{10,9},{11,... | collective-permute-start | bytes 786440 | tf_op jit(solution)/shard_map/ppermute | solution.py:30
  5.5 3.6 %collective-permute-start.3 = (f32[4,128,128]{2,1,0:T(8,128)S(1)}, f32[4,128,128]{2,1,0:T(8,128)S(1)}, u32[]{:S(2)}, u32[]{:S(2)}) collective-permute-start(f32[4,128,128]{2,1,0:T(8,128)S(1)} %shard_map.79.message), channel_id=1, source_target_pairs={{4,8},{8,4},{12,16},{16,12},{20,24},{24,20},{28,0},{0,28},{5,9},{9... | collective-permute-start | bytes 786440 | tf_op jit(solution)/shard_map/ppermute | solution.py:30
  9.1 1.0 %shard_map.80.after = f32[8,128,128]{2,1,0:T(8,128)S(1)} custom-call(s32[1,1,5]{2,1,0:T(1,128)} %cutoff_hbm.5, f32[1,1,5,128,128]{4,3,2,1,0:T(8,128)} %ham_hbm.5, f32[1,1,5,128,128]{4,3,2,1,0:T(8,128)} %inv_hbm.5, f32[2,1,1,5,128,128]{5,4,3,2,1,0:T(8,128)} %rho_hbm.5, f32[4,128,128]{2,1,0:T(8,128)S(1)} %shard_map.79.message), custom_call_target="tpu_custom_call" | custom-call | flops 6291456000 | bytes 2097172 | tf_op jit(solution)/shard_map/pallas_call | solution.py:294
  10.2 0.7 %collective-permute-start = (f32[8,128,128]{2,1,0:T(8,128)S(1)}, f32[8,128,128]{2,1,0:T(8,128)S(1)}, u32[]{:S(2)}, u32[]{:S(2)}) collective-permute-start(f32[8,128,128]{2,1,0:T(8,128)S(1)} %shard_map.80.after), channel_id=1, source_target_pairs={{0,1},{1,0},{2,3},{3,2},{4,5},{5,4},{6,7},{7,6},{8,9},{9,8},{10,11... | collective-permute-start | bytes 1572872 | tf_op jit(solution)/shard_map/ppermute | solution.py:30
  10.9 1.4 %shard_map.81 = (f32[3,5,128,128]{3,2,1,0:T(8,128)S(1)}, bf16[384,640]{1,0:T(8,128)(2,1)S(1)}, bf16[384,640]{1,0:T(8,128)(2,1)S(1)}, bf16[128,640]{1,0:T(8,128)(...) custom-call(s32[1,1,5]{2,1,0:T(1,128)} %cutoff_hbm.5, f32[1,1,5,128,128]{4,3,2,1,0:T(8,128)} %ham_hbm.5, ...), custom_call_target="tpu_custom_call" | custom-call | flops 25165824000 | bytes 5472788 | tf_op jit(solution)/shard_map/pallas_call | solution.py:294
  12.3 0.1 collective-permute-done.three
  12.4 1.2 %shard_map.82 = (f32[384,640]{1,0:T(8,128)S(1)}, f32[384,128]{1,0:T(8,128)S(1)}, f32[2,2,128,128]{3,2,1,0:T(8,128)S(1)}, f32[3,1,1,5,128,128]{5,4,3,2,1,0:T(8,128)S(1)}) custom-call(bf16[384,640]{1,0:T(8,128)(2,1)S(1)} %get-tuple-element.46.left_high, bf16[384,640]{1,0:T(8,128)(2,1)S(1)} %get-tuple-element.47.left_low, ...), custom_call_target="tpu_custom_call" | custom-call | flops 100663296000 | bytes 7536640 | tf_op jit(solution)/shard_map/pallas_call | solution.py:294
  13.7 0.0 collective-permute-done.1.four
  13.7 0.6 %shard_map.83 = (f32[4,128,128]{2,1,0:T(8,128)S(1)}, bf16[384,128]{1,0:T(8,128)(2,1)S(1)}, bf16[384,128]{1,0:T(8,128)(2,1)S(1)}, f32[384,128]{1,0:T(8,128)S(1)}, f32[2,128,128]{2,1,0:T(8,128)S(1)}) custom-call(bf16[384,640]{1,0:T(8,128)(2,1)S(1)} %get-tuple-element.46.left_high, bf16[384,640]{1,0:T(8,128)(2,1)S(1)} %get-tuple-element.47.left_low, ...), custom_call_target="tpu_custom_call" | custom-call | flops 100663296 | bytes 5373952 | tf_op jit(solution)/shard_map/pallas_call | solution.py:294
  14.4 0.6 %collective-permute-start.4 = (f32[4,128,128]{2,1,0:T(8,128)S(1)}, f32[4,128,128]{2,1,0:T(8,128)S(1)}, u32[]{:S(2)}, u32[]{:S(2)}) collective-permute-start(f32[4,128,128]{2,1,0:T(8,128)S(1)} %get-tuple-element.72), channel_id=1, source_target_pairs={{1,2},{2,1},{3,0},{0,3},{5,6},{6,5},{7,4},{4,7},{9,10},{10,9},{11,... | collective-permute-start | bytes 786440 | tf_op jit(solution)/shard_map/ppermute | solution.py:30
  14.9 0.4 %collective-permute-start.5 = (f32[4,128,128]{2,1,0:T(8,128)S(1)}, f32[4,128,128]{2,1,0:T(8,128)S(1)}, u32[]{:S(2)}, u32[]{:S(2)}) collective-permute-start(f32[4,128,128]{2,1,0:T(8,128)S(1)} %get-tuple-element.71.after), channel_id=1, source_target_pairs={{0,4},{4,0},{8,12},{12,8},{16,20},{20,16},{24,28},{28,24},{1,5},{5... | collective-permute-start | bytes 786440 | tf_op jit(solution)/shard_map/ppermute | solution.py:30
  15.4 4.6 %collective-permute-start.6 = (f32[4,128,128]{2,1,0:T(8,128)S(1)}, f32[4,128,128]{2,1,0:T(8,128)S(1)}, u32[]{:S(2)}, u32[]{:S(2)}) collective-permute-start(f32[4,128,128]{2,1,0:T(8,128)S(1)} %get-tuple-element.76), channel_id=1, source_target_pairs={{4,8},{8,4},{12,16},{16,12},{20,24},{24,20},{28,0},{0,28},{5,9},{9... | collective-permute-start | bytes 786440 | tf_op jit(solution)/shard_map/ppermute | solution.py:30
  19.9 0.0 collective-permute-done.2.one
  19.9 0.6 %shard_map.84 = (bf16[384,128]{1,0:T(8,128)(2,1)S(1)}, bf16[384,128]{1,0:T(8,128)(2,1)S(1)}, f32[384,128]{1,0:T(8,128)S(1)}, f32[2,128,128]{2,1,0:T(8,128)S(1)}) custom-call(bf16[384,640]{1,0:T(8,128)(2,1)S(1)} %get-tuple-element.46.left_high, bf16[384,640]{1,0:T(8,128)(2,1)S(1)} %get-tuple-element.47.left_low, f32[384,640]{1,0:T(8,128)S(1)} %get-tuple-element.52.start, ...), custom_call_target="tpu_custom_call" | custom-call | flops 125829120 | bytes 4128768 | tf_op jit(solution)/shard_map/pallas_call | solution.py:294
  20.6 0.0 collective-permute-done.3.two
  20.6 0.9 %shard_map.85 = (f32[4,128,128]{2,1,0:T(8,128)S(1)}, bf16[384,128]{1,0:T(8,128)(2,1)S(1)}, bf16[384,128]{1,0:T(8,128)(2,1)S(1)}, bf16[384,128]{1,0:T(8,128)(2,1)...) custom-call(bf16[384,640]{1,0:T(8,128)(2,1)S(1)} %get-tuple-element., ...), custom_call_target="tpu_custom_call" | custom-call | flops 276824064 | bytes 7280640 | tf_op jit(solution)/shard_map/pallas_call | solution.py:294
  21.5 1.1 %collective-permute-done.4.four.arrived = f32[4,128,128]{2,1,0:T(8,128)S(1)} collective-permute-done((f32[4,128,128]{2,1,0:T(8,128)S(1)}, f32[4,128,128]{2,1,0:T(8,128)S(1)}, u32[]{:S(2)}, u32[]{:S(2)}) %collective-permute-start.4) | collective-permute-done | bytes 262176 | tf_op jit(solution)/shard_map/ppermute | solution.py:30
  22.6 1.2 %collective-permute-start.9 = (f32[3,128]{1,0:T(4,128)S(1)}, f32[3,128]{1,0:T(4,128)S(1)}, u32[]{:S(2)}, u32[]{:S(2)}) collective-permute-start(f32[3,128]{1,0:T(4,128)S(1)} %shard_map.88), channel_id=1, source_target_pairs={{1,2},{2,1},{3,0},{0,3},{5,6},{6,5},{7,4},{4,7},{9,10},{10,9},{11,... | collective-permute-start | bytes 4616 | tf_op jit(solution)/shard_map/ppermute | solution.py:30
  23.7 0.5 %collective-permute-start.7 = (f32[3,128]{1,0:T(4,128)S(1)}, f32[3,128]{1,0:T(4,128)S(1)}, u32[]{:S(2)}, u32[]{:S(2)}) collective-permute-start(f32[3,128]{1,0:T(4,128)S(1)} %get-tuple-element.77), channel_id=1, source_target_pairs={{0,4},{4,0},{8,12},{12,8},{16,20},{20,16},{24,28},{28,24},{1,5},{5... | collective-permute-start | bytes 4616 | tf_op jit(solution)/shard_map/ppermute | solution.py:30
  24.3 4.6 %collective-permute-start.8 = (f32[3,128]{1,0:T(4,128)S(1)}, f32[3,128]{1,0:T(4,128)S(1)}, u32[]{:S(2)}, u32[]{:S(2)}) collective-permute-start(f32[3,128]{1,0:T(4,128)S(1)} %get-tuple-element.78), channel_id=1, source_target_pairs={{4,8},{8,4},{12,16},{16,12},{20,24},{24,20},{28,0},{0,28},{5,9},{9... | collective-permute-start | bytes 4616 | tf_op jit(solution)/shard_map/ppermute | solution.py:30
  28.8 0.0 collective-permute-done.9.arrived.c4
  28.8 0.0 collective-permute-start.10
  28.8 1.2 %shard_map.87 = (f32[2,1,1,5,128,128]{5,4,3,2,1,0:T(8,128)}, f32[3,128,128]{2,1,0:T(8,128)S(1)}, f32[128,128]{1,0:T(8,128)S(1)}, f32[3,128]{1,0:T(4,128)S(1)}) custom-call(f32[3,5,128,128]{3,2,1,0:T(8,128)S(1)} %get-tuple-element.45.held, f32[4,128,128]{2,1,0:T(8,128)S(1)} %get-tuple-element.63.new, bf16[384,640]{1,0:T(8,128)(2,1)S(1)} %get-tuple-element.46.left_high, ...), custom_call_target="tpu_custom_call" | custom-call | flops 125829120 | bytes 6030848 | tf_op jit(solution)/shard_map/pallas_call | solution.py:294
  30.1 0.0 collective-permute-done.7.c1
  30.1 0.5 %collective-permute-done.8.c2 = f32[3,128]{1,0:T(4,128)S(1)} collective-permute-done((f32[3,128]{1,0:T(4,128)S(1)}, f32[3,128]{1,0:T(4,128)S(1)}, u32[]{:S(2)}, u32[]{:S(2)}) %collective-permute-start.8) | collective-permute-done | bytes 1568 | tf_op jit(solution)/shard_map/ppermute | solution.py:30
  30.5 0.0 collective-permute-done.5.one
  30.5 0.0 collective-permute-done.6.two
  30.5 0.0 collective-permute-done.10.c3
  30.5 1.3 %shard_map.90 = (f32[2,1,1,5,128,128]{5,4,3,2,1,0:T(8,128)}, f32[3,1,64]{2,1,0:T(1,128)}) custom-call(f32[3,5,128,128]{3,2,1,0:T(8,128)S(1)} %get-tuple-element.45.held, f32[3,1,1,5,128,128]{5,4,3,2,1,0:T(8,128)S(1)} %get-tuple-element.50.der_ref, f32[64,128]{1,0:T(8,128)S(1)} %get-tuple-element.51.members, ...), custom_call_target="tpu_custom_call", output_to_operand_aliasing={{0}: (16, {})} | custom-call | flops 125829120 | bytes 4890880 | tf_op jit(solution)/shard_map/pallas_call | solution.py:294
  (5 shorter events, 0.1 us)
Async XLA Ops:
  1.7 18.2 %collective-permute-start.2 = (f32[4,128,128]{2,1,0:T(8,128)S(1)}, f32[4,128,128]{2,1,0:T(8,128)S(1)}, u32[]{:S(2)}, u32[]{:S(2)}) collective-permute-start(f32[4,128,128]{2,1,0:T(8,128)S(1)} %get-tuple-element.43.message), channel_id=1, source_target_pairs={{0,4},{4,0},{8,12},{12,8},{16,20},{20,16},{24,28},{28,24},{1,5},{5... | collective-permute-start | bytes 786440 | tf_op jit(solution)/shard_map/ppermute | solution.py:30
  4.8 8.9 %collective-permute-start.1 = (f32[4,128,128]{2,1,0:T(8,128)S(1)}, f32[4,128,128]{2,1,0:T(8,128)S(1)}, u32[]{:S(2)}, u32[]{:S(2)}) collective-permute-start(f32[4,128,128]{2,1,0:T(8,128)S(1)} %shard_map.78.message), channel_id=1, source_target_pairs={{1,2},{2,1},{3,0},{0,3},{5,6},{6,5},{7,4},{4,7},{9,10},{10,9},{11,... | collective-permute-start | bytes 786440 | tf_op jit(solution)/shard_map/ppermute | solution.py:30
  5.5 15.0 %collective-permute-start.3 = (f32[4,128,128]{2,1,0:T(8,128)S(1)}, f32[4,128,128]{2,1,0:T(8,128)S(1)}, u32[]{:S(2)}, u32[]{:S(2)}) collective-permute-start(f32[4,128,128]{2,1,0:T(8,128)S(1)} %shard_map.79.message), channel_id=1, source_target_pairs={{4,8},{8,4},{12,16},{16,12},{20,24},{24,20},{28,0},{0,28},{5,9},{9... | collective-permute-start | bytes 786440 | tf_op jit(solution)/shard_map/ppermute | solution.py:30
  10.2 2.3 %collective-permute-start = (f32[8,128,128]{2,1,0:T(8,128)S(1)}, f32[8,128,128]{2,1,0:T(8,128)S(1)}, u32[]{:S(2)}, u32[]{:S(2)}) collective-permute-start(f32[8,128,128]{2,1,0:T(8,128)S(1)} %shard_map.80.after), channel_id=1, source_target_pairs={{0,1},{1,0},{2,3},{3,2},{4,5},{5,4},{6,7},{7,6},{8,9},{9,8},{10,11... | collective-permute-start | bytes 1572872 | tf_op jit(solution)/shard_map/ppermute | solution.py:30
  14.4 8.2 %collective-permute-start.4 = (f32[4,128,128]{2,1,0:T(8,128)S(1)}, f32[4,128,128]{2,1,0:T(8,128)S(1)}, u32[]{:S(2)}, u32[]{:S(2)}) collective-permute-start(f32[4,128,128]{2,1,0:T(8,128)S(1)} %get-tuple-element.72), channel_id=1, source_target_pairs={{1,2},{2,1},{3,0},{0,3},{5,6},{6,5},{7,4},{4,7},{9,10},{10,9},{11,... | collective-permute-start | bytes 786440 | tf_op jit(solution)/shard_map/ppermute | solution.py:30
  14.9 15.6 %collective-permute-start.5 = (f32[4,128,128]{2,1,0:T(8,128)S(1)}, f32[4,128,128]{2,1,0:T(8,128)S(1)}, u32[]{:S(2)}, u32[]{:S(2)}) collective-permute-start(f32[4,128,128]{2,1,0:T(8,128)S(1)} %get-tuple-element.71.after), channel_id=1, source_target_pairs={{0,4},{4,0},{8,12},{12,8},{16,20},{20,16},{24,28},{28,24},{1,5},{5... | collective-permute-start | bytes 786440 | tf_op jit(solution)/shard_map/ppermute | solution.py:30
  15.4 15.2 %collective-permute-start.6 = (f32[4,128,128]{2,1,0:T(8,128)S(1)}, f32[4,128,128]{2,1,0:T(8,128)S(1)}, u32[]{:S(2)}, u32[]{:S(2)}) collective-permute-start(f32[4,128,128]{2,1,0:T(8,128)S(1)} %get-tuple-element.76), channel_id=1, source_target_pairs={{4,8},{8,4},{12,16},{16,12},{20,24},{24,20},{28,0},{0,28},{5,9},{9... | collective-permute-start | bytes 786440 | tf_op jit(solution)/shard_map/ppermute | solution.py:30
  22.6 6.2 %collective-permute-start.9 = (f32[3,128]{1,0:T(4,128)S(1)}, f32[3,128]{1,0:T(4,128)S(1)}, u32[]{:S(2)}, u32[]{:S(2)}) collective-permute-start(f32[3,128]{1,0:T(4,128)S(1)} %shard_map.88), channel_id=1, source_target_pairs={{1,2},{2,1},{3,0},{0,3},{5,6},{6,5},{7,4},{4,7},{9,10},{10,9},{11,... | collective-permute-start | bytes 4616 | tf_op jit(solution)/shard_map/ppermute | solution.py:30
  23.7 6.3 %collective-permute-start.7 = (f32[3,128]{1,0:T(4,128)S(1)}, f32[3,128]{1,0:T(4,128)S(1)}, u32[]{:S(2)}, u32[]{:S(2)}) collective-permute-start(f32[3,128]{1,0:T(4,128)S(1)} %get-tuple-element.77), channel_id=1, source_target_pairs={{0,4},{4,0},{8,12},{12,8},{16,20},{20,16},{24,28},{28,24},{1,5},{5... | collective-permute-start | bytes 4616 | tf_op jit(solution)/shard_map/ppermute | solution.py:30
  24.3 6.3 %collective-permute-start.8 = (f32[3,128]{1,0:T(4,128)S(1)}, f32[3,128]{1,0:T(4,128)S(1)}, u32[]{:S(2)}, u32[]{:S(2)}) collective-permute-start(f32[3,128]{1,0:T(4,128)S(1)} %get-tuple-element.78), channel_id=1, source_target_pairs={{4,8},{8,4},{12,16},{16,12},{20,24},{24,20},{28,0},{0,28},{5,9},{9... | collective-permute-start | bytes 4616 | tf_op jit(solution)/shard_map/ppermute | solution.py:30
  28.8 1.7 %collective-permute-start.10 = (f32[3,128]{1,0:T(4,128)S(1)}, f32[3,128]{1,0:T(4,128)S(1)}, u32[]{:S(2)}, u32[]{:S(2)}) collective-permute-start(f32[3,128]{1,0:T(4,128)S(1)} %shard_map.89), channel_id=1, source_target_pairs={{0,1},{1,0},{2,3},{3,2},{4,5},{5,4},{6,7},{7,6},{8,9},{9,8},{10,11... | collective-permute-start | bytes 4616 | tf_op jit(solution)/shard_map/ppermute | solution.py:30

commit v13 on v12

--- a/solution.py
+++ b/solution.py
@@ -222,7 +222,7 @@
         weighted[direction] = sums[direction]
 
 
-def pass_kernel(arrived, column, out):
+def later_kernel(arrived, column, out):
     out[...] = column[...]
 
 
@@ -383,10 +383,8 @@
     )
     c1, c2, c3, c4 = columns
     c1, c2 = swapped(c1, 1), swapped(c2, 2)
-    (c4,) = call(pass_kernel, [shape(3, B)], [vmem] * 2, 0, (near_four_more, c4))
-    c4 = swapped(c4, 4)
-    (c3,) = call(pass_kernel, [shape(3, B)], [vmem] * 2, 0, (c4, c3))
-    columns = (c1, c2, swapped(c3, 3), c4)
+    (c3,) = call(later_kernel, [shape(3, B)], [vmem] * 2, 0, (near_four_more, c3))
+    columns = (c1, c2, swapped(c3, 3), swapped(c4, 4))
     args = (held, new, left_high, left_low, self_high, self_low, other_one, real_two, other_three, other_four, weighted)
     args += (imag_part, high_four, low_four, near_four_more)
     out, comm, imag_part, row_part = call(

time: 32.1 us -> 32.4 us (level)
  waiting for transfers between devices: 1.69 us -> 5.86 us
  starting transfers between devices: 19.9 us -> 15.9 us
    ppermute x11, waiting for transfers between devices: 1.69 us -> 5.86 us  [swapped(): return lax.ppermute(cells, axis, pairs)]
    ppermute x11, starting transfers between devices: 19.9 us -> 15.9 us  [swapped(): return lax.ppermute(cells, axis, pairs)]
    pallas_call x14 -> x13, Pallas kernels: 9.5 us -> 9.47 us  [call(): pl.pallas_call(kernel, out_shape=shapes, in_specs=in_specs, out_specs=out...]
  transfers between devices with their start and end apart: 11 -> 11, of which waited for: 3 -> 2; matrix products, arithmetic and copies ran while one was open for 0% -> 0% of each run, Pallas kernels for 22% -> 22%
where the time goes in v13:
time: 32.4 us; the launch traced here: 32 us
  starting transfers between devices  15.9 us (49%)
  Pallas kernels  9.47 us (29%)
  waiting for transfers between devices  5.86 us (18%)
  between operations  0.78 us (2%)
    ppermute x11, starting transfers between devices, swapped(): return lax.ppermute(cells, axis, pairs)  15.9 us
    pallas_call x13, Pallas kernels, call(): pl.pallas_call(kernel, out_shape=shapes, in_specs=in_specs, out_specs=out...  9.47 us
    ppermute x11, waiting for transfers between devices, swapped(): return lax.ppermute(cells, axis, pairs)  5.86 us
  transfers between devices with their start and end apart: 11, of which 2 were waited for; matrix products, arithmetic and copies ran while one was open for 0% of the time, Pallas kernels for 22%

profile of v13, /device:TPU:0, one launch (start us, length us, event | category | flops | bytes accessed | tf_op | source)
XLA Modules:
  0.0 32.0 jit_solution(18096500094891996004)
XLA Ops:
  0.6 1.1 %shard_map.77 = (f32[4,128,128]{2,1,0:T(8,128)S(1)}, f32[2,128,128]{2,1,0:T(8,128)S(1)}) custom-call(s32[1,1,5]{2,1,0:T(1,128)} %cutoff_hbm.5, f32[1,1,5,128,128]{4,3,2,1,0:T(8,128)} %ham_hbm.5, f32[1,1,5,128,128]{4,3,2,1,0:T(8,128)} %inv_hbm.5, f32[2,1,1,5,128,128]{5,4,3,2,1,0:T(8,128)} %rho_hbm.5), custom_call_target="tpu_custom_call" | custom-call | bytes 1703956 | tf_op jit(solution)/shard_map/pallas_call | solution.py:294
  1.7 3.0 %collective-permute-start.2 = (f32[4,128,128]{2,1,0:T(8,128)S(1)}, f32[4,128,128]{2,1,0:T(8,128)S(1)}, u32[]{:S(2)}, u32[]{:S(2)}) collective-permute-start(f32[4,128,128]{2,1,0:T(8,128)S(1)} %get-tuple-element.43.message), channel_id=1, source_target_pairs={{0,4},{4,0},{8,12},{12,8},{16,20},{20,16},{24,28},{28,24},{1,5},{5... | collective-permute-start | bytes 786440 | tf_op jit(solution)/shard_map/ppermute | solution.py:30
  4.8 0.7 %collective-permute-start.1 = (f32[4,128,128]{2,1,0:T(8,128)S(1)}, f32[4,128,128]{2,1,0:T(8,128)S(1)}, u32[]{:S(2)}, u32[]{:S(2)}) collective-permute-start(f32[4,128,128]{2,1,0:T(8,128)S(1)} %shard_map.78.message), channel_id=1, source_target_pairs={{1,2},{2,1},{3,0},{0,3},{5,6},{6,5},{7,4},{4,7},{9,10},{10,9},{11,... | collective-permute-start | bytes 786440 | tf_op jit(solution)/shard_map/ppermute | solution.py:30
  5.5 3.6 %collective-permute-start.3 = (f32[4,128,128]{2,1,0:T(8,128)S(1)}, f32[4,128,128]{2,1,0:T(8,128)S(1)}, u32[]{:S(2)}, u32[]{:S(2)}) collective-permute-start(f32[4,128,128]{2,1,0:T(8,128)S(1)} %shard_map.79.message), channel_id=1, source_target_pairs={{4,8},{8,4},{12,16},{16,12},{20,24},{24,20},{28,0},{0,28},{5,9},{9... | collective-permute-start | bytes 786440 | tf_op jit(solution)/shard_map/ppermute | solution.py:30
  9.1 1.0 %shard_map.80.after = f32[8,128,128]{2,1,0:T(8,128)S(1)} custom-call(s32[1,1,5]{2,1,0:T(1,128)} %cutoff_hbm.5, f32[1,1,5,128,128]{4,3,2,1,0:T(8,128)} %ham_hbm.5, f32[1,1,5,128,128]{4,3,2,1,0:T(8,128)} %inv_hbm.5, f32[2,1,1,5,128,128]{5,4,3,2,1,0:T(8,128)} %rho_hbm.5, f32[4,128,128]{2,1,0:T(8,128)S(1)} %shard_map.79.message), custom_call_target="tpu_custom_call" | custom-call | flops 6291456000 | bytes 2097172 | tf_op jit(solution)/shard_map/pallas_call | solution.py:294
  10.2 0.7 %collective-permute-start = (f32[8,128,128]{2,1,0:T(8,128)S(1)}, f32[8,128,128]{2,1,0:T(8,128)S(1)}, u32[]{:S(2)}, u32[]{:S(2)}) collective-permute-start(f32[8,128,128]{2,1,0:T(8,128)S(1)} %shard_map.80.after), channel_id=1, source_target_pairs={{0,1},{1,0},{2,3},{3,2},{4,5},{5,4},{6,7},{7,6},{8,9},{9,8},{10,11... | collective-permute-start | bytes 1572872 | tf_op jit(solution)/shard_map/ppermute | solution.py:30
  10.9 1.4 %shard_map.81 = (f32[3,5,128,128]{3,2,1,0:T(8,128)S(1)}, bf16[384,640]{1,0:T(8,128)(2,1)S(1)}, bf16[384,640]{1,0:T(8,128)(2,1)S(1)}, bf16[128,640]{1,0:T(8,128)(...) custom-call(s32[1,1,5]{2,1,0:T(1,128)} %cutoff_hbm.5, f32[1,1,5,128,128]{4,3,2,1,0:T(8,128)} %ham_hbm.5, ...), custom_call_target="tpu_custom_call" | custom-call | flops 25165824000 | bytes 5472788 | tf_op jit(solution)/shard_map/pallas_call | solution.py:294
  12.3 0.1 collective-permute-done.three
  12.4 1.2 %shard_map.82 = (f32[384,640]{1,0:T(8,128)S(1)}, f32[384,128]{1,0:T(8,128)S(1)}, f32[2,2,128,128]{3,2,1,0:T(8,128)S(1)}, f32[3,1,1,5,128,128]{5,4,3,2,1,0:T(8,128)S(1)}) custom-call(bf16[384,640]{1,0:T(8,128)(2,1)S(1)} %get-tuple-element.46.left_high, bf16[384,640]{1,0:T(8,128)(2,1)S(1)} %get-tuple-element.47.left_low, ...), custom_call_target="tpu_custom_call" | custom-call | flops 100663296000 | bytes 7536640 | tf_op jit(solution)/shard_map/pallas_call | solution.py:294
  13.7 0.0 collective-permute-done.1.four
  13.7 0.6 %shard_map.83 = (f32[4,128,128]{2,1,0:T(8,128)S(1)}, bf16[384,128]{1,0:T(8,128)(2,1)S(1)}, bf16[384,128]{1,0:T(8,128)(2,1)S(1)}, f32[384,128]{1,0:T(8,128)S(1)}, f32[2,128,128]{2,1,0:T(8,128)S(1)}) custom-call(bf16[384,640]{1,0:T(8,128)(2,1)S(1)} %get-tuple-element.46.left_high, bf16[384,640]{1,0:T(8,128)(2,1)S(1)} %get-tuple-element.47.left_low, ...), custom_call_target="tpu_custom_call" | custom-call | flops 100663296 | bytes 5373952 | tf_op jit(solution)/shard_map/pallas_call | solution.py:294
  14.4 0.6 %collective-permute-start.4 = (f32[4,128,128]{2,1,0:T(8,128)S(1)}, f32[4,128,128]{2,1,0:T(8,128)S(1)}, u32[]{:S(2)}, u32[]{:S(2)}) collective-permute-start(f32[4,128,128]{2,1,0:T(8,128)S(1)} %get-tuple-element.72), channel_id=1, source_target_pairs={{1,2},{2,1},{3,0},{0,3},{5,6},{6,5},{7,4},{4,7},{9,10},{10,9},{11,... | collective-permute-start | bytes 786440 | tf_op jit(solution)/shard_map/ppermute | solution.py:30
  14.9 0.4 %collective-permute-start.5 = (f32[4,128,128]{2,1,0:T(8,128)S(1)}, f32[4,128,128]{2,1,0:T(8,128)S(1)}, u32[]{:S(2)}, u32[]{:S(2)}) collective-permute-start(f32[4,128,128]{2,1,0:T(8,128)S(1)} %get-tuple-element.71.after), channel_id=1, source_target_pairs={{0,4},{4,0},{8,12},{12,8},{16,20},{20,16},{24,28},{28,24},{1,5},{5... | collective-permute-start | bytes 786440 | tf_op jit(solution)/shard_map/ppermute | solution.py:30
  15.4 4.6 %collective-permute-start.6 = (f32[4,128,128]{2,1,0:T(8,128)S(1)}, f32[4,128,128]{2,1,0:T(8,128)S(1)}, u32[]{:S(2)}, u32[]{:S(2)}) collective-permute-start(f32[4,128,128]{2,1,0:T(8,128)S(1)} %get-tuple-element.76), channel_id=1, source_target_pairs={{4,8},{8,4},{12,16},{16,12},{20,24},{24,20},{28,0},{0,28},{5,9},{9... | collective-permute-start | bytes 786440 | tf_op jit(solution)/shard_map/ppermute | solution.py:30
  19.9 0.0 collective-permute-done.2.one
  19.9 0.6 %shard_map.84 = (bf16[384,128]{1,0:T(8,128)(2,1)S(1)}, bf16[384,128]{1,0:T(8,128)(2,1)S(1)}, f32[384,128]{1,0:T(8,128)S(1)}, f32[2,128,128]{2,1,0:T(8,128)S(1)}) custom-call(bf16[384,640]{1,0:T(8,128)(2,1)S(1)} %get-tuple-element.46.left_high, bf16[384,640]{1,0:T(8,128)(2,1)S(1)} %get-tuple-element.47.left_low, f32[384,640]{1,0:T(8,128)S(1)} %get-tuple-element.52.start, ...), custom_call_target="tpu_custom_call" | custom-call | flops 125829120 | bytes 4128768 | tf_op jit(solution)/shard_map/pallas_call | solution.py:294
  20.6 0.0 collective-permute-done.3.two
  20.6 0.9 %shard_map.85 = (f32[4,128,128]{2,1,0:T(8,128)S(1)}, bf16[384,128]{1,0:T(8,128)(2,1)S(1)}, bf16[384,128]{1,0:T(8,128)(2,1)S(1)}, bf16[384,128]{1,0:T(8,128)(2,1)...) custom-call(bf16[384,640]{1,0:T(8,128)(2,1)S(1)} %get-tuple-element., ...), custom_call_target="tpu_custom_call" | custom-call | flops 276824064 | bytes 7280640 | tf_op jit(solution)/shard_map/pallas_call | solution.py:294
  21.5 0.1 collective-permute-start.7
  21.6 2.0 %collective-permute-start.8 = (f32[3,128]{1,0:T(4,128)S(1)}, f32[3,128]{1,0:T(4,128)S(1)}, u32[]{:S(2)}, u32[]{:S(2)}) collective-permute-start(f32[3,128]{1,0:T(4,128)S(1)} %get-tuple-element.78), channel_id=1, source_target_pairs={{4,8},{8,4},{12,16},{16,12},{20,24},{24,20},{28,0},{0,28},{5,9},{9... | collective-permute-start | bytes 4616 | tf_op jit(solution)/shard_map/ppermute | solution.py:30
  23.6 0.0 collective-permute-done.4.four.arrived
  23.6 0.1 collective-permute-start.10
  23.7 5.7 %collective-permute-done.7.c1 = f32[3,128]{1,0:T(4,128)S(1)} collective-permute-done((f32[3,128]{1,0:T(4,128)S(1)}, f32[3,128]{1,0:T(4,128)S(1)}, u32[]{:S(2)}, u32[]{:S(2)}) %collective-permute-start.7) | collective-permute-done | bytes 1568 | tf_op jit(solution)/shard_map/ppermute | solution.py:30
  29.4 0.0 collective-permute-start.9
  29.4 1.2 %shard_map.87 = (f32[2,1,1,5,128,128]{5,4,3,2,1,0:T(8,128)}, f32[3,128,128]{2,1,0:T(8,128)S(1)}, f32[128,128]{1,0:T(8,128)S(1)}, f32[3,128]{1,0:T(4,128)S(1)}) custom-call(f32[3,5,128,128]{3,2,1,0:T(8,128)S(1)} %get-tuple-element.45.held, f32[4,128,128]{2,1,0:T(8,128)S(1)} %get-tuple-element.63.new, bf16[384,640]{1,0:T(8,128)(2,1)S(1)} %get-tuple-element.46.left_high, ...), custom_call_target="tpu_custom_call" | custom-call | flops 125829120 | bytes 6030848 | tf_op jit(solution)/shard_map/pallas_call | solution.py:294
  30.6 0.0 collective-permute-done.8.c2
  30.7 0.0 collective-permute-done.10.c4
  30.7 0.0 collective-permute-done.5.one
  30.7 0.0 collective-permute-done.6.two
  30.7 0.0 collective-permute-done.9.c3
  30.7 1.3 %shard_map.89 = (f32[2,1,1,5,128,128]{5,4,3,2,1,0:T(8,128)}, f32[3,1,64]{2,1,0:T(1,128)}) custom-call(f32[3,5,128,128]{3,2,1,0:T(8,128)S(1)} %get-tuple-element.45.held, f32[3,1,1,5,128,128]{5,4,3,2,1,0:T(8,128)S(1)} %get-tuple-element.50.der_ref, f32[64,128]{1,0:T(8,128)S(1)} %get-tuple-element.51.members, ...), custom_call_target="tpu_custom_call", output_to_operand_aliasing={{0}: (16, {})} | custom-call | flops 125829120 | bytes 4890880 | tf_op jit(solution)/shard_map/pallas_call | solution.py:294
  (4 shorter events, 0.1 us)
Async XLA Ops:
  1.7 18.2 %collective-permute-start.2 = (f32[4,128,128]{2,1,0:T(8,128)S(1)}, f32[4,128,128]{2,1,0:T(8,128)S(1)}, u32[]{:S(2)}, u32[]{:S(2)}) collective-permute-start(f32[4,128,128]{2,1,0:T(8,128)S(1)} %get-tuple-element.43.message), channel_id=1, source_target_pairs={{0,4},{4,0},{8,12},{12,8},{16,20},{20,16},{24,28},{28,24},{1,5},{5... | collective-permute-start | bytes 786440 | tf_op jit(solution)/shard_map/ppermute | solution.py:30
  4.8 8.9 %collective-permute-start.1 = (f32[4,128,128]{2,1,0:T(8,128)S(1)}, f32[4,128,128]{2,1,0:T(8,128)S(1)}, u32[]{:S(2)}, u32[]{:S(2)}) collective-permute-start(f32[4,128,128]{2,1,0:T(8,128)S(1)} %shard_map.78.message), channel_id=1, source_target_pairs={{1,2},{2,1},{3,0},{0,3},{5,6},{6,5},{7,4},{4,7},{9,10},{10,9},{11,... | collective-permute-start | bytes 786440 | tf_op jit(solution)/shard_map/ppermute | solution.py:30
  5.5 15.0 %collective-permute-start.3 = (f32[4,128,128]{2,1,0:T(8,128)S(1)}, f32[4,128,128]{2,1,0:T(8,128)S(1)}, u32[]{:S(2)}, u32[]{:S(2)}) collective-permute-start(f32[4,128,128]{2,1,0:T(8,128)S(1)} %shard_map.79.message), channel_id=1, source_target_pairs={{4,8},{8,4},{12,16},{16,12},{20,24},{24,20},{28,0},{0,28},{5,9},{9... | collective-permute-start | bytes 786440 | tf_op jit(solution)/shard_map/ppermute | solution.py:30
  10.2 2.3 %collective-permute-start = (f32[8,128,128]{2,1,0:T(8,128)S(1)}, f32[8,128,128]{2,1,0:T(8,128)S(1)}, u32[]{:S(2)}, u32[]{:S(2)}) collective-permute-start(f32[8,128,128]{2,1,0:T(8,128)S(1)} %shard_map.80.after), channel_id=1, source_target_pairs={{0,1},{1,0},{2,3},{3,2},{4,5},{5,4},{6,7},{7,6},{8,9},{9,8},{10,11... | collective-permute-start | bytes 1572872 | tf_op jit(solution)/shard_map/ppermute | solution.py:30
  14.4 9.2 %collective-permute-start.4 = (f32[4,128,128]{2,1,0:T(8,128)S(1)}, f32[4,128,128]{2,1,0:T(8,128)S(1)}, u32[]{:S(2)}, u32[]{:S(2)}) collective-permute-start(f32[4,128,128]{2,1,0:T(8,128)S(1)} %get-tuple-element.72), channel_id=1, source_target_pairs={{1,2},{2,1},{3,0},{0,3},{5,6},{6,5},{7,4},{4,7},{9,10},{10,9},{11,... | collective-permute-start | bytes 786440 | tf_op jit(solution)/shard_map/ppermute | solution.py:30
  14.9 15.7 %collective-permute-start.5 = (f32[4,128,128]{2,1,0:T(8,128)S(1)}, f32[4,128,128]{2,1,0:T(8,128)S(1)}, u32[]{:S(2)}, u32[]{:S(2)}) collective-permute-start(f32[4,128,128]{2,1,0:T(8,128)S(1)} %get-tuple-element.71.after), channel_id=1, source_target_pairs={{0,4},{4,0},{8,12},{12,8},{16,20},{20,16},{24,28},{28,24},{1,5},{5... | collective-permute-start | bytes 786440 | tf_op jit(solution)/shard_map/ppermute | solution.py:30
  15.4 15.3 %collective-permute-start.6 = (f32[4,128,128]{2,1,0:T(8,128)S(1)}, f32[4,128,128]{2,1,0:T(8,128)S(1)}, u32[]{:S(2)}, u32[]{:S(2)}) collective-permute-start(f32[4,128,128]{2,1,0:T(8,128)S(1)} %get-tuple-element.76), channel_id=1, source_target_pairs={{4,8},{8,4},{12,16},{16,12},{20,24},{24,20},{28,0},{0,28},{5,9},{9... | collective-permute-start | bytes 786440 | tf_op jit(solution)/shard_map/ppermute | solution.py:30
  21.5 7.9 %collective-permute-start.7 = (f32[3,128]{1,0:T(4,128)S(1)}, f32[3,128]{1,0:T(4,128)S(1)}, u32[]{:S(2)}, u32[]{:S(2)}) collective-permute-start(f32[3,128]{1,0:T(4,128)S(1)} %get-tuple-element.77), channel_id=1, source_target_pairs={{0,4},{4,0},{8,12},{12,8},{16,20},{20,16},{24,28},{28,24},{1,5},{5... | collective-permute-start | bytes 4616 | tf_op jit(solution)/shard_map/ppermute | solution.py:30
  21.6 9.1 %collective-permute-start.8 = (f32[3,128]{1,0:T(4,128)S(1)}, f32[3,128]{1,0:T(4,128)S(1)}, u32[]{:S(2)}, u32[]{:S(2)}) collective-permute-start(f32[3,128]{1,0:T(4,128)S(1)} %get-tuple-element.78), channel_id=1, source_target_pairs={{4,8},{8,4},{12,16},{16,12},{20,24},{24,20},{28,0},{0,28},{5,9},{9... | collective-permute-start | bytes 4616 | tf_op jit(solution)/shard_map/ppermute | solution.py:30
  23.6 7.1 %collective-permute-start.10 = (f32[3,128]{1,0:T(4,128)S(1)}, f32[3,128]{1,0:T(4,128)S(1)}, u32[]{:S(2)}, u32[]{:S(2)}) collective-permute-start(f32[3,128]{1,0:T(4,128)S(1)} %get-tuple-element.80), channel_id=1, source_target_pairs={{1,2},{2,1},{3,0},{0,3},{5,6},{6,5},{7,4},{4,7},{9,10},{10,9},{11,... | collective-permute-start | bytes 4616 | tf_op jit(solution)/shard_map/ppermute | solution.py:30
  29.4 1.3 %collective-permute-start.9 = (f32[3,128]{1,0:T(4,128)S(1)}, f32[3,128]{1,0:T(4,128)S(1)}, u32[]{:S(2)}, u32[]{:S(2)}) collective-permute-start(f32[3,128]{1,0:T(4,128)S(1)} %shard_map.88), channel_id=1, source_target_pairs={{0,1},{1,0},{2,3},{3,2},{4,5},{5,4},{6,7},{7,6},{8,9},{9,8},{10,11... | collective-permute-start | bytes 4616 | tf_op jit(solution)/shard_map/ppermute | solution.py:30

commit v14 on v13

--- a/solution.py
+++ b/solution.py
@@ -382,9 +382,9 @@
         (left_high, left_low, start, diagonal, held, derivative, other_one, other_three, other_four, near_two),
     )
     c1, c2, c3, c4 = columns
-    c1, c2 = swapped(c1, 1), swapped(c2, 2)
-    (c3,) = call(later_kernel, [shape(3, B)], [vmem] * 2, 0, (near_four_more, c3))
-    columns = (c1, c2, swapped(c3, 3), swapped(c4, 4))
+    c1, c2, c3 = swapped(c1, 1), swapped(c2, 2), swapped(c3, 3)
+    (c4,) = call(later_kernel, [shape(3, B)], [vmem] * 2, 0, (c3, c4))
+    columns = (c1, c2, c3, swapped(c4, 4))
     args = (held, new, left_high, left_low, self_high, self_low, other_one, real_two, other_three, other_four, weighted)
     args += (imag_part, high_four, low_four, near_four_more)
     out, comm, imag_part, row_part = call(

time: 32.4 us -> 31.1 us (0.960)
  waiting for transfers between devices: 5.86 us -> 3.75 us
  starting transfers between devices: 15.9 us -> 16.8 us
    ppermute x11, waiting for transfers between devices: 5.86 us -> 3.75 us  [swapped(): return lax.ppermute(cells, axis, pairs)]
    ppermute x11, starting transfers between devices: 15.9 us -> 16.8 us  [swapped(): return lax.ppermute(cells, axis, pairs)]
  transfers between devices with their start and end apart: 11 -> 11, of which waited for: 2 -> 3; matrix products, arithmetic and copies ran while one was open for 0% -> 0% of each run, Pallas kernels for 22% -> 23%
where the time goes in v14:
time: 31.1 us; the launch traced here: 30.8 us
  starting transfers between devices  16.8 us (54%)
  Pallas kernels  9.48 us (30%)
  waiting for transfers between devices  3.75 us (12%)
  between operations  0.75 us (2%)
    ppermute x11, starting transfers between devices, swapped(): return lax.ppermute(cells, axis, pairs)  16.8 us
    pallas_call x13, Pallas kernels, call(): pl.pallas_call(kernel, out_shape=shapes, in_specs=in_specs, out_specs=out...  9.48 us
    ppermute x11, waiting for transfers between devices, swapped(): return lax.ppermute(cells, axis, pairs)  3.75 us
  transfers between devices with their start and end apart: 11, of which 3 were waited for; matrix products, arithmetic and copies ran while one was open for 0% of the time, Pallas kernels for 23%

profile of v14, /device:TPU:0, one launch (start us, length us, event | category | flops | bytes accessed | tf_op | source)
XLA Modules:
  0.0 30.8 jit_solution(2571157777904431473)
XLA Ops:
  0.6 1.1 %shard_map.77 = (f32[4,128,128]{2,1,0:T(8,128)S(1)}, f32[2,128,128]{2,1,0:T(8,128)S(1)}) custom-call(s32[1,1,5]{2,1,0:T(1,128)} %cutoff_hbm.5, f32[1,1,5,128,128]{4,3,2,1,0:T(8,128)} %ham_hbm.5, f32[1,1,5,128,128]{4,3,2,1,0:T(8,128)} %inv_hbm.5, f32[2,1,1,5,128,128]{5,4,3,2,1,0:T(8,128)} %rho_hbm.5), custom_call_target="tpu_custom_call" | custom-call | bytes 1703956 | tf_op jit(solution)/shard_map/pallas_call | solution.py:294
  1.7 3.0 %collective-permute-start.2 = (f32[4,128,128]{2,1,0:T(8,128)S(1)}, f32[4,128,128]{2,1,0:T(8,128)S(1)}, u32[]{:S(2)}, u32[]{:S(2)}) collective-permute-start(f32[4,128,128]{2,1,0:T(8,128)S(1)} %get-tuple-element.43.message), channel_id=1, source_target_pairs={{0,4},{4,0},{8,12},{12,8},{16,20},{20,16},{24,28},{28,24},{1,5},{5... | collective-permute-start | bytes 786440 | tf_op jit(solution)/shard_map/ppermute | solution.py:30
  4.8 0.7 %collective-permute-start.1 = (f32[4,128,128]{2,1,0:T(8,128)S(1)}, f32[4,128,128]{2,1,0:T(8,128)S(1)}, u32[]{:S(2)}, u32[]{:S(2)}) collective-permute-start(f32[4,128,128]{2,1,0:T(8,128)S(1)} %shard_map.78.message), channel_id=1, source_target_pairs={{1,2},{2,1},{3,0},{0,3},{5,6},{6,5},{7,4},{4,7},{9,10},{10,9},{11,... | collective-permute-start | bytes 786440 | tf_op jit(solution)/shard_map/ppermute | solution.py:30
  5.5 3.6 %collective-permute-start.3 = (f32[4,128,128]{2,1,0:T(8,128)S(1)}, f32[4,128,128]{2,1,0:T(8,128)S(1)}, u32[]{:S(2)}, u32[]{:S(2)}) collective-permute-start(f32[4,128,128]{2,1,0:T(8,128)S(1)} %shard_map.79.message), channel_id=1, source_target_pairs={{4,8},{8,4},{12,16},{16,12},{20,24},{24,20},{28,0},{0,28},{5,9},{9... | collective-permute-start | bytes 786440 | tf_op jit(solution)/shard_map/ppermute | solution.py:30
  9.1 1.0 %shard_map.80.after = f32[8,128,128]{2,1,0:T(8,128)S(1)} custom-call(s32[1,1,5]{2,1,0:T(1,128)} %cutoff_hbm.5, f32[1,1,5,128,128]{4,3,2,1,0:T(8,128)} %ham_hbm.5, f32[1,1,5,128,128]{4,3,2,1,0:T(8,128)} %inv_hbm.5, f32[2,1,1,5,128,128]{5,4,3,2,1,0:T(8,128)} %rho_hbm.5, f32[4,128,128]{2,1,0:T(8,128)S(1)} %shard_map.79.message), custom_call_target="tpu_custom_call" | custom-call | flops 6291456000 | bytes 2097172 | tf_op jit(solution)/shard_map/pallas_call | solution.py:294
  10.2 0.7 %collective-permute-start = (f32[8,128,128]{2,1,0:T(8,128)S(1)}, f32[8,128,128]{2,1,0:T(8,128)S(1)}, u32[]{:S(2)}, u32[]{:S(2)}) collective-permute-start(f32[8,128,128]{2,1,0:T(8,128)S(1)} %shard_map.80.after), channel_id=1, source_target_pairs={{0,1},{1,0},{2,3},{3,2},{4,5},{5,4},{6,7},{7,6},{8,9},{9,8},{10,11... | collective-permute-start | bytes 1572872 | tf_op jit(solution)/shard_map/ppermute | solution.py:30
  10.9 1.4 %shard_map.81 = (f32[3,5,128,128]{3,2,1,0:T(8,128)S(1)}, bf16[384,640]{1,0:T(8,128)(2,1)S(1)}, bf16[384,640]{1,0:T(8,128)(2,1)S(1)}, bf16[128,640]{1,0:T(8,128)(...) custom-call(s32[1,1,5]{2,1,0:T(1,128)} %cutoff_hbm.5, f32[1,1,5,128,128]{4,3,2,1,0:T(8,128)} %ham_hbm.5, ...), custom_call_target="tpu_custom_call" | custom-call | flops 25165824000 | bytes 5472788 | tf_op jit(solution)/shard_map/pallas_call | solution.py:294
  12.3 0.1 collective-permute-done.three
  12.4 1.2 %shard_map.82 = (f32[384,640]{1,0:T(8,128)S(1)}, f32[384,128]{1,0:T(8,128)S(1)}, f32[2,2,128,128]{3,2,1,0:T(8,128)S(1)}, f32[3,1,1,5,128,128]{5,4,3,2,1,0:T(8,128)S(1)}) custom-call(bf16[384,640]{1,0:T(8,128)(2,1)S(1)} %get-tuple-element.46.left_high, bf16[384,640]{1,0:T(8,128)(2,1)S(1)} %get-tuple-element.47.left_low, ...), custom_call_target="tpu_custom_call" | custom-call | flops 100663296000 | bytes 7536640 | tf_op jit(solution)/shard_map/pallas_call | solution.py:294
  13.7 0.0 collective-permute-done.1.four
  13.7 0.6 %shard_map.83 = (f32[4,128,128]{2,1,0:T(8,128)S(1)}, bf16[384,128]{1,0:T(8,128)(2,1)S(1)}, bf16[384,128]{1,0:T(8,128)(2,1)S(1)}, f32[384,128]{1,0:T(8,128)S(1)}, f32[2,128,128]{2,1,0:T(8,128)S(1)}) custom-call(bf16[384,640]{1,0:T(8,128)(2,1)S(1)} %get-tuple-element.46.left_high, bf16[384,640]{1,0:T(8,128)(2,1)S(1)} %get-tuple-element.47.left_low, ...), custom_call_target="tpu_custom_call" | custom-call | flops 100663296 | bytes 5373952 | tf_op jit(solution)/shard_map/pallas_call | solution.py:294
  14.4 0.6 %collective-permute-start.4 = (f32[4,128,128]{2,1,0:T(8,128)S(1)}, f32[4,128,128]{2,1,0:T(8,128)S(1)}, u32[]{:S(2)}, u32[]{:S(2)}) collective-permute-start(f32[4,128,128]{2,1,0:T(8,128)S(1)} %get-tuple-element.72), channel_id=1, source_target_pairs={{1,2},{2,1},{3,0},{0,3},{5,6},{6,5},{7,4},{4,7},{9,10},{10,9},{11,... | collective-permute-start | bytes 786440 | tf_op jit(solution)/shard_map/ppermute | solution.py:30
  14.9 0.4 %collective-permute-start.5 = (f32[4,128,128]{2,1,0:T(8,128)S(1)}, f32[4,128,128]{2,1,0:T(8,128)S(1)}, u32[]{:S(2)}, u32[]{:S(2)}) collective-permute-start(f32[4,128,128]{2,1,0:T(8,128)S(1)} %get-tuple-element.71.after), channel_id=1, source_target_pairs={{0,4},{4,0},{8,12},{12,8},{16,20},{20,16},{24,28},{28,24},{1,5},{5... | collective-permute-start | bytes 786440 | tf_op jit(solution)/shard_map/ppermute | solution.py:30
  15.4 4.6 %collective-permute-start.6 = (f32[4,128,128]{2,1,0:T(8,128)S(1)}, f32[4,128,128]{2,1,0:T(8,128)S(1)}, u32[]{:S(2)}, u32[]{:S(2)}) collective-permute-start(f32[4,128,128]{2,1,0:T(8,128)S(1)} %get-tuple-element.76), channel_id=1, source_target_pairs={{4,8},{8,4},{12,16},{16,12},{20,24},{24,20},{28,0},{0,28},{5,9},{9... | collective-permute-start | bytes 786440 | tf_op jit(solution)/shard_map/ppermute | solution.py:30
  19.9 0.0 collective-permute-done.2.one
  19.9 0.6 %shard_map.84 = (bf16[384,128]{1,0:T(8,128)(2,1)S(1)}, bf16[384,128]{1,0:T(8,128)(2,1)S(1)}, f32[384,128]{1,0:T(8,128)S(1)}, f32[2,128,128]{2,1,0:T(8,128)S(1)}) custom-call(bf16[384,640]{1,0:T(8,128)(2,1)S(1)} %get-tuple-element.46.left_high, bf16[384,640]{1,0:T(8,128)(2,1)S(1)} %get-tuple-element.47.left_low, f32[384,640]{1,0:T(8,128)S(1)} %get-tuple-element.52.start, ...), custom_call_target="tpu_custom_call" | custom-call | flops 125829120 | bytes 4128768 | tf_op jit(solution)/shard_map/pallas_call | solution.py:294
  20.6 0.0 collective-permute-done.3.two
  20.6 0.9 %shard_map.85 = (f32[4,128,128]{2,1,0:T(8,128)S(1)}, bf16[384,128]{1,0:T(8,128)(2,1)S(1)}, bf16[384,128]{1,0:T(8,128)(2,1)S(1)}, bf16[384,128]{1,0:T(8,128)(2,1)...) custom-call(bf16[384,640]{1,0:T(8,128)(2,1)S(1)} %get-tuple-element., ...), custom_call_target="tpu_custom_call" | custom-call | flops 276824064 | bytes 7280640 | tf_op jit(solution)/shard_map/pallas_call | solution.py:294
  21.5 0.1 collective-permute-start.9
  21.7 0.0 collective-permute-start.7
  21.7 1.1 %collective-permute-done.9.arrived.c3 = f32[3,128]{1,0:T(4,128)S(1)} collective-permute-done((f32[3,128]{1,0:T(4,128)S(1)}, f32[3,128]{1,0:T(4,128)S(1)}, u32[]{:S(2)}, u32[]{:S(2)}) %collective-permute-start.9) | collective-permute-done | bytes 1568 | tf_op jit(solution)/shard_map/ppermute | solution.py:30
  22.7 1.5 %collective-permute-start.8 = (f32[3,128]{1,0:T(4,128)S(1)}, f32[3,128]{1,0:T(4,128)S(1)}, u32[]{:S(2)}, u32[]{:S(2)}) collective-permute-start(f32[3,128]{1,0:T(4,128)S(1)} %get-tuple-element.78), channel_id=1, source_target_pairs={{4,8},{8,4},{12,16},{16,12},{20,24},{24,20},{28,0},{0,28},{5,9},{9... | collective-permute-start | bytes 4616 | tf_op jit(solution)/shard_map/ppermute | solution.py:30
  24.2 0.0 collective-permute-done.4.four
  24.2 1.5 %collective-permute-start.10 = (f32[3,128]{1,0:T(4,128)S(1)}, f32[3,128]{1,0:T(4,128)S(1)}, u32[]{:S(2)}, u32[]{:S(2)}) collective-permute-start(f32[3,128]{1,0:T(4,128)S(1)} %shard_map.88), channel_id=1, source_target_pairs={{1,2},{2,1},{3,0},{0,3},{5,6},{6,5},{7,4},{4,7},{9,10},{10,9},{11,... | collective-permute-start | bytes 4616 | tf_op jit(solution)/shard_map/ppermute | solution.py:30
  25.7 1.2 %shard_map.87 = (f32[2,1,1,5,128,128]{5,4,3,2,1,0:T(8,128)}, f32[3,128,128]{2,1,0:T(8,128)S(1)}, f32[128,128]{1,0:T(8,128)S(1)}, f32[3,128]{1,0:T(4,128)S(1)}) custom-call(f32[3,5,128,128]{3,2,1,0:T(8,128)S(1)} %get-tuple-element.45.held, f32[4,128,128]{2,1,0:T(8,128)S(1)} %get-tuple-element.63.new, bf16[384,640]{1,0:T(8,128)(2,1)S(1)} %get-tuple-element.46.left_high, ...), custom_call_target="tpu_custom_call" | custom-call | flops 125829120 | bytes 6030848 | tf_op jit(solution)/shard_map/pallas_call | solution.py:294
  26.9 2.5 %collective-permute-done.7.c1 = f32[3,128]{1,0:T(4,128)S(1)} collective-permute-done((f32[3,128]{1,0:T(4,128)S(1)}, f32[3,128]{1,0:T(4,128)S(1)}, u32[]{:S(2)}, u32[]{:S(2)}) %collective-permute-start.7) | collective-permute-done | bytes 1568 | tf_op jit(solution)/shard_map/ppermute | solution.py:30
  29.4 0.0 collective-permute-done.8.c2
  29.4 0.0 collective-permute-done.10.c4
  29.4 0.0 collective-permute-done.5.one
  29.4 0.0 collective-permute-done.6.two
  29.5 1.3 %shard_map.89 = (f32[2,1,1,5,128,128]{5,4,3,2,1,0:T(8,128)}, f32[3,1,64]{2,1,0:T(1,128)}) custom-call(f32[3,5,128,128]{3,2,1,0:T(8,128)S(1)} %get-tuple-element.45.held, f32[3,1,1,5,128,128]{5,4,3,2,1,0:T(8,128)S(1)} %get-tuple-element.50.der_ref, f32[64,128]{1,0:T(8,128)S(1)} %get-tuple-element.51.members, ...), custom_call_target="tpu_custom_call", output_to_operand_aliasing={{0}: (16, {})} | custom-call | flops 125829120 | bytes 4890880 | tf_op jit(solution)/shard_map/pallas_call | solution.py:294
  (4 shorter events, 0.1 us)
Async XLA Ops:
  1.7 18.2 %collective-permute-start.2 = (f32[4,128,128]{2,1,0:T(8,128)S(1)}, f32[4,128,128]{2,1,0:T(8,128)S(1)}, u32[]{:S(2)}, u32[]{:S(2)}) collective-permute-start(f32[4,128,128]{2,1,0:T(8,128)S(1)} %get-tuple-element.43.message), channel_id=1, source_target_pairs={{0,4},{4,0},{8,12},{12,8},{16,20},{20,16},{24,28},{28,24},{1,5},{5... | collective-permute-start | bytes 786440 | tf_op jit(solution)/shard_map/ppermute | solution.py:30
  4.8 8.9 %collective-permute-start.1 = (f32[4,128,128]{2,1,0:T(8,128)S(1)}, f32[4,128,128]{2,1,0:T(8,128)S(1)}, u32[]{:S(2)}, u32[]{:S(2)}) collective-permute-start(f32[4,128,128]{2,1,0:T(8,128)S(1)} %shard_map.78.message), channel_id=1, source_target_pairs={{1,2},{2,1},{3,0},{0,3},{5,6},{6,5},{7,4},{4,7},{9,10},{10,9},{11,... | collective-permute-start | bytes 786440 | tf_op jit(solution)/shard_map/ppermute | solution.py:30
  5.5 15.0 %collective-permute-start.3 = (f32[4,128,128]{2,1,0:T(8,128)S(1)}, f32[4,128,128]{2,1,0:T(8,128)S(1)}, u32[]{:S(2)}, u32[]{:S(2)}) collective-permute-start(f32[4,128,128]{2,1,0:T(8,128)S(1)} %shard_map.79.message), channel_id=1, source_target_pairs={{4,8},{8,4},{12,16},{16,12},{20,24},{24,20},{28,0},{0,28},{5,9},{9... | collective-permute-start | bytes 786440 | tf_op jit(solution)/shard_map/ppermute | solution.py:30
  10.2 2.3 %collective-permute-start = (f32[8,128,128]{2,1,0:T(8,128)S(1)}, f32[8,128,128]{2,1,0:T(8,128)S(1)}, u32[]{:S(2)}, u32[]{:S(2)}) collective-permute-start(f32[8,128,128]{2,1,0:T(8,128)S(1)} %shard_map.80.after), channel_id=1, source_target_pairs={{0,1},{1,0},{2,3},{3,2},{4,5},{5,4},{6,7},{7,6},{8,9},{9,8},{10,11... | collective-permute-start | bytes 1572872 | tf_op jit(solution)/shard_map/ppermute | solution.py:30
  14.4 9.9 %collective-permute-start.4 = (f32[4,128,128]{2,1,0:T(8,128)S(1)}, f32[4,128,128]{2,1,0:T(8,128)S(1)}, u32[]{:S(2)}, u32[]{:S(2)}) collective-permute-start(f32[4,128,128]{2,1,0:T(8,128)S(1)} %get-tuple-element.72), channel_id=1, source_target_pairs={{1,2},{2,1},{3,0},{0,3},{5,6},{6,5},{7,4},{4,7},{9,10},{10,9},{11,... | collective-permute-start | bytes 786440 | tf_op jit(solution)/shard_map/ppermute | solution.py:30
  14.9 14.5 %collective-permute-start.5 = (f32[4,128,128]{2,1,0:T(8,128)S(1)}, f32[4,128,128]{2,1,0:T(8,128)S(1)}, u32[]{:S(2)}, u32[]{:S(2)}) collective-permute-start(f32[4,128,128]{2,1,0:T(8,128)S(1)} %get-tuple-element.71.after), channel_id=1, source_target_pairs={{0,4},{4,0},{8,12},{12,8},{16,20},{20,16},{24,28},{28,24},{1,5},{5... | collective-permute-start | bytes 786440 | tf_op jit(solution)/shard_map/ppermute | solution.py:30
  15.4 14.1 %collective-permute-start.6 = (f32[4,128,128]{2,1,0:T(8,128)S(1)}, f32[4,128,128]{2,1,0:T(8,128)S(1)}, u32[]{:S(2)}, u32[]{:S(2)}) collective-permute-start(f32[4,128,128]{2,1,0:T(8,128)S(1)} %get-tuple-element.76), channel_id=1, source_target_pairs={{4,8},{8,4},{12,16},{16,12},{20,24},{24,20},{28,0},{0,28},{5,9},{9... | collective-permute-start | bytes 786440 | tf_op jit(solution)/shard_map/ppermute | solution.py:30
  21.5 1.2 %collective-permute-start.9 = (f32[3,128]{1,0:T(4,128)S(1)}, f32[3,128]{1,0:T(4,128)S(1)}, u32[]{:S(2)}, u32[]{:S(2)}) collective-permute-start(f32[3,128]{1,0:T(4,128)S(1)} %get-tuple-element.79), channel_id=1, source_target_pairs={{0,1},{1,0},{2,3},{3,2},{4,5},{5,4},{6,7},{7,6},{8,9},{9,8},{10,11... | collective-permute-start | bytes 4616 | tf_op jit(solution)/shard_map/ppermute | solution.py:30
  21.7 7.8 %collective-permute-start.7 = (f32[3,128]{1,0:T(4,128)S(1)}, f32[3,128]{1,0:T(4,128)S(1)}, u32[]{:S(2)}, u32[]{:S(2)}) collective-permute-start(f32[3,128]{1,0:T(4,128)S(1)} %get-tuple-element.77), channel_id=1, source_target_pairs={{0,4},{4,0},{8,12},{12,8},{16,20},{20,16},{24,28},{28,24},{1,5},{5... | collective-permute-start | bytes 4616 | tf_op jit(solution)/shard_map/ppermute | solution.py:30
  22.7 6.7 %collective-permute-start.8 = (f32[3,128]{1,0:T(4,128)S(1)}, f32[3,128]{1,0:T(4,128)S(1)}, u32[]{:S(2)}, u32[]{:S(2)}) collective-permute-start(f32[3,128]{1,0:T(4,128)S(1)} %get-tuple-element.78), channel_id=1, source_target_pairs={{4,8},{8,4},{12,16},{16,12},{20,24},{24,20},{28,0},{0,28},{5,9},{9... | collective-permute-start | bytes 4616 | tf_op jit(solution)/shard_map/ppermute | solution.py:30
  24.2 5.2 %collective-permute-start.10 = (f32[3,128]{1,0:T(4,128)S(1)}, f32[3,128]{1,0:T(4,128)S(1)}, u32[]{:S(2)}, u32[]{:S(2)}) collective-permute-start(f32[3,128]{1,0:T(4,128)S(1)} %shard_map.88), channel_id=1, source_target_pairs={{1,2},{2,1},{3,0},{0,3},{5,6},{6,5},{7,4},{4,7},{9,10},{10,9},{11,... | collective-permute-start | bytes 4616 | tf_op jit(solution)/shard_map/ppermute | solution.py:30

commit v15 on v11

--- a/solution.py
+++ b/solution.py
@@ -30,6 +30,11 @@
     return lax.ppermute(cells, axis, pairs)
 
 
+def relayed(cells):
+    count = lax.axis_size("gx")
+    return lax.ppermute(cells, "gx", [(i, (i + (2 if i % 2 == 0 else count - 2)) % count) for i in range(count)])
+
+
 def order_of():
     odd_x = lax.rem(lax.axis_index("gx"), 2)
     odd_y = lax.rem(lax.axis_index("gy"), 2)
@@ -78,39 +83,47 @@
     flags = pltpu.make_async_copy(cutoff_hbm, cutoff_ref, cutoff_sem)
     flags.start()
     order = order_of()
-    sources = (ham_hbm.at[0, 0, 0], inv_hbm.at[0, 0, 0], rho_hbm.at[1, 0, 0, 0], ham_hbm.at[0, 0, order[1]])
+    sources = (ham_hbm.at[0, 0, 0], inv_hbm.at[0, 0, 0], rho_hbm.at[1, 0, 0, 0], ham_hbm.at[0, 0, order[1]], rho_hbm.at[0, 0, 0, 0])
     copies = [pltpu.make_async_copy(source, one.at[at], sems.at[at]) for at, source in enumerate(sources)]
-    sources = (ham_hbm.at[0, 0, order[2]], rho_hbm.at[0, 0, 0, 0])
-    for place in (3, 4):
-        sources += (ham_hbm.at[0, 0, order[place]], inv_hbm.at[0, 0, order[place]])
-        sources += (rho_hbm.at[0, 0, 0, order[place]], rho_hbm.at[1, 0, 0, order[place]])
-    copies += [pltpu.make_async_copy(source, rest.at[at], sems.at[4 + at]) for at, source in enumerate(sources)]
+    sources = (ham_hbm.at[0, 0, order[2]], ham_hbm.at[0, 0, order[4]], inv_hbm.at[0, 0, order[4]])
+    sources += (rho_hbm.at[0, 0, 0, order[4]], rho_hbm.at[1, 0, 0, order[4]])
+    copies += [pltpu.make_async_copy(source, rest.at[at], sems.at[5 + at]) for at, source in enumerate(sources)]
     start_all(copies)
     flags.wait()
     for copy in copies:
         copy.wait()
     one[3] = one[3] * cutoff_ref[0, 0, order[1]].astype(f32)
     rest[0] = rest[0] * cutoff_ref[0, 0, order[2]].astype(f32)
-    for place, first in ((3, 2), (4, 6)):
-        keep = cutoff_ref[0, 0, order[place]].astype(f32)
-        for at in range(first, first + 4):
-            rest[at] = rest[at] * keep
-
-
-def whole_first_kernel(first, after, message, rest, out):
+    for at in range(1, 5):
+        rest[at] = rest[at] * cutoff_ref[0, 0, order[4]].astype(f32)
+
+
+def four_first_kernel(message, rest, out):
     out[:3] = message[:3]
-    out[3] = rest[first]
-    out[4] = rest[1]
-    out[5:] = rest[first + 1 : first + 4]
-
-
-def two_first_kernel(message, rest, out):
+    out[3] = rest[1]
+    out[4] = message[4]
+    out[5:] = rest[2:]
+
+
+def two_first_kernel(after, message, rest, out):
     out[:3] = message[:3]
     out[3] = rest[0]
 
 
+def gate_kernel(rest, out):
+    out[...] = rest[0, :8]
+
+
+def whole_first_kernel(after, message, held, ham, out):
+    out[:3] = message[:3]
+    out[3] = ham[...]
+    out[4] = message[4]
+    for kind in range(3):
+        out[5 + kind] = held[kind, 3]
+
+
 def second_kernel(
-    cutoff_hbm, ham_hbm, inv_hbm, rho_hbm, atom_hbm, after, held, left_high, left_low, ham_high, ham_low, members,
+    cutoff_hbm, ham_hbm, inv_hbm, rho_hbm, atom_hbm, after, held, ham_three, left_high, left_low, ham_high, ham_low, members,
     raw, cutoff_ref, atom_ref, cutoff_sem, atom_sem, sems
 ):
     flags = pltpu.make_async_copy(cutoff_hbm, cutoff_ref, cutoff_sem)
@@ -129,6 +142,8 @@
             if place > 0:
                 block = block * keeps[place]
             if kind == 0:
+                if place == 3:
+                    ham_three[...] = block
                 store((ham_high, ham_low), cols(place), split(block))
             else:
                 held[kind - 1, place] = block
@@ -156,9 +171,8 @@
 
 
 def send_more(more, held, place):
-    more[0] = held[1, 0]
     for kind in range(3):
-        more[1 + kind] = held[kind, place]
+        more[kind] = held[kind, place]
 
 
 def whole_edge(left, place, start, near, diagonal, diagonal_out, other):
@@ -167,7 +181,7 @@
     other[0, 0] = real + added
 
 
-def third_kernel(left_high, left_low, ham_high, ham_low, held, three, der_hbm, one_more, two_more, start, diagonal, other, der, sem):
+def third_kernel(left_high, left_low, ham_high, ham_low, held, three, gate, der_hbm, one_more, two_more, start, diagonal, other, der, sem):
     copy = pltpu.make_async_copy(der_hbm, der, sem)
     copy.start()
     send_more(one_more, held, 1)
@@ -183,8 +197,9 @@
 
 
 def fourth_kernel(left_high, left_low, start, diagonal, one, mixed_high, mixed_low, diagonal_out, other):
-    mixed, diagonal_out[...], other[0], other[1] = first_half((left_high, left_low), 1, start, one, diagonal[...])
+    mixed, diagonal_out[...], real, other[1] = first_half((left_high, left_low), 1, start, one, diagonal[...])
     mixed_high[...], mixed_low[...] = mixed
+    other[0] = real + dot(rows_of(mixed)[0], split(one[4]))
 
 
 def fifth_kernel(
@@ -215,7 +230,7 @@
         weighted[direction] = sums[direction]
 
 
-def pass_kernel(arrived, column, out):
+def later_kernel(arrived, column, out):
     out[...] = column[...]
 
 
@@ -233,14 +248,14 @@
     ahead = dot(part(at_self, slice(0, B), cols(0)), part(left, slice(B, 2 * B), whole))
     behind = dot(part(at_self, slice(B, 2 * B), cols(0)), part(left, slice(0, B), whole))
     real_comm = ahead - behind
-    for at, (place, other) in enumerate(((3, other_three), (4, other_four))):
-        imag_new[at] = held[2, place] - time_step * (real_comm[:, cols(place)] + other[0, 0])
+    others = ((3, other_three[0, 0]), (4, other_four[0, 0]), (1, other_one[0]))
+    for at, (place, other) in enumerate(others):
+        imag_new[at] = held[2, place] - time_step * (real_comm[:, cols(place)] + other)
         copies += start_all(
             [pltpu.make_async_copy(imag_new.at[at], out_hbm.at[1, 0, 0, order[place]], sems.at[1, at])]
         )
     comm[0] = real_comm[:, cols(0)] + other_three[0, 1] + other_four[0, 1]
-    comm[1] = real_comm[:, cols(1)] + other_one[0]
-    comm[2] = real_comm[:, cols(2)] + real_two[...]
+    comm[1] = real_comm[:, cols(2)] + real_two[...]
     for direction in range(3):
         row_part[direction : direction + 1, :] = jnp.sum(weighted[direction].T, axis=0, keepdims=True)
     for copy in copies:
@@ -248,22 +263,21 @@
 
 
 def sixth_kernel(
-    held, der_ref, members, high_one, low_one, high_two, low_two, imag_part, comm, row_part, one, two, c1, c2, c3, c4, old_hbm,
+    held, der_ref, members, high_one, low_one, high_two, low_two, imag_part, comm, row_part, one, two, zero, c1, c2, c3, c4, old_hbm,
     out_hbm, forces_hbm, new, forces_ref, sems
 ):
     order = order_of()
     prop, inner = rows_of(beside((high_one[...], low_one[...]), (high_two[...], low_two[...])))
-    near = [tuple(jnp.concatenate(x, axis=0) for x in zip(split(one[1 + kind]), split(two[1 + kind]))) for kind in range(3)]
+    near = [tuple(jnp.concatenate(x, axis=0) for x in zip(split(one[kind]), split(two[kind]))) for kind in range(3)]
     behind = dot(inner, near[0])
     real_new = held[1, 0] + time_step * (imag_part[...] + dot(prop, near[2]) - behind[B:])
     new[0] = real_new
     copies = start_all([pltpu.make_async_copy(new.at[0], out_hbm.at[0, 0, 0, 0], sems.at[0])])
     new[1] = held[2, 0] - time_step * (comm[0] + dot(prop, near[1]) - behind[:B])
-    for place, message, mixed in ((1, one, (high_one, low_one)), (2, two, (high_two, low_two))):
-        added = dot(rows_of((mixed[0][...], mixed[1][...]))[0], split(message[0]))
-        new[1 + place] = held[2, place] - time_step * (comm[place] + added)
+    added = dot(rows_of((high_two[...], low_two[...]))[0], split(zero[0]))
+    new[2] = held[2, 2] - time_step * (comm[1] + added)
     copies += start_all(
-        [pltpu.make_async_copy(new.at[1 + at], out_hbm.at[1, 0, 0, order[at]], sems.at[1 + at]) for at in range(3)]
+        [pltpu.make_async_copy(new.at[1 + at], out_hbm.at[1, 0, 0, order[2 * at]], sems.at[1 + at]) for at in range(2)]
     )
     parts = []
     for direction in range(3):
@@ -275,7 +289,7 @@
     )
     for direction in range(3):
         forces_ref[direction] = forces[direction : direction + 1]
-    copies += start_all([pltpu.make_async_copy(forces_ref, forces_hbm, sems.at[4])])
+    copies += start_all([pltpu.make_async_copy(forces_ref, forces_hbm, sems.at[3])])
     for copy in copies:
         copy.wait()
 
@@ -306,44 +320,43 @@
     message = shape(4, B, B)
     first_one, rest = call(
         first_kernel,
-        [message, shape(10, B, B)],
+        [shape(5, B, B), shape(5, B, B)],
         [hbm] * 4,
         0,
         (cutoff, hamiltonian, inverse_margin, density),
-        scratch=[flags, dma(()), dma((14,))],
+        scratch=[flags, dma(()), dma((10,))],
     )
     near_one = swapped(first_one, 1)
-    whole = shape(8, B, B)
-    kernel = functools.partial(whole_first_kernel, 6)
-    (send_four,) = call(kernel, [whole], [vmem] * 3, 0, (first_one, first_one, rest))
+    (send_four,) = call(four_first_kernel, [shape(8, B, B)], [vmem] * 2, 0, (first_one, rest))
     near_four = swapped(send_four, 4)
-    (first_two,) = call(two_first_kernel, [message], [vmem] * 2, 500, (send_four, rest))
+    (first_two,) = call(two_first_kernel, [message], [vmem] * 3, 500, (send_four, first_one, rest))
     near_two = swapped(first_two, 2)
-    kernel = functools.partial(whole_first_kernel, 2)
-    (send_three,) = call(kernel, [whole], [vmem] * 3, 500, (first_two, first_one, rest))
-    near_three = swapped(send_three, 3)
     left = [shape(3 * B, 5 * B, kind=bf16)] * 2
     ham = [shape(B, 5 * B, kind=bf16)] * 2
-    held, left_high, left_low, ham_high, ham_low, members = call(
+    held, ham_three, left_high, left_low, ham_high, ham_low, members = call(
         second_kernel,
-        [shape(3, 5, B, B)] + left + ham + [shape(ATOMS, B)],
+        [shape(3, 5, B, B), shape(B, B)] + left + ham + [shape(ATOMS, B)],
         [hbm] * 6,
-        2000,
-        (cutoff, hamiltonian, inverse_margin, density, atom_of, send_three),
+        0,
+        (cutoff, hamiltonian, inverse_margin, density, atom_of, first_two),
         scratch=[pltpu.VMEM((4, 5, B, B), f32), flags, pltpu.VMEM((1, 1, B), jnp.int32), dma(()), dma(()), dma((4,))],
     )
+    (send_three,) = call(whole_first_kernel, [shape(8, B, B)], [vmem] * 4, 0, (held, first_one, held, ham_three))
+    near_three = swapped(send_three, 3)
+    (gate,) = call(gate_kernel, [shape(8, B)], [vmem], 500, (rest,))
     mixed = [shape(3 * B, B, kind=bf16)] * 2
+    both = shape(2, 2, B, B)
     both = shape(2, 2, B, B)
     one_more, two_more, start, diagonal, other_three, derivative = call(
         third_kernel,
-        [message, message, shape(3 * B, 5 * B), shape(3 * B, B), both, shape(*derivative.shape)],
-        [vmem] * 6 + [hbm],
-        8000,
-        (left_high, left_low, ham_high, ham_low, held, near_three, derivative),
+        [shape(3, B, B)] * 2 + [shape(3 * B, 5 * B), shape(3 * B, B), both, shape(*derivative.shape)],
+        [vmem] * 7 + [hbm],
+        14,
+        (left_high, left_low, ham_high, ham_low, held, near_three, gate, derivative),
         scratch=[dma(())],
     )
+    near_one_more = swapped(one_more, 1)
     near_two_more = swapped(two_more, 2)
-    near_one_more = swapped(one_more, 1)
     diagonal, other_four = call(
         four_kernel,
         [shape(3 * B, B), both],
@@ -351,6 +364,7 @@
         14,
         (left_high, left_low, start, diagonal, near_four),
     )
+    near_two_zero = relayed(near_one[4:])
     high_one, low_one, diagonal, other_one = call(
         fourth_kernel,
         mixed + [shape(3 * B, B), shape(2, B, B)],
@@ -367,30 +381,30 @@
         (left_high, left_low, start, diagonal, held, derivative, other_one, other_three, other_four, near_two),
     )
     c1, c2, c3, c4 = columns
-    c1, c2, c4 = swapped(c1, 1), swapped(c2, 2), swapped(c4, 4)
-    (c3,) = call(pass_kernel, [shape(3, B)], [vmem] * 2, 0, (c4, c3))
-    columns = (c1, c2, swapped(c3, 3), c4)
+    c1, c2, c3 = swapped(c1, 1), swapped(c2, 2), swapped(c3, 3)
+    (c4,) = call(later_kernel, [shape(3, B)], [vmem] * 2, 0, (c3, c4))
+    columns = (c1, c2, c3, swapped(c4, 4))
     args = (held, new, left_high, left_low, self_high, self_low, other_one, real_two, other_three, other_four, weighted)
     out, comm, row_part = call(
         real_kernel,
-        [shape(*density.shape), shape(3, B, B), shape(3, B)],
+        [shape(*density.shape), shape(2, B, B), shape(3, B)],
         [vmem] * 11,
         10,
         args,
         out_specs=[hbm] + [vmem] * 2,
-        scratch=[pltpu.VMEM((2, B, B), f32), dma((2, 4))],
+        scratch=[pltpu.VMEM((3, B, B), f32), dma((2, 4))],
     )
     args = (held, derivative, members, high_one, low_one, high_two, low_two, imag_part, comm, row_part)
-    args += (near_one_more, near_two_more, *columns, out)
+    args += (near_one_more, near_two_more, near_two_zero, *columns, out)
     new_density, forces = call(
         sixth_kernel,
         [shape(*density.shape), shape(3, 1, ATOMS)],
-        [vmem] * 16 + [hbm],
+        [vmem] * 17 + [hbm],
         10,
         args,
         out_specs=[hbm, hbm],
-        scratch=[pltpu.VMEM((4, B, B), f32), pltpu.VMEM((3, 1, ATOMS), f32), dma((5,))],
-        aliases={16: 0},
+        scratch=[pltpu.VMEM((3, B, B), f32), pltpu.VMEM((3, 1, ATOMS), f32), dma((4,))],
+        aliases={17: 0},
     )
     return new_density, forces.reshape(1, 1, 3, ATOMS)
 

time: 35 us -> 39.4 us (1.13)
  waiting for transfers between devices: 7.95 us -> 11.3 us
  starting transfers between devices: 17.2 us -> 18.3 us
    ppermute x10, waiting for transfers between devices: 7.95 us -> 11.3 us  [swapped(): return lax.ppermute(cells, axis, pairs)]
    ppermute x0 -> x1, starting transfers between devices: none -> 2.54 us  [relayed(): lax.ppermute(cells, 'gx', [(i, (i + (2 if i % 2 == 0 else count - 2)) % c...]
    ppermute x10, starting transfers between devices: 17.2 us -> 15.7 us  [swapped(): return lax.ppermute(cells, axis, pairs)]
    pallas_call x12 -> x13, Pallas kernels: 8.89 us -> 8.86 us  [call(): pl.pallas_call(kernel, out_shape=shapes, in_specs=in_specs, out_specs=out...]
  transfers between devices with their start and end apart: 10 -> 11, of which waited for: 4 -> 3; matrix products, arithmetic and copies ran while one was open for 0% -> 0% of each run, Pallas kernels for 18% -> 16%
where the time goes in v15:
time: 39.4 us; the launch traced here: 39.2 us
  starting transfers between devices  18.3 us (46%)
  waiting for transfers between devices  11.3 us (29%)
  Pallas kernels  8.86 us (22%)
  between operations  0.74 us (2%)
    ppermute x10, starting transfers between devices, swapped(): return lax.ppermute(cells, axis, pairs)  15.7 us
    ppermute x10, waiting for transfers between devices, swapped(): return lax.ppermute(cells, axis, pairs)  11.3 us
    pallas_call x13, Pallas kernels, call(): pl.pallas_call(kernel, out_shape=shapes, in_specs=in_specs, out_specs=out...  8.86 us
    ppermute x1, starting transfers between devices, relayed(): lax.ppermute(cells, 'gx', [(i, (i + (2 if i % 2 == 0 else count - 2)) % c...  2.54 us
  transfers between devices with their start and end apart: 11, of which 3 were waited for; matrix products, arithmetic and copies ran while one was open for 0% of the time, Pallas kernels for 16%

profile of v15, /device:TPU:0, one launch (start us, length us, event | category | flops | bytes accessed | tf_op | source)
XLA Modules:
  0.0 39.2 jit_solution(18404237931124120671)
XLA Ops:
  0.6 1.2 %shard_map.77 = (f32[5,128,128]{2,1,0:T(8,128)S(1)}, f32[5,128,128]{2,1,0:T(8,128)S(1)}) custom-call(s32[1,1,5]{2,1,0:T(1,128)} %cutoff_hbm.3, f32[1,1,5,128,128]{4,3,2,1,0:T(8,128)} %ham_hbm.3, f32[1,1,5,128,128]{4,3,2,1,0:T(8,128)} %inv_hbm.3, f32[2,1,1,5,128,128]{5,4,3,2,1,0:T(8,128)} %rho_hbm.3), custom_call_target="tpu_custom_call" | custom-call | bytes 1966100 | tf_op jit(solution)/shard_map/pallas_call | solution.py:299
  1.9 3.0 %collective-permute-start.2 = (f32[5,128,128]{2,1,0:T(8,128)S(1)}, f32[5,128,128]{2,1,0:T(8,128)S(1)}, u32[]{:S(2)}, u32[]{:S(2)}) collective-permute-start(f32[5,128,128]{2,1,0:T(8,128)S(1)} %get-tuple-element.40.message), channel_id=1, source_target_pairs={{0,4},{4,0},{8,12},{12,8},{16,20},{20,16},{24,28},{28,24},{1,5},{5... | collective-permute-start | bytes 983048 | tf_op jit(solution)/shard_map/ppermute | solution.py:30
  5.0 0.7 %collective-permute-start.1 = (f32[8,128,128]{2,1,0:T(8,128)S(1)}, f32[8,128,128]{2,1,0:T(8,128)S(1)}, u32[]{:S(2)}, u32[]{:S(2)}) collective-permute-start(f32[8,128,128]{2,1,0:T(8,128)S(1)} %shard_map.78.after), channel_id=1, source_target_pairs={{1,2},{2,1},{3,0},{0,3},{5,6},{6,5},{7,4},{4,7},{9,10},{10,9},{11,... | collective-permute-start | bytes 1572872 | tf_op jit(solution)/shard_map/ppermute | solution.py:30
  5.7 3.6 %collective-permute-start.3 = (f32[4,128,128]{2,1,0:T(8,128)S(1)}, f32[4,128,128]{2,1,0:T(8,128)S(1)}, u32[]{:S(2)}, u32[]{:S(2)}) collective-permute-start(f32[4,128,128]{2,1,0:T(8,128)S(1)} %shard_map.79.after), channel_id=1, source_target_pairs={{4,8},{8,4},{12,16},{16,12},{20,24},{24,20},{28,0},{0,28},{5,9},{9... | collective-permute-start | bytes 786440 | tf_op jit(solution)/shard_map/ppermute | solution.py:30
  9.3 1.4 %shard_map.80 = (f32[3,5,128,128]{3,2,1,0:T(8,128)S(1)}, f32[128,128]{1,0:T(8,128)S(1)}, bf16[384,640]{1,0:T(8,128)(2,1)S(1)}, bf16[384,640]{1,0:T(8,128)(2,1)S(...) custom-call(s32[1,1,5]{2,1,0:T(1,128)} %cutoff_hbm.3, ...), custom_call_target="tpu_custom_call" | custom-call | bytes 5276180 | tf_op jit(solution)/shard_map/pallas_call | solution.py:299
  10.8 0.7 %collective-permute-start = (f32[8,128,128]{2,1,0:T(8,128)S(1)}, f32[8,128,128]{2,1,0:T(8,128)S(1)}, u32[]{:S(2)}, u32[]{:S(2)}) collective-permute-start(f32[8,128,128]{2,1,0:T(8,128)S(1)} %shard_map.81), channel_id=1, source_target_pairs={{0,1},{1,0},{2,3},{3,2},{4,5},{5,4},{6,7},{7,6},{8,9},{9,8},{10,11... | collective-permute-start | bytes 1572872 | tf_op jit(solution)/shard_map/ppermute | solution.py:30
  11.5 1.5 %collective-permute-done.three = f32[8,128,128]{2,1,0:T(8,128)S(1)} collective-permute-done((f32[8,128,128]{2,1,0:T(8,128)S(1)}, f32[8,128,128]{2,1,0:T(8,128)S(1)}, u32[]{:S(2)}, u32[]{:S(2)}) %collective-permute-start) | collective-permute-done | bytes 524320 | tf_op jit(solution)/shard_map/ppermute | solution.py:30
  13.0 1.2 %shard_map.83 = (f32[3,128,128]{2,1,0:T(8,128)S(1)}, f32[3,128,128]{2,1,0:T(8,128)S(1)}, f32[384,640]{1,0:T(8,128)S(1)}, f32[384,128]{1,0:T(8,128)S(1)}, f32[2,2...) custom-call(bf16[384,640]{1,0:T(8,128)(2,1)S(1)} %get-tuple-element.43.left_high, ...), custom_call_target="tpu_custom_call" | custom-call | flops 176160768 | bytes 7933952 | tf_op jit(solution)/shard_map/pallas_call | solution.py:299
  14.3 0.1 collective-permute-start.4
  14.3 1.9 %collective-permute-start.5 = (f32[3,128,128]{2,1,0:T(8,128)S(1)}, f32[3,128,128]{2,1,0:T(8,128)S(1)}, u32[]{:S(2)}, u32[]{:S(2)}) collective-permute-start(f32[3,128,128]{2,1,0:T(8,128)S(1)} %get-tuple-element.70), channel_id=1, source_target_pairs={{4,8},{8,4},{12,16},{16,12},{20,24},{24,20},{28,0},{0,28},{5,9},{9... | collective-permute-start | bytes 589832 | tf_op jit(solution)/shard_map/ppermute | solution.py:30
  16.3 6.6 %collective-permute-done.2.one = f32[5,128,128]{2,1,0:T(8,128)S(1)} collective-permute-done((f32[5,128,128]{2,1,0:T(8,128)S(1)}, f32[5,128,128]{2,1,0:T(8,128)S(1)}, u32[]{:S(2)}, u32[]{:S(2)}) %collective-permute-start.2) | collective-permute-done | bytes 327712 | tf_op jit(solution)/shard_map/ppermute | solution.py:30
  22.9 2.5 %collective-permute-start.6 = (f32[1,128,128]{2,1,0:T(8,128)S(1)}, f32[1,128,128]{2,1,0:T(8,128)S(1)}, u32[]{:S(2)}, u32[]{:S(2)}) collective-permute-start(f32[1,128,128]{2,1,0:T(8,128)S(1)} %slice.4), channel_id=1, source_target_pairs={{0,8},{4,28},{8,16},{12,4},{16,24},{20,12},{24,0},{28,20},{1,9},{5... | collective-permute-start | bytes 196616 | tf_op jit(solution)/shard_map/ppermute | solution.py:35
  25.4 0.0 collective-permute-done.1.four
  25.4 0.8 %shard_map.84 = (f32[384,128]{1,0:T(8,128)S(1)}, f32[2,2,128,128]{3,2,1,0:T(8,128)S(1)}) custom-call(bf16[384,640]{1,0:T(8,128)(2,1)S(1)} %get-tuple-element.43.left_high, bf16[384,640]{1,0:T(8,128)(2,1)S(1)} %get-tuple-element.44.left_low, f32[384,640]{1,0:T(8,128)S(1)} %get-tuple-element.50.start, f32[384,128]{1,0:T(8,128)S(1)} %get-tuple-element.51.diagonal, ...), custom_call_target="tpu_custom_call" | custom-call | flops 176160768 | bytes 4128768 | tf_op jit(solution)/shard_map/pallas_call | solution.py:299
  26.2 0.7 %shard_map.85 = (bf16[384,128]{1,0:T(8,128)(2,1)S(1)}, bf16[384,128]{1,0:T(8,128)(2,1)S(1)}, f32[384,128]{1,0:T(8,128)S(1)}, f32[2,128,128]{2,1,0:T(8,128)S(1)}) custom-call(bf16[384,640]{1,0:T(8,128)(2,1)S(1)} %get-tuple-element.43.left_high, bf16[384,640]{1,0:T(8,128)(2,1)S(1)} %get-tuple-element.44.left_low, f32[384,640]{1,0:T(8,128)S(1)} %get-tuple-element.50.start, ...), custom_call_target="tpu_custom_call" | custom-call | flops 125829120 | bytes 4194304 | tf_op jit(solution)/shard_map/pallas_call | solution.py:299
  26.9 0.0 collective-permute-done.3.two
  26.9 0.9 %shard_map.86 = (f32[4,128,128]{2,1,0:T(8,128)S(1)}, bf16[384,128]{1,0:T(8,128)(2,1)S(1)}, bf16[384,128]{1,0:T(8,128)(2,1)S(1)}, bf16[384,128]{1,0:T(8,128)(2,1)...) custom-call(bf16[384,640]{1,0:T(8,128)(2,1)S(1)} %get-tuple-element., ...), custom_call_target="tpu_custom_call" | custom-call | flops 276824064 | bytes 7411712 | tf_op jit(solution)/shard_map/pallas_call | solution.py:299
  27.9 0.1 collective-permute-start.9
  28.0 3.6 %collective-permute-start.7 = (f32[3,128]{1,0:T(4,128)S(1)}, f32[3,128]{1,0:T(4,128)S(1)}, u32[]{:S(2)}, u32[]{:S(2)}) collective-permute-start(f32[3,128]{1,0:T(4,128)S(1)} %get-tuple-element.71), channel_id=1, source_target_pairs={{0,4},{4,0},{8,12},{12,8},{16,20},{20,16},{24,28},{28,24},{1,5},{5... | collective-permute-start | bytes 4616 | tf_op jit(solution)/shard_map/ppermute | solution.py:30
  31.6 0.0 collective-permute-done.9.arrived.c3
  31.6 1.0 %collective-permute-start.8 = (f32[3,128]{1,0:T(4,128)S(1)}, f32[3,128]{1,0:T(4,128)S(1)}, u32[]{:S(2)}, u32[]{:S(2)}) collective-permute-start(f32[3,128]{1,0:T(4,128)S(1)} %get-tuple-element.72), channel_id=1, source_target_pairs={{4,8},{8,4},{12,16},{16,12},{20,24},{24,20},{28,0},{0,28},{5,9},{9... | collective-permute-start | bytes 4616 | tf_op jit(solution)/shard_map/ppermute | solution.py:30
  32.6 0.0 collective-permute-done.6.zero
  32.6 1.0 %collective-permute-start.10 = (f32[3,128]{1,0:T(4,128)S(1)}, f32[3,128]{1,0:T(4,128)S(1)}, u32[]{:S(2)}, u32[]{:S(2)}) collective-permute-start(f32[3,128]{1,0:T(4,128)S(1)} %shard_map.88), channel_id=1, source_target_pairs={{1,2},{2,1},{3,0},{0,3},{5,6},{6,5},{7,4},{4,7},{9,10},{10,9},{11,... | collective-permute-start | bytes 4616 | tf_op jit(solution)/shard_map/ppermute | solution.py:30
  33.6 1.2 %shard_map.87 = (f32[2,1,1,5,128,128]{5,4,3,2,1,0:T(8,128)}, f32[2,128,128]{2,1,0:T(8,128)S(1)}, f32[3,128]{1,0:T(4,128)S(1)}) custom-call(f32[3,5,128,128]{3,2,1,0:T(8,128)S(1)} %get-tuple-element.42.after.held, f32[4,128,128]{2,1,0:T(8,128)S(1)} %get-tuple-element.62.new, bf16[384,640]{1,0:T(8,128)(2,1)S(1)} %get-tuple-element.43.left_high, ...), custom_call_target="tpu_custom_call" | custom-call | flops 125829120 | bytes 5309952 | tf_op jit(solution)/shard_map/pallas_call | solution.py:299
  34.7 0.0 collective-permute-done.7.c1
  34.7 3.1 %collective-permute-done.8.c2 = f32[3,128]{1,0:T(4,128)S(1)} collective-permute-done((f32[3,128]{1,0:T(4,128)S(1)}, f32[3,128]{1,0:T(4,128)S(1)}, u32[]{:S(2)}, u32[]{:S(2)}) %collective-permute-start.8) | collective-permute-done | bytes 1568 | tf_op jit(solution)/shard_map/ppermute | solution.py:30
  37.9 0.0 collective-permute-done.10.c4
  37.9 0.0 collective-permute-done.4.one
  37.9 0.0 collective-permute-done.5.two
  37.9 1.3 %shard_map.89 = (f32[2,1,1,5,128,128]{5,4,3,2,1,0:T(8,128)}, f32[3,1,64]{2,1,0:T(1,128)}) custom-call(f32[3,5,128,128]{3,2,1,0:T(8,128)S(1)} %get-tuple-element.42.after.held, f32[3,1,1,5,128,128]{5,4,3,2,1,0:T(8,128)S(1)} %get-tuple-element.48.der_ref, f32[64,128]{1,0:T(8,128)S(1)} %get-tuple-element.49.members, ...), custom_call_target="tpu_custom_call", output_to_operand_aliasing={{0}: (17, {})} | custom-call | flops 125829120 | bytes 4759808 | tf_op jit(solution)/shard_map/pallas_call | solution.py:299
  (6 shorter events, 0.1 us)
Async XLA Ops:
  1.9 21.0 %collective-permute-start.2 = (f32[5,128,128]{2,1,0:T(8,128)S(1)}, f32[5,128,128]{2,1,0:T(8,128)S(1)}, u32[]{:S(2)}, u32[]{:S(2)}) collective-permute-start(f32[5,128,128]{2,1,0:T(8,128)S(1)} %get-tuple-element.40.message), channel_id=1, source_target_pairs={{0,4},{4,0},{8,12},{12,8},{16,20},{20,16},{24,28},{28,24},{1,5},{5... | collective-permute-start | bytes 983048 | tf_op jit(solution)/shard_map/ppermute | solution.py:30
  5.0 20.5 %collective-permute-start.1 = (f32[8,128,128]{2,1,0:T(8,128)S(1)}, f32[8,128,128]{2,1,0:T(8,128)S(1)}, u32[]{:S(2)}, u32[]{:S(2)}) collective-permute-start(f32[8,128,128]{2,1,0:T(8,128)S(1)} %shard_map.78.after), channel_id=1, source_target_pairs={{1,2},{2,1},{3,0},{0,3},{5,6},{6,5},{7,4},{4,7},{9,10},{10,9},{11,... | collective-permute-start | bytes 1572872 | tf_op jit(solution)/shard_map/ppermute | solution.py:30
  5.7 21.2 %collective-permute-start.3 = (f32[4,128,128]{2,1,0:T(8,128)S(1)}, f32[4,128,128]{2,1,0:T(8,128)S(1)}, u32[]{:S(2)}, u32[]{:S(2)}) collective-permute-start(f32[4,128,128]{2,1,0:T(8,128)S(1)} %shard_map.79.after), channel_id=1, source_target_pairs={{4,8},{8,4},{12,16},{16,12},{20,24},{24,20},{28,0},{0,28},{5,9},{9... | collective-permute-start | bytes 786440 | tf_op jit(solution)/shard_map/ppermute | solution.py:30
  10.8 2.3 %collective-permute-start = (f32[8,128,128]{2,1,0:T(8,128)S(1)}, f32[8,128,128]{2,1,0:T(8,128)S(1)}, u32[]{:S(2)}, u32[]{:S(2)}) collective-permute-start(f32[8,128,128]{2,1,0:T(8,128)S(1)} %shard_map.81), channel_id=1, source_target_pairs={{0,1},{1,0},{2,3},{3,2},{4,5},{5,4},{6,7},{7,6},{8,9},{9,8},{10,11... | collective-permute-start | bytes 1572872 | tf_op jit(solution)/shard_map/ppermute | solution.py:30
  14.3 23.6 %collective-permute-start.4 = (f32[3,128,128]{2,1,0:T(8,128)S(1)}, f32[3,128,128]{2,1,0:T(8,128)S(1)}, u32[]{:S(2)}, u32[]{:S(2)}) collective-permute-start(f32[3,128,128]{2,1,0:T(8,128)S(1)} %get-tuple-element.69), channel_id=1, source_target_pairs={{0,4},{4,0},{8,12},{12,8},{16,20},{20,16},{24,28},{28,24},{1,5},{5... | collective-permute-start | bytes 589832 | tf_op jit(solution)/shard_map/ppermute | solution.py:30
  14.3 23.6 %collective-permute-start.5 = (f32[3,128,128]{2,1,0:T(8,128)S(1)}, f32[3,128,128]{2,1,0:T(8,128)S(1)}, u32[]{:S(2)}, u32[]{:S(2)}) collective-permute-start(f32[3,128,128]{2,1,0:T(8,128)S(1)} %get-tuple-element.70), channel_id=1, source_target_pairs={{4,8},{8,4},{12,16},{16,12},{20,24},{24,20},{28,0},{0,28},{5,9},{9... | collective-permute-start | bytes 589832 | tf_op jit(solution)/shard_map/ppermute | solution.py:30
  22.9 9.7 %collective-permute-start.6 = (f32[1,128,128]{2,1,0:T(8,128)S(1)}, f32[1,128,128]{2,1,0:T(8,128)S(1)}, u32[]{:S(2)}, u32[]{:S(2)}) collective-permute-start(f32[1,128,128]{2,1,0:T(8,128)S(1)} %slice.4), channel_id=1, source_target_pairs={{0,8},{4,28},{8,16},{12,4},{16,24},{20,12},{24,0},{28,20},{1,9},{5... | collective-permute-start | bytes 196616 | tf_op jit(solution)/shard_map/ppermute | solution.py:35
  27.9 3.7 %collective-permute-start.9 = (f32[3,128]{1,0:T(4,128)S(1)}, f32[3,128]{1,0:T(4,128)S(1)}, u32[]{:S(2)}, u32[]{:S(2)}) collective-permute-start(f32[3,128]{1,0:T(4,128)S(1)} %get-tuple-element.73), channel_id=1, source_target_pairs={{0,1},{1,0},{2,3},{3,2},{4,5},{5,4},{6,7},{7,6},{8,9},{9,8},{10,11... | collective-permute-start | bytes 4616 | tf_op jit(solution)/shard_map/ppermute | solution.py:30
  28.0 6.7 %collective-permute-start.7 = (f32[3,128]{1,0:T(4,128)S(1)}, f32[3,128]{1,0:T(4,128)S(1)}, u32[]{:S(2)}, u32[]{:S(2)}) collective-permute-start(f32[3,128]{1,0:T(4,128)S(1)} %get-tuple-element.71), channel_id=1, source_target_pairs={{0,4},{4,0},{8,12},{12,8},{16,20},{20,16},{24,28},{28,24},{1,5},{5... | collective-permute-start | bytes 4616 | tf_op jit(solution)/shard_map/ppermute | solution.py:30
  31.6 6.3 %collective-permute-start.8 = (f32[3,128]{1,0:T(4,128)S(1)}, f32[3,128]{1,0:T(4,128)S(1)}, u32[]{:S(2)}, u32[]{:S(2)}) collective-permute-start(f32[3,128]{1,0:T(4,128)S(1)} %get-tuple-element.72), channel_id=1, source_target_pairs={{4,8},{8,4},{12,16},{16,12},{20,24},{24,20},{28,0},{0,28},{5,9},{9... | collective-permute-start | bytes 4616 | tf_op jit(solution)/shard_map/ppermute | solution.py:30
  32.6 5.3 %collective-permute-start.10 = (f32[3,128]{1,0:T(4,128)S(1)}, f32[3,128]{1,0:T(4,128)S(1)}, u32[]{:S(2)}, u32[]{:S(2)}) collective-permute-start(f32[3,128]{1,0:T(4,128)S(1)} %shard_map.88), channel_id=1, source_target_pairs={{1,2},{2,1},{3,0},{0,3},{5,6},{6,5},{7,4},{4,7},{9,10},{10,9},{11,... | collective-permute-start | bytes 4616 | tf_op jit(solution)/shard_map/ppermute | solution.py:30

commit v16 on v14

--- a/solution.py
+++ b/solution.py
@@ -97,24 +97,8 @@
     out[3] = rest[at]
 
 
-def whole_first_kernel(cutoff_hbm, ham_hbm, inv_hbm, rho_hbm, message, out, cutoff_ref, cutoff_sem, sems):
-    flags = pltpu.make_async_copy(cutoff_hbm, cutoff_ref, cutoff_sem)
-    flags.start()
-    offset = order_of()[3]
-    sources = (ham_hbm.at[0, 0, offset], rho_hbm.at[0, 0, 0, 0], inv_hbm.at[0, 0, offset], rho_hbm.at[0, 0, 0, offset])
-    sources += (rho_hbm.at[1, 0, 0, offset],)
-    copies = start_all([pltpu.make_async_copy(source, out.at[3 + at], sems.at[at]) for at, source in enumerate(sources)])
-    out[:3] = message[:3]
-    flags.wait()
-    keep = cutoff_ref[0, 0, offset].astype(f32)
-    for copy in copies:
-        copy.wait()
-    for at in (3, 5, 6, 7):
-        out[at] = out[at] * keep
-
-
 def second_kernel(
-    cutoff_hbm, ham_hbm, inv_hbm, rho_hbm, atom_hbm, after, held, left_high, left_low, ham_high, ham_low, members,
+    cutoff_hbm, ham_hbm, inv_hbm, rho_hbm, atom_hbm, after, three, held, left_high, left_low, ham_high, ham_low, members,
     raw, cutoff_ref, atom_ref, cutoff_sem, atom_sem, sems
 ):
     flags = pltpu.make_async_copy(cutoff_hbm, cutoff_ref, cutoff_sem)
@@ -130,8 +114,12 @@
         copy.wait()
         for place, offset in enumerate(order):
             block = raw[kind, offset]
-            if place > 0:
+            if place == 0:
+                three[(0, 1, 4, 2)[kind]] = block
+            else:
                 block = block * keeps[place]
+                if place == 3:
+                    three[(3, 5, 6, 7)[kind]] = block
             if kind == 0:
                 store((ham_high, ham_low), cols(place), split(block))
             else:
@@ -165,23 +153,21 @@
         more[1 + kind] = held[kind, place]
 
 
-def third_kernel(left_high, left_low, ham_high, ham_low, held, three, der_hbm, start, diagonal, other, der, sem):
+def third_kernel(left_high, left_low, ham_high, ham_low, held, four, one_more, start, mixed_high, mixed_low, diagonal, other):
+    send_more(one_more, held, 1)
+    left = (left_high, left_low)
+    start[...] = dot(part(left, slice(0, 3 * B), cols(0)), part((ham_high, ham_low), slice(0, B), cols(0, 5)))
+    mixed, diagonal[...], other[0], other[1] = first_half(left, 4, start, four, start[:, cols(0)])
+    mixed_high[...], mixed_low[...] = mixed
+
+
+def whole_kernel(left_high, left_low, start, diagonal, three, der_hbm, diagonal_out, other, der, sem):
     copy = pltpu.make_async_copy(der_hbm, der, sem)
     copy.start()
-    left = (left_high, left_low)
-    start[...] = dot(part(left, slice(0, 3 * B), cols(0)), part((ham_high, ham_low), slice(0, B), cols(0, 5)))
-    mixed, diagonal[...], real, other[1, 0] = first_half(left, 3, start, three, start[:, cols(0)])
+    mixed, diagonal_out[...], real, other[1, 0] = first_half((left_high, left_low), 3, start, three, diagonal[...])
     added, other[0, 1], other[1, 1] = second_half(mixed, three[4:])
     other[0, 0] = real + added
     copy.wait()
-
-
-def four_kernel(
-    left_high, left_low, start, held, diagonal, four, one_more, mixed_high, mixed_low, diagonal_out, other
-):
-    send_more(one_more, held, 1)
-    mixed, diagonal_out[...], other[0], other[1] = first_half((left_high, left_low), 4, start, four, diagonal[...])
-    mixed_high[...], mixed_low[...] = mixed
 
 
 def more_kernel(after, held, two_more, four_more):
@@ -326,46 +312,38 @@
     near_four = swapped(first_four, 4)
     (first_two,) = call(functools.partial(next_kernel, 1), [message], [vmem] * 2, 500, (first_four, rest))
     near_two = swapped(first_two, 2)
-    (send_three,) = call(
-        whole_first_kernel,
-        [shape(8, B, B)],
-        [hbm] * 4 + [vmem],
-        500,
-        (cutoff, hamiltonian, inverse_margin, density, first_two),
-        scratch=[flags, dma(()), dma((5,))],
-    )
-    near_three = swapped(send_three, 3)
     left = [shape(3 * B, 5 * B, kind=bf16)] * 2
     ham = [shape(B, 5 * B, kind=bf16)] * 2
-    held, left_high, left_low, ham_high, ham_low, members = call(
+    send_three, held, left_high, left_low, ham_high, ham_low, members = call(
         second_kernel,
-        [shape(3, 5, B, B)] + left + ham + [shape(ATOMS, B)],
+        [shape(8, B, B), shape(3, 5, B, B)] + left + ham + [shape(ATOMS, B)],
         [hbm] * 6,
-        2000,
-        (cutoff, hamiltonian, inverse_margin, density, atom_of, send_three),
+        0,
+        (cutoff, hamiltonian, inverse_margin, density, atom_of, first_two),
         scratch=[pltpu.VMEM((4, 5, B, B), f32), flags, pltpu.VMEM((1, 1, B), jnp.int32), dma(()), dma(()), dma((4,))],
     )
+    near_three = swapped(send_three, 3)
     mixed = [shape(3 * B, B, kind=bf16)] * 2
     both = shape(2, 2, B, B)
-    start, diagonal, other_three, derivative = call(
+    one_more, start, high_four, low_four, diagonal, other_four = call(
         third_kernel,
-        [shape(3 * B, 5 * B), shape(3 * B, B), shape(2, 2, B, B), shape(*derivative.shape)],
-        [vmem] * 6 + [hbm],
+        [message, shape(3 * B, 5 * B)] + mixed + [shape(3 * B, B), shape(2, B, B)],
+        [vmem] * 6,
         8000,
-        (left_high, left_low, ham_high, ham_low, held, near_three, derivative),
-        scratch=[dma(())],
-    )
-    one_more, high_four, low_four, diagonal, other_four = call(
-        four_kernel,
-        [message] + mixed + [shape(3 * B, B), shape(2, B, B)],
-        [vmem] * 6,
-        8,
-        (left_high, left_low, start, held, diagonal, near_four),
+        (left_high, left_low, ham_high, ham_low, held, near_four),
     )
     near_one_more = swapped(one_more, 1)
     two_more, four_more = call(more_kernel, [message] * 2, [vmem] * 2, 300, (one_more, held))
     near_four_more = swapped(four_more, 4)
     near_two_more = swapped(two_more, 2)
+    diagonal, other_three, derivative = call(
+        whole_kernel,
+        [shape(3 * B, B), shape(2, 2, B, B), shape(*derivative.shape)],
+        [vmem] * 5 + [hbm],
+        14,
+        (left_high, left_low, start, diagonal, near_three, derivative),
+        scratch=[dma(())],
+    )
     high_one, low_one, diagonal, other_one = call(
         fourth_kernel,
         mixed + [shape(3 * B, B), shape(2, B, B)],

time: 31.1 us -> 32.6 us (1.048)
  waiting for transfers between devices: 3.75 us -> 6.9 us
  starting transfers between devices: 16.8 us -> 15.5 us
    ppermute x11, waiting for transfers between devices: 3.75 us -> 6.9 us  [swapped(): return lax.ppermute(cells, axis, pairs)]
    ppermute x11, starting transfers between devices: 16.8 us -> 15.5 us  [swapped(): return lax.ppermute(cells, axis, pairs)]
    pallas_call x13 -> x12, Pallas kernels: 9.48 us -> 9.2 us  [call(): pl.pallas_call(kernel, out_shape=shapes, in_specs=in_specs, out_specs=out...]
  transfers between devices with their start and end apart: 11 -> 11, of which waited for: 3 -> 4; matrix products, arithmetic and copies ran while one was open for 0% -> 0% of each run, Pallas kernels for 23% -> 21%
where the time goes in v16:
time: 32.6 us; the launch traced here: 32.3 us
  starting transfers between devices  15.5 us (48%)
  Pallas kernels  9.2 us (28%)
  waiting for transfers between devices  6.9 us (21%)
  between operations  0.73 us (2%)
    ppermute x11, starting transfers between devices, swapped(): return lax.ppermute(cells, axis, pairs)  15.5 us
    pallas_call x12, Pallas kernels, call(): pl.pallas_call(kernel, out_shape=shapes, in_specs=in_specs, out_specs=out...  9.2 us
    ppermute x11, waiting for transfers between devices, swapped(): return lax.ppermute(cells, axis, pairs)  6.9 us
  transfers between devices with their start and end apart: 11, of which 4 were waited for; matrix products, arithmetic and copies ran while one was open for 0% of the time, Pallas kernels for 21%

profile of v16, /device:TPU:0, one launch (start us, length us, event | category | flops | bytes accessed | tf_op | source)
XLA Modules:
  0.0 32.3 jit_solution(16764572890108422063)
XLA Ops:
  0.6 1.1 %shard_map.77 = (f32[4,128,128]{2,1,0:T(8,128)S(1)}, f32[2,128,128]{2,1,0:T(8,128)S(1)}) custom-call(s32[1,1,5]{2,1,0:T(1,128)} %cutoff_hbm.3, f32[1,1,5,128,128]{4,3,2,1,0:T(8,128)} %ham_hbm.3, f32[1,1,5,128,128]{4,3,2,1,0:T(8,128)} %inv_hbm.3, f32[2,1,1,5,128,128]{5,4,3,2,1,0:T(8,128)} %rho_hbm.3), custom_call_target="tpu_custom_call" | custom-call | bytes 1703956 | tf_op jit(solution)/shard_map/pallas_call | solution.py:280
  1.7 3.0 %collective-permute-start.2 = (f32[4,128,128]{2,1,0:T(8,128)S(1)}, f32[4,128,128]{2,1,0:T(8,128)S(1)}, u32[]{:S(2)}, u32[]{:S(2)}) collective-permute-start(f32[4,128,128]{2,1,0:T(8,128)S(1)} %get-tuple-element.44.message), channel_id=1, source_target_pairs={{0,4},{4,0},{8,12},{12,8},{16,20},{20,16},{24,28},{28,24},{1,5},{5... | collective-permute-start | bytes 786440 | tf_op jit(solution)/shard_map/ppermute | solution.py:30
  4.8 0.7 %collective-permute-start = (f32[4,128,128]{2,1,0:T(8,128)S(1)}, f32[4,128,128]{2,1,0:T(8,128)S(1)}, u32[]{:S(2)}, u32[]{:S(2)}) collective-permute-start(f32[4,128,128]{2,1,0:T(8,128)S(1)} %shard_map.78.message), channel_id=1, source_target_pairs={{1,2},{2,1},{3,0},{0,3},{5,6},{6,5},{7,4},{4,7},{9,10},{10,9},{11,... | collective-permute-start | bytes 786440 | tf_op jit(solution)/shard_map/ppermute | solution.py:30
  5.5 3.6 %collective-permute-start.3 = (f32[4,128,128]{2,1,0:T(8,128)S(1)}, f32[4,128,128]{2,1,0:T(8,128)S(1)}, u32[]{:S(2)}, u32[]{:S(2)}) collective-permute-start(f32[4,128,128]{2,1,0:T(8,128)S(1)} %shard_map.79.after), channel_id=1, source_target_pairs={{4,8},{8,4},{12,16},{16,12},{20,24},{24,20},{28,0},{0,28},{5,9},{9... | collective-permute-start | bytes 786440 | tf_op jit(solution)/shard_map/ppermute | solution.py:30
  9.1 1.4 %shard_map.80 = (f32[8,128,128]{2,1,0:T(8,128)S(1)}, f32[3,5,128,128]{3,2,1,0:T(8,128)S(1)}, bf16[384,640]{1,0:T(8,128)(2,1)S(1)}, bf16[384,640]{1,0:T(8,128)(2,...) custom-call(s32[1,1,5]{2,1,0:T(1,128)} %cutoff_hbm.3, ...), custom_call_target="tpu_custom_call" | custom-call | bytes 5734932 | tf_op jit(solution)/shard_map/pallas_call | solution.py:280
  10.5 0.7 %collective-permute-start.1 = (f32[8,128,128]{2,1,0:T(8,128)S(1)}, f32[8,128,128]{2,1,0:T(8,128)S(1)}, u32[]{:S(2)}, u32[]{:S(2)}) collective-permute-start(f32[8,128,128]{2,1,0:T(8,128)S(1)} %get-tuple-element.53), channel_id=1, source_target_pairs={{0,1},{1,0},{2,3},{3,2},{4,5},{5,4},{6,7},{7,6},{8,9},{9,8},{10,11... | collective-permute-start | bytes 1572872 | tf_op jit(solution)/shard_map/ppermute | solution.py:30
  11.3 2.1 %collective-permute-done.four = f32[4,128,128]{2,1,0:T(8,128)S(1)} collective-permute-done((f32[4,128,128]{2,1,0:T(8,128)S(1)}, f32[4,128,128]{2,1,0:T(8,128)S(1)}, u32[]{:S(2)}, u32[]{:S(2)}) %collective-permute-start) | collective-permute-done | bytes 262176 | tf_op jit(solution)/shard_map/ppermute | solution.py:30
  13.4 1.0 %shard_map.81 = (f32[4,128,128]{2,1,0:T(8,128)S(1)}, f32[384,640]{1,0:T(8,128)S(1)}, bf16[384,128]{1,0:T(8,128)(2,1)S(1)}, bf16[384,128]{1,0:T(8,128)(2,1)S(1)},...) custom-call(bf16[384,640]{1,0:T(8,128)(2,1)S(1)} %get-tuple-element.47.left_high, ...), custom_call_target="tpu_custom_call" | custom-call | flops 100663296000 | bytes 5832704 | tf_op jit(solution)/shard_map/pallas_call | solution.py:280
  14.5 0.8 %collective-permute-start.4 = (f32[4,128,128]{2,1,0:T(8,128)S(1)}, f32[4,128,128]{2,1,0:T(8,128)S(1)}, u32[]{:S(2)}, u32[]{:S(2)}) collective-permute-start(f32[4,128,128]{2,1,0:T(8,128)S(1)} %get-tuple-element.74), channel_id=1, source_target_pairs={{1,2},{2,1},{3,0},{0,3},{5,6},{6,5},{7,4},{4,7},{9,10},{10,9},{11,... | collective-permute-start | bytes 786440 | tf_op jit(solution)/shard_map/ppermute | solution.py:30
  15.2 0.5 %collective-permute-start.5 = (f32[4,128,128]{2,1,0:T(8,128)S(1)}, f32[4,128,128]{2,1,0:T(8,128)S(1)}, u32[]{:S(2)}, u32[]{:S(2)}) collective-permute-start(f32[4,128,128]{2,1,0:T(8,128)S(1)} %get-tuple-element.73.after), channel_id=1, source_target_pairs={{0,4},{4,0},{8,12},{12,8},{16,20},{20,16},{24,28},{28,24},{1,5},{5... | collective-permute-start | bytes 786440 | tf_op jit(solution)/shard_map/ppermute | solution.py:30
  15.8 0.0 collective-permute-done.1.three
  15.8 4.6 %collective-permute-start.6 = (f32[4,128,128]{2,1,0:T(8,128)S(1)}, f32[4,128,128]{2,1,0:T(8,128)S(1)}, u32[]{:S(2)}, u32[]{:S(2)}) collective-permute-start(f32[4,128,128]{2,1,0:T(8,128)S(1)} %get-tuple-element.78), channel_id=1, source_target_pairs={{4,8},{8,4},{12,16},{16,12},{20,24},{24,20},{28,0},{0,28},{5,9},{9... | collective-permute-start | bytes 786440 | tf_op jit(solution)/shard_map/ppermute | solution.py:30
  20.3 1.6 %shard_map.82 = (f32[384,128]{1,0:T(8,128)S(1)}, f32[2,2,128,128]{3,2,1,0:T(8,128)S(1)}, f32[3,1,1,5,128,128]{5,4,3,2,1,0:T(8,128)S(1)}) custom-call(bf16[384,640]{1,0:T(8,128)(2,1)S(1)} %get-tuple-element.47.left_high, bf16[384,640]{1,0:T(8,128)(2,1)S(1)} %get-tuple-element.48.left_low, f32[384,640]{1,0:T(8,128)S(1)} %get-tuple-element.51.start, ...), custom_call_target="tpu_custom_call" | custom-call | flops 176160768 | bytes 6094848 | tf_op jit(solution)/shard_map/pallas_call | solution.py:280
  22.0 0.0 collective-permute-done.2.one
  22.0 0.6 %shard_map.83 = (bf16[384,128]{1,0:T(8,128)(2,1)S(1)}, bf16[384,128]{1,0:T(8,128)(2,1)S(1)}, f32[384,128]{1,0:T(8,128)S(1)}, f32[2,128,128]{2,1,0:T(8,128)S(1)}) custom-call(bf16[384,640]{1,0:T(8,128)(2,1)S(1)} %get-tuple-element.47.left_high, bf16[384,640]{1,0:T(8,128)(2,1)S(1)} %get-tuple-element.48.left_low, f32[384,640]{1,0:T(8,128)S(1)} %get-tuple-element.51.start, ...), custom_call_target="tpu_custom_call" | custom-call | flops 125829120 | bytes 4128768 | tf_op jit(solution)/shard_map/pallas_call | solution.py:280
  22.6 0.0 collective-permute-done.3.two
  22.6 0.9 %shard_map.84 = (f32[4,128,128]{2,1,0:T(8,128)S(1)}, bf16[384,128]{1,0:T(8,128)(2,1)S(1)}, bf16[384,128]{1,0:T(8,128)(2,1)S(1)}, bf16[384,128]{1,0:T(8,128)(2,1)...) custom-call(bf16[384,640]{1,0:T(8,128)(2,1)S(1)} %get-tuple-element., ...), custom_call_target="tpu_custom_call" | custom-call | flops 276824064 | bytes 7280640 | tf_op jit(solution)/shard_map/pallas_call | solution.py:280
  23.5 0.1 collective-permute-start.9
  23.7 0.0 collective-permute-start.7
  23.7 1.1 %collective-permute-done.9.arrived.c3 = f32[3,128]{1,0:T(4,128)S(1)} collective-permute-done((f32[3,128]{1,0:T(4,128)S(1)}, f32[3,128]{1,0:T(4,128)S(1)}, u32[]{:S(2)}, u32[]{:S(2)}) %collective-permute-start.9) | collective-permute-done | bytes 1568 | tf_op jit(solution)/shard_map/ppermute | solution.py:30
  24.7 0.8 %collective-permute-start.8 = (f32[3,128]{1,0:T(4,128)S(1)}, f32[3,128]{1,0:T(4,128)S(1)}, u32[]{:S(2)}, u32[]{:S(2)}) collective-permute-start(f32[3,128]{1,0:T(4,128)S(1)} %get-tuple-element.80), channel_id=1, source_target_pairs={{4,8},{8,4},{12,16},{16,12},{20,24},{24,20},{28,0},{0,28},{5,9},{9... | collective-permute-start | bytes 4616 | tf_op jit(solution)/shard_map/ppermute | solution.py:30
  25.6 0.0 collective-permute-done.4.four
  25.6 0.5 %collective-permute-start.10 = (f32[3,128]{1,0:T(4,128)S(1)}, f32[3,128]{1,0:T(4,128)S(1)}, u32[]{:S(2)}, u32[]{:S(2)}) collective-permute-start(f32[3,128]{1,0:T(4,128)S(1)} %shard_map.87), channel_id=1, source_target_pairs={{1,2},{2,1},{3,0},{0,3},{5,6},{6,5},{7,4},{4,7},{9,10},{10,9},{11,... | collective-permute-start | bytes 4616 | tf_op jit(solution)/shard_map/ppermute | solution.py:30
  26.1 1.2 %shard_map.86 = (f32[2,1,1,5,128,128]{5,4,3,2,1,0:T(8,128)}, f32[3,128,128]{2,1,0:T(8,128)S(1)}, f32[128,128]{1,0:T(8,128)S(1)}, f32[3,128]{1,0:T(4,128)S(1)}) custom-call(f32[3,5,128,128]{3,2,1,0:T(8,128)S(1)} %get-tuple-element.46.held, f32[4,128,128]{2,1,0:T(8,128)S(1)} %get-tuple-element.65.new, bf16[384,640]{1,0:T(8,128)(2,1)S(1)} %get-tuple-element.47.left_high, ...), custom_call_target="tpu_custom_call" | custom-call | flops 125829120 | bytes 6030848 | tf_op jit(solution)/shard_map/pallas_call | solution.py:280
  27.3 2.4 %collective-permute-done.5.one = f32[4,128,128]{2,1,0:T(8,128)S(1)} collective-permute-done((f32[4,128,128]{2,1,0:T(8,128)S(1)}, f32[4,128,128]{2,1,0:T(8,128)S(1)}, u32[]{:S(2)}, u32[]{:S(2)}) %collective-permute-start.5) | collective-permute-done | bytes 262176 | tf_op jit(solution)/shard_map/ppermute | solution.py:30
  29.8 0.0 collective-permute-done.6.two
  29.8 0.0 collective-permute-done.7.c1
  29.8 1.2 %collective-permute-done.8.c2 = f32[3,128]{1,0:T(4,128)S(1)} collective-permute-done((f32[3,128]{1,0:T(4,128)S(1)}, f32[3,128]{1,0:T(4,128)S(1)}, u32[]{:S(2)}, u32[]{:S(2)}) %collective-permute-start.8) | collective-permute-done | bytes 1568 | tf_op jit(solution)/shard_map/ppermute | solution.py:30
  31.0 0.0 collective-permute-done.10.c4
  31.0 1.3 %shard_map.88 = (f32[2,1,1,5,128,128]{5,4,3,2,1,0:T(8,128)}, f32[3,1,64]{2,1,0:T(1,128)}) custom-call(f32[3,5,128,128]{3,2,1,0:T(8,128)S(1)} %get-tuple-element.46.held, f32[3,1,1,5,128,128]{5,4,3,2,1,0:T(8,128)S(1)} %get-tuple-element.54.der_ref, f32[64,128]{1,0:T(8,128)S(1)} %get-tuple-element.55.members, ...), custom_call_target="tpu_custom_call", output_to_operand_aliasing={{0}: (16, {})} | custom-call | flops 125829120 | bytes 4890880 | tf_op jit(solution)/shard_map/pallas_call | solution.py:280
  (4 shorter events, 0.1 us)
Async XLA Ops:
  1.7 20.2 %collective-permute-start.2 = (f32[4,128,128]{2,1,0:T(8,128)S(1)}, f32[4,128,128]{2,1,0:T(8,128)S(1)}, u32[]{:S(2)}, u32[]{:S(2)}) collective-permute-start(f32[4,128,128]{2,1,0:T(8,128)S(1)} %get-tuple-element.44.message), channel_id=1, source_target_pairs={{0,4},{4,0},{8,12},{12,8},{16,20},{20,16},{24,28},{28,24},{1,5},{5... | collective-permute-start | bytes 786440 | tf_op jit(solution)/shard_map/ppermute | solution.py:30
  4.8 8.6 %collective-permute-start = (f32[4,128,128]{2,1,0:T(8,128)S(1)}, f32[4,128,128]{2,1,0:T(8,128)S(1)}, u32[]{:S(2)}, u32[]{:S(2)}) collective-permute-start(f32[4,128,128]{2,1,0:T(8,128)S(1)} %shard_map.78.message), channel_id=1, source_target_pairs={{1,2},{2,1},{3,0},{0,3},{5,6},{6,5},{7,4},{4,7},{9,10},{10,9},{11,... | collective-permute-start | bytes 786440 | tf_op jit(solution)/shard_map/ppermute | solution.py:30
  5.5 17.1 %collective-permute-start.3 = (f32[4,128,128]{2,1,0:T(8,128)S(1)}, f32[4,128,128]{2,1,0:T(8,128)S(1)}, u32[]{:S(2)}, u32[]{:S(2)}) collective-permute-start(f32[4,128,128]{2,1,0:T(8,128)S(1)} %shard_map.79.after), channel_id=1, source_target_pairs={{4,8},{8,4},{12,16},{16,12},{20,24},{24,20},{28,0},{0,28},{5,9},{9... | collective-permute-start | bytes 786440 | tf_op jit(solution)/shard_map/ppermute | solution.py:30
  10.5 5.2 %collective-permute-start.1 = (f32[8,128,128]{2,1,0:T(8,128)S(1)}, f32[8,128,128]{2,1,0:T(8,128)S(1)}, u32[]{:S(2)}, u32[]{:S(2)}) collective-permute-start(f32[8,128,128]{2,1,0:T(8,128)S(1)} %get-tuple-element.53), channel_id=1, source_target_pairs={{0,1},{1,0},{2,3},{3,2},{4,5},{5,4},{6,7},{7,6},{8,9},{9,8},{10,11... | collective-permute-start | bytes 1572872 | tf_op jit(solution)/shard_map/ppermute | solution.py:30
  14.5 11.1 %collective-permute-start.4 = (f32[4,128,128]{2,1,0:T(8,128)S(1)}, f32[4,128,128]{2,1,0:T(8,128)S(1)}, u32[]{:S(2)}, u32[]{:S(2)}) collective-permute-start(f32[4,128,128]{2,1,0:T(8,128)S(1)} %get-tuple-element.74), channel_id=1, source_target_pairs={{1,2},{2,1},{3,0},{0,3},{5,6},{6,5},{7,4},{4,7},{9,10},{10,9},{11,... | collective-permute-start | bytes 786440 | tf_op jit(solution)/shard_map/ppermute | solution.py:30
  15.2 14.5 %collective-permute-start.5 = (f32[4,128,128]{2,1,0:T(8,128)S(1)}, f32[4,128,128]{2,1,0:T(8,128)S(1)}, u32[]{:S(2)}, u32[]{:S(2)}) collective-permute-start(f32[4,128,128]{2,1,0:T(8,128)S(1)} %get-tuple-element.73.after), channel_id=1, source_target_pairs={{0,4},{4,0},{8,12},{12,8},{16,20},{20,16},{24,28},{28,24},{1,5},{5... | collective-permute-start | bytes 786440 | tf_op jit(solution)/shard_map/ppermute | solution.py:30
  15.8 14.0 %collective-permute-start.6 = (f32[4,128,128]{2,1,0:T(8,128)S(1)}, f32[4,128,128]{2,1,0:T(8,128)S(1)}, u32[]{:S(2)}, u32[]{:S(2)}) collective-permute-start(f32[4,128,128]{2,1,0:T(8,128)S(1)} %get-tuple-element.78), channel_id=1, source_target_pairs={{4,8},{8,4},{12,16},{16,12},{20,24},{24,20},{28,0},{0,28},{5,9},{9... | collective-permute-start | bytes 786440 | tf_op jit(solution)/shard_map/ppermute | solution.py:30
  23.5 1.2 %collective-permute-start.9 = (f32[3,128]{1,0:T(4,128)S(1)}, f32[3,128]{1,0:T(4,128)S(1)}, u32[]{:S(2)}, u32[]{:S(2)}) collective-permute-start(f32[3,128]{1,0:T(4,128)S(1)} %get-tuple-element.81), channel_id=1, source_target_pairs={{0,1},{1,0},{2,3},{3,2},{4,5},{5,4},{6,7},{7,6},{8,9},{9,8},{10,11... | collective-permute-start | bytes 4616 | tf_op jit(solution)/shard_map/ppermute | solution.py:30
  23.7 6.1 %collective-permute-start.7 = (f32[3,128]{1,0:T(4,128)S(1)}, f32[3,128]{1,0:T(4,128)S(1)}, u32[]{:S(2)}, u32[]{:S(2)}) collective-permute-start(f32[3,128]{1,0:T(4,128)S(1)} %get-tuple-element.79), channel_id=1, source_target_pairs={{0,4},{4,0},{8,12},{12,8},{16,20},{20,16},{24,28},{28,24},{1,5},{5... | collective-permute-start | bytes 4616 | tf_op jit(solution)/shard_map/ppermute | solution.py:30
  24.7 6.3 %collective-permute-start.8 = (f32[3,128]{1,0:T(4,128)S(1)}, f32[3,128]{1,0:T(4,128)S(1)}, u32[]{:S(2)}, u32[]{:S(2)}) collective-permute-start(f32[3,128]{1,0:T(4,128)S(1)} %get-tuple-element.80), channel_id=1, source_target_pairs={{4,8},{8,4},{12,16},{16,12},{20,24},{24,20},{28,0},{0,28},{5,9},{9... | collective-permute-start | bytes 4616 | tf_op jit(solution)/shard_map/ppermute | solution.py:30
  25.6 5.4 %collective-permute-start.10 = (f32[3,128]{1,0:T(4,128)S(1)}, f32[3,128]{1,0:T(4,128)S(1)}, u32[]{:S(2)}, u32[]{:S(2)}) collective-permute-start(f32[3,128]{1,0:T(4,128)S(1)} %shard_map.87), channel_id=1, source_target_pairs={{1,2},{2,1},{3,0},{0,3},{5,6},{6,5},{7,4},{4,7},{9,10},{10,9},{11,... | collective-permute-start | bytes 4616 | tf_op jit(solution)/shard_map/ppermute | solution.py:30

commit v17 on v14

--- a/solution.py
+++ b/solution.py
@@ -140,7 +140,7 @@
                 left_high[rows, cols(place)], left_low[rows, cols(place)] = split(block)
     owners.wait()
     atoms = jnp.broadcast_to(atom_ref[0], (ATOMS, B))
-    members[...] = -(lax.broadcasted_iota(jnp.int32, (ATOMS, B), 0) == atoms).astype(f32)
+    members[...] = (-(lax.broadcasted_iota(jnp.int32, (ATOMS, B), 0) == atoms).astype(f32)).astype(bf16)
 
 
 def first_half(left, place, start, near, diagonal):
@@ -264,27 +264,28 @@
     prop, inner = rows_of(beside((high_one[...], low_one[...]), (high_two[...], low_two[...])))
     near = [tuple(jnp.concatenate(x, axis=0) for x in zip(split(one[1 + kind]), split(two[1 + kind]))) for kind in range(3)]
     behind = dot(inner, near[0])
-    real_new = held[1, 0] + time_step * (imag_part[...] + dot(prop, near[2]) - behind[B:])
+    ahead = dot(prop, beside(near[2], near[1]))
+    real_new = held[1, 0] + time_step * (imag_part[...] + ahead[:, :B] - behind[B:])
     new[0] = real_new
-    copies = start_all([pltpu.make_async_copy(new.at[0], out_hbm.at[0, 0, 0, 0], sems.at[0])])
-    new[1] = held[2, 0] - time_step * (comm[0] + dot(prop, near[1]) - behind[:B])
-    for place, message, mixed in ((1, one, (high_one, low_one)), (2, two, (high_two, low_two))):
-        added = dot(rows_of((mixed[0][...], mixed[1][...]))[0], split(message[0]))
-        new[1 + place] = held[2, place] - time_step * (comm[place] + added)
-    copies += start_all(
-        [pltpu.make_async_copy(new.at[1 + at], out_hbm.at[1, 0, 0, order[at]], sems.at[1 + at]) for at in range(3)]
-    )
+    new[1] = held[2, 0] - time_step * (comm[0] + ahead[:, B:] - behind[:B])
+    copies = start_all([pltpu.make_async_copy(new.at[at], out_hbm.at[at, 0, 0, 0], sems.at[at]) for at in range(2)])
     parts = []
     for direction in range(3):
         product = real_new * der_ref[direction, 0, 0, 0]
         parts.append(jnp.sum(product + product.T, axis=0, keepdims=True))
     orbital = jnp.concatenate(parts, axis=0) + row_part[...] + ((c1[...] + c2[...]) + (c3[...] + c4[...]))
-    forces = lax.dot_general(
-        orbital, members[...], (((1,), (1,)), ((), ())), precision=lax.Precision.HIGHEST, preferred_element_type=f32
-    )
+    forces = jnp.zeros((3, ATOMS), f32)
+    for some in split(orbital):
+        forces = forces + lax.dot_general(some, members[...], (((1,), (1,)), ((), ())), preferred_element_type=f32)
     for direction in range(3):
         forces_ref[direction] = forces[direction : direction + 1]
     copies += start_all([pltpu.make_async_copy(forces_ref, forces_hbm, sems.at[4])])
+    for place, message, mixed in ((1, one, (high_one, low_one)), (2, two, (high_two, low_two))):
+        added = dot(rows_of((mixed[0][...], mixed[1][...]))[0], split(message[0]))
+        new[1 + place] = held[2, place] - time_step * (comm[place] + added)
+        copies += start_all(
+            [pltpu.make_async_copy(new.at[1 + place], out_hbm.at[1, 0, 0, order[place]], sems.at[1 + place])]
+        )
     for copy in copies:
         copy.wait()
 
@@ -339,7 +340,7 @@
     ham = [shape(B, 5 * B, kind=bf16)] * 2
     held, left_high, left_low, ham_high, ham_low, members = call(
         second_kernel,
-        [shape(3, 5, B, B)] + left + ham + [shape(ATOMS, B)],
+        [shape(3, 5, B, B)] + left + ham + [shape(ATOMS, B, kind=bf16)],
         [hbm] * 6,
         2000,
         (cutoff, hamiltonian, inverse_margin, density, atom_of, send_three),

time: 31.1 us -> 31.1 us (level)
  no operation moved by 1% of the time
where the time goes in v17:
time: 31.1 us; the launch traced here: 30.8 us
  starting transfers between devices  16.8 us (54%)
  Pallas kernels  9.54 us (31%)
  waiting for transfers between devices  3.74 us (12%)
  between operations  0.75 us (2%)
    ppermute x11, starting transfers between devices, swapped(): return lax.ppermute(cells, axis, pairs)  16.8 us
    pallas_call x13, Pallas kernels, call(): pl.pallas_call(kernel, out_shape=shapes, in_specs=in_specs, out_specs=out...  9.54 us
    ppermute x11, waiting for transfers between devices, swapped(): return lax.ppermute(cells, axis, pairs)  3.74 us
  transfers between devices with their start and end apart: 11, of which 3 were waited for; matrix products, arithmetic and copies ran while one was open for 0% of the time, Pallas kernels for 23%

profile of v17, /device:TPU:0, one launch (start us, length us, event | category | flops | bytes accessed | tf_op | source)
XLA Modules:
  0.0 30.8 jit_solution(17388954921109209316)
XLA Ops:
  0.6 1.1 %shard_map.77 = (f32[4,128,128]{2,1,0:T(8,128)S(1)}, f32[2,128,128]{2,1,0:T(8,128)S(1)}) custom-call(s32[1,1,5]{2,1,0:T(1,128)} %cutoff_hbm.5, f32[1,1,5,128,128]{4,3,2,1,0:T(8,128)} %ham_hbm.5, f32[1,1,5,128,128]{4,3,2,1,0:T(8,128)} %inv_hbm.5, f32[2,1,1,5,128,128]{5,4,3,2,1,0:T(8,128)} %rho_hbm.5), custom_call_target="tpu_custom_call" | custom-call | bytes 1703956 | tf_op jit(solution)/shard_map/pallas_call | solution.py:295
  1.7 3.0 %collective-permute-start.2 = (f32[4,128,128]{2,1,0:T(8,128)S(1)}, f32[4,128,128]{2,1,0:T(8,128)S(1)}, u32[]{:S(2)}, u32[]{:S(2)}) collective-permute-start(f32[4,128,128]{2,1,0:T(8,128)S(1)} %get-tuple-element.43.message), channel_id=1, source_target_pairs={{0,4},{4,0},{8,12},{12,8},{16,20},{20,16},{24,28},{28,24},{1,5},{5... | collective-permute-start | bytes 786440 | tf_op jit(solution)/shard_map/ppermute | solution.py:30
  4.8 0.7 %collective-permute-start.1 = (f32[4,128,128]{2,1,0:T(8,128)S(1)}, f32[4,128,128]{2,1,0:T(8,128)S(1)}, u32[]{:S(2)}, u32[]{:S(2)}) collective-permute-start(f32[4,128,128]{2,1,0:T(8,128)S(1)} %shard_map.78.message), channel_id=1, source_target_pairs={{1,2},{2,1},{3,0},{0,3},{5,6},{6,5},{7,4},{4,7},{9,10},{10,9},{11,... | collective-permute-start | bytes 786440 | tf_op jit(solution)/shard_map/ppermute | solution.py:30
  5.5 3.6 %collective-permute-start.3 = (f32[4,128,128]{2,1,0:T(8,128)S(1)}, f32[4,128,128]{2,1,0:T(8,128)S(1)}, u32[]{:S(2)}, u32[]{:S(2)}) collective-permute-start(f32[4,128,128]{2,1,0:T(8,128)S(1)} %shard_map.79.message), channel_id=1, source_target_pairs={{4,8},{8,4},{12,16},{16,12},{20,24},{24,20},{28,0},{0,28},{5,9},{9... | collective-permute-start | bytes 786440 | tf_op jit(solution)/shard_map/ppermute | solution.py:30
  9.1 1.0 %shard_map.80.after = f32[8,128,128]{2,1,0:T(8,128)S(1)} custom-call(s32[1,1,5]{2,1,0:T(1,128)} %cutoff_hbm.5, f32[1,1,5,128,128]{4,3,2,1,0:T(8,128)} %ham_hbm.5, f32[1,1,5,128,128]{4,3,2,1,0:T(8,128)} %inv_hbm.5, f32[2,1,1,5,128,128]{5,4,3,2,1,0:T(8,128)} %rho_hbm.5, f32[4,128,128]{2,1,0:T(8,128)S(1)} %shard_map.79.message), custom_call_target="tpu_custom_call" | custom-call | flops 6291456000 | bytes 2097172 | tf_op jit(solution)/shard_map/pallas_call | solution.py:295
  10.2 0.7 %collective-permute-start = (f32[8,128,128]{2,1,0:T(8,128)S(1)}, f32[8,128,128]{2,1,0:T(8,128)S(1)}, u32[]{:S(2)}, u32[]{:S(2)}) collective-permute-start(f32[8,128,128]{2,1,0:T(8,128)S(1)} %shard_map.80.after), channel_id=1, source_target_pairs={{0,1},{1,0},{2,3},{3,2},{4,5},{5,4},{6,7},{7,6},{8,9},{9,8},{10,11... | collective-permute-start | bytes 1572872 | tf_op jit(solution)/shard_map/ppermute | solution.py:30
  10.9 1.4 %shard_map.81 = (f32[3,5,128,128]{3,2,1,0:T(8,128)S(1)}, bf16[384,640]{1,0:T(8,128)(2,1)S(1)}, bf16[384,640]{1,0:T(8,128)(2,1)S(1)}, bf16[128,640]{1,0:T(8,128)(...) custom-call(s32[1,1,5]{2,1,0:T(1,128)} %cutoff_hbm.5, f32[1,1,5,128,128]{4,3,2,1,0:T(8,128)} %ham_hbm.5, ...), custom_call_target="tpu_custom_call" | custom-call | flops 25165824000 | bytes 5472788 | tf_op jit(solution)/shard_map/pallas_call | solution.py:295
  12.3 0.1 collective-permute-done.three
  12.4 1.2 %shard_map.82 = (f32[384,640]{1,0:T(8,128)S(1)}, f32[384,128]{1,0:T(8,128)S(1)}, f32[2,2,128,128]{3,2,1,0:T(8,128)S(1)}, f32[3,1,1,5,128,128]{5,4,3,2,1,0:T(8,128)S(1)}) custom-call(bf16[384,640]{1,0:T(8,128)(2,1)S(1)} %get-tuple-element.46.left_high, bf16[384,640]{1,0:T(8,128)(2,1)S(1)} %get-tuple-element.47.left_low, ...), custom_call_target="tpu_custom_call" | custom-call | flops 100663296000 | bytes 7536640 | tf_op jit(solution)/shard_map/pallas_call | solution.py:295
  13.7 0.0 collective-permute-done.1.four
  13.7 0.6 %shard_map.83 = (f32[4,128,128]{2,1,0:T(8,128)S(1)}, bf16[384,128]{1,0:T(8,128)(2,1)S(1)}, bf16[384,128]{1,0:T(8,128)(2,1)S(1)}, f32[384,128]{1,0:T(8,128)S(1)}, f32[2,128,128]{2,1,0:T(8,128)S(1)}) custom-call(bf16[384,640]{1,0:T(8,128)(2,1)S(1)} %get-tuple-element.46.left_high, bf16[384,640]{1,0:T(8,128)(2,1)S(1)} %get-tuple-element.47.left_low, ...), custom_call_target="tpu_custom_call" | custom-call | flops 100663296 | bytes 5373952 | tf_op jit(solution)/shard_map/pallas_call | solution.py:295
  14.4 0.6 %collective-permute-start.4 = (f32[4,128,128]{2,1,0:T(8,128)S(1)}, f32[4,128,128]{2,1,0:T(8,128)S(1)}, u32[]{:S(2)}, u32[]{:S(2)}) collective-permute-start(f32[4,128,128]{2,1,0:T(8,128)S(1)} %get-tuple-element.72), channel_id=1, source_target_pairs={{1,2},{2,1},{3,0},{0,3},{5,6},{6,5},{7,4},{4,7},{9,10},{10,9},{11,... | collective-permute-start | bytes 786440 | tf_op jit(solution)/shard_map/ppermute | solution.py:30
  14.9 0.4 %collective-permute-start.5 = (f32[4,128,128]{2,1,0:T(8,128)S(1)}, f32[4,128,128]{2,1,0:T(8,128)S(1)}, u32[]{:S(2)}, u32[]{:S(2)}) collective-permute-start(f32[4,128,128]{2,1,0:T(8,128)S(1)} %get-tuple-element.71.after), channel_id=1, source_target_pairs={{0,4},{4,0},{8,12},{12,8},{16,20},{20,16},{24,28},{28,24},{1,5},{5... | collective-permute-start | bytes 786440 | tf_op jit(solution)/shard_map/ppermute | solution.py:30
  15.4 4.6 %collective-permute-start.6 = (f32[4,128,128]{2,1,0:T(8,128)S(1)}, f32[4,128,128]{2,1,0:T(8,128)S(1)}, u32[]{:S(2)}, u32[]{:S(2)}) collective-permute-start(f32[4,128,128]{2,1,0:T(8,128)S(1)} %get-tuple-element.76), channel_id=1, source_target_pairs={{4,8},{8,4},{12,16},{16,12},{20,24},{24,20},{28,0},{0,28},{5,9},{9... | collective-permute-start | bytes 786440 | tf_op jit(solution)/shard_map/ppermute | solution.py:30
  19.9 0.0 collective-permute-done.2.one
  19.9 0.6 %shard_map.84 = (bf16[384,128]{1,0:T(8,128)(2,1)S(1)}, bf16[384,128]{1,0:T(8,128)(2,1)S(1)}, f32[384,128]{1,0:T(8,128)S(1)}, f32[2,128,128]{2,1,0:T(8,128)S(1)}) custom-call(bf16[384,640]{1,0:T(8,128)(2,1)S(1)} %get-tuple-element.46.left_high, bf16[384,640]{1,0:T(8,128)(2,1)S(1)} %get-tuple-element.47.left_low, f32[384,640]{1,0:T(8,128)S(1)} %get-tuple-element.52.start, ...), custom_call_target="tpu_custom_call" | custom-call | flops 125829120 | bytes 4128768 | tf_op jit(solution)/shard_map/pallas_call | solution.py:295
  20.6 0.0 collective-permute-done.3.two
  20.6 0.9 %shard_map.85 = (f32[4,128,128]{2,1,0:T(8,128)S(1)}, bf16[384,128]{1,0:T(8,128)(2,1)S(1)}, bf16[384,128]{1,0:T(8,128)(2,1)S(1)}, bf16[384,128]{1,0:T(8,128)(2,1)...) custom-call(bf16[384,640]{1,0:T(8,128)(2,1)S(1)} %get-tuple-element., ...), custom_call_target="tpu_custom_call" | custom-call | flops 276824064 | bytes 7280640 | tf_op jit(solution)/shard_map/pallas_call | solution.py:295
  21.5 0.1 collective-permute-start.9
  21.7 0.0 collective-permute-start.7
  21.7 1.1 %collective-permute-done.9.arrived.c3 = f32[3,128]{1,0:T(4,128)S(1)} collective-permute-done((f32[3,128]{1,0:T(4,128)S(1)}, f32[3,128]{1,0:T(4,128)S(1)}, u32[]{:S(2)}, u32[]{:S(2)}) %collective-permute-start.9) | collective-permute-done | bytes 1568 | tf_op jit(solution)/shard_map/ppermute | solution.py:30
  22.7 1.5 %collective-permute-start.8 = (f32[3,128]{1,0:T(4,128)S(1)}, f32[3,128]{1,0:T(4,128)S(1)}, u32[]{:S(2)}, u32[]{:S(2)}) collective-permute-start(f32[3,128]{1,0:T(4,128)S(1)} %get-tuple-element.78), channel_id=1, source_target_pairs={{4,8},{8,4},{12,16},{16,12},{20,24},{24,20},{28,0},{0,28},{5,9},{9... | collective-permute-start | bytes 4616 | tf_op jit(solution)/shard_map/ppermute | solution.py:30
  24.2 0.0 collective-permute-done.4.four
  24.2 1.5 %collective-permute-start.10 = (f32[3,128]{1,0:T(4,128)S(1)}, f32[3,128]{1,0:T(4,128)S(1)}, u32[]{:S(2)}, u32[]{:S(2)}) collective-permute-start(f32[3,128]{1,0:T(4,128)S(1)} %shard_map.88), channel_id=1, source_target_pairs={{1,2},{2,1},{3,0},{0,3},{5,6},{6,5},{7,4},{4,7},{9,10},{10,9},{11,... | collective-permute-start | bytes 4616 | tf_op jit(solution)/shard_map/ppermute | solution.py:30
  25.7 1.2 %shard_map.87 = (f32[2,1,1,5,128,128]{5,4,3,2,1,0:T(8,128)}, f32[3,128,128]{2,1,0:T(8,128)S(1)}, f32[128,128]{1,0:T(8,128)S(1)}, f32[3,128]{1,0:T(4,128)S(1)}) custom-call(f32[3,5,128,128]{3,2,1,0:T(8,128)S(1)} %get-tuple-element.45.held, f32[4,128,128]{2,1,0:T(8,128)S(1)} %get-tuple-element.63.new, bf16[384,640]{1,0:T(8,128)(2,1)S(1)} %get-tuple-element.46.left_high, ...), custom_call_target="tpu_custom_call" | custom-call | flops 125829120 | bytes 6030848 | tf_op jit(solution)/shard_map/pallas_call | solution.py:295
  26.9 2.5 %collective-permute-done.7.c1 = f32[3,128]{1,0:T(4,128)S(1)} collective-permute-done((f32[3,128]{1,0:T(4,128)S(1)}, f32[3,128]{1,0:T(4,128)S(1)}, u32[]{:S(2)}, u32[]{:S(2)}) %collective-permute-start.7) | collective-permute-done | bytes 1568 | tf_op jit(solution)/shard_map/ppermute | solution.py:30
  29.4 0.0 collective-permute-done.8.c2
  29.4 0.0 collective-permute-done.10.c4
  29.4 0.0 collective-permute-done.5.one
  29.4 0.0 collective-permute-done.6.two
  29.5 1.4 %shard_map.89 = (f32[2,1,1,5,128,128]{5,4,3,2,1,0:T(8,128)}, f32[3,1,64]{2,1,0:T(1,128)}) custom-call(f32[3,5,128,128]{3,2,1,0:T(8,128)S(1)} %get-tuple-element.45.held, f32[3,1,1,5,128,128]{5,4,3,2,1,0:T(8,128)S(1)} %get-tuple-element.50.der_ref, bf16[64,128]{1,0:T(8,128)(2,1)S(1)} %get-tuple-element.51.members, ...), custom_call_target="tpu_custom_call", output_to_operand_aliasing={{0}: (16, {})} | custom-call | flops 125829120 | bytes 4890880 | tf_op jit(solution)/shard_map/pallas_call | solution.py:295
  (4 shorter events, 0.1 us)
Async XLA Ops:
  1.7 18.2 %collective-permute-start.2 = (f32[4,128,128]{2,1,0:T(8,128)S(1)}, f32[4,128,128]{2,1,0:T(8,128)S(1)}, u32[]{:S(2)}, u32[]{:S(2)}) collective-permute-start(f32[4,128,128]{2,1,0:T(8,128)S(1)} %get-tuple-element.43.message), channel_id=1, source_target_pairs={{0,4},{4,0},{8,12},{12,8},{16,20},{20,16},{24,28},{28,24},{1,5},{5... | collective-permute-start | bytes 786440 | tf_op jit(solution)/shard_map/ppermute | solution.py:30
  4.8 8.9 %collective-permute-start.1 = (f32[4,128,128]{2,1,0:T(8,128)S(1)}, f32[4,128,128]{2,1,0:T(8,128)S(1)}, u32[]{:S(2)}, u32[]{:S(2)}) collective-permute-start(f32[4,128,128]{2,1,0:T(8,128)S(1)} %shard_map.78.message), channel_id=1, source_target_pairs={{1,2},{2,1},{3,0},{0,3},{5,6},{6,5},{7,4},{4,7},{9,10},{10,9},{11,... | collective-permute-start | bytes 786440 | tf_op jit(solution)/shard_map/ppermute | solution.py:30
  5.5 15.0 %collective-permute-start.3 = (f32[4,128,128]{2,1,0:T(8,128)S(1)}, f32[4,128,128]{2,1,0:T(8,128)S(1)}, u32[]{:S(2)}, u32[]{:S(2)}) collective-permute-start(f32[4,128,128]{2,1,0:T(8,128)S(1)} %shard_map.79.message), channel_id=1, source_target_pairs={{4,8},{8,4},{12,16},{16,12},{20,24},{24,20},{28,0},{0,28},{5,9},{9... | collective-permute-start | bytes 786440 | tf_op jit(solution)/shard_map/ppermute | solution.py:30
  10.2 2.3 %collective-permute-start = (f32[8,128,128]{2,1,0:T(8,128)S(1)}, f32[8,128,128]{2,1,0:T(8,128)S(1)}, u32[]{:S(2)}, u32[]{:S(2)}) collective-permute-start(f32[8,128,128]{2,1,0:T(8,128)S(1)} %shard_map.80.after), channel_id=1, source_target_pairs={{0,1},{1,0},{2,3},{3,2},{4,5},{5,4},{6,7},{7,6},{8,9},{9,8},{10,11... | collective-permute-start | bytes 1572872 | tf_op jit(solution)/shard_map/ppermute | solution.py:30
  14.4 9.9 %collective-permute-start.4 = (f32[4,128,128]{2,1,0:T(8,128)S(1)}, f32[4,128,128]{2,1,0:T(8,128)S(1)}, u32[]{:S(2)}, u32[]{:S(2)}) collective-permute-start(f32[4,128,128]{2,1,0:T(8,128)S(1)} %get-tuple-element.72), channel_id=1, source_target_pairs={{1,2},{2,1},{3,0},{0,3},{5,6},{6,5},{7,4},{4,7},{9,10},{10,9},{11,... | collective-permute-start | bytes 786440 | tf_op jit(solution)/shard_map/ppermute | solution.py:30
  14.9 14.5 %collective-permute-start.5 = (f32[4,128,128]{2,1,0:T(8,128)S(1)}, f32[4,128,128]{2,1,0:T(8,128)S(1)}, u32[]{:S(2)}, u32[]{:S(2)}) collective-permute-start(f32[4,128,128]{2,1,0:T(8,128)S(1)} %get-tuple-element.71.after), channel_id=1, source_target_pairs={{0,4},{4,0},{8,12},{12,8},{16,20},{20,16},{24,28},{28,24},{1,5},{5... | collective-permute-start | bytes 786440 | tf_op jit(solution)/shard_map/ppermute | solution.py:30
  15.4 14.1 %collective-permute-start.6 = (f32[4,128,128]{2,1,0:T(8,128)S(1)}, f32[4,128,128]{2,1,0:T(8,128)S(1)}, u32[]{:S(2)}, u32[]{:S(2)}) collective-permute-start(f32[4,128,128]{2,1,0:T(8,128)S(1)} %get-tuple-element.76), channel_id=1, source_target_pairs={{4,8},{8,4},{12,16},{16,12},{20,24},{24,20},{28,0},{0,28},{5,9},{9... | collective-permute-start | bytes 786440 | tf_op jit(solution)/shard_map/ppermute | solution.py:30
  21.5 1.2 %collective-permute-start.9 = (f32[3,128]{1,0:T(4,128)S(1)}, f32[3,128]{1,0:T(4,128)S(1)}, u32[]{:S(2)}, u32[]{:S(2)}) collective-permute-start(f32[3,128]{1,0:T(4,128)S(1)} %get-tuple-element.79), channel_id=1, source_target_pairs={{0,1},{1,0},{2,3},{3,2},{4,5},{5,4},{6,7},{7,6},{8,9},{9,8},{10,11... | collective-permute-start | bytes 4616 | tf_op jit(solution)/shard_map/ppermute | solution.py:30
  21.7 7.8 %collective-permute-start.7 = (f32[3,128]{1,0:T(4,128)S(1)}, f32[3,128]{1,0:T(4,128)S(1)}, u32[]{:S(2)}, u32[]{:S(2)}) collective-permute-start(f32[3,128]{1,0:T(4,128)S(1)} %get-tuple-element.77), channel_id=1, source_target_pairs={{0,4},{4,0},{8,12},{12,8},{16,20},{20,16},{24,28},{28,24},{1,5},{5... | collective-permute-start | bytes 4616 | tf_op jit(solution)/shard_map/ppermute | solution.py:30
  22.7 6.7 %collective-permute-start.8 = (f32[3,128]{1,0:T(4,128)S(1)}, f32[3,128]{1,0:T(4,128)S(1)}, u32[]{:S(2)}, u32[]{:S(2)}) collective-permute-start(f32[3,128]{1,0:T(4,128)S(1)} %get-tuple-element.78), channel_id=1, source_target_pairs={{4,8},{8,4},{12,16},{16,12},{20,24},{24,20},{28,0},{0,28},{5,9},{9... | collective-permute-start | bytes 4616 | tf_op jit(solution)/shard_map/ppermute | solution.py:30
  24.2 5.2 %collective-permute-start.10 = (f32[3,128]{1,0:T(4,128)S(1)}, f32[3,128]{1,0:T(4,128)S(1)}, u32[]{:S(2)}, u32[]{:S(2)}) collective-permute-start(f32[3,128]{1,0:T(4,128)S(1)} %shard_map.88), channel_id=1, source_target_pairs={{1,2},{2,1},{3,0},{0,3},{5,6},{6,5},{7,4},{4,7},{9,10},{10,9},{11,... | collective-permute-start | bytes 4616 | tf_op jit(solution)/shard_map/ppermute | solution.py:30

commit v18 on v14

--- a/solution.py
+++ b/solution.py
@@ -28,6 +28,12 @@
         j = (i + 1) % count
         pairs += [(i, j), (j, i)]
     return lax.ppermute(cells, axis, pairs)
+
+
+def one_way(cells, first):
+    count = lax.axis_size("gy")
+    assert count % 2 == 0
+    return lax.ppermute(cells, "gy", [(i + first, i + 1 - first) for i in range(0, count, 2)])
 
 
 def order_of():
@@ -165,7 +171,8 @@
         more[1 + kind] = held[kind, place]
 
 
-def third_kernel(left_high, left_low, ham_high, ham_low, held, three, der_hbm, start, diagonal, other, der, sem):
+def third_kernel(left_high, left_low, ham_high, ham_low, held, up, down, der_hbm, start, diagonal, other, der, three, sem):
+    three[...] = up[...] + down[...]
     copy = pltpu.make_async_copy(der_hbm, der, sem)
     copy.start()
     left = (left_high, left_low)
@@ -334,7 +341,7 @@
         (cutoff, hamiltonian, inverse_margin, density, first_two),
         scratch=[flags, dma(()), dma((5,))],
     )
-    near_three = swapped(send_three, 3)
+    near_three = (one_way(send_three, 0), one_way(send_three, 1))
     left = [shape(3 * B, 5 * B, kind=bf16)] * 2
     ham = [shape(B, 5 * B, kind=bf16)] * 2
     held, left_high, left_low, ham_high, ham_low, members = call(
@@ -350,10 +357,10 @@
     start, diagonal, other_three, derivative = call(
         third_kernel,
         [shape(3 * B, 5 * B), shape(3 * B, B), shape(2, 2, B, B), shape(*derivative.shape)],
-        [vmem] * 6 + [hbm],
+        [vmem] * 7 + [hbm],
         8000,
-        (left_high, left_low, ham_high, ham_low, held, near_three, derivative),
-        scratch=[dma(())],
+        (left_high, left_low, ham_high, ham_low, held, *near_three, derivative),
+        scratch=[pltpu.VMEM((8, B, B), f32), dma(())],
     )
     one_more, high_four, low_four, diagonal, other_four = call(
         four_kernel,

time: 31.1 us -> 34.6 us (1.11)
  starting transfers between devices: 16.8 us -> 19 us
  waiting for transfers between devices: 3.75 us -> 5.04 us
    ppermute x0 -> x2, starting transfers between devices: none -> 4.38 us  [one_way(): lax.ppermute(cells, 'gy', [(i + first, i + 1 - first) for i in range(0, c...]
    ppermute x11 -> x10, starting transfers between devices: 16.8 us -> 14.6 us  [swapped(): return lax.ppermute(cells, axis, pairs)]
    ppermute x11 -> x10, waiting for transfers between devices: 3.75 us -> 4.98 us  [swapped(): return lax.ppermute(cells, axis, pairs)]
  transfers between devices with their start and end apart: 11 -> 12, of which waited for: 3 -> 3; matrix products, arithmetic and copies ran while one was open for 0% -> 0% of each run, Pallas kernels for 23% -> 21%
where the time goes in v18:
time: 34.6 us; the launch traced here: 34.3 us
  starting transfers between devices  19 us (55%)
  Pallas kernels  9.48 us (27%)
  waiting for transfers between devices  5.04 us (15%)
  between operations  0.77 us (2%)
    ppermute x10, starting transfers between devices, swapped(): return lax.ppermute(cells, axis, pairs)  14.6 us
    pallas_call x13, Pallas kernels, call(): pl.pallas_call(kernel, out_shape=shapes, in_specs=in_specs, out_specs=out...  9.48 us
    ppermute x10, waiting for transfers between devices, swapped(): return lax.ppermute(cells, axis, pairs)  4.98 us
    ppermute x2, starting transfers between devices, one_way(): lax.ppermute(cells, 'gy', [(i + first, i + 1 - first) for i in range(0, c...  4.38 us
  transfers between devices with their start and end apart: 12, of which 3 were waited for; matrix products, arithmetic and copies ran while one was open for 0% of the time, Pallas kernels for 21%

profile of v18, /device:TPU:0, one launch (start us, length us, event | category | flops | bytes accessed | tf_op | source)
XLA Modules:
  0.0 34.3 jit_solution(8359888927945390161)
XLA Ops:
  0.6 1.1 %shard_map.77 = (f32[4,128,128]{2,1,0:T(8,128)S(1)}, f32[2,128,128]{2,1,0:T(8,128)S(1)}) custom-call(s32[1,1,5]{2,1,0:T(1,128)} %cutoff_hbm.5, f32[1,1,5,128,128]{4,3,2,1,0:T(8,128)} %ham_hbm.5, f32[1,1,5,128,128]{4,3,2,1,0:T(8,128)} %inv_hbm.5, f32[2,1,1,5,128,128]{5,4,3,2,1,0:T(8,128)} %rho_hbm.5), custom_call_target="tpu_custom_call" | custom-call | bytes 1703956 | tf_op jit(solution)/shard_map/pallas_call | solution.py:301
  1.7 3.0 %collective-permute-start.3 = (f32[4,128,128]{2,1,0:T(8,128)S(1)}, f32[4,128,128]{2,1,0:T(8,128)S(1)}, u32[]{:S(2)}, u32[]{:S(2)}) collective-permute-start(f32[4,128,128]{2,1,0:T(8,128)S(1)} %get-tuple-element.43.message), channel_id=1, source_target_pairs={{0,4},{4,0},{8,12},{12,8},{16,20},{20,16},{24,28},{28,24},{1,5},{5... | collective-permute-start | bytes 786440 | tf_op jit(solution)/shard_map/ppermute | solution.py:30
  4.8 0.7 %collective-permute-start.2 = (f32[4,128,128]{2,1,0:T(8,128)S(1)}, f32[4,128,128]{2,1,0:T(8,128)S(1)}, u32[]{:S(2)}, u32[]{:S(2)}) collective-permute-start(f32[4,128,128]{2,1,0:T(8,128)S(1)} %shard_map.78.message), channel_id=1, source_target_pairs={{1,2},{2,1},{3,0},{0,3},{5,6},{6,5},{7,4},{4,7},{9,10},{10,9},{11,... | collective-permute-start | bytes 786440 | tf_op jit(solution)/shard_map/ppermute | solution.py:30
  5.5 3.6 %collective-permute-start.4 = (f32[4,128,128]{2,1,0:T(8,128)S(1)}, f32[4,128,128]{2,1,0:T(8,128)S(1)}, u32[]{:S(2)}, u32[]{:S(2)}) collective-permute-start(f32[4,128,128]{2,1,0:T(8,128)S(1)} %shard_map.79.message), channel_id=1, source_target_pairs={{4,8},{8,4},{12,16},{16,12},{20,24},{24,20},{28,0},{0,28},{5,9},{9... | collective-permute-start | bytes 786440 | tf_op jit(solution)/shard_map/ppermute | solution.py:30
  9.1 1.0 %shard_map.80.after = f32[8,128,128]{2,1,0:T(8,128)S(1)} custom-call(s32[1,1,5]{2,1,0:T(1,128)} %cutoff_hbm.5, f32[1,1,5,128,128]{4,3,2,1,0:T(8,128)} %ham_hbm.5, f32[1,1,5,128,128]{4,3,2,1,0:T(8,128)} %inv_hbm.5, f32[2,1,1,5,128,128]{5,4,3,2,1,0:T(8,128)} %rho_hbm.5, f32[4,128,128]{2,1,0:T(8,128)S(1)} %shard_map.79.message), custom_call_target="tpu_custom_call" | custom-call | flops 6291456000 | bytes 2097172 | tf_op jit(solution)/shard_map/pallas_call | solution.py:301
  10.2 1.3 %collective-permute-start.1 = (f32[8,128,128]{2,1,0:T(8,128)S(1)}, f32[8,128,128]{2,1,0:T(8,128)S(1)}, u32[]{:S(2)}, u32[]{:S(2)}) collective-permute-start(f32[8,128,128]{2,1,0:T(8,128)S(1)} %shard_map.80.after), channel_id=1, source_target_pairs={{1,0},{3,2},{5,4},{7,6},{9,8},{11,10},{13,12},{15,14},{17,16},{19,... | collective-permute-start | bytes 1572872 | tf_op jit(solution)/shard_map/ppermute | solution.py:36
  11.5 3.1 %collective-permute-start = (f32[8,128,128]{2,1,0:T(8,128)S(1)}, f32[8,128,128]{2,1,0:T(8,128)S(1)}, u32[]{:S(2)}, u32[]{:S(2)}) collective-permute-start(f32[8,128,128]{2,1,0:T(8,128)S(1)} %shard_map.80.after), channel_id=1, source_target_pairs={{0,1},{2,3},{4,5},{6,7},{8,9},{10,11},{12,13},{14,15},{16,17},{18,... | collective-permute-start | bytes 1572872 | tf_op jit(solution)/shard_map/ppermute | solution.py:36
  14.6 1.4 %shard_map.81 = (f32[3,5,128,128]{3,2,1,0:T(8,128)S(1)}, bf16[384,640]{1,0:T(8,128)(2,1)S(1)}, bf16[384,640]{1,0:T(8,128)(2,1)S(1)}, bf16[128,640]{1,0:T(8,128)(...) custom-call(s32[1,1,5]{2,1,0:T(1,128)} %cutoff_hbm.5, f32[1,1,5,128,128]{4,3,2,1,0:T(8,128)} %ham_hbm.5, ...), custom_call_target="tpu_custom_call" | custom-call | flops 25165824000 | bytes 5472788 | tf_op jit(solution)/shard_map/pallas_call | solution.py:301
  16.0 0.0 collective-permute-done.1.down
  16.0 0.1 collective-permute-done.up
  16.1 1.2 %shard_map.82 = (f32[384,640]{1,0:T(8,128)S(1)}, f32[384,128]{1,0:T(8,128)S(1)}, f32[2,2,128,128]{3,2,1,0:T(8,128)S(1)}, f32[3,1,1,5,128,128]{5,4,3,2,1,0:T(8,128)S(1)}) custom-call(bf16[384,640]{1,0:T(8,128)(2,1)S(1)} %get-tuple-element.46.left_high, bf16[384,640]{1,0:T(8,128)(2,1)S(1)} %get-tuple-element.47.left_low, ...), custom_call_target="tpu_custom_call" | custom-call | flops 100663296000 | bytes 8060928 | tf_op jit(solution)/shard_map/pallas_call | solution.py:301
  17.3 0.0 collective-permute-done.2.four
  17.3 0.6 %shard_map.83 = (f32[4,128,128]{2,1,0:T(8,128)S(1)}, bf16[384,128]{1,0:T(8,128)(2,1)S(1)}, bf16[384,128]{1,0:T(8,128)(2,1)S(1)}, f32[384,128]{1,0:T(8,128)S(1)}, f32[2,128,128]{2,1,0:T(8,128)S(1)}) custom-call(bf16[384,640]{1,0:T(8,128)(2,1)S(1)} %get-tuple-element.46.left_high, bf16[384,640]{1,0:T(8,128)(2,1)S(1)} %get-tuple-element.47.left_low, ...), custom_call_target="tpu_custom_call" | custom-call | flops 100663296 | bytes 5373952 | tf_op jit(solution)/shard_map/pallas_call | solution.py:301
  18.0 0.9 %collective-permute-start.5 = (f32[4,128,128]{2,1,0:T(8,128)S(1)}, f32[4,128,128]{2,1,0:T(8,128)S(1)}, u32[]{:S(2)}, u32[]{:S(2)}) collective-permute-start(f32[4,128,128]{2,1,0:T(8,128)S(1)} %get-tuple-element.72), channel_id=1, source_target_pairs={{1,2},{2,1},{3,0},{0,3},{5,6},{6,5},{7,4},{4,7},{9,10},{10,9},{11,... | collective-permute-start | bytes 786440 | tf_op jit(solution)/shard_map/ppermute | solution.py:30
  18.9 0.0 collective-permute-start.6
  18.9 1.9 %collective-permute-start.7 = (f32[4,128,128]{2,1,0:T(8,128)S(1)}, f32[4,128,128]{2,1,0:T(8,128)S(1)}, u32[]{:S(2)}, u32[]{:S(2)}) collective-permute-start(f32[4,128,128]{2,1,0:T(8,128)S(1)} %get-tuple-element.76), channel_id=1, source_target_pairs={{4,8},{8,4},{12,16},{16,12},{20,24},{24,20},{28,0},{0,28},{5,9},{9... | collective-permute-start | bytes 786440 | tf_op jit(solution)/shard_map/ppermute | solution.py:30
  20.8 0.0 collective-permute-done.3.one
  20.8 0.6 %shard_map.84 = (bf16[384,128]{1,0:T(8,128)(2,1)S(1)}, bf16[384,128]{1,0:T(8,128)(2,1)S(1)}, f32[384,128]{1,0:T(8,128)S(1)}, f32[2,128,128]{2,1,0:T(8,128)S(1)}) custom-call(bf16[384,640]{1,0:T(8,128)(2,1)S(1)} %get-tuple-element.46.left_high, bf16[384,640]{1,0:T(8,128)(2,1)S(1)} %get-tuple-element.47.left_low, f32[384,640]{1,0:T(8,128)S(1)} %get-tuple-element.52.start, ...), custom_call_target="tpu_custom_call" | custom-call | flops 125829120 | bytes 4128768 | tf_op jit(solution)/shard_map/pallas_call | solution.py:301
  21.4 0.0 collective-permute-done.4.two
  21.4 0.9 %shard_map.85 = (f32[4,128,128]{2,1,0:T(8,128)S(1)}, bf16[384,128]{1,0:T(8,128)(2,1)S(1)}, bf16[384,128]{1,0:T(8,128)(2,1)S(1)}, bf16[384,128]{1,0:T(8,128)(2,1)...) custom-call(bf16[384,640]{1,0:T(8,128)(2,1)S(1)} %get-tuple-element., ...), custom_call_target="tpu_custom_call" | custom-call | flops 276824064 | bytes 7280640 | tf_op jit(solution)/shard_map/pallas_call | solution.py:301
  22.4 0.1 collective-permute-start.10
  22.4 0.7 %collective-permute-start.8 = (f32[3,128]{1,0:T(4,128)S(1)}, f32[3,128]{1,0:T(4,128)S(1)}, u32[]{:S(2)}, u32[]{:S(2)}) collective-permute-start(f32[3,128]{1,0:T(4,128)S(1)} %get-tuple-element.77), channel_id=1, source_target_pairs={{0,4},{4,0},{8,12},{12,8},{16,20},{20,16},{24,28},{28,24},{1,5},{5... | collective-permute-start | bytes 4616 | tf_op jit(solution)/shard_map/ppermute | solution.py:30
  23.1 0.5 %collective-permute-done.10.arrived.c3 = f32[3,128]{1,0:T(4,128)S(1)} collective-permute-done((f32[3,128]{1,0:T(4,128)S(1)}, f32[3,128]{1,0:T(4,128)S(1)}, u32[]{:S(2)}, u32[]{:S(2)}) %collective-permute-start.10) | collective-permute-done | bytes 1568 | tf_op jit(solution)/shard_map/ppermute | solution.py:30
  23.6 2.8 %collective-permute-start.9 = (f32[3,128]{1,0:T(4,128)S(1)}, f32[3,128]{1,0:T(4,128)S(1)}, u32[]{:S(2)}, u32[]{:S(2)}) collective-permute-start(f32[3,128]{1,0:T(4,128)S(1)} %get-tuple-element.78), channel_id=1, source_target_pairs={{4,8},{8,4},{12,16},{16,12},{20,24},{24,20},{28,0},{0,28},{5,9},{9... | collective-permute-start | bytes 4616 | tf_op jit(solution)/shard_map/ppermute | solution.py:30
  26.4 0.0 collective-permute-done.5.four
  26.4 0.8 %collective-permute-start.11 = (f32[3,128]{1,0:T(4,128)S(1)}, f32[3,128]{1,0:T(4,128)S(1)}, u32[]{:S(2)}, u32[]{:S(2)}) collective-permute-start(f32[3,128]{1,0:T(4,128)S(1)} %shard_map.88), channel_id=1, source_target_pairs={{1,2},{2,1},{3,0},{0,3},{5,6},{6,5},{7,4},{4,7},{9,10},{10,9},{11,... | collective-permute-start | bytes 4616 | tf_op jit(solution)/shard_map/ppermute | solution.py:30
  27.2 1.2 %shard_map.87 = (f32[2,1,1,5,128,128]{5,4,3,2,1,0:T(8,128)}, f32[3,128,128]{2,1,0:T(8,128)S(1)}, f32[128,128]{1,0:T(8,128)S(1)}, f32[3,128]{1,0:T(4,128)S(1)}) custom-call(f32[3,5,128,128]{3,2,1,0:T(8,128)S(1)} %get-tuple-element.45.held, f32[4,128,128]{2,1,0:T(8,128)S(1)} %get-tuple-element.63.new, bf16[384,640]{1,0:T(8,128)(2,1)S(1)} %get-tuple-element.46.left_high, ...), custom_call_target="tpu_custom_call" | custom-call | flops 125829120 | bytes 6030848 | tf_op jit(solution)/shard_map/pallas_call | solution.py:301
  28.4 4.5 %collective-permute-done.8.c1 = f32[3,128]{1,0:T(4,128)S(1)} collective-permute-done((f32[3,128]{1,0:T(4,128)S(1)}, f32[3,128]{1,0:T(4,128)S(1)}, u32[]{:S(2)}, u32[]{:S(2)}) %collective-permute-start.8) | collective-permute-done | bytes 1568 | tf_op jit(solution)/shard_map/ppermute | solution.py:30
  32.9 0.0 collective-permute-done.9.c2
  32.9 0.0 collective-permute-done.11.c4
  32.9 0.0 collective-permute-done.6.one
  33.0 0.0 collective-permute-done.7.two
  33.0 1.3 %shard_map.89 = (f32[2,1,1,5,128,128]{5,4,3,2,1,0:T(8,128)}, f32[3,1,64]{2,1,0:T(1,128)}) custom-call(f32[3,5,128,128]{3,2,1,0:T(8,128)S(1)} %get-tuple-element.45.held, f32[3,1,1,5,128,128]{5,4,3,2,1,0:T(8,128)S(1)} %get-tuple-element.50.der_ref, f32[64,128]{1,0:T(8,128)S(1)} %get-tuple-element.51.members, ...), custom_call_target="tpu_custom_call", output_to_operand_aliasing={{0}: (16, {})} | custom-call | flops 125829120 | bytes 4890880 | tf_op jit(solution)/shard_map/pallas_call | solution.py:301
  (4 shorter events, 0.1 us)
Async XLA Ops:
  1.7 19.1 %collective-permute-start.3 = (f32[4,128,128]{2,1,0:T(8,128)S(1)}, f32[4,128,128]{2,1,0:T(8,128)S(1)}, u32[]{:S(2)}, u32[]{:S(2)}) collective-permute-start(f32[4,128,128]{2,1,0:T(8,128)S(1)} %get-tuple-element.43.message), channel_id=1, source_target_pairs={{0,4},{4,0},{8,12},{12,8},{16,20},{20,16},{24,28},{28,24},{1,5},{5... | collective-permute-start | bytes 786440 | tf_op jit(solution)/shard_map/ppermute | solution.py:30
  4.8 12.5 %collective-permute-start.2 = (f32[4,128,128]{2,1,0:T(8,128)S(1)}, f32[4,128,128]{2,1,0:T(8,128)S(1)}, u32[]{:S(2)}, u32[]{:S(2)}) collective-permute-start(f32[4,128,128]{2,1,0:T(8,128)S(1)} %shard_map.78.message), channel_id=1, source_target_pairs={{1,2},{2,1},{3,0},{0,3},{5,6},{6,5},{7,4},{4,7},{9,10},{10,9},{11,... | collective-permute-start | bytes 786440 | tf_op jit(solution)/shard_map/ppermute | solution.py:30
  5.5 15.9 %collective-permute-start.4 = (f32[4,128,128]{2,1,0:T(8,128)S(1)}, f32[4,128,128]{2,1,0:T(8,128)S(1)}, u32[]{:S(2)}, u32[]{:S(2)}) collective-permute-start(f32[4,128,128]{2,1,0:T(8,128)S(1)} %shard_map.79.message), channel_id=1, source_target_pairs={{4,8},{8,4},{12,16},{16,12},{20,24},{24,20},{28,0},{0,28},{5,9},{9... | collective-permute-start | bytes 786440 | tf_op jit(solution)/shard_map/ppermute | solution.py:30
  10.2 5.8 %collective-permute-start.1 = (f32[8,128,128]{2,1,0:T(8,128)S(1)}, f32[8,128,128]{2,1,0:T(8,128)S(1)}, u32[]{:S(2)}, u32[]{:S(2)}) collective-permute-start(f32[8,128,128]{2,1,0:T(8,128)S(1)} %shard_map.80.after), channel_id=1, source_target_pairs={{1,0},{3,2},{5,4},{7,6},{9,8},{11,10},{13,12},{15,14},{17,16},{19,... | collective-permute-start | bytes 1572872 | tf_op jit(solution)/shard_map/ppermute | solution.py:36
  11.5 4.6 %collective-permute-start = (f32[8,128,128]{2,1,0:T(8,128)S(1)}, f32[8,128,128]{2,1,0:T(8,128)S(1)}, u32[]{:S(2)}, u32[]{:S(2)}) collective-permute-start(f32[8,128,128]{2,1,0:T(8,128)S(1)} %shard_map.80.after), channel_id=1, source_target_pairs={{0,1},{2,3},{4,5},{6,7},{8,9},{10,11},{12,13},{14,15},{16,17},{18,... | collective-permute-start | bytes 1572872 | tf_op jit(solution)/shard_map/ppermute | solution.py:36
  18.0 8.4 %collective-permute-start.5 = (f32[4,128,128]{2,1,0:T(8,128)S(1)}, f32[4,128,128]{2,1,0:T(8,128)S(1)}, u32[]{:S(2)}, u32[]{:S(2)}) collective-permute-start(f32[4,128,128]{2,1,0:T(8,128)S(1)} %get-tuple-element.72), channel_id=1, source_target_pairs={{1,2},{2,1},{3,0},{0,3},{5,6},{6,5},{7,4},{4,7},{9,10},{10,9},{11,... | collective-permute-start | bytes 786440 | tf_op jit(solution)/shard_map/ppermute | solution.py:30
  18.9 14.1 %collective-permute-start.6 = (f32[4,128,128]{2,1,0:T(8,128)S(1)}, f32[4,128,128]{2,1,0:T(8,128)S(1)}, u32[]{:S(2)}, u32[]{:S(2)}) collective-permute-start(f32[4,128,128]{2,1,0:T(8,128)S(1)} %get-tuple-element.71.after), channel_id=1, source_target_pairs={{0,4},{4,0},{8,12},{12,8},{16,20},{20,16},{24,28},{28,24},{1,5},{5... | collective-permute-start | bytes 786440 | tf_op jit(solution)/shard_map/ppermute | solution.py:30
  18.9 14.1 %collective-permute-start.7 = (f32[4,128,128]{2,1,0:T(8,128)S(1)}, f32[4,128,128]{2,1,0:T(8,128)S(1)}, u32[]{:S(2)}, u32[]{:S(2)}) collective-permute-start(f32[4,128,128]{2,1,0:T(8,128)S(1)} %get-tuple-element.76), channel_id=1, source_target_pairs={{4,8},{8,4},{12,16},{16,12},{20,24},{24,20},{28,0},{0,28},{5,9},{9... | collective-permute-start | bytes 786440 | tf_op jit(solution)/shard_map/ppermute | solution.py:30
  22.4 1.2 %collective-permute-start.10 = (f32[3,128]{1,0:T(4,128)S(1)}, f32[3,128]{1,0:T(4,128)S(1)}, u32[]{:S(2)}, u32[]{:S(2)}) collective-permute-start(f32[3,128]{1,0:T(4,128)S(1)} %get-tuple-element.79), channel_id=1, source_target_pairs={{0,1},{1,0},{2,3},{3,2},{4,5},{5,4},{6,7},{7,6},{8,9},{9,8},{10,11... | collective-permute-start | bytes 4616 | tf_op jit(solution)/shard_map/ppermute | solution.py:30
  22.4 10.5 %collective-permute-start.8 = (f32[3,128]{1,0:T(4,128)S(1)}, f32[3,128]{1,0:T(4,128)S(1)}, u32[]{:S(2)}, u32[]{:S(2)}) collective-permute-start(f32[3,128]{1,0:T(4,128)S(1)} %get-tuple-element.77), channel_id=1, source_target_pairs={{0,4},{4,0},{8,12},{12,8},{16,20},{20,16},{24,28},{28,24},{1,5},{5... | collective-permute-start | bytes 4616 | tf_op jit(solution)/shard_map/ppermute | solution.py:30
  23.6 9.4 %collective-permute-start.9 = (f32[3,128]{1,0:T(4,128)S(1)}, f32[3,128]{1,0:T(4,128)S(1)}, u32[]{:S(2)}, u32[]{:S(2)}) collective-permute-start(f32[3,128]{1,0:T(4,128)S(1)} %get-tuple-element.78), channel_id=1, source_target_pairs={{4,8},{8,4},{12,16},{16,12},{20,24},{24,20},{28,0},{0,28},{5,9},{9... | collective-permute-start | bytes 4616 | tf_op jit(solution)/shard_map/ppermute | solution.py:30
  26.4 6.6 %collective-permute-start.11 = (f32[3,128]{1,0:T(4,128)S(1)}, f32[3,128]{1,0:T(4,128)S(1)}, u32[]{:S(2)}, u32[]{:S(2)}) collective-permute-start(f32[3,128]{1,0:T(4,128)S(1)} %shard_map.88), channel_id=1, source_target_pairs={{1,2},{2,1},{3,0},{0,3},{5,6},{6,5},{7,4},{4,7},{9,10},{10,9},{11,... | collective-permute-start | bytes 4616 | tf_op jit(solution)/shard_map/ppermute | solution.py:30

commit v19 on v14

--- a/solution.py
+++ b/solution.py
@@ -177,19 +177,16 @@
 
 
 def four_kernel(
-    left_high, left_low, start, held, diagonal, four, one_more, mixed_high, mixed_low, diagonal_out, other
+    left_high, left_low, start, held, diagonal, four, one_more, two_more, mixed_high, mixed_low, diagonal_out, other
 ):
     send_more(one_more, held, 1)
+    send_more(two_more, held, 2)
     mixed, diagonal_out[...], other[0], other[1] = first_half((left_high, left_low), 4, start, four, diagonal[...])
     mixed_high[...], mixed_low[...] = mixed
 
 
-def more_kernel(after, held, two_more, four_more):
-    send_more(two_more, held, 2)
+def fourth_kernel(left_high, left_low, start, held, diagonal, one, four_more, mixed_high, mixed_low, diagonal_out, other):
     send_more(four_more, held, 4)
-
-
-def fourth_kernel(left_high, left_low, start, diagonal, one, mixed_high, mixed_low, diagonal_out, other):
     mixed, diagonal_out[...], other[0], other[1] = first_half((left_high, left_low), 1, start, one, diagonal[...])
     mixed_high[...], mixed_low[...] = mixed
 
@@ -228,7 +225,7 @@
 
 def real_kernel(
     held, new, left_high, left_low, self_high, self_low, other_one, real_two, other_three, other_four, weighted,
-    imag_part, high_four, low_four, four, out_hbm, comm, imag_out, row_part, imag_new, sems
+    out_hbm, comm, row_part, imag_new, sems
 ):
     order = order_of()
     copies = start_all(
@@ -240,16 +237,15 @@
     ahead = dot(part(at_self, slice(0, B), cols(0)), part(left, slice(B, 2 * B), whole))
     behind = dot(part(at_self, slice(B, 2 * B), cols(0)), part(left, slice(0, B), whole))
     real_comm = ahead - behind
-    added, real_four, imag_four = second_half((high_four[...], low_four[...]), four)
-    imag_out[...] = imag_part[...] + imag_four
-    for at, (place, other) in enumerate(((3, other_three[0, 0]), (4, other_four[0] + added))):
+    for at, (place, other) in enumerate(((3, other_three[0, 0]),)):
         imag_new[at] = held[2, place] - time_step * (real_comm[:, cols(place)] + other)
         copies += start_all(
             [pltpu.make_async_copy(imag_new.at[at], out_hbm.at[1, 0, 0, order[place]], sems.at[1, at])]
         )
-    comm[0] = real_comm[:, cols(0)] + other_three[0, 1] + real_four
+    comm[0] = real_comm[:, cols(0)] + other_three[0, 1]
     comm[1] = real_comm[:, cols(1)] + other_one[0]
     comm[2] = real_comm[:, cols(2)] + real_two[...]
+    comm[3] = real_comm[:, cols(4)] + other_four[0]
     for direction in range(3):
         row_part[direction : direction + 1, :] = jnp.sum(weighted[direction].T, axis=0, keepdims=True)
     for copy in copies:
@@ -257,22 +253,25 @@
 
 
 def sixth_kernel(
-    held, der_ref, members, high_one, low_one, high_two, low_two, imag_part, comm, row_part, one, two, c1, c2, c3, c4, old_hbm,
+    held, der_ref, members, high_one, low_one, high_two, low_two, high_four, low_four, imag_part, comm, row_part, one, two, four, c1, c2, c3, c4, old_hbm,
     out_hbm, forces_hbm, new, forces_ref, sems
 ):
     order = order_of()
+    added_four, real_four, imag_four = second_half((high_four[...], low_four[...]), four)
     prop, inner = rows_of(beside((high_one[...], low_one[...]), (high_two[...], low_two[...])))
     near = [tuple(jnp.concatenate(x, axis=0) for x in zip(split(one[1 + kind]), split(two[1 + kind]))) for kind in range(3)]
     behind = dot(inner, near[0])
-    real_new = held[1, 0] + time_step * (imag_part[...] + dot(prop, near[2]) - behind[B:])
+    real_new = held[1, 0] + time_step * (imag_part[...] + imag_four + dot(prop, near[2]) - behind[B:])
     new[0] = real_new
     copies = start_all([pltpu.make_async_copy(new.at[0], out_hbm.at[0, 0, 0, 0], sems.at[0])])
-    new[1] = held[2, 0] - time_step * (comm[0] + dot(prop, near[1]) - behind[:B])
+    new[1] = held[2, 0] - time_step * (comm[0] + real_four + dot(prop, near[1]) - behind[:B])
     for place, message, mixed in ((1, one, (high_one, low_one)), (2, two, (high_two, low_two))):
         added = dot(rows_of((mixed[0][...], mixed[1][...]))[0], split(message[0]))
         new[1 + place] = held[2, place] - time_step * (comm[place] + added)
+    new[4] = held[2, 4] - time_step * (comm[3] + added_four)
+    places = (0, 1, 2, 4)
     copies += start_all(
-        [pltpu.make_async_copy(new.at[1 + at], out_hbm.at[1, 0, 0, order[at]], sems.at[1 + at]) for at in range(3)]
+        [pltpu.make_async_copy(new.at[1 + at], out_hbm.at[1, 0, 0, order[x]], sems.at[1 + at]) for at, x in enumerate(places)]
     )
     parts = []
     for direction in range(3):
@@ -284,7 +283,7 @@
     )
     for direction in range(3):
         forces_ref[direction] = forces[direction : direction + 1]
-    copies += start_all([pltpu.make_async_copy(forces_ref, forces_hbm, sems.at[4])])
+    copies += start_all([pltpu.make_async_copy(forces_ref, forces_hbm, sems.at[5])])
     for copy in copies:
         copy.wait()
 
@@ -355,24 +354,23 @@
         (left_high, left_low, ham_high, ham_low, held, near_three, derivative),
         scratch=[dma(())],
     )
-    one_more, high_four, low_four, diagonal, other_four = call(
+    one_more, two_more, high_four, low_four, diagonal, other_four = call(
         four_kernel,
-        [message] + mixed + [shape(3 * B, B), shape(2, B, B)],
+        [message] * 2 + mixed + [shape(3 * B, B), shape(2, B, B)],
         [vmem] * 6,
         8,
         (left_high, left_low, start, held, diagonal, near_four),
     )
     near_one_more = swapped(one_more, 1)
-    two_more, four_more = call(more_kernel, [message] * 2, [vmem] * 2, 300, (one_more, held))
+    near_two_more = swapped(two_more, 2)
+    four_more, high_one, low_one, diagonal, other_one = call(
+        fourth_kernel,
+        [message] + mixed + [shape(3 * B, B), shape(2, B, B)],
+        [vmem] * 6,
+        10,
+        (left_high, left_low, start, held, diagonal, near_one),
+    )
     near_four_more = swapped(four_more, 4)
-    near_two_more = swapped(two_more, 2)
-    high_one, low_one, diagonal, other_one = call(
-        fourth_kernel,
-        mixed + [shape(3 * B, B), shape(2, B, B)],
-        [vmem] * 5,
-        10,
-        (left_high, left_low, start, diagonal, near_one),
-    )
     block = shape(B, B)
     new, high_two, low_two, self_high, self_low, real_two, imag_part, weighted, *columns = call(
         fifth_kernel,
@@ -382,31 +380,31 @@
         (left_high, left_low, start, diagonal, held, derivative, other_one, other_three, other_four, near_two),
     )
     c1, c2, c3, c4 = columns
-    c1, c2, c3 = swapped(c1, 1), swapped(c2, 2), swapped(c3, 3)
-    (c4,) = call(later_kernel, [shape(3, B)], [vmem] * 2, 0, (c3, c4))
-    columns = (c1, c2, c3, swapped(c4, 4))
+    c3, c4 = swapped(c3, 3), swapped(c4, 4)
+    (c1,) = call(later_kernel, [shape(3, B)], [vmem] * 2, 0, (c3, c1))
+    (c2,) = call(later_kernel, [shape(3, B)], [vmem] * 2, 0, (c4, c2))
+    columns = (swapped(c1, 1), swapped(c2, 2), c3, c4)
     args = (held, new, left_high, left_low, self_high, self_low, other_one, real_two, other_three, other_four, weighted)
-    args += (imag_part, high_four, low_four, near_four_more)
-    out, comm, imag_part, row_part = call(
+    out, comm, row_part = call(
         real_kernel,
-        [shape(*density.shape), shape(3, B, B), shape(B, B), shape(3, B)],
-        [vmem] * 15,
+        [shape(*density.shape), shape(4, B, B), shape(3, B)],
+        [vmem] * 11,
         10,
         args,
-        out_specs=[hbm] + [vmem] * 3,
-        scratch=[pltpu.VMEM((2, B, B), f32), dma((2, 4))],
-    )
-    args = (held, derivative, members, high_one, low_one, high_two, low_two, imag_part, comm, row_part)
-    args += (near_one_more, near_two_more, *columns, out)
+        out_specs=[hbm] + [vmem] * 2,
+        scratch=[pltpu.VMEM((1, B, B), f32), dma((2, 4))],
+    )
+    args = (held, derivative, members, high_one, low_one, high_two, low_two, high_four, low_four, imag_part, comm, row_part)
+    args += (near_one_more, near_two_more, near_four_more, *columns, out)
     new_density, forces = call(
         sixth_kernel,
         [shape(*density.shape), shape(3, 1, ATOMS)],
-        [vmem] * 16 + [hbm],
+        [vmem] * 19 + [hbm],
         10,
         args,
         out_specs=[hbm, hbm],
-        scratch=[pltpu.VMEM((4, B, B), f32), pltpu.VMEM((3, 1, ATOMS), f32), dma((5,))],
-        aliases={16: 0},
+        scratch=[pltpu.VMEM((5, B, B), f32), pltpu.VMEM((3, 1, ATOMS), f32), dma((6,))],
+        aliases={19: 0},
     )
     return new_density, forces.reshape(1, 1, 3, ATOMS)
 

time: 31.1 us -> 37.4 us (1.20)
  starting transfers between devices: 16.8 us -> 21.6 us
  waiting for transfers between devices: 3.75 us -> 5.15 us
    ppermute x11, starting transfers between devices: 16.8 us -> 21.6 us  [swapped(): return lax.ppermute(cells, axis, pairs)]
    ppermute x11, waiting for transfers between devices: 3.75 us -> 5.15 us  [swapped(): return lax.ppermute(cells, axis, pairs)]
  transfers between devices with their start and end apart: 11 -> 11, of which waited for: 3 -> 3; matrix products, arithmetic and copies ran while one was open for 0% -> 0% of each run, Pallas kernels for 23% -> 19%
where the time goes in v19:
time: 37.4 us; the launch traced here: 37.1 us
  starting transfers between devices  21.6 us (58%)
  Pallas kernels  9.54 us (26%)
  waiting for transfers between devices  5.15 us (14%)
  between operations  0.74 us (2%)
    ppermute x11, starting transfers between devices, swapped(): return lax.ppermute(cells, axis, pairs)  21.6 us
    pallas_call x13, Pallas kernels, call(): pl.pallas_call(kernel, out_shape=shapes, in_specs=in_specs, out_specs=out...  9.54 us
    ppermute x11, waiting for transfers between devices, swapped(): return lax.ppermute(cells, axis, pairs)  5.15 us
  transfers between devices with their start and end apart: 11, of which 3 were waited for; matrix products, arithmetic and copies ran while one was open for 0% of the time, Pallas kernels for 19%

profile of v19, /device:TPU:0, one launch (start us, length us, event | category | flops | bytes accessed | tf_op | source)
XLA Modules:
  0.0 37.1 jit_solution(10831880351954146169)
XLA Ops:
  0.6 1.1 %shard_map.77 = (f32[4,128,128]{2,1,0:T(8,128)S(1)}, f32[2,128,128]{2,1,0:T(8,128)S(1)}) custom-call(s32[1,1,5]{2,1,0:T(1,128)} %cutoff_hbm.5, f32[1,1,5,128,128]{4,3,2,1,0:T(8,128)} %ham_hbm.5, f32[1,1,5,128,128]{4,3,2,1,0:T(8,128)} %inv_hbm.5, f32[2,1,1,5,128,128]{5,4,3,2,1,0:T(8,128)} %rho_hbm.5), custom_call_target="tpu_custom_call" | custom-call | bytes 1703956 | tf_op jit(solution)/shard_map/pallas_call | solution.py:293
  1.7 3.0 %collective-permute-start.2 = (f32[4,128,128]{2,1,0:T(8,128)S(1)}, f32[4,128,128]{2,1,0:T(8,128)S(1)}, u32[]{:S(2)}, u32[]{:S(2)}) collective-permute-start(f32[4,128,128]{2,1,0:T(8,128)S(1)} %get-tuple-element.42.message), channel_id=1, source_target_pairs={{0,4},{4,0},{8,12},{12,8},{16,20},{20,16},{24,28},{28,24},{1,5},{5... | collective-permute-start | bytes 786440 | tf_op jit(solution)/shard_map/ppermute | solution.py:30
  4.8 0.7 %collective-permute-start.1 = (f32[4,128,128]{2,1,0:T(8,128)S(1)}, f32[4,128,128]{2,1,0:T(8,128)S(1)}, u32[]{:S(2)}, u32[]{:S(2)}) collective-permute-start(f32[4,128,128]{2,1,0:T(8,128)S(1)} %shard_map.78.message), channel_id=1, source_target_pairs={{1,2},{2,1},{3,0},{0,3},{5,6},{6,5},{7,4},{4,7},{9,10},{10,9},{11,... | collective-permute-start | bytes 786440 | tf_op jit(solution)/shard_map/ppermute | solution.py:30
  5.5 3.6 %collective-permute-start.3 = (f32[4,128,128]{2,1,0:T(8,128)S(1)}, f32[4,128,128]{2,1,0:T(8,128)S(1)}, u32[]{:S(2)}, u32[]{:S(2)}) collective-permute-start(f32[4,128,128]{2,1,0:T(8,128)S(1)} %shard_map.79.message), channel_id=1, source_target_pairs={{4,8},{8,4},{12,16},{16,12},{20,24},{24,20},{28,0},{0,28},{5,9},{9... | collective-permute-start | bytes 786440 | tf_op jit(solution)/shard_map/ppermute | solution.py:30
  9.1 1.0 %shard_map.80.after = f32[8,128,128]{2,1,0:T(8,128)S(1)} custom-call(s32[1,1,5]{2,1,0:T(1,128)} %cutoff_hbm.5, f32[1,1,5,128,128]{4,3,2,1,0:T(8,128)} %ham_hbm.5, f32[1,1,5,128,128]{4,3,2,1,0:T(8,128)} %inv_hbm.5, f32[2,1,1,5,128,128]{5,4,3,2,1,0:T(8,128)} %rho_hbm.5, f32[4,128,128]{2,1,0:T(8,128)S(1)} %shard_map.79.message), custom_call_target="tpu_custom_call" | custom-call | flops 6291456000 | bytes 2097172 | tf_op jit(solution)/shard_map/pallas_call | solution.py:293
  10.2 0.7 %collective-permute-start = (f32[8,128,128]{2,1,0:T(8,128)S(1)}, f32[8,128,128]{2,1,0:T(8,128)S(1)}, u32[]{:S(2)}, u32[]{:S(2)}) collective-permute-start(f32[8,128,128]{2,1,0:T(8,128)S(1)} %shard_map.80.after), channel_id=1, source_target_pairs={{0,1},{1,0},{2,3},{3,2},{4,5},{5,4},{6,7},{7,6},{8,9},{9,8},{10,11... | collective-permute-start | bytes 1572872 | tf_op jit(solution)/shard_map/ppermute | solution.py:30
  10.9 1.4 %shard_map.81 = (f32[3,5,128,128]{3,2,1,0:T(8,128)S(1)}, bf16[384,640]{1,0:T(8,128)(2,1)S(1)}, bf16[384,640]{1,0:T(8,128)(2,1)S(1)}, bf16[128,640]{1,0:T(8,128)(...) custom-call(s32[1,1,5]{2,1,0:T(1,128)} %cutoff_hbm.5, f32[1,1,5,128,128]{4,3,2,1,0:T(8,128)} %ham_hbm.5, ...), custom_call_target="tpu_custom_call" | custom-call | flops 25165824000 | bytes 5472788 | tf_op jit(solution)/shard_map/pallas_call | solution.py:293
  12.3 0.1 collective-permute-done.three
  12.4 1.2 %shard_map.82 = (f32[384,640]{1,0:T(8,128)S(1)}, f32[384,128]{1,0:T(8,128)S(1)}, f32[2,2,128,128]{3,2,1,0:T(8,128)S(1)}, f32[3,1,1,5,128,128]{5,4,3,2,1,0:T(8,128)S(1)}) custom-call(bf16[384,640]{1,0:T(8,128)(2,1)S(1)} %get-tuple-element.45.left_high, bf16[384,640]{1,0:T(8,128)(2,1)S(1)} %get-tuple-element.46.left_low, ...), custom_call_target="tpu_custom_call" | custom-call | flops 100663296000 | bytes 7536640 | tf_op jit(solution)/shard_map/pallas_call | solution.py:293
  13.7 0.0 collective-permute-done.1.four
  13.7 0.6 %shard_map.83 = (f32[4,128,128]{2,1,0:T(8,128)S(1)}, f32[4,128,128]{2,1,0:T(8,128)S(1)}, bf16[384,128]{1,0:T(8,128)(2,1)S(1)}, bf16[384,128]{1,0:T(8,128)(2,1)S(...) custom-call(bf16[384,640]{1,0:T(8,128)(2,1)S(1)} %get-tuple-element.45.left_high, ...), custom_call_target="tpu_custom_call" | custom-call | flops 100663296 | bytes 5636096 | tf_op jit(solution)/shard_map/pallas_call | solution.py:293
  14.3 0.1 collective-permute-start.4
  14.4 4.8 %collective-permute-start.5 = (f32[4,128,128]{2,1,0:T(8,128)S(1)}, f32[4,128,128]{2,1,0:T(8,128)S(1)}, u32[]{:S(2)}, u32[]{:S(2)}) collective-permute-start(f32[4,128,128]{2,1,0:T(8,128)S(1)} %get-tuple-element.73), channel_id=1, source_target_pairs={{4,8},{8,4},{12,16},{16,12},{20,24},{24,20},{28,0},{0,28},{5,9},{9... | collective-permute-start | bytes 786440 | tf_op jit(solution)/shard_map/ppermute | solution.py:30
  19.2 0.0 collective-permute-done.2.one
  19.2 0.6 %shard_map.84 = (f32[4,128,128]{2,1,0:T(8,128)S(1)}, bf16[384,128]{1,0:T(8,128)(2,1)S(1)}, bf16[384,128]{1,0:T(8,128)(2,1)S(1)}, f32[384,128]{1,0:T(8,128)S(1)}, f32[2,128,128]{2,1,0:T(8,128)S(1)}) custom-call(bf16[384,640]{1,0:T(8,128)(2,1)S(1)} %get-tuple-element.45.left_high, bf16[384,640]{1,0:T(8,128)(2,1)S(1)} %get-tuple-element.46.left_low, ...), custom_call_target="tpu_custom_call" | custom-call | flops 125829120 | bytes 5373952 | tf_op jit(solution)/shard_map/pallas_call | solution.py:293
  19.8 0.2 collective-permute-start.6
  20.0 0.0 collective-permute-done.3.two
  20.0 0.9 %shard_map.85 = (f32[4,128,128]{2,1,0:T(8,128)S(1)}, bf16[384,128]{1,0:T(8,128)(2,1)S(1)}, bf16[384,128]{1,0:T(8,128)(2,1)S(1)}, bf16[384,128]{1,0:T(8,128)(2,1)...) custom-call(bf16[384,640]{1,0:T(8,128)(2,1)S(1)} %get-tuple-element., ...), custom_call_target="tpu_custom_call" | custom-call | flops 276824064 | bytes 7280640 | tf_op jit(solution)/shard_map/pallas_call | solution.py:293
  20.9 4.9 %collective-permute-start.7 = (f32[3,128]{1,0:T(4,128)S(1)}, f32[3,128]{1,0:T(4,128)S(1)}, u32[]{:S(2)}, u32[]{:S(2)}) collective-permute-start(f32[3,128]{1,0:T(4,128)S(1)} %get-tuple-element.75), channel_id=1, source_target_pairs={{0,1},{1,0},{2,3},{3,2},{4,5},{5,4},{6,7},{7,6},{8,9},{9,8},{10,11... | collective-permute-start | bytes 4616 | tf_op jit(solution)/shard_map/ppermute | solution.py:30
  25.8 0.0 collective-permute-start.9
  25.9 0.8 %collective-permute-done.7.arrived.c3 = f32[3,128]{1,0:T(4,128)S(1)} collective-permute-done((f32[3,128]{1,0:T(4,128)S(1)}, f32[3,128]{1,0:T(4,128)S(1)}, u32[]{:S(2)}, u32[]{:S(2)}) %collective-permute-start.7) | collective-permute-done | bytes 1568 | tf_op jit(solution)/shard_map/ppermute | solution.py:30
  26.7 2.6 %collective-permute-start.8 = (f32[3,128]{1,0:T(4,128)S(1)}, f32[3,128]{1,0:T(4,128)S(1)}, u32[]{:S(2)}, u32[]{:S(2)}) collective-permute-start(f32[3,128]{1,0:T(4,128)S(1)} %shard_map.87), channel_id=1, source_target_pairs={{0,4},{4,0},{8,12},{12,8},{16,20},{20,16},{24,28},{28,24},{1,5},{5... | collective-permute-start | bytes 4616 | tf_op jit(solution)/shard_map/ppermute | solution.py:30
  29.3 0.0 collective-permute-done.9.arrived.c4
  29.3 0.9 %collective-permute-start.10 = (f32[3,128]{1,0:T(4,128)S(1)}, f32[3,128]{1,0:T(4,128)S(1)}, u32[]{:S(2)}, u32[]{:S(2)}) collective-permute-start(f32[3,128]{1,0:T(4,128)S(1)} %shard_map.88), channel_id=1, source_target_pairs={{4,8},{8,4},{12,16},{16,12},{20,24},{24,20},{28,0},{0,28},{5,9},{9... | collective-permute-start | bytes 4616 | tf_op jit(solution)/shard_map/ppermute | solution.py:30
  30.2 1.1 %shard_map.86 = (f32[2,1,1,5,128,128]{5,4,3,2,1,0:T(8,128)}, f32[4,128,128]{2,1,0:T(8,128)S(1)}, f32[3,128]{1,0:T(4,128)S(1)}) custom-call(f32[3,5,128,128]{3,2,1,0:T(8,128)S(1)} %get-tuple-element.44.held, f32[4,128,128]{2,1,0:T(8,128)S(1)} %get-tuple-element.65.new, bf16[384,640]{1,0:T(8,128)(2,1)S(1)} %get-tuple-element.45.left_high, ...), custom_call_target="tpu_custom_call" | custom-call | flops 125829120 | bytes 5309952 | tf_op jit(solution)/shard_map/pallas_call | solution.py:293
  31.4 0.0 collective-permute-done.8.c1
  31.4 4.2 %collective-permute-done.10.c2 = f32[3,128]{1,0:T(4,128)S(1)} collective-permute-done((f32[3,128]{1,0:T(4,128)S(1)}, f32[3,128]{1,0:T(4,128)S(1)}, u32[]{:S(2)}, u32[]{:S(2)}) %collective-permute-start.10) | collective-permute-done | bytes 1568 | tf_op jit(solution)/shard_map/ppermute | solution.py:30
  35.6 0.0 collective-permute-done.4.one
  35.6 0.0 collective-permute-done.5.two
  35.6 0.0 collective-permute-done.6.four
  35.6 1.5 %shard_map.89 = (f32[2,1,1,5,128,128]{5,4,3,2,1,0:T(8,128)}, f32[3,1,64]{2,1,0:T(1,128)}) custom-call(f32[3,5,128,128]{3,2,1,0:T(8,128)S(1)} %get-tuple-element.44.held, f32[3,1,1,5,128,128]{5,4,3,2,1,0:T(8,128)S(1)} %get-tuple-element.49.der_ref, f32[64,128]{1,0:T(8,128)S(1)} %get-tuple-element.50.members, ...), custom_call_target="tpu_custom_call", output_to_operand_aliasing={{0}: (19, {})} | custom-call | flops 125829120 | bytes 5611776 | tf_op jit(solution)/shard_map/pallas_call | solution.py:293
  (4 shorter events, 0.0 us)
Async XLA Ops:
  1.7 17.4 %collective-permute-start.2 = (f32[4,128,128]{2,1,0:T(8,128)S(1)}, f32[4,128,128]{2,1,0:T(8,128)S(1)}, u32[]{:S(2)}, u32[]{:S(2)}) collective-permute-start(f32[4,128,128]{2,1,0:T(8,128)S(1)} %get-tuple-element.42.message), channel_id=1, source_target_pairs={{0,4},{4,0},{8,12},{12,8},{16,20},{20,16},{24,28},{28,24},{1,5},{5... | collective-permute-start | bytes 786440 | tf_op jit(solution)/shard_map/ppermute | solution.py:30
  4.8 8.9 %collective-permute-start.1 = (f32[4,128,128]{2,1,0:T(8,128)S(1)}, f32[4,128,128]{2,1,0:T(8,128)S(1)}, u32[]{:S(2)}, u32[]{:S(2)}) collective-permute-start(f32[4,128,128]{2,1,0:T(8,128)S(1)} %shard_map.78.message), channel_id=1, source_target_pairs={{1,2},{2,1},{3,0},{0,3},{5,6},{6,5},{7,4},{4,7},{9,10},{10,9},{11,... | collective-permute-start | bytes 786440 | tf_op jit(solution)/shard_map/ppermute | solution.py:30
  5.5 14.5 %collective-permute-start.3 = (f32[4,128,128]{2,1,0:T(8,128)S(1)}, f32[4,128,128]{2,1,0:T(8,128)S(1)}, u32[]{:S(2)}, u32[]{:S(2)}) collective-permute-start(f32[4,128,128]{2,1,0:T(8,128)S(1)} %shard_map.79.message), channel_id=1, source_target_pairs={{4,8},{8,4},{12,16},{16,12},{20,24},{24,20},{28,0},{0,28},{5,9},{9... | collective-permute-start | bytes 786440 | tf_op jit(solution)/shard_map/ppermute | solution.py:30
  10.2 2.3 %collective-permute-start = (f32[8,128,128]{2,1,0:T(8,128)S(1)}, f32[8,128,128]{2,1,0:T(8,128)S(1)}, u32[]{:S(2)}, u32[]{:S(2)}) collective-permute-start(f32[8,128,128]{2,1,0:T(8,128)S(1)} %shard_map.80.after), channel_id=1, source_target_pairs={{0,1},{1,0},{2,3},{3,2},{4,5},{5,4},{6,7},{7,6},{8,9},{9,8},{10,11... | collective-permute-start | bytes 1572872 | tf_op jit(solution)/shard_map/ppermute | solution.py:30
  14.3 21.3 %collective-permute-start.4 = (f32[4,128,128]{2,1,0:T(8,128)S(1)}, f32[4,128,128]{2,1,0:T(8,128)S(1)}, u32[]{:S(2)}, u32[]{:S(2)}) collective-permute-start(f32[4,128,128]{2,1,0:T(8,128)S(1)} %get-tuple-element.72), channel_id=1, source_target_pairs={{0,4},{4,0},{8,12},{12,8},{16,20},{20,16},{24,28},{28,24},{1,5},{5... | collective-permute-start | bytes 786440 | tf_op jit(solution)/shard_map/ppermute | solution.py:30
  14.4 21.2 %collective-permute-start.5 = (f32[4,128,128]{2,1,0:T(8,128)S(1)}, f32[4,128,128]{2,1,0:T(8,128)S(1)}, u32[]{:S(2)}, u32[]{:S(2)}) collective-permute-start(f32[4,128,128]{2,1,0:T(8,128)S(1)} %get-tuple-element.73), channel_id=1, source_target_pairs={{4,8},{8,4},{12,16},{16,12},{20,24},{24,20},{28,0},{0,28},{5,9},{9... | collective-permute-start | bytes 786440 | tf_op jit(solution)/shard_map/ppermute | solution.py:30
  19.8 15.8 %collective-permute-start.6 = (f32[4,128,128]{2,1,0:T(8,128)S(1)}, f32[4,128,128]{2,1,0:T(8,128)S(1)}, u32[]{:S(2)}, u32[]{:S(2)}) collective-permute-start(f32[4,128,128]{2,1,0:T(8,128)S(1)} %get-tuple-element.74), channel_id=1, source_target_pairs={{1,2},{2,1},{3,0},{0,3},{5,6},{6,5},{7,4},{4,7},{9,10},{10,9},{11,... | collective-permute-start | bytes 786440 | tf_op jit(solution)/shard_map/ppermute | solution.py:30
  20.9 5.7 %collective-permute-start.7 = (f32[3,128]{1,0:T(4,128)S(1)}, f32[3,128]{1,0:T(4,128)S(1)}, u32[]{:S(2)}, u32[]{:S(2)}) collective-permute-start(f32[3,128]{1,0:T(4,128)S(1)} %get-tuple-element.75), channel_id=1, source_target_pairs={{0,1},{1,0},{2,3},{3,2},{4,5},{5,4},{6,7},{7,6},{8,9},{9,8},{10,11... | collective-permute-start | bytes 4616 | tf_op jit(solution)/shard_map/ppermute | solution.py:30
  25.8 3.4 %collective-permute-start.9 = (f32[3,128]{1,0:T(4,128)S(1)}, f32[3,128]{1,0:T(4,128)S(1)}, u32[]{:S(2)}, u32[]{:S(2)}) collective-permute-start(f32[3,128]{1,0:T(4,128)S(1)} %get-tuple-element.77), channel_id=1, source_target_pairs={{1,2},{2,1},{3,0},{0,3},{5,6},{6,5},{7,4},{4,7},{9,10},{10,9},{11,... | collective-permute-start | bytes 4616 | tf_op jit(solution)/shard_map/ppermute | solution.py:30
  26.7 4.7 %collective-permute-start.8 = (f32[3,128]{1,0:T(4,128)S(1)}, f32[3,128]{1,0:T(4,128)S(1)}, u32[]{:S(2)}, u32[]{:S(2)}) collective-permute-start(f32[3,128]{1,0:T(4,128)S(1)} %shard_map.87), channel_id=1, source_target_pairs={{0,4},{4,0},{8,12},{12,8},{16,20},{20,16},{24,28},{28,24},{1,5},{5... | collective-permute-start | bytes 4616 | tf_op jit(solution)/shard_map/ppermute | solution.py:30
  29.3 6.3 %collective-permute-start.10 = (f32[3,128]{1,0:T(4,128)S(1)}, f32[3,128]{1,0:T(4,128)S(1)}, u32[]{:S(2)}, u32[]{:S(2)}) collective-permute-start(f32[3,128]{1,0:T(4,128)S(1)} %shard_map.88), channel_id=1, source_target_pairs={{4,8},{8,4},{12,16},{16,12},{20,24},{24,20},{28,0},{0,28},{5,9},{9... | collective-permute-start | bytes 4616 | tf_op jit(solution)/shard_map/ppermute | solution.py:30

commit v20 on v14

--- a/solution.py
+++ b/solution.py
@@ -177,14 +177,14 @@
 
 
 def four_kernel(
-    left_high, left_low, start, held, diagonal, four, one_more, mixed_high, mixed_low, diagonal_out, other
+    left_high, left_low, start, diagonal, four, mixed_high, mixed_low, diagonal_out, other
 ):
-    send_more(one_more, held, 1)
     mixed, diagonal_out[...], other[0], other[1] = first_half((left_high, left_low), 4, start, four, diagonal[...])
     mixed_high[...], mixed_low[...] = mixed
 
 
-def more_kernel(after, held, two_more, four_more):
+def more_kernel(arrived, after, held, one_more, two_more, four_more):
+    send_more(one_more, held, 1)
     send_more(two_more, held, 2)
     send_more(four_more, held, 4)
 
@@ -355,17 +355,17 @@
         (left_high, left_low, ham_high, ham_low, held, near_three, derivative),
         scratch=[dma(())],
     )
-    one_more, high_four, low_four, diagonal, other_four = call(
+    one_more, two_more, four_more = call(more_kernel, [message] * 3, [vmem] * 3, 300, (near_four, other_three, held))
+    near_four_more = swapped(four_more, 4)
+    near_one_more = swapped(one_more, 1)
+    near_two_more = swapped(two_more, 2)
+    high_four, low_four, diagonal, other_four = call(
         four_kernel,
-        [message] + mixed + [shape(3 * B, B), shape(2, B, B)],
-        [vmem] * 6,
+        mixed + [shape(3 * B, B), shape(2, B, B)],
+        [vmem] * 5,
         8,
-        (left_high, left_low, start, held, diagonal, near_four),
-    )
-    near_one_more = swapped(one_more, 1)
-    two_more, four_more = call(more_kernel, [message] * 2, [vmem] * 2, 300, (one_more, held))
-    near_four_more = swapped(four_more, 4)
-    near_two_more = swapped(two_more, 2)
+        (left_high, left_low, start, diagonal, near_four),
+    )
     high_one, low_one, diagonal, other_one = call(
         fourth_kernel,
         mixed + [shape(3 * B, B), shape(2, B, B)],

time: 31.1 us -> 30.6 us (0.984)
  waiting for transfers between devices: 3.75 us -> 2.71 us
  starting transfers between devices: 16.8 us -> 17.4 us
    ppermute x11, waiting for transfers between devices: 3.75 us -> 2.71 us  [swapped(): return lax.ppermute(cells, axis, pairs)]
    ppermute x11, starting transfers between devices: 16.8 us -> 17.4 us  [swapped(): return lax.ppermute(cells, axis, pairs)]
  transfers between devices with their start and end apart: 11 -> 11, of which waited for: 3 -> 4; matrix products, arithmetic and copies ran while one was open for 0% -> 0% of each run, Pallas kernels for 23% -> 23%
where the time goes in v20:
time: 30.6 us; the launch traced here: 30.3 us
  starting transfers between devices  17.4 us (57%)
  Pallas kernels  9.49 us (31%)
  waiting for transfers between devices  2.71 us (9%)
  between operations  0.75 us (2%)
    ppermute x11, starting transfers between devices, swapped(): return lax.ppermute(cells, axis, pairs)  17.4 us
    pallas_call x13, Pallas kernels, call(): pl.pallas_call(kernel, out_shape=shapes, in_specs=in_specs, out_specs=out...  9.49 us
    ppermute x11, waiting for transfers between devices, swapped(): return lax.ppermute(cells, axis, pairs)  2.71 us
  transfers between devices with their start and end apart: 11, of which 4 were waited for; matrix products, arithmetic and copies ran while one was open for 0% of the time, Pallas kernels for 23%

profile of v20, /device:TPU:0, one launch (start us, length us, event | category | flops | bytes accessed | tf_op | source)
XLA Modules:
  0.0 30.3 jit_solution(14924504174844601974)
XLA Ops:
  0.6 1.1 %shard_map.77 = (f32[4,128,128]{2,1,0:T(8,128)S(1)}, f32[2,128,128]{2,1,0:T(8,128)S(1)}) custom-call(s32[1,1,5]{2,1,0:T(1,128)} %cutoff_hbm.5, f32[1,1,5,128,128]{4,3,2,1,0:T(8,128)} %ham_hbm.5, f32[1,1,5,128,128]{4,3,2,1,0:T(8,128)} %inv_hbm.5, f32[2,1,1,5,128,128]{5,4,3,2,1,0:T(8,128)} %rho_hbm.5), custom_call_target="tpu_custom_call" | custom-call | bytes 1703956 | tf_op jit(solution)/shard_map/pallas_call | solution.py:294
  1.7 3.0 %collective-permute-start.2 = (f32[4,128,128]{2,1,0:T(8,128)S(1)}, f32[4,128,128]{2,1,0:T(8,128)S(1)}, u32[]{:S(2)}, u32[]{:S(2)}) collective-permute-start(f32[4,128,128]{2,1,0:T(8,128)S(1)} %get-tuple-element.43.message), channel_id=1, source_target_pairs={{0,4},{4,0},{8,12},{12,8},{16,20},{20,16},{24,28},{28,24},{1,5},{5... | collective-permute-start | bytes 786440 | tf_op jit(solution)/shard_map/ppermute | solution.py:30
  4.8 0.7 %collective-permute-start.1 = (f32[4,128,128]{2,1,0:T(8,128)S(1)}, f32[4,128,128]{2,1,0:T(8,128)S(1)}, u32[]{:S(2)}, u32[]{:S(2)}) collective-permute-start(f32[4,128,128]{2,1,0:T(8,128)S(1)} %shard_map.78.message), channel_id=1, source_target_pairs={{1,2},{2,1},{3,0},{0,3},{5,6},{6,5},{7,4},{4,7},{9,10},{10,9},{11,... | collective-permute-start | bytes 786440 | tf_op jit(solution)/shard_map/ppermute | solution.py:30
  5.5 3.6 %collective-permute-start.3 = (f32[4,128,128]{2,1,0:T(8,128)S(1)}, f32[4,128,128]{2,1,0:T(8,128)S(1)}, u32[]{:S(2)}, u32[]{:S(2)}) collective-permute-start(f32[4,128,128]{2,1,0:T(8,128)S(1)} %shard_map.79.message), channel_id=1, source_target_pairs={{4,8},{8,4},{12,16},{16,12},{20,24},{24,20},{28,0},{0,28},{5,9},{9... | collective-permute-start | bytes 786440 | tf_op jit(solution)/shard_map/ppermute | solution.py:30
  9.1 1.0 %shard_map.80.after = f32[8,128,128]{2,1,0:T(8,128)S(1)} custom-call(s32[1,1,5]{2,1,0:T(1,128)} %cutoff_hbm.5, f32[1,1,5,128,128]{4,3,2,1,0:T(8,128)} %ham_hbm.5, f32[1,1,5,128,128]{4,3,2,1,0:T(8,128)} %inv_hbm.5, f32[2,1,1,5,128,128]{5,4,3,2,1,0:T(8,128)} %rho_hbm.5, f32[4,128,128]{2,1,0:T(8,128)S(1)} %shard_map.79.message), custom_call_target="tpu_custom_call" | custom-call | flops 6291456000 | bytes 2097172 | tf_op jit(solution)/shard_map/pallas_call | solution.py:294
  10.2 0.7 %collective-permute-start = (f32[8,128,128]{2,1,0:T(8,128)S(1)}, f32[8,128,128]{2,1,0:T(8,128)S(1)}, u32[]{:S(2)}, u32[]{:S(2)}) collective-permute-start(f32[8,128,128]{2,1,0:T(8,128)S(1)} %shard_map.80.after), channel_id=1, source_target_pairs={{0,1},{1,0},{2,3},{3,2},{4,5},{5,4},{6,7},{7,6},{8,9},{9,8},{10,11... | collective-permute-start | bytes 1572872 | tf_op jit(solution)/shard_map/ppermute | solution.py:30
  10.9 1.4 %shard_map.81 = (f32[3,5,128,128]{3,2,1,0:T(8,128)S(1)}, bf16[384,640]{1,0:T(8,128)(2,1)S(1)}, bf16[384,640]{1,0:T(8,128)(2,1)S(1)}, bf16[128,640]{1,0:T(8,128)(...) custom-call(s32[1,1,5]{2,1,0:T(1,128)} %cutoff_hbm.5, f32[1,1,5,128,128]{4,3,2,1,0:T(8,128)} %ham_hbm.5, ...), custom_call_target="tpu_custom_call" | custom-call | flops 25165824000 | bytes 5472788 | tf_op jit(solution)/shard_map/pallas_call | solution.py:294
  12.3 0.1 collective-permute-done.three
  12.4 1.2 %shard_map.82 = (f32[384,640]{1,0:T(8,128)S(1)}, f32[384,128]{1,0:T(8,128)S(1)}, f32[2,2,128,128]{3,2,1,0:T(8,128)S(1)}, f32[3,1,1,5,128,128]{5,4,3,2,1,0:T(8,128)S(1)}) custom-call(bf16[384,640]{1,0:T(8,128)(2,1)S(1)} %get-tuple-element.46.left_high, bf16[384,640]{1,0:T(8,128)(2,1)S(1)} %get-tuple-element.47.left_low, ...), custom_call_target="tpu_custom_call" | custom-call | flops 100663296000 | bytes 7536640 | tf_op jit(solution)/shard_map/pallas_call | solution.py:294
  13.7 0.0 collective-permute-done.1.four.arrived
  13.7 0.1 shard_map.86
  13.8 0.6 %collective-permute-start.4 = (f32[4,128,128]{2,1,0:T(8,128)S(1)}, f32[4,128,128]{2,1,0:T(8,128)S(1)}, u32[]{:S(2)}, u32[]{:S(2)}) collective-permute-start(f32[4,128,128]{2,1,0:T(8,128)S(1)} %get-tuple-element.71), channel_id=1, source_target_pairs={{1,2},{2,1},{3,0},{0,3},{5,6},{6,5},{7,4},{4,7},{9,10},{10,9},{11,... | collective-permute-start | bytes 786440 | tf_op jit(solution)/shard_map/ppermute | solution.py:30
  14.3 0.4 %collective-permute-start.5 = (f32[4,128,128]{2,1,0:T(8,128)S(1)}, f32[4,128,128]{2,1,0:T(8,128)S(1)}, u32[]{:S(2)}, u32[]{:S(2)}) collective-permute-start(f32[4,128,128]{2,1,0:T(8,128)S(1)} %get-tuple-element.75), channel_id=1, source_target_pairs={{0,4},{4,0},{8,12},{12,8},{16,20},{20,16},{24,28},{28,24},{1,5},{5... | collective-permute-start | bytes 786440 | tf_op jit(solution)/shard_map/ppermute | solution.py:30
  14.7 4.6 %collective-permute-start.6 = (f32[4,128,128]{2,1,0:T(8,128)S(1)}, f32[4,128,128]{2,1,0:T(8,128)S(1)}, u32[]{:S(2)}, u32[]{:S(2)}) collective-permute-start(f32[4,128,128]{2,1,0:T(8,128)S(1)} %get-tuple-element.76), channel_id=1, source_target_pairs={{4,8},{8,4},{12,16},{16,12},{20,24},{24,20},{28,0},{0,28},{5,9},{9... | collective-permute-start | bytes 786440 | tf_op jit(solution)/shard_map/ppermute | solution.py:30
  19.3 0.6 %shard_map.83 = (bf16[384,128]{1,0:T(8,128)(2,1)S(1)}, bf16[384,128]{1,0:T(8,128)(2,1)S(1)}, f32[384,128]{1,0:T(8,128)S(1)}, f32[2,128,128]{2,1,0:T(8,128)S(1)}) custom-call(bf16[384,640]{1,0:T(8,128)(2,1)S(1)} %get-tuple-element.46.left_high, bf16[384,640]{1,0:T(8,128)(2,1)S(1)} %get-tuple-element.47.left_low, f32[384,640]{1,0:T(8,128)S(1)} %get-tuple-element.52.start, ...), custom_call_target="tpu_custom_call" | custom-call | flops 100663296 | bytes 4128768 | tf_op jit(solution)/shard_map/pallas_call | solution.py:294
  19.9 0.0 collective-permute-done.2.one
  19.9 0.6 %shard_map.84 = (bf16[384,128]{1,0:T(8,128)(2,1)S(1)}, bf16[384,128]{1,0:T(8,128)(2,1)S(1)}, f32[384,128]{1,0:T(8,128)S(1)}, f32[2,128,128]{2,1,0:T(8,128)S(1)}) custom-call(bf16[384,640]{1,0:T(8,128)(2,1)S(1)} %get-tuple-element.46.left_high, bf16[384,640]{1,0:T(8,128)(2,1)S(1)} %get-tuple-element.47.left_low, f32[384,640]{1,0:T(8,128)S(1)} %get-tuple-element.52.start, ...), custom_call_target="tpu_custom_call" | custom-call | flops 125829120 | bytes 4128768 | tf_op jit(solution)/shard_map/pallas_call | solution.py:294
  20.6 0.0 collective-permute-done.3.two
  20.6 0.9 %shard_map.85 = (f32[4,128,128]{2,1,0:T(8,128)S(1)}, bf16[384,128]{1,0:T(8,128)(2,1)S(1)}, bf16[384,128]{1,0:T(8,128)(2,1)S(1)}, bf16[384,128]{1,0:T(8,128)(2,1)...) custom-call(bf16[384,640]{1,0:T(8,128)(2,1)S(1)} %get-tuple-element., ...), custom_call_target="tpu_custom_call" | custom-call | flops 276824064 | bytes 7280640 | tf_op jit(solution)/shard_map/pallas_call | solution.py:294
  21.5 0.1 collective-permute-start.9
  21.7 0.0 collective-permute-start.7
  21.7 1.1 %collective-permute-done.9.arrived.c3 = f32[3,128]{1,0:T(4,128)S(1)} collective-permute-done((f32[3,128]{1,0:T(4,128)S(1)}, f32[3,128]{1,0:T(4,128)S(1)}, u32[]{:S(2)}, u32[]{:S(2)}) %collective-permute-start.9) | collective-permute-done | bytes 1568 | tf_op jit(solution)/shard_map/ppermute | solution.py:30
  22.7 1.8 %collective-permute-start.8 = (f32[3,128]{1,0:T(4,128)S(1)}, f32[3,128]{1,0:T(4,128)S(1)}, u32[]{:S(2)}, u32[]{:S(2)}) collective-permute-start(f32[3,128]{1,0:T(4,128)S(1)} %get-tuple-element.78), channel_id=1, source_target_pairs={{4,8},{8,4},{12,16},{16,12},{20,24},{24,20},{28,0},{0,28},{5,9},{9... | collective-permute-start | bytes 4616 | tf_op jit(solution)/shard_map/ppermute | solution.py:30
  24.6 0.0 collective-permute-done.4.four
  24.6 1.8 %collective-permute-start.10 = (f32[3,128]{1,0:T(4,128)S(1)}, f32[3,128]{1,0:T(4,128)S(1)}, u32[]{:S(2)}, u32[]{:S(2)}) collective-permute-start(f32[3,128]{1,0:T(4,128)S(1)} %shard_map.88), channel_id=1, source_target_pairs={{1,2},{2,1},{3,0},{0,3},{5,6},{6,5},{7,4},{4,7},{9,10},{10,9},{11,... | collective-permute-start | bytes 4616 | tf_op jit(solution)/shard_map/ppermute | solution.py:30
  26.3 1.2 %shard_map.87 = (f32[2,1,1,5,128,128]{5,4,3,2,1,0:T(8,128)}, f32[3,128,128]{2,1,0:T(8,128)S(1)}, f32[128,128]{1,0:T(8,128)S(1)}, f32[3,128]{1,0:T(4,128)S(1)}) custom-call(f32[3,5,128,128]{3,2,1,0:T(8,128)S(1)} %get-tuple-element.45.held, f32[4,128,128]{2,1,0:T(8,128)S(1)} %get-tuple-element.63.new, bf16[384,640]{1,0:T(8,128)(2,1)S(1)} %get-tuple-element.46.left_high, ...), custom_call_target="tpu_custom_call" | custom-call | flops 125829120 | bytes 6030848 | tf_op jit(solution)/shard_map/pallas_call | solution.py:294
  27.5 1.3 %collective-permute-done.7.c1 = f32[3,128]{1,0:T(4,128)S(1)} collective-permute-done((f32[3,128]{1,0:T(4,128)S(1)}, f32[3,128]{1,0:T(4,128)S(1)}, u32[]{:S(2)}, u32[]{:S(2)}) %collective-permute-start.7) | collective-permute-done | bytes 1568 | tf_op jit(solution)/shard_map/ppermute | solution.py:30
  28.8 0.2 collective-permute-done.8.c2
  29.0 0.0 collective-permute-done.10.c4
  29.0 0.0 collective-permute-done.5.one
  29.0 0.0 collective-permute-done.6.two
  29.0 1.3 %shard_map.89 = (f32[2,1,1,5,128,128]{5,4,3,2,1,0:T(8,128)}, f32[3,1,64]{2,1,0:T(1,128)}) custom-call(f32[3,5,128,128]{3,2,1,0:T(8,128)S(1)} %get-tuple-element.45.held, f32[3,1,1,5,128,128]{5,4,3,2,1,0:T(8,128)S(1)} %get-tuple-element.50.der_ref, f32[64,128]{1,0:T(8,128)S(1)} %get-tuple-element.51.members, ...), custom_call_target="tpu_custom_call", output_to_operand_aliasing={{0}: (16, {})} | custom-call | flops 125829120 | bytes 4890880 | tf_op jit(solution)/shard_map/pallas_call | solution.py:294
  (3 shorter events, 0.0 us)
Async XLA Ops:
  1.7 18.2 %collective-permute-start.2 = (f32[4,128,128]{2,1,0:T(8,128)S(1)}, f32[4,128,128]{2,1,0:T(8,128)S(1)}, u32[]{:S(2)}, u32[]{:S(2)}) collective-permute-start(f32[4,128,128]{2,1,0:T(8,128)S(1)} %get-tuple-element.43.message), channel_id=1, source_target_pairs={{0,4},{4,0},{8,12},{12,8},{16,20},{20,16},{24,28},{28,24},{1,5},{5... | collective-permute-start | bytes 786440 | tf_op jit(solution)/shard_map/ppermute | solution.py:30
  4.8 8.9 %collective-permute-start.1 = (f32[4,128,128]{2,1,0:T(8,128)S(1)}, f32[4,128,128]{2,1,0:T(8,128)S(1)}, u32[]{:S(2)}, u32[]{:S(2)}) collective-permute-start(f32[4,128,128]{2,1,0:T(8,128)S(1)} %shard_map.78.message), channel_id=1, source_target_pairs={{1,2},{2,1},{3,0},{0,3},{5,6},{6,5},{7,4},{4,7},{9,10},{10,9},{11,... | collective-permute-start | bytes 786440 | tf_op jit(solution)/shard_map/ppermute | solution.py:30
  5.5 15.0 %collective-permute-start.3 = (f32[4,128,128]{2,1,0:T(8,128)S(1)}, f32[4,128,128]{2,1,0:T(8,128)S(1)}, u32[]{:S(2)}, u32[]{:S(2)}) collective-permute-start(f32[4,128,128]{2,1,0:T(8,128)S(1)} %shard_map.79.message), channel_id=1, source_target_pairs={{4,8},{8,4},{12,16},{16,12},{20,24},{24,20},{28,0},{0,28},{5,9},{9... | collective-permute-start | bytes 786440 | tf_op jit(solution)/shard_map/ppermute | solution.py:30
  10.2 2.3 %collective-permute-start = (f32[8,128,128]{2,1,0:T(8,128)S(1)}, f32[8,128,128]{2,1,0:T(8,128)S(1)}, u32[]{:S(2)}, u32[]{:S(2)}) collective-permute-start(f32[8,128,128]{2,1,0:T(8,128)S(1)} %shard_map.80.after), channel_id=1, source_target_pairs={{0,1},{1,0},{2,3},{3,2},{4,5},{5,4},{6,7},{7,6},{8,9},{9,8},{10,11... | collective-permute-start | bytes 1572872 | tf_op jit(solution)/shard_map/ppermute | solution.py:30
  13.8 10.8 %collective-permute-start.4 = (f32[4,128,128]{2,1,0:T(8,128)S(1)}, f32[4,128,128]{2,1,0:T(8,128)S(1)}, u32[]{:S(2)}, u32[]{:S(2)}) collective-permute-start(f32[4,128,128]{2,1,0:T(8,128)S(1)} %get-tuple-element.71), channel_id=1, source_target_pairs={{1,2},{2,1},{3,0},{0,3},{5,6},{6,5},{7,4},{4,7},{9,10},{10,9},{11,... | collective-permute-start | bytes 786440 | tf_op jit(solution)/shard_map/ppermute | solution.py:30
  14.3 14.7 %collective-permute-start.5 = (f32[4,128,128]{2,1,0:T(8,128)S(1)}, f32[4,128,128]{2,1,0:T(8,128)S(1)}, u32[]{:S(2)}, u32[]{:S(2)}) collective-permute-start(f32[4,128,128]{2,1,0:T(8,128)S(1)} %get-tuple-element.75), channel_id=1, source_target_pairs={{0,4},{4,0},{8,12},{12,8},{16,20},{20,16},{24,28},{28,24},{1,5},{5... | collective-permute-start | bytes 786440 | tf_op jit(solution)/shard_map/ppermute | solution.py:30
  14.7 14.3 %collective-permute-start.6 = (f32[4,128,128]{2,1,0:T(8,128)S(1)}, f32[4,128,128]{2,1,0:T(8,128)S(1)}, u32[]{:S(2)}, u32[]{:S(2)}) collective-permute-start(f32[4,128,128]{2,1,0:T(8,128)S(1)} %get-tuple-element.76), channel_id=1, source_target_pairs={{4,8},{8,4},{12,16},{16,12},{20,24},{24,20},{28,0},{0,28},{5,9},{9... | collective-permute-start | bytes 786440 | tf_op jit(solution)/shard_map/ppermute | solution.py:30
  21.5 1.2 %collective-permute-start.9 = (f32[3,128]{1,0:T(4,128)S(1)}, f32[3,128]{1,0:T(4,128)S(1)}, u32[]{:S(2)}, u32[]{:S(2)}) collective-permute-start(f32[3,128]{1,0:T(4,128)S(1)} %get-tuple-element.79), channel_id=1, source_target_pairs={{0,1},{1,0},{2,3},{3,2},{4,5},{5,4},{6,7},{7,6},{8,9},{9,8},{10,11... | collective-permute-start | bytes 4616 | tf_op jit(solution)/shard_map/ppermute | solution.py:30
  21.7 7.1 %collective-permute-start.7 = (f32[3,128]{1,0:T(4,128)S(1)}, f32[3,128]{1,0:T(4,128)S(1)}, u32[]{:S(2)}, u32[]{:S(2)}) collective-permute-start(f32[3,128]{1,0:T(4,128)S(1)} %get-tuple-element.77), channel_id=1, source_target_pairs={{0,4},{4,0},{8,12},{12,8},{16,20},{20,16},{24,28},{28,24},{1,5},{5... | collective-permute-start | bytes 4616 | tf_op jit(solution)/shard_map/ppermute | solution.py:30
  22.7 6.3 %collective-permute-start.8 = (f32[3,128]{1,0:T(4,128)S(1)}, f32[3,128]{1,0:T(4,128)S(1)}, u32[]{:S(2)}, u32[]{:S(2)}) collective-permute-start(f32[3,128]{1,0:T(4,128)S(1)} %get-tuple-element.78), channel_id=1, source_target_pairs={{4,8},{8,4},{12,16},{16,12},{20,24},{24,20},{28,0},{0,28},{5,9},{9... | collective-permute-start | bytes 4616 | tf_op jit(solution)/shard_map/ppermute | solution.py:30
  24.6 4.5 %collective-permute-start.10 = (f32[3,128]{1,0:T(4,128)S(1)}, f32[3,128]{1,0:T(4,128)S(1)}, u32[]{:S(2)}, u32[]{:S(2)}) collective-permute-start(f32[3,128]{1,0:T(4,128)S(1)} %shard_map.88), channel_id=1, source_target_pairs={{1,2},{2,1},{3,0},{0,3},{5,6},{6,5},{7,4},{4,7},{9,10},{10,9},{11,... | collective-permute-start | bytes 4616 | tf_op jit(solution)/shard_map/ppermute | solution.py:30

commit v21 on v20

--- a/solution.py
+++ b/solution.py
@@ -183,10 +183,13 @@
     mixed_high[...], mixed_low[...] = mixed
 
 
-def more_kernel(arrived, after, held, one_more, two_more, four_more):
+def four_more_kernel(after, held, four_more):
+    send_more(four_more, held, 4)
+
+
+def more_kernel(arrived, after, held, one_more, two_more):
     send_more(one_more, held, 1)
     send_more(two_more, held, 2)
-    send_more(four_more, held, 4)
 
 
 def fourth_kernel(left_high, left_low, start, diagonal, one, mixed_high, mixed_low, diagonal_out, other):
@@ -355,7 +358,8 @@
         (left_high, left_low, ham_high, ham_low, held, near_three, derivative),
         scratch=[dma(())],
     )
-    one_more, two_more, four_more = call(more_kernel, [message] * 3, [vmem] * 3, 300, (near_four, other_three, held))
+    (four_more,) = call(four_more_kernel, [message], [vmem] * 2, 7, (other_three, held))
+    one_more, two_more = call(more_kernel, [message] * 2, [vmem] * 3, 300, (near_four, four_more, held))
     near_four_more = swapped(four_more, 4)
     near_one_more = swapped(one_more, 1)
     near_two_more = swapped(two_more, 2)

time: 30.6 us -> 34.5 us (1.13)
  starting transfers between devices: 17.4 us -> 22.6 us
  waiting for transfers between devices: 2.71 us -> 1.17 us
    ppermute x11, starting transfers between devices: 17.4 us -> 22.6 us  [swapped(): return lax.ppermute(cells, axis, pairs)]
    ppermute x11, waiting for transfers between devices: 2.71 us -> 1.17 us  [swapped(): return lax.ppermute(cells, axis, pairs)]
    pallas_call x13 -> x14, Pallas kernels: 9.49 us -> 9.47 us  [call(): pl.pallas_call(kernel, out_shape=shapes, in_specs=in_specs, out_specs=out...]
  transfers between devices with their start and end apart: 11 -> 11, of which waited for: 4 -> 3; matrix products, arithmetic and copies ran while one was open for 0% -> 0% of each run, Pallas kernels for 23% -> 21%
where the time goes in v21:
time: 34.5 us; the launch traced here: 34 us
  starting transfers between devices  22.6 us (66%)
  Pallas kernels  9.47 us (27%)
  waiting for transfers between devices  1.17 us (3%)
  between operations  0.77 us (2%)
    ppermute x11, starting transfers between devices, swapped(): return lax.ppermute(cells, axis, pairs)  22.6 us
    pallas_call x14, Pallas kernels, call(): pl.pallas_call(kernel, out_shape=shapes, in_specs=in_specs, out_specs=out...  9.47 us
    ppermute x11, waiting for transfers between devices, swapped(): return lax.ppermute(cells, axis, pairs)  1.17 us
  transfers between devices with their start and end apart: 11, of which 3 were waited for; matrix products, arithmetic and copies ran while one was open for 0% of the time, Pallas kernels for 21%

profile of v21, /device:TPU:0, one launch (start us, length us, event | category | flops | bytes accessed | tf_op | source)
XLA Modules:
  0.0 34.0 jit_solution(9406203987822021089)
XLA Ops:
  0.6 1.1 %shard_map.77 = (f32[4,128,128]{2,1,0:T(8,128)S(1)}, f32[2,128,128]{2,1,0:T(8,128)S(1)}) custom-call(s32[1,1,5]{2,1,0:T(1,128)} %cutoff_hbm.5, f32[1,1,5,128,128]{4,3,2,1,0:T(8,128)} %ham_hbm.5, f32[1,1,5,128,128]{4,3,2,1,0:T(8,128)} %inv_hbm.5, f32[2,1,1,5,128,128]{5,4,3,2,1,0:T(8,128)} %rho_hbm.5), custom_call_target="tpu_custom_call" | custom-call | bytes 1703956 | tf_op jit(solution)/shard_map/pallas_call | solution.py:297
  1.7 3.0 %collective-permute-start.2 = (f32[4,128,128]{2,1,0:T(8,128)S(1)}, f32[4,128,128]{2,1,0:T(8,128)S(1)}, u32[]{:S(2)}, u32[]{:S(2)}) collective-permute-start(f32[4,128,128]{2,1,0:T(8,128)S(1)} %get-tuple-element.42.message), channel_id=1, source_target_pairs={{0,4},{4,0},{8,12},{12,8},{16,20},{20,16},{24,28},{28,24},{1,5},{5... | collective-permute-start | bytes 786440 | tf_op jit(solution)/shard_map/ppermute | solution.py:30
  4.8 0.7 %collective-permute-start.1 = (f32[4,128,128]{2,1,0:T(8,128)S(1)}, f32[4,128,128]{2,1,0:T(8,128)S(1)}, u32[]{:S(2)}, u32[]{:S(2)}) collective-permute-start(f32[4,128,128]{2,1,0:T(8,128)S(1)} %shard_map.78.message), channel_id=1, source_target_pairs={{1,2},{2,1},{3,0},{0,3},{5,6},{6,5},{7,4},{4,7},{9,10},{10,9},{11,... | collective-permute-start | bytes 786440 | tf_op jit(solution)/shard_map/ppermute | solution.py:30
  5.5 3.6 %collective-permute-start.3 = (f32[4,128,128]{2,1,0:T(8,128)S(1)}, f32[4,128,128]{2,1,0:T(8,128)S(1)}, u32[]{:S(2)}, u32[]{:S(2)}) collective-permute-start(f32[4,128,128]{2,1,0:T(8,128)S(1)} %shard_map.79.message), channel_id=1, source_target_pairs={{4,8},{8,4},{12,16},{16,12},{20,24},{24,20},{28,0},{0,28},{5,9},{9... | collective-permute-start | bytes 786440 | tf_op jit(solution)/shard_map/ppermute | solution.py:30
  9.1 1.0 %shard_map.80.after = f32[8,128,128]{2,1,0:T(8,128)S(1)} custom-call(s32[1,1,5]{2,1,0:T(1,128)} %cutoff_hbm.5, f32[1,1,5,128,128]{4,3,2,1,0:T(8,128)} %ham_hbm.5, f32[1,1,5,128,128]{4,3,2,1,0:T(8,128)} %inv_hbm.5, f32[2,1,1,5,128,128]{5,4,3,2,1,0:T(8,128)} %rho_hbm.5, f32[4,128,128]{2,1,0:T(8,128)S(1)} %shard_map.79.message), custom_call_target="tpu_custom_call" | custom-call | flops 6291456000 | bytes 2097172 | tf_op jit(solution)/shard_map/pallas_call | solution.py:297
  10.2 0.7 %collective-permute-start = (f32[8,128,128]{2,1,0:T(8,128)S(1)}, f32[8,128,128]{2,1,0:T(8,128)S(1)}, u32[]{:S(2)}, u32[]{:S(2)}) collective-permute-start(f32[8,128,128]{2,1,0:T(8,128)S(1)} %shard_map.80.after), channel_id=1, source_target_pairs={{0,1},{1,0},{2,3},{3,2},{4,5},{5,4},{6,7},{7,6},{8,9},{9,8},{10,11... | collective-permute-start | bytes 1572872 | tf_op jit(solution)/shard_map/ppermute | solution.py:30
  10.9 1.4 %shard_map.81 = (f32[3,5,128,128]{3,2,1,0:T(8,128)S(1)}, bf16[384,640]{1,0:T(8,128)(2,1)S(1)}, bf16[384,640]{1,0:T(8,128)(2,1)S(1)}, bf16[128,640]{1,0:T(8,128)(...) custom-call(s32[1,1,5]{2,1,0:T(1,128)} %cutoff_hbm.5, f32[1,1,5,128,128]{4,3,2,1,0:T(8,128)} %ham_hbm.5, ...), custom_call_target="tpu_custom_call" | custom-call | flops 25165824000 | bytes 5472788 | tf_op jit(solution)/shard_map/pallas_call | solution.py:297
  12.3 0.1 collective-permute-done.three
  12.4 1.2 %shard_map.82 = (f32[384,640]{1,0:T(8,128)S(1)}, f32[384,128]{1,0:T(8,128)S(1)}, f32[2,2,128,128]{3,2,1,0:T(8,128)S(1)}, f32[3,1,1,5,128,128]{5,4,3,2,1,0:T(8,128)S(1)}) custom-call(bf16[384,640]{1,0:T(8,128)(2,1)S(1)} %get-tuple-element.45.left_high, bf16[384,640]{1,0:T(8,128)(2,1)S(1)} %get-tuple-element.46.left_low, ...), custom_call_target="tpu_custom_call" | custom-call | flops 100663296000 | bytes 7536640 | tf_op jit(solution)/shard_map/pallas_call | solution.py:297
  13.7 0.6 %collective-permute-start.4 = (f32[4,128,128]{2,1,0:T(8,128)S(1)}, f32[4,128,128]{2,1,0:T(8,128)S(1)}, u32[]{:S(2)}, u32[]{:S(2)}) collective-permute-start(f32[4,128,128]{2,1,0:T(8,128)S(1)} %shard_map.86.after), channel_id=1, source_target_pairs={{1,2},{2,1},{3,0},{0,3},{5,6},{6,5},{7,4},{4,7},{9,10},{10,9},{11,... | collective-permute-start | bytes 786440 | tf_op jit(solution)/shard_map/ppermute | solution.py:30
  14.3 0.0 collective-permute-done.1.four.arrived
  14.3 0.1 collective-permute-start.5
  14.4 4.2 %collective-permute-start.6 = (f32[4,128,128]{2,1,0:T(8,128)S(1)}, f32[4,128,128]{2,1,0:T(8,128)S(1)}, u32[]{:S(2)}, u32[]{:S(2)}) collective-permute-start(f32[4,128,128]{2,1,0:T(8,128)S(1)} %get-tuple-element.74), channel_id=1, source_target_pairs={{4,8},{8,4},{12,16},{16,12},{20,24},{24,20},{28,0},{0,28},{5,9},{9... | collective-permute-start | bytes 786440 | tf_op jit(solution)/shard_map/ppermute | solution.py:30
  18.6 0.6 %shard_map.83 = (bf16[384,128]{1,0:T(8,128)(2,1)S(1)}, bf16[384,128]{1,0:T(8,128)(2,1)S(1)}, f32[384,128]{1,0:T(8,128)S(1)}, f32[2,128,128]{2,1,0:T(8,128)S(1)}) custom-call(bf16[384,640]{1,0:T(8,128)(2,1)S(1)} %get-tuple-element.45.left_high, bf16[384,640]{1,0:T(8,128)(2,1)S(1)} %get-tuple-element.46.left_low, f32[384,640]{1,0:T(8,128)S(1)} %get-tuple-element.51.start, ...), custom_call_target="tpu_custom_call" | custom-call | flops 100663296 | bytes 4128768 | tf_op jit(solution)/shard_map/pallas_call | solution.py:297
  19.2 0.0 collective-permute-done.2.one
  19.2 0.6 %shard_map.84 = (bf16[384,128]{1,0:T(8,128)(2,1)S(1)}, bf16[384,128]{1,0:T(8,128)(2,1)S(1)}, f32[384,128]{1,0:T(8,128)S(1)}, f32[2,128,128]{2,1,0:T(8,128)S(1)}) custom-call(bf16[384,640]{1,0:T(8,128)(2,1)S(1)} %get-tuple-element.45.left_high, bf16[384,640]{1,0:T(8,128)(2,1)S(1)} %get-tuple-element.46.left_low, f32[384,640]{1,0:T(8,128)S(1)} %get-tuple-element.51.start, ...), custom_call_target="tpu_custom_call" | custom-call | flops 125829120 | bytes 4128768 | tf_op jit(solution)/shard_map/pallas_call | solution.py:297
  19.8 0.0 collective-permute-done.3.two
  19.8 0.9 %shard_map.85 = (f32[4,128,128]{2,1,0:T(8,128)S(1)}, bf16[384,128]{1,0:T(8,128)(2,1)S(1)}, bf16[384,128]{1,0:T(8,128)(2,1)S(1)}, bf16[384,128]{1,0:T(8,128)(2,1)...) custom-call(bf16[384,640]{1,0:T(8,128)(2,1)S(1)} %get-tuple-element., ...), custom_call_target="tpu_custom_call" | custom-call | flops 276824064 | bytes 7280640 | tf_op jit(solution)/shard_map/pallas_call | solution.py:297
  20.7 0.1 collective-permute-start.9
  20.8 0.2 collective-permute-start.7
  21.0 0.9 %collective-permute-done.9.arrived.c3 = f32[3,128]{1,0:T(4,128)S(1)} collective-permute-done((f32[3,128]{1,0:T(4,128)S(1)}, f32[3,128]{1,0:T(4,128)S(1)}, u32[]{:S(2)}, u32[]{:S(2)}) %collective-permute-start.9) | collective-permute-done | bytes 1568 | tf_op jit(solution)/shard_map/ppermute | solution.py:30
  22.0 2.6 %collective-permute-start.8 = (f32[3,128]{1,0:T(4,128)S(1)}, f32[3,128]{1,0:T(4,128)S(1)}, u32[]{:S(2)}, u32[]{:S(2)}) collective-permute-start(f32[3,128]{1,0:T(4,128)S(1)} %get-tuple-element.76), channel_id=1, source_target_pairs={{4,8},{8,4},{12,16},{16,12},{20,24},{24,20},{28,0},{0,28},{5,9},{9... | collective-permute-start | bytes 4616 | tf_op jit(solution)/shard_map/ppermute | solution.py:30
  24.5 0.0 collective-permute-done.4.four
  24.5 6.9 %collective-permute-start.10 = (f32[3,128]{1,0:T(4,128)S(1)}, f32[3,128]{1,0:T(4,128)S(1)}, u32[]{:S(2)}, u32[]{:S(2)}) collective-permute-start(f32[3,128]{1,0:T(4,128)S(1)} %shard_map.89), channel_id=1, source_target_pairs={{1,2},{2,1},{3,0},{0,3},{5,6},{6,5},{7,4},{4,7},{9,10},{10,9},{11,... | collective-permute-start | bytes 4616 | tf_op jit(solution)/shard_map/ppermute | solution.py:30
  31.4 1.2 %shard_map.87 = (f32[2,1,1,5,128,128]{5,4,3,2,1,0:T(8,128)}, f32[3,128,128]{2,1,0:T(8,128)S(1)}, f32[128,128]{1,0:T(8,128)S(1)}, f32[3,128]{1,0:T(4,128)S(1)}) custom-call(f32[3,5,128,128]{3,2,1,0:T(8,128)S(1)} %get-tuple-element.44.held, f32[4,128,128]{2,1,0:T(8,128)S(1)} %get-tuple-element.62.new, bf16[384,640]{1,0:T(8,128)(2,1)S(1)} %get-tuple-element.45.left_high, ...), custom_call_target="tpu_custom_call" | custom-call | flops 125829120 | bytes 6030848 | tf_op jit(solution)/shard_map/pallas_call | solution.py:297
  32.6 0.0 collective-permute-done.7.c1
  32.6 0.0 collective-permute-done.8.c2
  32.7 0.1 collective-permute-done.10.c4
  32.7 0.0 collective-permute-done.5.one
  32.7 0.0 collective-permute-done.6.two
  32.7 1.3 %shard_map.90 = (f32[2,1,1,5,128,128]{5,4,3,2,1,0:T(8,128)}, f32[3,1,64]{2,1,0:T(1,128)}) custom-call(f32[3,5,128,128]{3,2,1,0:T(8,128)S(1)} %get-tuple-element.44.held, f32[3,1,1,5,128,128]{5,4,3,2,1,0:T(8,128)S(1)} %get-tuple-element.49.der_ref, f32[64,128]{1,0:T(8,128)S(1)} %get-tuple-element.50.members, ...), custom_call_target="tpu_custom_call", output_to_operand_aliasing={{0}: (16, {})} | custom-call | flops 125829120 | bytes 4890880 | tf_op jit(solution)/shard_map/pallas_call | solution.py:297
  (5 shorter events, 0.1 us)
Async XLA Ops:
  1.7 17.5 %collective-permute-start.2 = (f32[4,128,128]{2,1,0:T(8,128)S(1)}, f32[4,128,128]{2,1,0:T(8,128)S(1)}, u32[]{:S(2)}, u32[]{:S(2)}) collective-permute-start(f32[4,128,128]{2,1,0:T(8,128)S(1)} %get-tuple-element.42.message), channel_id=1, source_target_pairs={{0,4},{4,0},{8,12},{12,8},{16,20},{20,16},{24,28},{28,24},{1,5},{5... | collective-permute-start | bytes 786440 | tf_op jit(solution)/shard_map/ppermute | solution.py:30
  4.8 9.5 %collective-permute-start.1 = (f32[4,128,128]{2,1,0:T(8,128)S(1)}, f32[4,128,128]{2,1,0:T(8,128)S(1)}, u32[]{:S(2)}, u32[]{:S(2)}) collective-permute-start(f32[4,128,128]{2,1,0:T(8,128)S(1)} %shard_map.78.message), channel_id=1, source_target_pairs={{1,2},{2,1},{3,0},{0,3},{5,6},{6,5},{7,4},{4,7},{9,10},{10,9},{11,... | collective-permute-start | bytes 786440 | tf_op jit(solution)/shard_map/ppermute | solution.py:30
  5.5 14.3 %collective-permute-start.3 = (f32[4,128,128]{2,1,0:T(8,128)S(1)}, f32[4,128,128]{2,1,0:T(8,128)S(1)}, u32[]{:S(2)}, u32[]{:S(2)}) collective-permute-start(f32[4,128,128]{2,1,0:T(8,128)S(1)} %shard_map.79.message), channel_id=1, source_target_pairs={{4,8},{8,4},{12,16},{16,12},{20,24},{24,20},{28,0},{0,28},{5,9},{9... | collective-permute-start | bytes 786440 | tf_op jit(solution)/shard_map/ppermute | solution.py:30
  10.2 2.3 %collective-permute-start = (f32[8,128,128]{2,1,0:T(8,128)S(1)}, f32[8,128,128]{2,1,0:T(8,128)S(1)}, u32[]{:S(2)}, u32[]{:S(2)}) collective-permute-start(f32[8,128,128]{2,1,0:T(8,128)S(1)} %shard_map.80.after), channel_id=1, source_target_pairs={{0,1},{1,0},{2,3},{3,2},{4,5},{5,4},{6,7},{7,6},{8,9},{9,8},{10,11... | collective-permute-start | bytes 1572872 | tf_op jit(solution)/shard_map/ppermute | solution.py:30
  13.7 10.8 %collective-permute-start.4 = (f32[4,128,128]{2,1,0:T(8,128)S(1)}, f32[4,128,128]{2,1,0:T(8,128)S(1)}, u32[]{:S(2)}, u32[]{:S(2)}) collective-permute-start(f32[4,128,128]{2,1,0:T(8,128)S(1)} %shard_map.86.after), channel_id=1, source_target_pairs={{1,2},{2,1},{3,0},{0,3},{5,6},{6,5},{7,4},{4,7},{9,10},{10,9},{11,... | collective-permute-start | bytes 786440 | tf_op jit(solution)/shard_map/ppermute | solution.py:30
  14.3 18.4 %collective-permute-start.5 = (f32[4,128,128]{2,1,0:T(8,128)S(1)}, f32[4,128,128]{2,1,0:T(8,128)S(1)}, u32[]{:S(2)}, u32[]{:S(2)}) collective-permute-start(f32[4,128,128]{2,1,0:T(8,128)S(1)} %get-tuple-element.73), channel_id=1, source_target_pairs={{0,4},{4,0},{8,12},{12,8},{16,20},{20,16},{24,28},{28,24},{1,5},{5... | collective-permute-start | bytes 786440 | tf_op jit(solution)/shard_map/ppermute | solution.py:30
  14.4 18.3 %collective-permute-start.6 = (f32[4,128,128]{2,1,0:T(8,128)S(1)}, f32[4,128,128]{2,1,0:T(8,128)S(1)}, u32[]{:S(2)}, u32[]{:S(2)}) collective-permute-start(f32[4,128,128]{2,1,0:T(8,128)S(1)} %get-tuple-element.74), channel_id=1, source_target_pairs={{4,8},{8,4},{12,16},{16,12},{20,24},{24,20},{28,0},{0,28},{5,9},{9... | collective-permute-start | bytes 786440 | tf_op jit(solution)/shard_map/ppermute | solution.py:30
  20.7 1.2 %collective-permute-start.9 = (f32[3,128]{1,0:T(4,128)S(1)}, f32[3,128]{1,0:T(4,128)S(1)}, u32[]{:S(2)}, u32[]{:S(2)}) collective-permute-start(f32[3,128]{1,0:T(4,128)S(1)} %get-tuple-element.77), channel_id=1, source_target_pairs={{0,1},{1,0},{2,3},{3,2},{4,5},{5,4},{6,7},{7,6},{8,9},{9,8},{10,11... | collective-permute-start | bytes 4616 | tf_op jit(solution)/shard_map/ppermute | solution.py:30
  20.8 11.8 %collective-permute-start.7 = (f32[3,128]{1,0:T(4,128)S(1)}, f32[3,128]{1,0:T(4,128)S(1)}, u32[]{:S(2)}, u32[]{:S(2)}) collective-permute-start(f32[3,128]{1,0:T(4,128)S(1)} %get-tuple-element.75), channel_id=1, source_target_pairs={{0,4},{4,0},{8,12},{12,8},{16,20},{20,16},{24,28},{28,24},{1,5},{5... | collective-permute-start | bytes 4616 | tf_op jit(solution)/shard_map/ppermute | solution.py:30
  22.0 10.7 %collective-permute-start.8 = (f32[3,128]{1,0:T(4,128)S(1)}, f32[3,128]{1,0:T(4,128)S(1)}, u32[]{:S(2)}, u32[]{:S(2)}) collective-permute-start(f32[3,128]{1,0:T(4,128)S(1)} %get-tuple-element.76), channel_id=1, source_target_pairs={{4,8},{8,4},{12,16},{16,12},{20,24},{24,20},{28,0},{0,28},{5,9},{9... | collective-permute-start | bytes 4616 | tf_op jit(solution)/shard_map/ppermute | solution.py:30
  24.5 8.2 %collective-permute-start.10 = (f32[3,128]{1,0:T(4,128)S(1)}, f32[3,128]{1,0:T(4,128)S(1)}, u32[]{:S(2)}, u32[]{:S(2)}) collective-permute-start(f32[3,128]{1,0:T(4,128)S(1)} %shard_map.89), channel_id=1, source_target_pairs={{1,2},{2,1},{3,0},{0,3},{5,6},{6,5},{7,4},{4,7},{9,10},{10,9},{11,... | collective-permute-start | bytes 4616 | tf_op jit(solution)/shard_map/ppermute | solution.py:30

commit v22 on v20

--- a/solution.py
+++ b/solution.py
@@ -74,22 +74,23 @@
     return copies
 
 
-def first_kernel(cutoff_hbm, ham_hbm, inv_hbm, rho_hbm, one, rest, cutoff_ref, cutoff_sem, sems):
+def first_kernel(cutoff_hbm, ham_hbm, inv_hbm, rho_hbm, one, rest, ham, cutoff_ref, cutoff_sem, sems):
     flags = pltpu.make_async_copy(cutoff_hbm, cutoff_ref, cutoff_sem)
     flags.start()
+    copies = start_all(
+        [
+            pltpu.make_async_copy(ham_hbm.at[0, 0], ham, sems.at[0]),
+            pltpu.make_async_copy(inv_hbm.at[0, 0, 0], one.at[1], sems.at[1]),
+            pltpu.make_async_copy(rho_hbm.at[1, 0, 0, 0], one.at[2], sems.at[2]),
+        ]
+    )
     order = order_of()
-    sources = (ham_hbm.at[0, 0, 0], inv_hbm.at[0, 0, 0], rho_hbm.at[1, 0, 0, 0], ham_hbm.at[0, 0, order[1]])
-    copies = [pltpu.make_async_copy(source, one.at[at], sems.at[at]) for at, source in enumerate(sources)]
-    copies += [
-        pltpu.make_async_copy(ham_hbm.at[0, 0, order[place]], rest.at[at], sems.at[4 + at]) for at, place in enumerate((4, 2))
-    ]
-    start_all(copies)
     flags.wait()
     for copy in copies:
         copy.wait()
-    one[3] = one[3] * cutoff_ref[0, 0, order[1]].astype(f32)
-    for at, place in enumerate((4, 2)):
-        rest[at] = rest[at] * cutoff_ref[0, 0, order[place]].astype(f32)
+    one[0] = ham[0]
+    for target, at, place in ((one, 3, 1), (rest, 0, 4), (rest, 1, 2)):
+        target[at] = ham[order[place]] * cutoff_ref[0, 0, order[place]].astype(f32)
 
 
 def next_kernel(at, message, rest, out):
@@ -319,7 +320,7 @@
         [hbm] * 4,
         0,
         (cutoff, hamiltonian, inverse_margin, density),
-        scratch=[flags, dma(()), dma((6,))],
+        scratch=[pltpu.VMEM((5, B, B), f32), flags, dma(()), dma((3,))],
     )
     near_one = swapped(first_one, 1)
     (first_four,) = call(functools.partial(next_kernel, 0), [message], [vmem] * 2, 0, (first_one, rest))

time: 30.6 us -> 30.5 us (level)
  no operation moved by 1% of the time
where the time goes in v22:
time: 30.5 us; the launch traced here: 30.3 us
  starting transfers between devices  17.4 us (57%)
  Pallas kernels  9.44 us (31%)
  waiting for transfers between devices  2.71 us (9%)
  between operations  0.75 us (2%)
    ppermute x11, starting transfers between devices, swapped(): return lax.ppermute(cells, axis, pairs)  17.4 us
    pallas_call x13, Pallas kernels, call(): pl.pallas_call(kernel, out_shape=shapes, in_specs=in_specs, out_specs=out...  9.44 us
    ppermute x11, waiting for transfers between devices, swapped(): return lax.ppermute(cells, axis, pairs)  2.71 us
  transfers between devices with their start and end apart: 11, of which 4 were waited for; matrix products, arithmetic and copies ran while one was open for 0% of the time, Pallas kernels for 23%

profile of v22, /device:TPU:0, one launch (start us, length us, event | category | flops | bytes accessed | tf_op | source)
XLA Modules:
  0.0 30.3 jit_solution(15998713773499306373)
XLA Ops:
  0.6 1.0 %shard_map.77 = (f32[4,128,128]{2,1,0:T(8,128)S(1)}, f32[2,128,128]{2,1,0:T(8,128)S(1)}) custom-call(s32[1,1,5]{2,1,0:T(1,128)} %cutoff_hbm.5, f32[1,1,5,128,128]{4,3,2,1,0:T(8,128)} %ham_hbm.5, f32[1,1,5,128,128]{4,3,2,1,0:T(8,128)} %inv_hbm.5, f32[2,1,1,5,128,128]{5,4,3,2,1,0:T(8,128)} %rho_hbm.5), custom_call_target="tpu_custom_call" | custom-call | bytes 1703956 | tf_op jit(solution)/shard_map/pallas_call | solution.py:295
  1.7 3.0 %collective-permute-start.2 = (f32[4,128,128]{2,1,0:T(8,128)S(1)}, f32[4,128,128]{2,1,0:T(8,128)S(1)}, u32[]{:S(2)}, u32[]{:S(2)}) collective-permute-start(f32[4,128,128]{2,1,0:T(8,128)S(1)} %get-tuple-element.43.message), channel_id=1, source_target_pairs={{0,4},{4,0},{8,12},{12,8},{16,20},{20,16},{24,28},{28,24},{1,5},{5... | collective-permute-start | bytes 786440 | tf_op jit(solution)/shard_map/ppermute | solution.py:30
  4.7 0.7 %collective-permute-start.1 = (f32[4,128,128]{2,1,0:T(8,128)S(1)}, f32[4,128,128]{2,1,0:T(8,128)S(1)}, u32[]{:S(2)}, u32[]{:S(2)}) collective-permute-start(f32[4,128,128]{2,1,0:T(8,128)S(1)} %shard_map.78.message), channel_id=1, source_target_pairs={{1,2},{2,1},{3,0},{0,3},{5,6},{6,5},{7,4},{4,7},{9,10},{10,9},{11,... | collective-permute-start | bytes 786440 | tf_op jit(solution)/shard_map/ppermute | solution.py:30
  5.5 3.6 %collective-permute-start.3 = (f32[4,128,128]{2,1,0:T(8,128)S(1)}, f32[4,128,128]{2,1,0:T(8,128)S(1)}, u32[]{:S(2)}, u32[]{:S(2)}) collective-permute-start(f32[4,128,128]{2,1,0:T(8,128)S(1)} %shard_map.79.message), channel_id=1, source_target_pairs={{4,8},{8,4},{12,16},{16,12},{20,24},{24,20},{28,0},{0,28},{5,9},{9... | collective-permute-start | bytes 786440 | tf_op jit(solution)/shard_map/ppermute | solution.py:30
  9.1 1.0 %shard_map.80.after = f32[8,128,128]{2,1,0:T(8,128)S(1)} custom-call(s32[1,1,5]{2,1,0:T(1,128)} %cutoff_hbm.5, f32[1,1,5,128,128]{4,3,2,1,0:T(8,128)} %ham_hbm.5, f32[1,1,5,128,128]{4,3,2,1,0:T(8,128)} %inv_hbm.5, f32[2,1,1,5,128,128]{5,4,3,2,1,0:T(8,128)} %rho_hbm.5, f32[4,128,128]{2,1,0:T(8,128)S(1)} %shard_map.79.message), custom_call_target="tpu_custom_call" | custom-call | flops 6291456000 | bytes 2097172 | tf_op jit(solution)/shard_map/pallas_call | solution.py:295
  10.1 0.7 %collective-permute-start = (f32[8,128,128]{2,1,0:T(8,128)S(1)}, f32[8,128,128]{2,1,0:T(8,128)S(1)}, u32[]{:S(2)}, u32[]{:S(2)}) collective-permute-start(f32[8,128,128]{2,1,0:T(8,128)S(1)} %shard_map.80.after), channel_id=1, source_target_pairs={{0,1},{1,0},{2,3},{3,2},{4,5},{5,4},{6,7},{7,6},{8,9},{9,8},{10,11... | collective-permute-start | bytes 1572872 | tf_op jit(solution)/shard_map/ppermute | solution.py:30
  10.9 1.4 %shard_map.81 = (f32[3,5,128,128]{3,2,1,0:T(8,128)S(1)}, bf16[384,640]{1,0:T(8,128)(2,1)S(1)}, bf16[384,640]{1,0:T(8,128)(2,1)S(1)}, bf16[128,640]{1,0:T(8,128)(...) custom-call(s32[1,1,5]{2,1,0:T(1,128)} %cutoff_hbm.5, f32[1,1,5,128,128]{4,3,2,1,0:T(8,128)} %ham_hbm.5, ...), custom_call_target="tpu_custom_call" | custom-call | flops 25165824000 | bytes 5472788 | tf_op jit(solution)/shard_map/pallas_call | solution.py:295
  12.3 0.1 collective-permute-done.three
  12.4 1.2 %shard_map.82 = (f32[384,640]{1,0:T(8,128)S(1)}, f32[384,128]{1,0:T(8,128)S(1)}, f32[2,2,128,128]{3,2,1,0:T(8,128)S(1)}, f32[3,1,1,5,128,128]{5,4,3,2,1,0:T(8,128)S(1)}) custom-call(bf16[384,640]{1,0:T(8,128)(2,1)S(1)} %get-tuple-element.46.left_high, bf16[384,640]{1,0:T(8,128)(2,1)S(1)} %get-tuple-element.47.left_low, ...), custom_call_target="tpu_custom_call" | custom-call | flops 100663296000 | bytes 7536640 | tf_op jit(solution)/shard_map/pallas_call | solution.py:295
  13.6 0.0 collective-permute-done.1.four.arrived
  13.6 0.1 shard_map.86
  13.7 0.6 %collective-permute-start.4 = (f32[4,128,128]{2,1,0:T(8,128)S(1)}, f32[4,128,128]{2,1,0:T(8,128)S(1)}, u32[]{:S(2)}, u32[]{:S(2)}) collective-permute-start(f32[4,128,128]{2,1,0:T(8,128)S(1)} %get-tuple-element.71), channel_id=1, source_target_pairs={{1,2},{2,1},{3,0},{0,3},{5,6},{6,5},{7,4},{4,7},{9,10},{10,9},{11,... | collective-permute-start | bytes 786440 | tf_op jit(solution)/shard_map/ppermute | solution.py:30
  14.3 0.4 %collective-permute-start.5 = (f32[4,128,128]{2,1,0:T(8,128)S(1)}, f32[4,128,128]{2,1,0:T(8,128)S(1)}, u32[]{:S(2)}, u32[]{:S(2)}) collective-permute-start(f32[4,128,128]{2,1,0:T(8,128)S(1)} %get-tuple-element.75), channel_id=1, source_target_pairs={{0,4},{4,0},{8,12},{12,8},{16,20},{20,16},{24,28},{28,24},{1,5},{5... | collective-permute-start | bytes 786440 | tf_op jit(solution)/shard_map/ppermute | solution.py:30
  14.7 4.6 %collective-permute-start.6 = (f32[4,128,128]{2,1,0:T(8,128)S(1)}, f32[4,128,128]{2,1,0:T(8,128)S(1)}, u32[]{:S(2)}, u32[]{:S(2)}) collective-permute-start(f32[4,128,128]{2,1,0:T(8,128)S(1)} %get-tuple-element.76), channel_id=1, source_target_pairs={{4,8},{8,4},{12,16},{16,12},{20,24},{24,20},{28,0},{0,28},{5,9},{9... | collective-permute-start | bytes 786440 | tf_op jit(solution)/shard_map/ppermute | solution.py:30
  19.3 0.6 %shard_map.83 = (bf16[384,128]{1,0:T(8,128)(2,1)S(1)}, bf16[384,128]{1,0:T(8,128)(2,1)S(1)}, f32[384,128]{1,0:T(8,128)S(1)}, f32[2,128,128]{2,1,0:T(8,128)S(1)}) custom-call(bf16[384,640]{1,0:T(8,128)(2,1)S(1)} %get-tuple-element.46.left_high, bf16[384,640]{1,0:T(8,128)(2,1)S(1)} %get-tuple-element.47.left_low, f32[384,640]{1,0:T(8,128)S(1)} %get-tuple-element.52.start, ...), custom_call_target="tpu_custom_call" | custom-call | flops 100663296 | bytes 4128768 | tf_op jit(solution)/shard_map/pallas_call | solution.py:295
  19.9 0.0 collective-permute-done.2.one
  19.9 0.6 %shard_map.84 = (bf16[384,128]{1,0:T(8,128)(2,1)S(1)}, bf16[384,128]{1,0:T(8,128)(2,1)S(1)}, f32[384,128]{1,0:T(8,128)S(1)}, f32[2,128,128]{2,1,0:T(8,128)S(1)}) custom-call(bf16[384,640]{1,0:T(8,128)(2,1)S(1)} %get-tuple-element.46.left_high, bf16[384,640]{1,0:T(8,128)(2,1)S(1)} %get-tuple-element.47.left_low, f32[384,640]{1,0:T(8,128)S(1)} %get-tuple-element.52.start, ...), custom_call_target="tpu_custom_call" | custom-call | flops 125829120 | bytes 4128768 | tf_op jit(solution)/shard_map/pallas_call | solution.py:295
  20.5 0.0 collective-permute-done.3.two
  20.5 0.9 %shard_map.85 = (f32[4,128,128]{2,1,0:T(8,128)S(1)}, bf16[384,128]{1,0:T(8,128)(2,1)S(1)}, bf16[384,128]{1,0:T(8,128)(2,1)S(1)}, bf16[384,128]{1,0:T(8,128)(2,1)...) custom-call(bf16[384,640]{1,0:T(8,128)(2,1)S(1)} %get-tuple-element., ...), custom_call_target="tpu_custom_call" | custom-call | flops 276824064 | bytes 7280640 | tf_op jit(solution)/shard_map/pallas_call | solution.py:295
  21.5 0.1 collective-permute-start.9
  21.6 0.0 collective-permute-start.7
  21.6 1.1 %collective-permute-done.9.arrived.c3 = f32[3,128]{1,0:T(4,128)S(1)} collective-permute-done((f32[3,128]{1,0:T(4,128)S(1)}, f32[3,128]{1,0:T(4,128)S(1)}, u32[]{:S(2)}, u32[]{:S(2)}) %collective-permute-start.9) | collective-permute-done | bytes 1568 | tf_op jit(solution)/shard_map/ppermute | solution.py:30
  22.7 1.8 %collective-permute-start.8 = (f32[3,128]{1,0:T(4,128)S(1)}, f32[3,128]{1,0:T(4,128)S(1)}, u32[]{:S(2)}, u32[]{:S(2)}) collective-permute-start(f32[3,128]{1,0:T(4,128)S(1)} %get-tuple-element.78), channel_id=1, source_target_pairs={{4,8},{8,4},{12,16},{16,12},{20,24},{24,20},{28,0},{0,28},{5,9},{9... | collective-permute-start | bytes 4616 | tf_op jit(solution)/shard_map/ppermute | solution.py:30
  24.5 0.0 collective-permute-done.4.four
  24.5 1.8 %collective-permute-start.10 = (f32[3,128]{1,0:T(4,128)S(1)}, f32[3,128]{1,0:T(4,128)S(1)}, u32[]{:S(2)}, u32[]{:S(2)}) collective-permute-start(f32[3,128]{1,0:T(4,128)S(1)} %shard_map.88), channel_id=1, source_target_pairs={{1,2},{2,1},{3,0},{0,3},{5,6},{6,5},{7,4},{4,7},{9,10},{10,9},{11,... | collective-permute-start | bytes 4616 | tf_op jit(solution)/shard_map/ppermute | solution.py:30
  26.3 1.2 %shard_map.87 = (f32[2,1,1,5,128,128]{5,4,3,2,1,0:T(8,128)}, f32[3,128,128]{2,1,0:T(8,128)S(1)}, f32[128,128]{1,0:T(8,128)S(1)}, f32[3,128]{1,0:T(4,128)S(1)}) custom-call(f32[3,5,128,128]{3,2,1,0:T(8,128)S(1)} %get-tuple-element.45.held, f32[4,128,128]{2,1,0:T(8,128)S(1)} %get-tuple-element.63.new, bf16[384,640]{1,0:T(8,128)(2,1)S(1)} %get-tuple-element.46.left_high, ...), custom_call_target="tpu_custom_call" | custom-call | flops 125829120 | bytes 6030848 | tf_op jit(solution)/shard_map/pallas_call | solution.py:295
  27.5 1.3 %collective-permute-done.7.c1 = f32[3,128]{1,0:T(4,128)S(1)} collective-permute-done((f32[3,128]{1,0:T(4,128)S(1)}, f32[3,128]{1,0:T(4,128)S(1)}, u32[]{:S(2)}, u32[]{:S(2)}) %collective-permute-start.7) | collective-permute-done | bytes 1568 | tf_op jit(solution)/shard_map/ppermute | solution.py:30
  28.8 0.2 collective-permute-done.8.c2
  29.0 0.0 collective-permute-done.10.c4
  29.0 0.0 collective-permute-done.5.one
  29.0 0.0 collective-permute-done.6.two
  29.0 1.3 %shard_map.89 = (f32[2,1,1,5,128,128]{5,4,3,2,1,0:T(8,128)}, f32[3,1,64]{2,1,0:T(1,128)}) custom-call(f32[3,5,128,128]{3,2,1,0:T(8,128)S(1)} %get-tuple-element.45.held, f32[3,1,1,5,128,128]{5,4,3,2,1,0:T(8,128)S(1)} %get-tuple-element.50.der_ref, f32[64,128]{1,0:T(8,128)S(1)} %get-tuple-element.51.members, ...), custom_call_target="tpu_custom_call", output_to_operand_aliasing={{0}: (16, {})} | custom-call | flops 125829120 | bytes 4890880 | tf_op jit(solution)/shard_map/pallas_call | solution.py:295
  (3 shorter events, 0.0 us)
Async XLA Ops:
  1.7 18.2 %collective-permute-start.2 = (f32[4,128,128]{2,1,0:T(8,128)S(1)}, f32[4,128,128]{2,1,0:T(8,128)S(1)}, u32[]{:S(2)}, u32[]{:S(2)}) collective-permute-start(f32[4,128,128]{2,1,0:T(8,128)S(1)} %get-tuple-element.43.message), channel_id=1, source_target_pairs={{0,4},{4,0},{8,12},{12,8},{16,20},{20,16},{24,28},{28,24},{1,5},{5... | collective-permute-start | bytes 786440 | tf_op jit(solution)/shard_map/ppermute | solution.py:30
  4.7 8.9 %collective-permute-start.1 = (f32[4,128,128]{2,1,0:T(8,128)S(1)}, f32[4,128,128]{2,1,0:T(8,128)S(1)}, u32[]{:S(2)}, u32[]{:S(2)}) collective-permute-start(f32[4,128,128]{2,1,0:T(8,128)S(1)} %shard_map.78.message), channel_id=1, source_target_pairs={{1,2},{2,1},{3,0},{0,3},{5,6},{6,5},{7,4},{4,7},{9,10},{10,9},{11,... | collective-permute-start | bytes 786440 | tf_op jit(solution)/shard_map/ppermute | solution.py:30
  5.5 15.0 %collective-permute-start.3 = (f32[4,128,128]{2,1,0:T(8,128)S(1)}, f32[4,128,128]{2,1,0:T(8,128)S(1)}, u32[]{:S(2)}, u32[]{:S(2)}) collective-permute-start(f32[4,128,128]{2,1,0:T(8,128)S(1)} %shard_map.79.message), channel_id=1, source_target_pairs={{4,8},{8,4},{12,16},{16,12},{20,24},{24,20},{28,0},{0,28},{5,9},{9... | collective-permute-start | bytes 786440 | tf_op jit(solution)/shard_map/ppermute | solution.py:30
  10.1 2.3 %collective-permute-start = (f32[8,128,128]{2,1,0:T(8,128)S(1)}, f32[8,128,128]{2,1,0:T(8,128)S(1)}, u32[]{:S(2)}, u32[]{:S(2)}) collective-permute-start(f32[8,128,128]{2,1,0:T(8,128)S(1)} %shard_map.80.after), channel_id=1, source_target_pairs={{0,1},{1,0},{2,3},{3,2},{4,5},{5,4},{6,7},{7,6},{8,9},{9,8},{10,11... | collective-permute-start | bytes 1572872 | tf_op jit(solution)/shard_map/ppermute | solution.py:30
  13.7 10.8 %collective-permute-start.4 = (f32[4,128,128]{2,1,0:T(8,128)S(1)}, f32[4,128,128]{2,1,0:T(8,128)S(1)}, u32[]{:S(2)}, u32[]{:S(2)}) collective-permute-start(f32[4,128,128]{2,1,0:T(8,128)S(1)} %get-tuple-element.71), channel_id=1, source_target_pairs={{1,2},{2,1},{3,0},{0,3},{5,6},{6,5},{7,4},{4,7},{9,10},{10,9},{11,... | collective-permute-start | bytes 786440 | tf_op jit(solution)/shard_map/ppermute | solution.py:30
  14.3 14.7 %collective-permute-start.5 = (f32[4,128,128]{2,1,0:T(8,128)S(1)}, f32[4,128,128]{2,1,0:T(8,128)S(1)}, u32[]{:S(2)}, u32[]{:S(2)}) collective-permute-start(f32[4,128,128]{2,1,0:T(8,128)S(1)} %get-tuple-element.75), channel_id=1, source_target_pairs={{0,4},{4,0},{8,12},{12,8},{16,20},{20,16},{24,28},{28,24},{1,5},{5... | collective-permute-start | bytes 786440 | tf_op jit(solution)/shard_map/ppermute | solution.py:30
  14.7 14.3 %collective-permute-start.6 = (f32[4,128,128]{2,1,0:T(8,128)S(1)}, f32[4,128,128]{2,1,0:T(8,128)S(1)}, u32[]{:S(2)}, u32[]{:S(2)}) collective-permute-start(f32[4,128,128]{2,1,0:T(8,128)S(1)} %get-tuple-element.76), channel_id=1, source_target_pairs={{4,8},{8,4},{12,16},{16,12},{20,24},{24,20},{28,0},{0,28},{5,9},{9... | collective-permute-start | bytes 786440 | tf_op jit(solution)/shard_map/ppermute | solution.py:30
  21.5 1.2 %collective-permute-start.9 = (f32[3,128]{1,0:T(4,128)S(1)}, f32[3,128]{1,0:T(4,128)S(1)}, u32[]{:S(2)}, u32[]{:S(2)}) collective-permute-start(f32[3,128]{1,0:T(4,128)S(1)} %get-tuple-element.79), channel_id=1, source_target_pairs={{0,1},{1,0},{2,3},{3,2},{4,5},{5,4},{6,7},{7,6},{8,9},{9,8},{10,11... | collective-permute-start | bytes 4616 | tf_op jit(solution)/shard_map/ppermute | solution.py:30
  21.6 7.1 %collective-permute-start.7 = (f32[3,128]{1,0:T(4,128)S(1)}, f32[3,128]{1,0:T(4,128)S(1)}, u32[]{:S(2)}, u32[]{:S(2)}) collective-permute-start(f32[3,128]{1,0:T(4,128)S(1)} %get-tuple-element.77), channel_id=1, source_target_pairs={{0,4},{4,0},{8,12},{12,8},{16,20},{20,16},{24,28},{28,24},{1,5},{5... | collective-permute-start | bytes 4616 | tf_op jit(solution)/shard_map/ppermute | solution.py:30
  22.7 6.3 %collective-permute-start.8 = (f32[3,128]{1,0:T(4,128)S(1)}, f32[3,128]{1,0:T(4,128)S(1)}, u32[]{:S(2)}, u32[]{:S(2)}) collective-permute-start(f32[3,128]{1,0:T(4,128)S(1)} %get-tuple-element.78), channel_id=1, source_target_pairs={{4,8},{8,4},{12,16},{16,12},{20,24},{24,20},{28,0},{0,28},{5,9},{9... | collective-permute-start | bytes 4616 | tf_op jit(solution)/shard_map/ppermute | solution.py:30
  24.5 4.5 %collective-permute-start.10 = (f32[3,128]{1,0:T(4,128)S(1)}, f32[3,128]{1,0:T(4,128)S(1)}, u32[]{:S(2)}, u32[]{:S(2)}) collective-permute-start(f32[3,128]{1,0:T(4,128)S(1)} %shard_map.88), channel_id=1, source_target_pairs={{1,2},{2,1},{3,0},{0,3},{5,6},{6,5},{7,4},{4,7},{9,10},{10,9},{11,... | collective-permute-start | bytes 4616 | tf_op jit(solution)/shard_map/ppermute | solution.py:30

commit v23 on v22

--- a/solution.py
+++ b/solution.py
@@ -98,14 +98,14 @@
     out[3] = rest[at]
 
 
-def whole_first_kernel(cutoff_hbm, ham_hbm, inv_hbm, rho_hbm, message, out, cutoff_ref, cutoff_sem, sems):
+def whole_first_kernel(cutoff_hbm, row, inv_hbm, rho_hbm, message, out, cutoff_ref, cutoff_sem, sems):
     flags = pltpu.make_async_copy(cutoff_hbm, cutoff_ref, cutoff_sem)
     flags.start()
     offset = order_of()[3]
-    sources = (ham_hbm.at[0, 0, offset], rho_hbm.at[0, 0, 0, 0], inv_hbm.at[0, 0, offset], rho_hbm.at[0, 0, 0, offset])
-    sources += (rho_hbm.at[1, 0, 0, offset],)
-    copies = start_all([pltpu.make_async_copy(source, out.at[3 + at], sems.at[at]) for at, source in enumerate(sources)])
+    sources = (rho_hbm.at[0, 0, 0, 0], inv_hbm.at[0, 0, offset], rho_hbm.at[0, 0, 0, offset], rho_hbm.at[1, 0, 0, offset])
+    copies = start_all([pltpu.make_async_copy(source, out.at[4 + at], sems.at[at]) for at, source in enumerate(sources)])
     out[:3] = message[:3]
+    out[3] = row[offset]
     flags.wait()
     keep = cutoff_ref[0, 0, offset].astype(f32)
     for copy in copies:
@@ -115,22 +115,23 @@
 
 
 def second_kernel(
-    cutoff_hbm, ham_hbm, inv_hbm, rho_hbm, atom_hbm, after, held, left_high, left_low, ham_high, ham_low, members,
+    cutoff_hbm, row, inv_hbm, rho_hbm, atom_hbm, after, held, left_high, left_low, ham_high, ham_low, members,
     raw, cutoff_ref, atom_ref, cutoff_sem, atom_sem, sems
 ):
     flags = pltpu.make_async_copy(cutoff_hbm, cutoff_ref, cutoff_sem)
     flags.start()
-    sources = (ham_hbm.at[0, 0], inv_hbm.at[0, 0], rho_hbm.at[0, 0, 0], rho_hbm.at[1, 0, 0])
+    sources = (inv_hbm.at[0, 0], rho_hbm.at[0, 0, 0], rho_hbm.at[1, 0, 0])
     copies = start_all([pltpu.make_async_copy(source, raw.at[at], sems.at[at]) for at, source in enumerate(sources)])
     owners = pltpu.make_async_copy(atom_hbm, atom_ref, atom_sem)
     owners.start()
     order = order_of()
     flags.wait()
     keeps = [cutoff_ref[0, 0, offset].astype(f32) for offset in order]
-    for kind, copy in enumerate(copies):
-        copy.wait()
+    for kind in range(4):
+        if kind > 0:
+            copies[kind - 1].wait()
         for place, offset in enumerate(order):
-            block = raw[kind, offset]
+            block = row[offset] if kind == 0 else raw[kind - 1, offset]
             if place > 0:
                 block = block * keeps[place]
             if kind == 0:
@@ -314,13 +315,13 @@
     )
     flags = pltpu.SMEM((1, 1, 5), jnp.int32)
     message = shape(4, B, B)
-    first_one, rest = call(
+    first_one, rest, row = call(
         first_kernel,
-        [message, shape(2, B, B)],
+        [message, shape(2, B, B), shape(5, B, B)],
         [hbm] * 4,
         0,
         (cutoff, hamiltonian, inverse_margin, density),
-        scratch=[pltpu.VMEM((5, B, B), f32), flags, dma(()), dma((3,))],
+        scratch=[flags, dma(()), dma((3,))],
     )
     near_one = swapped(first_one, 1)
     (first_four,) = call(functools.partial(next_kernel, 0), [message], [vmem] * 2, 0, (first_one, rest))
@@ -330,10 +331,10 @@
     (send_three,) = call(
         whole_first_kernel,
         [shape(8, B, B)],
-        [hbm] * 4 + [vmem],
+        [hbm, vmem, hbm, hbm, vmem],
         500,
-        (cutoff, hamiltonian, inverse_margin, density, first_two),
-        scratch=[flags, dma(()), dma((5,))],
+        (cutoff, row, inverse_margin, density, first_two),
+        scratch=[flags, dma(()), dma((4,))],
     )
     near_three = swapped(send_three, 3)
     left = [shape(3 * B, 5 * B, kind=bf16)] * 2
@@ -341,10 +342,10 @@
     held, left_high, left_low, ham_high, ham_low, members = call(
         second_kernel,
         [shape(3, 5, B, B)] + left + ham + [shape(ATOMS, B)],
-        [hbm] * 6,
+        [hbm, vmem] + [hbm] * 4,
         2000,
-        (cutoff, hamiltonian, inverse_margin, density, atom_of, send_three),
-        scratch=[pltpu.VMEM((4, 5, B, B), f32), flags, pltpu.VMEM((1, 1, B), jnp.int32), dma(()), dma(()), dma((4,))],
+        (cutoff, row, inverse_margin, density, atom_of, send_three),
+        scratch=[pltpu.VMEM((3, 5, B, B), f32), flags, pltpu.VMEM((1, 1, B), jnp.int32), dma(()), dma(()), dma((3,))],
     )
     mixed = [shape(3 * B, B, kind=bf16)] * 2
     both = shape(2, 2, B, B)

time: 30.5 us -> 30.5 us (level)
  no operation moved by 1% of the time
where the time goes in v23:
time: 30.5 us; the launch traced here: 30.3 us
  starting transfers between devices  17.4 us (57%)
  Pallas kernels  9.29 us (30%)
  waiting for transfers between devices  2.8 us (9%)
  between operations  0.75 us (2%)
    ppermute x11, starting transfers between devices, swapped(): return lax.ppermute(cells, axis, pairs)  17.4 us
    pallas_call x13, Pallas kernels, call(): pl.pallas_call(kernel, out_shape=shapes, in_specs=in_specs, out_specs=out...  9.29 us
    ppermute x11, waiting for transfers between devices, swapped(): return lax.ppermute(cells, axis, pairs)  2.8 us
  transfers between devices with their start and end apart: 11, of which 4 were waited for; matrix products, arithmetic and copies ran while one was open for 0% of the time, Pallas kernels for 23%

profile of v23, /device:TPU:0, one launch (start us, length us, event | category | flops | bytes accessed | tf_op | source)
XLA Modules:
  0.0 30.3 jit_solution(15457014896821363319)
XLA Ops:
  0.6 1.0 %shard_map.77 = (f32[4,128,128]{2,1,0:T(8,128)S(1)}, f32[2,128,128]{2,1,0:T(8,128)S(1)}, f32[5,128,128]{2,1,0:T(8,128)S(1)}) custom-call(s32[1,1,5]{2,1,0:T(1,128)} %cutoff_hbm.5, f32[1,1,5,128,128]{4,3,2,1,0:T(8,128)} %ham_hbm.1, f32[1,1,5,128,128]{4,3,2,1,0:T(8,128)} %inv_hbm.5, f32[2,1,1,5,128,128]{5,4,3,2,1,0:T(8,128)} %rho_hbm.5), custom_call_target="tpu_custom_call" | custom-call | bytes 2031636 | tf_op jit(solution)/shard_map/pallas_call | solution.py:296
  1.7 3.0 %collective-permute-start.2 = (f32[4,128,128]{2,1,0:T(8,128)S(1)}, f32[4,128,128]{2,1,0:T(8,128)S(1)}, u32[]{:S(2)}, u32[]{:S(2)}) collective-permute-start(f32[4,128,128]{2,1,0:T(8,128)S(1)} %get-tuple-element.45.message), channel_id=1, source_target_pairs={{0,4},{4,0},{8,12},{12,8},{16,20},{20,16},{24,28},{28,24},{1,5},{5... | collective-permute-start | bytes 786440 | tf_op jit(solution)/shard_map/ppermute | solution.py:30
  4.7 0.7 %collective-permute-start.1 = (f32[4,128,128]{2,1,0:T(8,128)S(1)}, f32[4,128,128]{2,1,0:T(8,128)S(1)}, u32[]{:S(2)}, u32[]{:S(2)}) collective-permute-start(f32[4,128,128]{2,1,0:T(8,128)S(1)} %shard_map.78.message), channel_id=1, source_target_pairs={{1,2},{2,1},{3,0},{0,3},{5,6},{6,5},{7,4},{4,7},{9,10},{10,9},{11,... | collective-permute-start | bytes 786440 | tf_op jit(solution)/shard_map/ppermute | solution.py:30
  5.5 3.6 %collective-permute-start.3 = (f32[4,128,128]{2,1,0:T(8,128)S(1)}, f32[4,128,128]{2,1,0:T(8,128)S(1)}, u32[]{:S(2)}, u32[]{:S(2)}) collective-permute-start(f32[4,128,128]{2,1,0:T(8,128)S(1)} %shard_map.79.message), channel_id=1, source_target_pairs={{4,8},{8,4},{12,16},{16,12},{20,24},{24,20},{28,0},{0,28},{5,9},{9... | collective-permute-start | bytes 786440 | tf_op jit(solution)/shard_map/ppermute | solution.py:30
  9.1 1.0 %shard_map.80.after = f32[8,128,128]{2,1,0:T(8,128)S(1)} custom-call(s32[1,1,5]{2,1,0:T(1,128)} %cutoff_hbm.5, f32[5,128,128]{2,1,0:T(8,128)S(1)} %get-tuple-element.44.row, f32[1,1,5,128,128]{4,3,2,1,0:T(8,128)} %inv_hbm.5, f32[2,1,1,5,128,128]{5,4,3,2,1,0:T(8,128)} %rho_hbm.5, f32[4,128,128]{2,1,0:T(8,128)S(1)} %shard_map.79.message), custom_call_target="tpu_custom_call" | custom-call | flops 6291456000 | bytes 2097172 | tf_op jit(solution)/shard_map/pallas_call | solution.py:296
  10.1 0.7 %collective-permute-start = (f32[8,128,128]{2,1,0:T(8,128)S(1)}, f32[8,128,128]{2,1,0:T(8,128)S(1)}, u32[]{:S(2)}, u32[]{:S(2)}) collective-permute-start(f32[8,128,128]{2,1,0:T(8,128)S(1)} %shard_map.80.after), channel_id=1, source_target_pairs={{0,1},{1,0},{2,3},{3,2},{4,5},{5,4},{6,7},{7,6},{8,9},{9,8},{10,11... | collective-permute-start | bytes 1572872 | tf_op jit(solution)/shard_map/ppermute | solution.py:30
  10.8 1.3 %shard_map.81 = (f32[3,5,128,128]{3,2,1,0:T(8,128)S(1)}, bf16[384,640]{1,0:T(8,128)(2,1)S(1)}, bf16[384,640]{1,0:T(8,128)(2,1)S(1)}, bf16[128,640]{1,0:T(8,128)(...) custom-call(s32[1,1,5]{2,1,0:T(1,128)} %cutoff_hbm.5, f32[5,128,128]{2,1,0:T(8,128)S(1)} %get-tuple-element.44.row, ...), custom_call_target="tpu_custom_call" | custom-call | flops 25165824000 | bytes 5472788 | tf_op jit(solution)/shard_map/pallas_call | solution.py:296
  12.1 0.2 collective-permute-done.three
  12.4 1.2 %shard_map.82 = (f32[384,640]{1,0:T(8,128)S(1)}, f32[384,128]{1,0:T(8,128)S(1)}, f32[2,2,128,128]{3,2,1,0:T(8,128)S(1)}, f32[3,1,1,5,128,128]{5,4,3,2,1,0:T(8,128)S(1)}) custom-call(bf16[384,640]{1,0:T(8,128)(2,1)S(1)} %get-tuple-element.48.left_high, bf16[384,640]{1,0:T(8,128)(2,1)S(1)} %get-tuple-element.49.left_low, ...), custom_call_target="tpu_custom_call" | custom-call | flops 100663296000 | bytes 7536640 | tf_op jit(solution)/shard_map/pallas_call | solution.py:296
  13.6 0.0 collective-permute-done.1.four.arrived
  13.6 0.1 shard_map.86
  13.7 0.6 %collective-permute-start.4 = (f32[4,128,128]{2,1,0:T(8,128)S(1)}, f32[4,128,128]{2,1,0:T(8,128)S(1)}, u32[]{:S(2)}, u32[]{:S(2)}) collective-permute-start(f32[4,128,128]{2,1,0:T(8,128)S(1)} %get-tuple-element.73), channel_id=1, source_target_pairs={{1,2},{2,1},{3,0},{0,3},{5,6},{6,5},{7,4},{4,7},{9,10},{10,9},{11,... | collective-permute-start | bytes 786440 | tf_op jit(solution)/shard_map/ppermute | solution.py:30
  14.2 0.5 %collective-permute-start.5 = (f32[4,128,128]{2,1,0:T(8,128)S(1)}, f32[4,128,128]{2,1,0:T(8,128)S(1)}, u32[]{:S(2)}, u32[]{:S(2)}) collective-permute-start(f32[4,128,128]{2,1,0:T(8,128)S(1)} %get-tuple-element.77), channel_id=1, source_target_pairs={{0,4},{4,0},{8,12},{12,8},{16,20},{20,16},{24,28},{28,24},{1,5},{5... | collective-permute-start | bytes 786440 | tf_op jit(solution)/shard_map/ppermute | solution.py:30
  14.7 4.6 %collective-permute-start.6 = (f32[4,128,128]{2,1,0:T(8,128)S(1)}, f32[4,128,128]{2,1,0:T(8,128)S(1)}, u32[]{:S(2)}, u32[]{:S(2)}) collective-permute-start(f32[4,128,128]{2,1,0:T(8,128)S(1)} %get-tuple-element.78), channel_id=1, source_target_pairs={{4,8},{8,4},{12,16},{16,12},{20,24},{24,20},{28,0},{0,28},{5,9},{9... | collective-permute-start | bytes 786440 | tf_op jit(solution)/shard_map/ppermute | solution.py:30
  19.3 0.6 %shard_map.83 = (bf16[384,128]{1,0:T(8,128)(2,1)S(1)}, bf16[384,128]{1,0:T(8,128)(2,1)S(1)}, f32[384,128]{1,0:T(8,128)S(1)}, f32[2,128,128]{2,1,0:T(8,128)S(1)}) custom-call(bf16[384,640]{1,0:T(8,128)(2,1)S(1)} %get-tuple-element.48.left_high, bf16[384,640]{1,0:T(8,128)(2,1)S(1)} %get-tuple-element.49.left_low, f32[384,640]{1,0:T(8,128)S(1)} %get-tuple-element.54.start, ...), custom_call_target="tpu_custom_call" | custom-call | flops 100663296 | bytes 4128768 | tf_op jit(solution)/shard_map/pallas_call | solution.py:296
  19.9 0.0 collective-permute-done.2.one
  19.9 0.6 %shard_map.84 = (bf16[384,128]{1,0:T(8,128)(2,1)S(1)}, bf16[384,128]{1,0:T(8,128)(2,1)S(1)}, f32[384,128]{1,0:T(8,128)S(1)}, f32[2,128,128]{2,1,0:T(8,128)S(1)}) custom-call(bf16[384,640]{1,0:T(8,128)(2,1)S(1)} %get-tuple-element.48.left_high, bf16[384,640]{1,0:T(8,128)(2,1)S(1)} %get-tuple-element.49.left_low, f32[384,640]{1,0:T(8,128)S(1)} %get-tuple-element.54.start, ...), custom_call_target="tpu_custom_call" | custom-call | flops 125829120 | bytes 4128768 | tf_op jit(solution)/shard_map/pallas_call | solution.py:296
  20.5 0.0 collective-permute-done.3.two
  20.5 0.9 %shard_map.85 = (f32[4,128,128]{2,1,0:T(8,128)S(1)}, bf16[384,128]{1,0:T(8,128)(2,1)S(1)}, bf16[384,128]{1,0:T(8,128)(2,1)S(1)}, bf16[384,128]{1,0:T(8,128)(2,1)...) custom-call(bf16[384,640]{1,0:T(8,128)(2,1)S(1)} %get-tuple-element., ...), custom_call_target="tpu_custom_call" | custom-call | flops 276824064 | bytes 7280640 | tf_op jit(solution)/shard_map/pallas_call | solution.py:296
  21.5 0.1 collective-permute-start.9
  21.6 0.0 collective-permute-start.7
  21.6 1.1 %collective-permute-done.9.arrived.c3 = f32[3,128]{1,0:T(4,128)S(1)} collective-permute-done((f32[3,128]{1,0:T(4,128)S(1)}, f32[3,128]{1,0:T(4,128)S(1)}, u32[]{:S(2)}, u32[]{:S(2)}) %collective-permute-start.9) | collective-permute-done | bytes 1568 | tf_op jit(solution)/shard_map/ppermute | solution.py:30
  22.7 1.8 %collective-permute-start.8 = (f32[3,128]{1,0:T(4,128)S(1)}, f32[3,128]{1,0:T(4,128)S(1)}, u32[]{:S(2)}, u32[]{:S(2)}) collective-permute-start(f32[3,128]{1,0:T(4,128)S(1)} %get-tuple-element.80), channel_id=1, source_target_pairs={{4,8},{8,4},{12,16},{16,12},{20,24},{24,20},{28,0},{0,28},{5,9},{9... | collective-permute-start | bytes 4616 | tf_op jit(solution)/shard_map/ppermute | solution.py:30
  24.5 0.0 collective-permute-done.4.four
  24.5 1.8 %collective-permute-start.10 = (f32[3,128]{1,0:T(4,128)S(1)}, f32[3,128]{1,0:T(4,128)S(1)}, u32[]{:S(2)}, u32[]{:S(2)}) collective-permute-start(f32[3,128]{1,0:T(4,128)S(1)} %shard_map.88), channel_id=1, source_target_pairs={{1,2},{2,1},{3,0},{0,3},{5,6},{6,5},{7,4},{4,7},{9,10},{10,9},{11,... | collective-permute-start | bytes 4616 | tf_op jit(solution)/shard_map/ppermute | solution.py:30
  26.3 1.2 %shard_map.87 = (f32[2,1,1,5,128,128]{5,4,3,2,1,0:T(8,128)}, f32[3,128,128]{2,1,0:T(8,128)S(1)}, f32[128,128]{1,0:T(8,128)S(1)}, f32[3,128]{1,0:T(4,128)S(1)}) custom-call(f32[3,5,128,128]{3,2,1,0:T(8,128)S(1)} %get-tuple-element.47.held, f32[4,128,128]{2,1,0:T(8,128)S(1)} %get-tuple-element.65.new, bf16[384,640]{1,0:T(8,128)(2,1)S(1)} %get-tuple-element.48.left_high, ...), custom_call_target="tpu_custom_call" | custom-call | flops 125829120 | bytes 6030848 | tf_op jit(solution)/shard_map/pallas_call | solution.py:296
  27.5 1.3 %collective-permute-done.7.c1 = f32[3,128]{1,0:T(4,128)S(1)} collective-permute-done((f32[3,128]{1,0:T(4,128)S(1)}, f32[3,128]{1,0:T(4,128)S(1)}, u32[]{:S(2)}, u32[]{:S(2)}) %collective-permute-start.7) | collective-permute-done | bytes 1568 | tf_op jit(solution)/shard_map/ppermute | solution.py:30
  28.8 0.2 collective-permute-done.8.c2
  29.0 0.0 collective-permute-done.10.c4
  29.0 0.0 collective-permute-done.5.one
  29.0 0.0 collective-permute-done.6.two
  29.0 1.3 %shard_map.89 = (f32[2,1,1,5,128,128]{5,4,3,2,1,0:T(8,128)}, f32[3,1,64]{2,1,0:T(1,128)}) custom-call(f32[3,5,128,128]{3,2,1,0:T(8,128)S(1)} %get-tuple-element.47.held, f32[3,1,1,5,128,128]{5,4,3,2,1,0:T(8,128)S(1)} %get-tuple-element.52.der_ref, f32[64,128]{1,0:T(8,128)S(1)} %get-tuple-element.53.members, ...), custom_call_target="tpu_custom_call", output_to_operand_aliasing={{0}: (16, {})} | custom-call | flops 125829120 | bytes 4890880 | tf_op jit(solution)/shard_map/pallas_call | solution.py:296
  (3 shorter events, 0.0 us)
Async XLA Ops:
  1.7 18.2 %collective-permute-start.2 = (f32[4,128,128]{2,1,0:T(8,128)S(1)}, f32[4,128,128]{2,1,0:T(8,128)S(1)}, u32[]{:S(2)}, u32[]{:S(2)}) collective-permute-start(f32[4,128,128]{2,1,0:T(8,128)S(1)} %get-tuple-element.45.message), channel_id=1, source_target_pairs={{0,4},{4,0},{8,12},{12,8},{16,20},{20,16},{24,28},{28,24},{1,5},{5... | collective-permute-start | bytes 786440 | tf_op jit(solution)/shard_map/ppermute | solution.py:30
  4.7 8.9 %collective-permute-start.1 = (f32[4,128,128]{2,1,0:T(8,128)S(1)}, f32[4,128,128]{2,1,0:T(8,128)S(1)}, u32[]{:S(2)}, u32[]{:S(2)}) collective-permute-start(f32[4,128,128]{2,1,0:T(8,128)S(1)} %shard_map.78.message), channel_id=1, source_target_pairs={{1,2},{2,1},{3,0},{0,3},{5,6},{6,5},{7,4},{4,7},{9,10},{10,9},{11,... | collective-permute-start | bytes 786440 | tf_op jit(solution)/shard_map/ppermute | solution.py:30
  5.5 15.0 %collective-permute-start.3 = (f32[4,128,128]{2,1,0:T(8,128)S(1)}, f32[4,128,128]{2,1,0:T(8,128)S(1)}, u32[]{:S(2)}, u32[]{:S(2)}) collective-permute-start(f32[4,128,128]{2,1,0:T(8,128)S(1)} %shard_map.79.message), channel_id=1, source_target_pairs={{4,8},{8,4},{12,16},{16,12},{20,24},{24,20},{28,0},{0,28},{5,9},{9... | collective-permute-start | bytes 786440 | tf_op jit(solution)/shard_map/ppermute | solution.py:30
  10.1 2.3 %collective-permute-start = (f32[8,128,128]{2,1,0:T(8,128)S(1)}, f32[8,128,128]{2,1,0:T(8,128)S(1)}, u32[]{:S(2)}, u32[]{:S(2)}) collective-permute-start(f32[8,128,128]{2,1,0:T(8,128)S(1)} %shard_map.80.after), channel_id=1, source_target_pairs={{0,1},{1,0},{2,3},{3,2},{4,5},{5,4},{6,7},{7,6},{8,9},{9,8},{10,11... | collective-permute-start | bytes 1572872 | tf_op jit(solution)/shard_map/ppermute | solution.py:30
  13.7 10.8 %collective-permute-start.4 = (f32[4,128,128]{2,1,0:T(8,128)S(1)}, f32[4,128,128]{2,1,0:T(8,128)S(1)}, u32[]{:S(2)}, u32[]{:S(2)}) collective-permute-start(f32[4,128,128]{2,1,0:T(8,128)S(1)} %get-tuple-element.73), channel_id=1, source_target_pairs={{1,2},{2,1},{3,0},{0,3},{5,6},{6,5},{7,4},{4,7},{9,10},{10,9},{11,... | collective-permute-start | bytes 786440 | tf_op jit(solution)/shard_map/ppermute | solution.py:30
  14.2 14.7 %collective-permute-start.5 = (f32[4,128,128]{2,1,0:T(8,128)S(1)}, f32[4,128,128]{2,1,0:T(8,128)S(1)}, u32[]{:S(2)}, u32[]{:S(2)}) collective-permute-start(f32[4,128,128]{2,1,0:T(8,128)S(1)} %get-tuple-element.77), channel_id=1, source_target_pairs={{0,4},{4,0},{8,12},{12,8},{16,20},{20,16},{24,28},{28,24},{1,5},{5... | collective-permute-start | bytes 786440 | tf_op jit(solution)/shard_map/ppermute | solution.py:30
  14.7 14.3 %collective-permute-start.6 = (f32[4,128,128]{2,1,0:T(8,128)S(1)}, f32[4,128,128]{2,1,0:T(8,128)S(1)}, u32[]{:S(2)}, u32[]{:S(2)}) collective-permute-start(f32[4,128,128]{2,1,0:T(8,128)S(1)} %get-tuple-element.78), channel_id=1, source_target_pairs={{4,8},{8,4},{12,16},{16,12},{20,24},{24,20},{28,0},{0,28},{5,9},{9... | collective-permute-start | bytes 786440 | tf_op jit(solution)/shard_map/ppermute | solution.py:30
  21.5 1.2 %collective-permute-start.9 = (f32[3,128]{1,0:T(4,128)S(1)}, f32[3,128]{1,0:T(4,128)S(1)}, u32[]{:S(2)}, u32[]{:S(2)}) collective-permute-start(f32[3,128]{1,0:T(4,128)S(1)} %get-tuple-element.81), channel_id=1, source_target_pairs={{0,1},{1,0},{2,3},{3,2},{4,5},{5,4},{6,7},{7,6},{8,9},{9,8},{10,11... | collective-permute-start | bytes 4616 | tf_op jit(solution)/shard_map/ppermute | solution.py:30
  21.6 7.1 %collective-permute-start.7 = (f32[3,128]{1,0:T(4,128)S(1)}, f32[3,128]{1,0:T(4,128)S(1)}, u32[]{:S(2)}, u32[]{:S(2)}) collective-permute-start(f32[3,128]{1,0:T(4,128)S(1)} %get-tuple-element.79), channel_id=1, source_target_pairs={{0,4},{4,0},{8,12},{12,8},{16,20},{20,16},{24,28},{28,24},{1,5},{5... | collective-permute-start | bytes 4616 | tf_op jit(solution)/shard_map/ppermute | solution.py:30
  22.7 6.3 %collective-permute-start.8 = (f32[3,128]{1,0:T(4,128)S(1)}, f32[3,128]{1,0:T(4,128)S(1)}, u32[]{:S(2)}, u32[]{:S(2)}) collective-permute-start(f32[3,128]{1,0:T(4,128)S(1)} %get-tuple-element.80), channel_id=1, source_target_pairs={{4,8},{8,4},{12,16},{16,12},{20,24},{24,20},{28,0},{0,28},{5,9},{9... | collective-permute-start | bytes 4616 | tf_op jit(solution)/shard_map/ppermute | solution.py:30
  24.5 4.5 %collective-permute-start.10 = (f32[3,128]{1,0:T(4,128)S(1)}, f32[3,128]{1,0:T(4,128)S(1)}, u32[]{:S(2)}, u32[]{:S(2)}) collective-permute-start(f32[3,128]{1,0:T(4,128)S(1)} %shard_map.88), channel_id=1, source_target_pairs={{1,2},{2,1},{3,0},{0,3},{5,6},{6,5},{7,4},{4,7},{9,10},{10,9},{11,... | collective-permute-start | bytes 4616 | tf_op jit(solution)/shard_map/ppermute | solution.py:30

commit v24 on v22

--- a/solution.py
+++ b/solution.py
@@ -223,8 +223,9 @@
         weighted[direction] = sums[direction]
 
 
-def later_kernel(arrived, column, out):
-    out[...] = column[...]
+def later_kernel(arrived, c1, c4, c1_out, c4_out):
+    c1_out[...] = c1[...]
+    c4_out[...] = c4[...]
 
 
 def real_kernel(
@@ -383,9 +384,9 @@
         (left_high, left_low, start, diagonal, held, derivative, other_one, other_three, other_four, near_two),
     )
     c1, c2, c3, c4 = columns
-    c1, c2, c3 = swapped(c1, 1), swapped(c2, 2), swapped(c3, 3)
-    (c4,) = call(later_kernel, [shape(3, B)], [vmem] * 2, 0, (c3, c4))
-    columns = (c1, c2, c3, swapped(c4, 4))
+    c2, c3 = swapped(c2, 2), swapped(c3, 3)
+    c1, c4 = call(later_kernel, [shape(3, B)] * 2, [vmem] * 3, 0, (c3, c1, c4))
+    columns = (swapped(c1, 1), c2, c3, swapped(c4, 4))
     args = (held, new, left_high, left_low, self_high, self_low, other_one, real_two, other_three, other_four, weighted)
     args += (imag_part, high_four, low_four, near_four_more)
     out, comm, imag_part, row_part = call(

time: 30.5 us -> 30.3 us (level)
  waiting for transfers between devices: 2.71 us -> 2.18 us
    ppermute x11, waiting for transfers between devices: 2.71 us -> 2.18 us  [swapped(): return lax.ppermute(cells, axis, pairs)]
    ppermute x11, starting transfers between devices: 17.4 us -> 17.7 us  [swapped(): return lax.ppermute(cells, axis, pairs)]
  transfers between devices with their start and end apart: 11 -> 11, of which waited for: 4 -> 3; matrix products, arithmetic and copies ran while one was open for 0% -> 0% of each run, Pallas kernels for 23% -> 24%
where the time goes in v24:
time: 30.3 us; the launch traced here: 30.1 us
  starting transfers between devices  17.7 us (58%)
  Pallas kernels  9.42 us (31%)
  waiting for transfers between devices  2.18 us (7%)
  between operations  0.75 us (2%)
    ppermute x11, starting transfers between devices, swapped(): return lax.ppermute(cells, axis, pairs)  17.7 us
    pallas_call x13, Pallas kernels, call(): pl.pallas_call(kernel, out_shape=shapes, in_specs=in_specs, out_specs=out...  9.42 us
    ppermute x11, waiting for transfers between devices, swapped(): return lax.ppermute(cells, axis, pairs)  2.18 us
  transfers between devices with their start and end apart: 11, of which 3 were waited for; matrix products, arithmetic and copies ran while one was open for 0% of the time, Pallas kernels for 24%

profile of v24, /device:TPU:0, one launch (start us, length us, event | category | flops | bytes accessed | tf_op | source)
XLA Modules:
  0.0 30.1 jit_solution(8146821567415759093)
XLA Ops:
  0.6 1.0 %shard_map.77 = (f32[4,128,128]{2,1,0:T(8,128)S(1)}, f32[2,128,128]{2,1,0:T(8,128)S(1)}) custom-call(s32[1,1,5]{2,1,0:T(1,128)} %cutoff_hbm.5, f32[1,1,5,128,128]{4,3,2,1,0:T(8,128)} %ham_hbm.5, f32[1,1,5,128,128]{4,3,2,1,0:T(8,128)} %inv_hbm.5, f32[2,1,1,5,128,128]{5,4,3,2,1,0:T(8,128)} %rho_hbm.5), custom_call_target="tpu_custom_call" | custom-call | bytes 1703956 | tf_op jit(solution)/shard_map/pallas_call | solution.py:296
  1.7 3.0 %collective-permute-start.2 = (f32[4,128,128]{2,1,0:T(8,128)S(1)}, f32[4,128,128]{2,1,0:T(8,128)S(1)}, u32[]{:S(2)}, u32[]{:S(2)}) collective-permute-start(f32[4,128,128]{2,1,0:T(8,128)S(1)} %get-tuple-element.45.message), channel_id=1, source_target_pairs={{0,4},{4,0},{8,12},{12,8},{16,20},{20,16},{24,28},{28,24},{1,5},{5... | collective-permute-start | bytes 786440 | tf_op jit(solution)/shard_map/ppermute | solution.py:30
  4.7 0.7 %collective-permute-start.1 = (f32[4,128,128]{2,1,0:T(8,128)S(1)}, f32[4,128,128]{2,1,0:T(8,128)S(1)}, u32[]{:S(2)}, u32[]{:S(2)}) collective-permute-start(f32[4,128,128]{2,1,0:T(8,128)S(1)} %shard_map.78.message), channel_id=1, source_target_pairs={{1,2},{2,1},{3,0},{0,3},{5,6},{6,5},{7,4},{4,7},{9,10},{10,9},{11,... | collective-permute-start | bytes 786440 | tf_op jit(solution)/shard_map/ppermute | solution.py:30
  5.5 3.6 %collective-permute-start.3 = (f32[4,128,128]{2,1,0:T(8,128)S(1)}, f32[4,128,128]{2,1,0:T(8,128)S(1)}, u32[]{:S(2)}, u32[]{:S(2)}) collective-permute-start(f32[4,128,128]{2,1,0:T(8,128)S(1)} %shard_map.79.message), channel_id=1, source_target_pairs={{4,8},{8,4},{12,16},{16,12},{20,24},{24,20},{28,0},{0,28},{5,9},{9... | collective-permute-start | bytes 786440 | tf_op jit(solution)/shard_map/ppermute | solution.py:30
  9.1 1.0 %shard_map.80.after = f32[8,128,128]{2,1,0:T(8,128)S(1)} custom-call(s32[1,1,5]{2,1,0:T(1,128)} %cutoff_hbm.5, f32[1,1,5,128,128]{4,3,2,1,0:T(8,128)} %ham_hbm.5, f32[1,1,5,128,128]{4,3,2,1,0:T(8,128)} %inv_hbm.5, f32[2,1,1,5,128,128]{5,4,3,2,1,0:T(8,128)} %rho_hbm.5, f32[4,128,128]{2,1,0:T(8,128)S(1)} %shard_map.79.message), custom_call_target="tpu_custom_call" | custom-call | flops 6291456000 | bytes 2097172 | tf_op jit(solution)/shard_map/pallas_call | solution.py:296
  10.1 0.7 %collective-permute-start = (f32[8,128,128]{2,1,0:T(8,128)S(1)}, f32[8,128,128]{2,1,0:T(8,128)S(1)}, u32[]{:S(2)}, u32[]{:S(2)}) collective-permute-start(f32[8,128,128]{2,1,0:T(8,128)S(1)} %shard_map.80.after), channel_id=1, source_target_pairs={{0,1},{1,0},{2,3},{3,2},{4,5},{5,4},{6,7},{7,6},{8,9},{9,8},{10,11... | collective-permute-start | bytes 1572872 | tf_op jit(solution)/shard_map/ppermute | solution.py:30
  10.9 1.4 %shard_map.81 = (f32[3,5,128,128]{3,2,1,0:T(8,128)S(1)}, bf16[384,640]{1,0:T(8,128)(2,1)S(1)}, bf16[384,640]{1,0:T(8,128)(2,1)S(1)}, bf16[128,640]{1,0:T(8,128)(...) custom-call(s32[1,1,5]{2,1,0:T(1,128)} %cutoff_hbm.5, f32[1,1,5,128,128]{4,3,2,1,0:T(8,128)} %ham_hbm.5, ...), custom_call_target="tpu_custom_call" | custom-call | flops 25165824000 | bytes 5472788 | tf_op jit(solution)/shard_map/pallas_call | solution.py:296
  12.3 0.1 collective-permute-done.three
  12.4 1.2 %shard_map.82 = (f32[384,640]{1,0:T(8,128)S(1)}, f32[384,128]{1,0:T(8,128)S(1)}, f32[2,2,128,128]{3,2,1,0:T(8,128)S(1)}, f32[3,1,1,5,128,128]{5,4,3,2,1,0:T(8,128)S(1)}) custom-call(bf16[384,640]{1,0:T(8,128)(2,1)S(1)} %get-tuple-element.48.left_high, bf16[384,640]{1,0:T(8,128)(2,1)S(1)} %get-tuple-element.49.left_low, ...), custom_call_target="tpu_custom_call" | custom-call | flops 100663296000 | bytes 7536640 | tf_op jit(solution)/shard_map/pallas_call | solution.py:296
  13.6 0.0 collective-permute-done.1.four.arrived
  13.6 0.1 shard_map.86
  13.7 0.6 %collective-permute-start.4 = (f32[4,128,128]{2,1,0:T(8,128)S(1)}, f32[4,128,128]{2,1,0:T(8,128)S(1)}, u32[]{:S(2)}, u32[]{:S(2)}) collective-permute-start(f32[4,128,128]{2,1,0:T(8,128)S(1)} %get-tuple-element.73), channel_id=1, source_target_pairs={{1,2},{2,1},{3,0},{0,3},{5,6},{6,5},{7,4},{4,7},{9,10},{10,9},{11,... | collective-permute-start | bytes 786440 | tf_op jit(solution)/shard_map/ppermute | solution.py:30
  14.3 0.4 %collective-permute-start.5 = (f32[4,128,128]{2,1,0:T(8,128)S(1)}, f32[4,128,128]{2,1,0:T(8,128)S(1)}, u32[]{:S(2)}, u32[]{:S(2)}) collective-permute-start(f32[4,128,128]{2,1,0:T(8,128)S(1)} %get-tuple-element.77), channel_id=1, source_target_pairs={{0,4},{4,0},{8,12},{12,8},{16,20},{20,16},{24,28},{28,24},{1,5},{5... | collective-permute-start | bytes 786440 | tf_op jit(solution)/shard_map/ppermute | solution.py:30
  14.7 4.6 %collective-permute-start.6 = (f32[4,128,128]{2,1,0:T(8,128)S(1)}, f32[4,128,128]{2,1,0:T(8,128)S(1)}, u32[]{:S(2)}, u32[]{:S(2)}) collective-permute-start(f32[4,128,128]{2,1,0:T(8,128)S(1)} %get-tuple-element.78), channel_id=1, source_target_pairs={{4,8},{8,4},{12,16},{16,12},{20,24},{24,20},{28,0},{0,28},{5,9},{9... | collective-permute-start | bytes 786440 | tf_op jit(solution)/shard_map/ppermute | solution.py:30
  19.3 0.6 %shard_map.83 = (bf16[384,128]{1,0:T(8,128)(2,1)S(1)}, bf16[384,128]{1,0:T(8,128)(2,1)S(1)}, f32[384,128]{1,0:T(8,128)S(1)}, f32[2,128,128]{2,1,0:T(8,128)S(1)}) custom-call(bf16[384,640]{1,0:T(8,128)(2,1)S(1)} %get-tuple-element.48.left_high, bf16[384,640]{1,0:T(8,128)(2,1)S(1)} %get-tuple-element.49.left_low, f32[384,640]{1,0:T(8,128)S(1)} %get-tuple-element.54.start, ...), custom_call_target="tpu_custom_call" | custom-call | flops 100663296 | bytes 4128768 | tf_op jit(solution)/shard_map/pallas_call | solution.py:296
  19.9 0.0 collective-permute-done.2.one
  19.9 0.6 %shard_map.84 = (bf16[384,128]{1,0:T(8,128)(2,1)S(1)}, bf16[384,128]{1,0:T(8,128)(2,1)S(1)}, f32[384,128]{1,0:T(8,128)S(1)}, f32[2,128,128]{2,1,0:T(8,128)S(1)}) custom-call(bf16[384,640]{1,0:T(8,128)(2,1)S(1)} %get-tuple-element.48.left_high, bf16[384,640]{1,0:T(8,128)(2,1)S(1)} %get-tuple-element.49.left_low, f32[384,640]{1,0:T(8,128)S(1)} %get-tuple-element.54.start, ...), custom_call_target="tpu_custom_call" | custom-call | flops 125829120 | bytes 4128768 | tf_op jit(solution)/shard_map/pallas_call | solution.py:296
  20.5 0.0 collective-permute-done.3.two
  20.5 0.9 %shard_map.85 = (f32[4,128,128]{2,1,0:T(8,128)S(1)}, bf16[384,128]{1,0:T(8,128)(2,1)S(1)}, bf16[384,128]{1,0:T(8,128)(2,1)S(1)}, bf16[384,128]{1,0:T(8,128)(2,1)...) custom-call(bf16[384,640]{1,0:T(8,128)(2,1)S(1)} %get-tuple-element., ...), custom_call_target="tpu_custom_call" | custom-call | flops 276824064 | bytes 7280640 | tf_op jit(solution)/shard_map/pallas_call | solution.py:296
  21.5 0.1 collective-permute-start.7
  21.6 1.8 %collective-permute-start.9 = (f32[3,128]{1,0:T(4,128)S(1)}, f32[3,128]{1,0:T(4,128)S(1)}, u32[]{:S(2)}, u32[]{:S(2)}) collective-permute-start(f32[3,128]{1,0:T(4,128)S(1)} %get-tuple-element.83), channel_id=1, source_target_pairs={{4,8},{8,4},{12,16},{16,12},{20,24},{24,20},{28,0},{0,28},{5,9},{9... | collective-permute-start | bytes 4616 | tf_op jit(solution)/shard_map/ppermute | solution.py:30
  23.4 0.0 collective-permute-done.7.arrived.c3
  23.4 0.0 collective-permute-start.8
  23.4 0.0 collective-permute-done.4.four
  23.4 2.1 %collective-permute-start.10 = (f32[3,128]{1,0:T(4,128)S(1)}, f32[3,128]{1,0:T(4,128)S(1)}, u32[]{:S(2)}, u32[]{:S(2)}) collective-permute-start(f32[3,128]{1,0:T(4,128)S(1)} %get-tuple-element.84), channel_id=1, source_target_pairs={{1,2},{2,1},{3,0},{0,3},{5,6},{6,5},{7,4},{4,7},{9,10},{10,9},{11,... | collective-permute-start | bytes 4616 | tf_op jit(solution)/shard_map/ppermute | solution.py:30
  25.5 1.2 %shard_map.87 = (f32[2,1,1,5,128,128]{5,4,3,2,1,0:T(8,128)}, f32[3,128,128]{2,1,0:T(8,128)S(1)}, f32[128,128]{1,0:T(8,128)S(1)}, f32[3,128]{1,0:T(4,128)S(1)}) custom-call(f32[3,5,128,128]{3,2,1,0:T(8,128)S(1)} %get-tuple-element.47.held, f32[4,128,128]{2,1,0:T(8,128)S(1)} %get-tuple-element.65.new, bf16[384,640]{1,0:T(8,128)(2,1)S(1)} %get-tuple-element.48.left_high, ...), custom_call_target="tpu_custom_call" | custom-call | flops 125829120 | bytes 6030848 | tf_op jit(solution)/shard_map/pallas_call | solution.py:296
  26.7 1.1 %collective-permute-done.9.c2 = f32[3,128]{1,0:T(4,128)S(1)} collective-permute-done((f32[3,128]{1,0:T(4,128)S(1)}, f32[3,128]{1,0:T(4,128)S(1)}, u32[]{:S(2)}, u32[]{:S(2)}) %collective-permute-start.9) | collective-permute-done | bytes 1568 | tf_op jit(solution)/shard_map/ppermute | solution.py:30
  27.9 0.9 %collective-permute-done.8.c1 = f32[3,128]{1,0:T(4,128)S(1)} collective-permute-done((f32[3,128]{1,0:T(4,128)S(1)}, f32[3,128]{1,0:T(4,128)S(1)}, u32[]{:S(2)}, u32[]{:S(2)}) %collective-permute-start.8) | collective-permute-done | bytes 1568 | tf_op jit(solution)/shard_map/ppermute | solution.py:30
  28.8 0.0 collective-permute-done.10.c4
  28.8 0.0 collective-permute-done.5.one
  28.8 0.0 collective-permute-done.6.two
  28.8 1.3 %shard_map.89 = (f32[2,1,1,5,128,128]{5,4,3,2,1,0:T(8,128)}, f32[3,1,64]{2,1,0:T(1,128)}) custom-call(f32[3,5,128,128]{3,2,1,0:T(8,128)S(1)} %get-tuple-element.47.held, f32[3,1,1,5,128,128]{5,4,3,2,1,0:T(8,128)S(1)} %get-tuple-element.52.der_ref, f32[64,128]{1,0:T(8,128)S(1)} %get-tuple-element.53.members, ...), custom_call_target="tpu_custom_call", output_to_operand_aliasing={{0}: (16, {})} | custom-call | flops 125829120 | bytes 4890880 | tf_op jit(solution)/shard_map/pallas_call | solution.py:296
  (3 shorter events, 0.0 us)
Async XLA Ops:
  1.7 18.2 %collective-permute-start.2 = (f32[4,128,128]{2,1,0:T(8,128)S(1)}, f32[4,128,128]{2,1,0:T(8,128)S(1)}, u32[]{:S(2)}, u32[]{:S(2)}) collective-permute-start(f32[4,128,128]{2,1,0:T(8,128)S(1)} %get-tuple-element.45.message), channel_id=1, source_target_pairs={{0,4},{4,0},{8,12},{12,8},{16,20},{20,16},{24,28},{28,24},{1,5},{5... | collective-permute-start | bytes 786440 | tf_op jit(solution)/shard_map/ppermute | solution.py:30
  4.7 8.9 %collective-permute-start.1 = (f32[4,128,128]{2,1,0:T(8,128)S(1)}, f32[4,128,128]{2,1,0:T(8,128)S(1)}, u32[]{:S(2)}, u32[]{:S(2)}) collective-permute-start(f32[4,128,128]{2,1,0:T(8,128)S(1)} %shard_map.78.message), channel_id=1, source_target_pairs={{1,2},{2,1},{3,0},{0,3},{5,6},{6,5},{7,4},{4,7},{9,10},{10,9},{11,... | collective-permute-start | bytes 786440 | tf_op jit(solution)/shard_map/ppermute | solution.py:30
  5.5 15.0 %collective-permute-start.3 = (f32[4,128,128]{2,1,0:T(8,128)S(1)}, f32[4,128,128]{2,1,0:T(8,128)S(1)}, u32[]{:S(2)}, u32[]{:S(2)}) collective-permute-start(f32[4,128,128]{2,1,0:T(8,128)S(1)} %shard_map.79.message), channel_id=1, source_target_pairs={{4,8},{8,4},{12,16},{16,12},{20,24},{24,20},{28,0},{0,28},{5,9},{9... | collective-permute-start | bytes 786440 | tf_op jit(solution)/shard_map/ppermute | solution.py:30
  10.1 2.3 %collective-permute-start = (f32[8,128,128]{2,1,0:T(8,128)S(1)}, f32[8,128,128]{2,1,0:T(8,128)S(1)}, u32[]{:S(2)}, u32[]{:S(2)}) collective-permute-start(f32[8,128,128]{2,1,0:T(8,128)S(1)} %shard_map.80.after), channel_id=1, source_target_pairs={{0,1},{1,0},{2,3},{3,2},{4,5},{5,4},{6,7},{7,6},{8,9},{9,8},{10,11... | collective-permute-start | bytes 1572872 | tf_op jit(solution)/shard_map/ppermute | solution.py:30
  13.7 9.7 %collective-permute-start.4 = (f32[4,128,128]{2,1,0:T(8,128)S(1)}, f32[4,128,128]{2,1,0:T(8,128)S(1)}, u32[]{:S(2)}, u32[]{:S(2)}) collective-permute-start(f32[4,128,128]{2,1,0:T(8,128)S(1)} %get-tuple-element.73), channel_id=1, source_target_pairs={{1,2},{2,1},{3,0},{0,3},{5,6},{6,5},{7,4},{4,7},{9,10},{10,9},{11,... | collective-permute-start | bytes 786440 | tf_op jit(solution)/shard_map/ppermute | solution.py:30
  14.3 14.5 %collective-permute-start.5 = (f32[4,128,128]{2,1,0:T(8,128)S(1)}, f32[4,128,128]{2,1,0:T(8,128)S(1)}, u32[]{:S(2)}, u32[]{:S(2)}) collective-permute-start(f32[4,128,128]{2,1,0:T(8,128)S(1)} %get-tuple-element.77), channel_id=1, source_target_pairs={{0,4},{4,0},{8,12},{12,8},{16,20},{20,16},{24,28},{28,24},{1,5},{5... | collective-permute-start | bytes 786440 | tf_op jit(solution)/shard_map/ppermute | solution.py:30
  14.7 14.1 %collective-permute-start.6 = (f32[4,128,128]{2,1,0:T(8,128)S(1)}, f32[4,128,128]{2,1,0:T(8,128)S(1)}, u32[]{:S(2)}, u32[]{:S(2)}) collective-permute-start(f32[4,128,128]{2,1,0:T(8,128)S(1)} %get-tuple-element.78), channel_id=1, source_target_pairs={{4,8},{8,4},{12,16},{16,12},{20,24},{24,20},{28,0},{0,28},{5,9},{9... | collective-permute-start | bytes 786440 | tf_op jit(solution)/shard_map/ppermute | solution.py:30
  21.5 2.0 %collective-permute-start.7 = (f32[3,128]{1,0:T(4,128)S(1)}, f32[3,128]{1,0:T(4,128)S(1)}, u32[]{:S(2)}, u32[]{:S(2)}) collective-permute-start(f32[3,128]{1,0:T(4,128)S(1)} %get-tuple-element.79), channel_id=1, source_target_pairs={{0,1},{1,0},{2,3},{3,2},{4,5},{5,4},{6,7},{7,6},{8,9},{9,8},{10,11... | collective-permute-start | bytes 4616 | tf_op jit(solution)/shard_map/ppermute | solution.py:30
  21.6 6.3 %collective-permute-start.9 = (f32[3,128]{1,0:T(4,128)S(1)}, f32[3,128]{1,0:T(4,128)S(1)}, u32[]{:S(2)}, u32[]{:S(2)}) collective-permute-start(f32[3,128]{1,0:T(4,128)S(1)} %get-tuple-element.83), channel_id=1, source_target_pairs={{4,8},{8,4},{12,16},{16,12},{20,24},{24,20},{28,0},{0,28},{5,9},{9... | collective-permute-start | bytes 4616 | tf_op jit(solution)/shard_map/ppermute | solution.py:30
  23.4 5.4 %collective-permute-start.8 = (f32[3,128]{1,0:T(4,128)S(1)}, f32[3,128]{1,0:T(4,128)S(1)}, u32[]{:S(2)}, u32[]{:S(2)}) collective-permute-start(f32[3,128]{1,0:T(4,128)S(1)} %get-tuple-element.82), channel_id=1, source_target_pairs={{0,4},{4,0},{8,12},{12,8},{16,20},{20,16},{24,28},{28,24},{1,5},{5... | collective-permute-start | bytes 4616 | tf_op jit(solution)/shard_map/ppermute | solution.py:30
  23.4 5.3 %collective-permute-start.10 = (f32[3,128]{1,0:T(4,128)S(1)}, f32[3,128]{1,0:T(4,128)S(1)}, u32[]{:S(2)}, u32[]{:S(2)}) collective-permute-start(f32[3,128]{1,0:T(4,128)S(1)} %get-tuple-element.84), channel_id=1, source_target_pairs={{1,2},{2,1},{3,0},{0,3},{5,6},{6,5},{7,4},{4,7},{9,10},{10,9},{11,... | collective-permute-start | bytes 4616 | tf_op jit(solution)/shard_map/ppermute | solution.py:30

commit v25 on v24

--- a/solution.py
+++ b/solution.py
@@ -141,7 +141,7 @@
                 left_high[rows, cols(place)], left_low[rows, cols(place)] = split(block)
     owners.wait()
     atoms = jnp.broadcast_to(atom_ref[0], (ATOMS, B))
-    members[...] = -(lax.broadcasted_iota(jnp.int32, (ATOMS, B), 0) == atoms).astype(f32)
+    members[...] = (-(lax.broadcasted_iota(jnp.int32, (ATOMS, B), 0) == atoms).astype(f32)).astype(bf16)
 
 
 def first_half(left, place, start, near, diagonal):
@@ -281,9 +281,10 @@
         product = real_new * der_ref[direction, 0, 0, 0]
         parts.append(jnp.sum(product + product.T, axis=0, keepdims=True))
     orbital = jnp.concatenate(parts, axis=0) + row_part[...] + ((c1[...] + c2[...]) + (c3[...] + c4[...]))
-    forces = lax.dot_general(
-        orbital, members[...], (((1,), (1,)), ((), ())), precision=lax.Precision.HIGHEST, preferred_element_type=f32
-    )
+    high, low = [
+        lax.dot_general(some, members[...], (((1,), (1,)), ((), ())), preferred_element_type=f32) for some in split(orbital)
+    ]
+    forces = high + low
     for direction in range(3):
         forces_ref[direction] = forces[direction : direction + 1]
     copies += start_all([pltpu.make_async_copy(forces_ref, forces_hbm, sems.at[4])])
@@ -341,7 +342,7 @@
     ham = [shape(B, 5 * B, kind=bf16)] * 2
     held, left_high, left_low, ham_high, ham_low, members = call(
         second_kernel,
-        [shape(3, 5, B, B)] + left + ham + [shape(ATOMS, B)],
+        [shape(3, 5, B, B)] + left + ham + [shape(ATOMS, B, kind=bf16)],
         [hbm] * 6,
         2000,
         (cutoff, hamiltonian, inverse_margin, density, atom_of, send_three),

time: 30.3 us -> 30.3 us (level)
  no operation moved by 1% of the time
where the time goes in v25:
time: 30.3 us; the launch traced here: 30 us
  starting transfers between devices  17.7 us (58%)
  Pallas kernels  9.35 us (31%)
  waiting for transfers between devices  2.18 us (7%)
  between operations  0.75 us (2%)
    ppermute x11, starting transfers between devices, swapped(): return lax.ppermute(cells, axis, pairs)  17.7 us
    pallas_call x13, Pallas kernels, call(): pl.pallas_call(kernel, out_shape=shapes, in_specs=in_specs, out_specs=out...  9.35 us
    ppermute x11, waiting for transfers between devices, swapped(): return lax.ppermute(cells, axis, pairs)  2.18 us
  transfers between devices with their start and end apart: 11, of which 3 were waited for; matrix products, arithmetic and copies ran while one was open for 0% of the time, Pallas kernels for 24%

profile of v25, /device:TPU:0, one launch (start us, length us, event | category | flops | bytes accessed | tf_op | source)
XLA Modules:
  0.0 30.0 jit_solution(1601272613286191235)
XLA Ops:
  0.6 1.0 %shard_map.77 = (f32[4,128,128]{2,1,0:T(8,128)S(1)}, f32[2,128,128]{2,1,0:T(8,128)S(1)}) custom-call(s32[1,1,5]{2,1,0:T(1,128)} %cutoff_hbm.5, f32[1,1,5,128,128]{4,3,2,1,0:T(8,128)} %ham_hbm.5, f32[1,1,5,128,128]{4,3,2,1,0:T(8,128)} %inv_hbm.5, f32[2,1,1,5,128,128]{5,4,3,2,1,0:T(8,128)} %rho_hbm.5), custom_call_target="tpu_custom_call" | custom-call | bytes 1703956 | tf_op jit(solution)/shard_map/pallas_call | solution.py:297
  1.7 3.0 %collective-permute-start.2 = (f32[4,128,128]{2,1,0:T(8,128)S(1)}, f32[4,128,128]{2,1,0:T(8,128)S(1)}, u32[]{:S(2)}, u32[]{:S(2)}) collective-permute-start(f32[4,128,128]{2,1,0:T(8,128)S(1)} %get-tuple-element.45.message), channel_id=1, source_target_pairs={{0,4},{4,0},{8,12},{12,8},{16,20},{20,16},{24,28},{28,24},{1,5},{5... | collective-permute-start | bytes 786440 | tf_op jit(solution)/shard_map/ppermute | solution.py:30
  4.7 0.7 %collective-permute-start.1 = (f32[4,128,128]{2,1,0:T(8,128)S(1)}, f32[4,128,128]{2,1,0:T(8,128)S(1)}, u32[]{:S(2)}, u32[]{:S(2)}) collective-permute-start(f32[4,128,128]{2,1,0:T(8,128)S(1)} %shard_map.78.message), channel_id=1, source_target_pairs={{1,2},{2,1},{3,0},{0,3},{5,6},{6,5},{7,4},{4,7},{9,10},{10,9},{11,... | collective-permute-start | bytes 786440 | tf_op jit(solution)/shard_map/ppermute | solution.py:30
  5.5 3.6 %collective-permute-start.3 = (f32[4,128,128]{2,1,0:T(8,128)S(1)}, f32[4,128,128]{2,1,0:T(8,128)S(1)}, u32[]{:S(2)}, u32[]{:S(2)}) collective-permute-start(f32[4,128,128]{2,1,0:T(8,128)S(1)} %shard_map.79.message), channel_id=1, source_target_pairs={{4,8},{8,4},{12,16},{16,12},{20,24},{24,20},{28,0},{0,28},{5,9},{9... | collective-permute-start | bytes 786440 | tf_op jit(solution)/shard_map/ppermute | solution.py:30
  9.1 1.0 %shard_map.80.after = f32[8,128,128]{2,1,0:T(8,128)S(1)} custom-call(s32[1,1,5]{2,1,0:T(1,128)} %cutoff_hbm.5, f32[1,1,5,128,128]{4,3,2,1,0:T(8,128)} %ham_hbm.5, f32[1,1,5,128,128]{4,3,2,1,0:T(8,128)} %inv_hbm.5, f32[2,1,1,5,128,128]{5,4,3,2,1,0:T(8,128)} %rho_hbm.5, f32[4,128,128]{2,1,0:T(8,128)S(1)} %shard_map.79.message), custom_call_target="tpu_custom_call" | custom-call | flops 6291456000 | bytes 2097172 | tf_op jit(solution)/shard_map/pallas_call | solution.py:297
  10.1 0.7 %collective-permute-start = (f32[8,128,128]{2,1,0:T(8,128)S(1)}, f32[8,128,128]{2,1,0:T(8,128)S(1)}, u32[]{:S(2)}, u32[]{:S(2)}) collective-permute-start(f32[8,128,128]{2,1,0:T(8,128)S(1)} %shard_map.80.after), channel_id=1, source_target_pairs={{0,1},{1,0},{2,3},{3,2},{4,5},{5,4},{6,7},{7,6},{8,9},{9,8},{10,11... | collective-permute-start | bytes 1572872 | tf_op jit(solution)/shard_map/ppermute | solution.py:30
  10.9 1.4 %shard_map.81 = (f32[3,5,128,128]{3,2,1,0:T(8,128)S(1)}, bf16[384,640]{1,0:T(8,128)(2,1)S(1)}, bf16[384,640]{1,0:T(8,128)(2,1)S(1)}, bf16[128,640]{1,0:T(8,128)(...) custom-call(s32[1,1,5]{2,1,0:T(1,128)} %cutoff_hbm.5, f32[1,1,5,128,128]{4,3,2,1,0:T(8,128)} %ham_hbm.5, ...), custom_call_target="tpu_custom_call" | custom-call | flops 25165824000 | bytes 5472788 | tf_op jit(solution)/shard_map/pallas_call | solution.py:297
  12.3 0.1 collective-permute-done.three
  12.4 1.2 %shard_map.82 = (f32[384,640]{1,0:T(8,128)S(1)}, f32[384,128]{1,0:T(8,128)S(1)}, f32[2,2,128,128]{3,2,1,0:T(8,128)S(1)}, f32[3,1,1,5,128,128]{5,4,3,2,1,0:T(8,128)S(1)}) custom-call(bf16[384,640]{1,0:T(8,128)(2,1)S(1)} %get-tuple-element.48.left_high, bf16[384,640]{1,0:T(8,128)(2,1)S(1)} %get-tuple-element.49.left_low, ...), custom_call_target="tpu_custom_call" | custom-call | flops 100663296000 | bytes 7536640 | tf_op jit(solution)/shard_map/pallas_call | solution.py:297
  13.6 0.0 collective-permute-done.1.four.arrived
  13.6 0.1 shard_map.86
  13.7 0.6 %collective-permute-start.4 = (f32[4,128,128]{2,1,0:T(8,128)S(1)}, f32[4,128,128]{2,1,0:T(8,128)S(1)}, u32[]{:S(2)}, u32[]{:S(2)}) collective-permute-start(f32[4,128,128]{2,1,0:T(8,128)S(1)} %get-tuple-element.73), channel_id=1, source_target_pairs={{1,2},{2,1},{3,0},{0,3},{5,6},{6,5},{7,4},{4,7},{9,10},{10,9},{11,... | collective-permute-start | bytes 786440 | tf_op jit(solution)/shard_map/ppermute | solution.py:30
  14.3 0.4 %collective-permute-start.5 = (f32[4,128,128]{2,1,0:T(8,128)S(1)}, f32[4,128,128]{2,1,0:T(8,128)S(1)}, u32[]{:S(2)}, u32[]{:S(2)}) collective-permute-start(f32[4,128,128]{2,1,0:T(8,128)S(1)} %get-tuple-element.77), channel_id=1, source_target_pairs={{0,4},{4,0},{8,12},{12,8},{16,20},{20,16},{24,28},{28,24},{1,5},{5... | collective-permute-start | bytes 786440 | tf_op jit(solution)/shard_map/ppermute | solution.py:30
  14.7 4.6 %collective-permute-start.6 = (f32[4,128,128]{2,1,0:T(8,128)S(1)}, f32[4,128,128]{2,1,0:T(8,128)S(1)}, u32[]{:S(2)}, u32[]{:S(2)}) collective-permute-start(f32[4,128,128]{2,1,0:T(8,128)S(1)} %get-tuple-element.78), channel_id=1, source_target_pairs={{4,8},{8,4},{12,16},{16,12},{20,24},{24,20},{28,0},{0,28},{5,9},{9... | collective-permute-start | bytes 786440 | tf_op jit(solution)/shard_map/ppermute | solution.py:30
  19.3 0.6 %shard_map.83 = (bf16[384,128]{1,0:T(8,128)(2,1)S(1)}, bf16[384,128]{1,0:T(8,128)(2,1)S(1)}, f32[384,128]{1,0:T(8,128)S(1)}, f32[2,128,128]{2,1,0:T(8,128)S(1)}) custom-call(bf16[384,640]{1,0:T(8,128)(2,1)S(1)} %get-tuple-element.48.left_high, bf16[384,640]{1,0:T(8,128)(2,1)S(1)} %get-tuple-element.49.left_low, f32[384,640]{1,0:T(8,128)S(1)} %get-tuple-element.54.start, ...), custom_call_target="tpu_custom_call" | custom-call | flops 100663296 | bytes 4128768 | tf_op jit(solution)/shard_map/pallas_call | solution.py:297
  19.9 0.0 collective-permute-done.2.one
  19.9 0.6 %shard_map.84 = (bf16[384,128]{1,0:T(8,128)(2,1)S(1)}, bf16[384,128]{1,0:T(8,128)(2,1)S(1)}, f32[384,128]{1,0:T(8,128)S(1)}, f32[2,128,128]{2,1,0:T(8,128)S(1)}) custom-call(bf16[384,640]{1,0:T(8,128)(2,1)S(1)} %get-tuple-element.48.left_high, bf16[384,640]{1,0:T(8,128)(2,1)S(1)} %get-tuple-element.49.left_low, f32[384,640]{1,0:T(8,128)S(1)} %get-tuple-element.54.start, ...), custom_call_target="tpu_custom_call" | custom-call | flops 125829120 | bytes 4128768 | tf_op jit(solution)/shard_map/pallas_call | solution.py:297
  20.5 0.0 collective-permute-done.3.two
  20.5 0.9 %shard_map.85 = (f32[4,128,128]{2,1,0:T(8,128)S(1)}, bf16[384,128]{1,0:T(8,128)(2,1)S(1)}, bf16[384,128]{1,0:T(8,128)(2,1)S(1)}, bf16[384,128]{1,0:T(8,128)(2,1)...) custom-call(bf16[384,640]{1,0:T(8,128)(2,1)S(1)} %get-tuple-element., ...), custom_call_target="tpu_custom_call" | custom-call | flops 276824064 | bytes 7280640 | tf_op jit(solution)/shard_map/pallas_call | solution.py:297
  21.5 0.1 collective-permute-start.7
  21.6 1.8 %collective-permute-start.9 = (f32[3,128]{1,0:T(4,128)S(1)}, f32[3,128]{1,0:T(4,128)S(1)}, u32[]{:S(2)}, u32[]{:S(2)}) collective-permute-start(f32[3,128]{1,0:T(4,128)S(1)} %get-tuple-element.83), channel_id=1, source_target_pairs={{4,8},{8,4},{12,16},{16,12},{20,24},{24,20},{28,0},{0,28},{5,9},{9... | collective-permute-start | bytes 4616 | tf_op jit(solution)/shard_map/ppermute | solution.py:30
  23.4 0.0 collective-permute-done.7.arrived.c3
  23.4 0.0 collective-permute-start.8
  23.4 0.0 collective-permute-done.4.four
  23.4 2.1 %collective-permute-start.10 = (f32[3,128]{1,0:T(4,128)S(1)}, f32[3,128]{1,0:T(4,128)S(1)}, u32[]{:S(2)}, u32[]{:S(2)}) collective-permute-start(f32[3,128]{1,0:T(4,128)S(1)} %get-tuple-element.84), channel_id=1, source_target_pairs={{1,2},{2,1},{3,0},{0,3},{5,6},{6,5},{7,4},{4,7},{9,10},{10,9},{11,... | collective-permute-start | bytes 4616 | tf_op jit(solution)/shard_map/ppermute | solution.py:30
  25.5 1.2 %shard_map.87 = (f32[2,1,1,5,128,128]{5,4,3,2,1,0:T(8,128)}, f32[3,128,128]{2,1,0:T(8,128)S(1)}, f32[128,128]{1,0:T(8,128)S(1)}, f32[3,128]{1,0:T(4,128)S(1)}) custom-call(f32[3,5,128,128]{3,2,1,0:T(8,128)S(1)} %get-tuple-element.47.held, f32[4,128,128]{2,1,0:T(8,128)S(1)} %get-tuple-element.65.new, bf16[384,640]{1,0:T(8,128)(2,1)S(1)} %get-tuple-element.48.left_high, ...), custom_call_target="tpu_custom_call" | custom-call | flops 125829120 | bytes 6030848 | tf_op jit(solution)/shard_map/pallas_call | solution.py:297
  26.7 1.1 %collective-permute-done.9.c2 = f32[3,128]{1,0:T(4,128)S(1)} collective-permute-done((f32[3,128]{1,0:T(4,128)S(1)}, f32[3,128]{1,0:T(4,128)S(1)}, u32[]{:S(2)}, u32[]{:S(2)}) %collective-permute-start.9) | collective-permute-done | bytes 1568 | tf_op jit(solution)/shard_map/ppermute | solution.py:30
  27.9 0.9 %collective-permute-done.8.c1 = f32[3,128]{1,0:T(4,128)S(1)} collective-permute-done((f32[3,128]{1,0:T(4,128)S(1)}, f32[3,128]{1,0:T(4,128)S(1)}, u32[]{:S(2)}, u32[]{:S(2)}) %collective-permute-start.8) | collective-permute-done | bytes 1568 | tf_op jit(solution)/shard_map/ppermute | solution.py:30
  28.8 0.0 collective-permute-done.10.c4
  28.8 0.0 collective-permute-done.5.one
  28.8 0.0 collective-permute-done.6.two
  28.8 1.2 %shard_map.89 = (f32[2,1,1,5,128,128]{5,4,3,2,1,0:T(8,128)}, f32[3,1,64]{2,1,0:T(1,128)}) custom-call(f32[3,5,128,128]{3,2,1,0:T(8,128)S(1)} %get-tuple-element.47.held, f32[3,1,1,5,128,128]{5,4,3,2,1,0:T(8,128)S(1)} %get-tuple-element.52.der_ref, bf16[64,128]{1,0:T(8,128)(2,1)S(1)} %get-tuple-element.53.members, ...), custom_call_target="tpu_custom_call", output_to_operand_aliasing={{0}: (16, {})} | custom-call | flops 125829120 | bytes 4890880 | tf_op jit(solution)/shard_map/pallas_call | solution.py:297
  (3 shorter events, 0.0 us)
Async XLA Ops:
  1.7 18.2 %collective-permute-start.2 = (f32[4,128,128]{2,1,0:T(8,128)S(1)}, f32[4,128,128]{2,1,0:T(8,128)S(1)}, u32[]{:S(2)}, u32[]{:S(2)}) collective-permute-start(f32[4,128,128]{2,1,0:T(8,128)S(1)} %get-tuple-element.45.message), channel_id=1, source_target_pairs={{0,4},{4,0},{8,12},{12,8},{16,20},{20,16},{24,28},{28,24},{1,5},{5... | collective-permute-start | bytes 786440 | tf_op jit(solution)/shard_map/ppermute | solution.py:30
  4.7 8.9 %collective-permute-start.1 = (f32[4,128,128]{2,1,0:T(8,128)S(1)}, f32[4,128,128]{2,1,0:T(8,128)S(1)}, u32[]{:S(2)}, u32[]{:S(2)}) collective-permute-start(f32[4,128,128]{2,1,0:T(8,128)S(1)} %shard_map.78.message), channel_id=1, source_target_pairs={{1,2},{2,1},{3,0},{0,3},{5,6},{6,5},{7,4},{4,7},{9,10},{10,9},{11,... | collective-permute-start | bytes 786440 | tf_op jit(solution)/shard_map/ppermute | solution.py:30
  5.5 15.0 %collective-permute-start.3 = (f32[4,128,128]{2,1,0:T(8,128)S(1)}, f32[4,128,128]{2,1,0:T(8,128)S(1)}, u32[]{:S(2)}, u32[]{:S(2)}) collective-permute-start(f32[4,128,128]{2,1,0:T(8,128)S(1)} %shard_map.79.message), channel_id=1, source_target_pairs={{4,8},{8,4},{12,16},{16,12},{20,24},{24,20},{28,0},{0,28},{5,9},{9... | collective-permute-start | bytes 786440 | tf_op jit(solution)/shard_map/ppermute | solution.py:30
  10.1 2.3 %collective-permute-start = (f32[8,128,128]{2,1,0:T(8,128)S(1)}, f32[8,128,128]{2,1,0:T(8,128)S(1)}, u32[]{:S(2)}, u32[]{:S(2)}) collective-permute-start(f32[8,128,128]{2,1,0:T(8,128)S(1)} %shard_map.80.after), channel_id=1, source_target_pairs={{0,1},{1,0},{2,3},{3,2},{4,5},{5,4},{6,7},{7,6},{8,9},{9,8},{10,11... | collective-permute-start | bytes 1572872 | tf_op jit(solution)/shard_map/ppermute | solution.py:30
  13.7 9.7 %collective-permute-start.4 = (f32[4,128,128]{2,1,0:T(8,128)S(1)}, f32[4,128,128]{2,1,0:T(8,128)S(1)}, u32[]{:S(2)}, u32[]{:S(2)}) collective-permute-start(f32[4,128,128]{2,1,0:T(8,128)S(1)} %get-tuple-element.73), channel_id=1, source_target_pairs={{1,2},{2,1},{3,0},{0,3},{5,6},{6,5},{7,4},{4,7},{9,10},{10,9},{11,... | collective-permute-start | bytes 786440 | tf_op jit(solution)/shard_map/ppermute | solution.py:30
  14.3 14.5 %collective-permute-start.5 = (f32[4,128,128]{2,1,0:T(8,128)S(1)}, f32[4,128,128]{2,1,0:T(8,128)S(1)}, u32[]{:S(2)}, u32[]{:S(2)}) collective-permute-start(f32[4,128,128]{2,1,0:T(8,128)S(1)} %get-tuple-element.77), channel_id=1, source_target_pairs={{0,4},{4,0},{8,12},{12,8},{16,20},{20,16},{24,28},{28,24},{1,5},{5... | collective-permute-start | bytes 786440 | tf_op jit(solution)/shard_map/ppermute | solution.py:30
  14.7 14.1 %collective-permute-start.6 = (f32[4,128,128]{2,1,0:T(8,128)S(1)}, f32[4,128,128]{2,1,0:T(8,128)S(1)}, u32[]{:S(2)}, u32[]{:S(2)}) collective-permute-start(f32[4,128,128]{2,1,0:T(8,128)S(1)} %get-tuple-element.78), channel_id=1, source_target_pairs={{4,8},{8,4},{12,16},{16,12},{20,24},{24,20},{28,0},{0,28},{5,9},{9... | collective-permute-start | bytes 786440 | tf_op jit(solution)/shard_map/ppermute | solution.py:30
  21.5 2.0 %collective-permute-start.7 = (f32[3,128]{1,0:T(4,128)S(1)}, f32[3,128]{1,0:T(4,128)S(1)}, u32[]{:S(2)}, u32[]{:S(2)}) collective-permute-start(f32[3,128]{1,0:T(4,128)S(1)} %get-tuple-element.79), channel_id=1, source_target_pairs={{0,1},{1,0},{2,3},{3,2},{4,5},{5,4},{6,7},{7,6},{8,9},{9,8},{10,11... | collective-permute-start | bytes 4616 | tf_op jit(solution)/shard_map/ppermute | solution.py:30
  21.6 6.3 %collective-permute-start.9 = (f32[3,128]{1,0:T(4,128)S(1)}, f32[3,128]{1,0:T(4,128)S(1)}, u32[]{:S(2)}, u32[]{:S(2)}) collective-permute-start(f32[3,128]{1,0:T(4,128)S(1)} %get-tuple-element.83), channel_id=1, source_target_pairs={{4,8},{8,4},{12,16},{16,12},{20,24},{24,20},{28,0},{0,28},{5,9},{9... | collective-permute-start | bytes 4616 | tf_op jit(solution)/shard_map/ppermute | solution.py:30
  23.4 5.4 %collective-permute-start.8 = (f32[3,128]{1,0:T(4,128)S(1)}, f32[3,128]{1,0:T(4,128)S(1)}, u32[]{:S(2)}, u32[]{:S(2)}) collective-permute-start(f32[3,128]{1,0:T(4,128)S(1)} %get-tuple-element.82), channel_id=1, source_target_pairs={{0,4},{4,0},{8,12},{12,8},{16,20},{20,16},{24,28},{28,24},{1,5},{5... | collective-permute-start | bytes 4616 | tf_op jit(solution)/shard_map/ppermute | solution.py:30
  23.4 5.3 %collective-permute-start.10 = (f32[3,128]{1,0:T(4,128)S(1)}, f32[3,128]{1,0:T(4,128)S(1)}, u32[]{:S(2)}, u32[]{:S(2)}) collective-permute-start(f32[3,128]{1,0:T(4,128)S(1)} %get-tuple-element.84), channel_id=1, source_target_pairs={{1,2},{2,1},{3,0},{0,3},{5,6},{6,5},{7,4},{4,7},{9,10},{10,9},{11,... | collective-permute-start | bytes 4616 | tf_op jit(solution)/shard_map/ppermute | solution.py:30

commit v26 on v25

--- a/solution.py
+++ b/solution.py
@@ -266,10 +266,11 @@
     prop, inner = rows_of(beside((high_one[...], low_one[...]), (high_two[...], low_two[...])))
     near = [tuple(jnp.concatenate(x, axis=0) for x in zip(split(one[1 + kind]), split(two[1 + kind]))) for kind in range(3)]
     behind = dot(inner, near[0])
-    real_new = held[1, 0] + time_step * (imag_part[...] + dot(prop, near[2]) - behind[B:])
+    ahead = dot(prop, beside(near[2], near[1]))
+    real_new = held[1, 0] + time_step * (imag_part[...] + ahead[:, :B] - behind[B:])
     new[0] = real_new
     copies = start_all([pltpu.make_async_copy(new.at[0], out_hbm.at[0, 0, 0, 0], sems.at[0])])
-    new[1] = held[2, 0] - time_step * (comm[0] + dot(prop, near[1]) - behind[:B])
+    new[1] = held[2, 0] - time_step * (comm[0] + ahead[:, B:] - behind[:B])
     for place, message, mixed in ((1, one, (high_one, low_one)), (2, two, (high_two, low_two))):
         added = dot(rows_of((mixed[0][...], mixed[1][...]))[0], split(message[0]))
         new[1 + place] = held[2, place] - time_step * (comm[place] + added)

time: 30.3 us -> 30.3 us (level)
  no operation moved by 1% of the time
where the time goes in v26:
time: 30.3 us; the launch traced here: 30 us
  starting transfers between devices  17.7 us (58%)
  Pallas kernels  9.36 us (31%)
  waiting for transfers between devices  2.18 us (7%)
  between operations  0.75 us (2%)
    ppermute x11, starting transfers between devices, swapped(): return lax.ppermute(cells, axis, pairs)  17.7 us
    pallas_call x13, Pallas kernels, call(): pl.pallas_call(kernel, out_shape=shapes, in_specs=in_specs, out_specs=out...  9.36 us
    ppermute x11, waiting for transfers between devices, swapped(): return lax.ppermute(cells, axis, pairs)  2.18 us
  transfers between devices with their start and end apart: 11, of which 3 were waited for; matrix products, arithmetic and copies ran while one was open for 0% of the time, Pallas kernels for 24%

profile of v26, /device:TPU:0, one launch (start us, length us, event | category | flops | bytes accessed | tf_op | source)
XLA Modules:
  0.0 30.0 jit_solution(18300456202154584869)
XLA Ops:
  0.6 1.0 %shard_map.77 = (f32[4,128,128]{2,1,0:T(8,128)S(1)}, f32[2,128,128]{2,1,0:T(8,128)S(1)}) custom-call(s32[1,1,5]{2,1,0:T(1,128)} %cutoff_hbm.5, f32[1,1,5,128,128]{4,3,2,1,0:T(8,128)} %ham_hbm.5, f32[1,1,5,128,128]{4,3,2,1,0:T(8,128)} %inv_hbm.5, f32[2,1,1,5,128,128]{5,4,3,2,1,0:T(8,128)} %rho_hbm.5), custom_call_target="tpu_custom_call" | custom-call | bytes 1703956 | tf_op jit(solution)/shard_map/pallas_call | solution.py:298
  1.7 3.0 %collective-permute-start.2 = (f32[4,128,128]{2,1,0:T(8,128)S(1)}, f32[4,128,128]{2,1,0:T(8,128)S(1)}, u32[]{:S(2)}, u32[]{:S(2)}) collective-permute-start(f32[4,128,128]{2,1,0:T(8,128)S(1)} %get-tuple-element.45.message), channel_id=1, source_target_pairs={{0,4},{4,0},{8,12},{12,8},{16,20},{20,16},{24,28},{28,24},{1,5},{5... | collective-permute-start | bytes 786440 | tf_op jit(solution)/shard_map/ppermute | solution.py:30
  4.7 0.7 %collective-permute-start.1 = (f32[4,128,128]{2,1,0:T(8,128)S(1)}, f32[4,128,128]{2,1,0:T(8,128)S(1)}, u32[]{:S(2)}, u32[]{:S(2)}) collective-permute-start(f32[4,128,128]{2,1,0:T(8,128)S(1)} %shard_map.78.message), channel_id=1, source_target_pairs={{1,2},{2,1},{3,0},{0,3},{5,6},{6,5},{7,4},{4,7},{9,10},{10,9},{11,... | collective-permute-start | bytes 786440 | tf_op jit(solution)/shard_map/ppermute | solution.py:30
  5.5 3.6 %collective-permute-start.3 = (f32[4,128,128]{2,1,0:T(8,128)S(1)}, f32[4,128,128]{2,1,0:T(8,128)S(1)}, u32[]{:S(2)}, u32[]{:S(2)}) collective-permute-start(f32[4,128,128]{2,1,0:T(8,128)S(1)} %shard_map.79.message), channel_id=1, source_target_pairs={{4,8},{8,4},{12,16},{16,12},{20,24},{24,20},{28,0},{0,28},{5,9},{9... | collective-permute-start | bytes 786440 | tf_op jit(solution)/shard_map/ppermute | solution.py:30
  9.1 1.0 %shard_map.80.after = f32[8,128,128]{2,1,0:T(8,128)S(1)} custom-call(s32[1,1,5]{2,1,0:T(1,128)} %cutoff_hbm.5, f32[1,1,5,128,128]{4,3,2,1,0:T(8,128)} %ham_hbm.5, f32[1,1,5,128,128]{4,3,2,1,0:T(8,128)} %inv_hbm.5, f32[2,1,1,5,128,128]{5,4,3,2,1,0:T(8,128)} %rho_hbm.5, f32[4,128,128]{2,1,0:T(8,128)S(1)} %shard_map.79.message), custom_call_target="tpu_custom_call" | custom-call | flops 6291456000 | bytes 2097172 | tf_op jit(solution)/shard_map/pallas_call | solution.py:298
  10.1 0.7 %collective-permute-start = (f32[8,128,128]{2,1,0:T(8,128)S(1)}, f32[8,128,128]{2,1,0:T(8,128)S(1)}, u32[]{:S(2)}, u32[]{:S(2)}) collective-permute-start(f32[8,128,128]{2,1,0:T(8,128)S(1)} %shard_map.80.after), channel_id=1, source_target_pairs={{0,1},{1,0},{2,3},{3,2},{4,5},{5,4},{6,7},{7,6},{8,9},{9,8},{10,11... | collective-permute-start | bytes 1572872 | tf_op jit(solution)/shard_map/ppermute | solution.py:30
  10.9 1.4 %shard_map.81 = (f32[3,5,128,128]{3,2,1,0:T(8,128)S(1)}, bf16[384,640]{1,0:T(8,128)(2,1)S(1)}, bf16[384,640]{1,0:T(8,128)(2,1)S(1)}, bf16[128,640]{1,0:T(8,128)(...) custom-call(s32[1,1,5]{2,1,0:T(1,128)} %cutoff_hbm.5, f32[1,1,5,128,128]{4,3,2,1,0:T(8,128)} %ham_hbm.5, ...), custom_call_target="tpu_custom_call" | custom-call | flops 25165824000 | bytes 5472788 | tf_op jit(solution)/shard_map/pallas_call | solution.py:298
  12.3 0.1 collective-permute-done.three
  12.4 1.2 %shard_map.82 = (f32[384,640]{1,0:T(8,128)S(1)}, f32[384,128]{1,0:T(8,128)S(1)}, f32[2,2,128,128]{3,2,1,0:T(8,128)S(1)}, f32[3,1,1,5,128,128]{5,4,3,2,1,0:T(8,128)S(1)}) custom-call(bf16[384,640]{1,0:T(8,128)(2,1)S(1)} %get-tuple-element.48.left_high, bf16[384,640]{1,0:T(8,128)(2,1)S(1)} %get-tuple-element.49.left_low, ...), custom_call_target="tpu_custom_call" | custom-call | flops 100663296000 | bytes 7536640 | tf_op jit(solution)/shard_map/pallas_call | solution.py:298
  13.6 0.0 collective-permute-done.1.four.arrived
  13.6 0.1 shard_map.86
  13.7 0.6 %collective-permute-start.4 = (f32[4,128,128]{2,1,0:T(8,128)S(1)}, f32[4,128,128]{2,1,0:T(8,128)S(1)}, u32[]{:S(2)}, u32[]{:S(2)}) collective-permute-start(f32[4,128,128]{2,1,0:T(8,128)S(1)} %get-tuple-element.73), channel_id=1, source_target_pairs={{1,2},{2,1},{3,0},{0,3},{5,6},{6,5},{7,4},{4,7},{9,10},{10,9},{11,... | collective-permute-start | bytes 786440 | tf_op jit(solution)/shard_map/ppermute | solution.py:30
  14.3 0.4 %collective-permute-start.5 = (f32[4,128,128]{2,1,0:T(8,128)S(1)}, f32[4,128,128]{2,1,0:T(8,128)S(1)}, u32[]{:S(2)}, u32[]{:S(2)}) collective-permute-start(f32[4,128,128]{2,1,0:T(8,128)S(1)} %get-tuple-element.77), channel_id=1, source_target_pairs={{0,4},{4,0},{8,12},{12,8},{16,20},{20,16},{24,28},{28,24},{1,5},{5... | collective-permute-start | bytes 786440 | tf_op jit(solution)/shard_map/ppermute | solution.py:30
  14.7 4.6 %collective-permute-start.6 = (f32[4,128,128]{2,1,0:T(8,128)S(1)}, f32[4,128,128]{2,1,0:T(8,128)S(1)}, u32[]{:S(2)}, u32[]{:S(2)}) collective-permute-start(f32[4,128,128]{2,1,0:T(8,128)S(1)} %get-tuple-element.78), channel_id=1, source_target_pairs={{4,8},{8,4},{12,16},{16,12},{20,24},{24,20},{28,0},{0,28},{5,9},{9... | collective-permute-start | bytes 786440 | tf_op jit(solution)/shard_map/ppermute | solution.py:30
  19.3 0.6 %shard_map.83 = (bf16[384,128]{1,0:T(8,128)(2,1)S(1)}, bf16[384,128]{1,0:T(8,128)(2,1)S(1)}, f32[384,128]{1,0:T(8,128)S(1)}, f32[2,128,128]{2,1,0:T(8,128)S(1)}) custom-call(bf16[384,640]{1,0:T(8,128)(2,1)S(1)} %get-tuple-element.48.left_high, bf16[384,640]{1,0:T(8,128)(2,1)S(1)} %get-tuple-element.49.left_low, f32[384,640]{1,0:T(8,128)S(1)} %get-tuple-element.54.start, ...), custom_call_target="tpu_custom_call" | custom-call | flops 100663296 | bytes 4128768 | tf_op jit(solution)/shard_map/pallas_call | solution.py:298
  19.9 0.0 collective-permute-done.2.one
  19.9 0.6 %shard_map.84 = (bf16[384,128]{1,0:T(8,128)(2,1)S(1)}, bf16[384,128]{1,0:T(8,128)(2,1)S(1)}, f32[384,128]{1,0:T(8,128)S(1)}, f32[2,128,128]{2,1,0:T(8,128)S(1)}) custom-call(bf16[384,640]{1,0:T(8,128)(2,1)S(1)} %get-tuple-element.48.left_high, bf16[384,640]{1,0:T(8,128)(2,1)S(1)} %get-tuple-element.49.left_low, f32[384,640]{1,0:T(8,128)S(1)} %get-tuple-element.54.start, ...), custom_call_target="tpu_custom_call" | custom-call | flops 125829120 | bytes 4128768 | tf_op jit(solution)/shard_map/pallas_call | solution.py:298
  20.5 0.0 collective-permute-done.3.two
  20.5 0.9 %shard_map.85 = (f32[4,128,128]{2,1,0:T(8,128)S(1)}, bf16[384,128]{1,0:T(8,128)(2,1)S(1)}, bf16[384,128]{1,0:T(8,128)(2,1)S(1)}, bf16[384,128]{1,0:T(8,128)(2,1)...) custom-call(bf16[384,640]{1,0:T(8,128)(2,1)S(1)} %get-tuple-element., ...), custom_call_target="tpu_custom_call" | custom-call | flops 276824064 | bytes 7280640 | tf_op jit(solution)/shard_map/pallas_call | solution.py:298
  21.5 0.1 collective-permute-start.7
  21.6 1.8 %collective-permute-start.9 = (f32[3,128]{1,0:T(4,128)S(1)}, f32[3,128]{1,0:T(4,128)S(1)}, u32[]{:S(2)}, u32[]{:S(2)}) collective-permute-start(f32[3,128]{1,0:T(4,128)S(1)} %get-tuple-element.83), channel_id=1, source_target_pairs={{4,8},{8,4},{12,16},{16,12},{20,24},{24,20},{28,0},{0,28},{5,9},{9... | collective-permute-start | bytes 4616 | tf_op jit(solution)/shard_map/ppermute | solution.py:30
  23.4 0.0 collective-permute-done.7.arrived.c3
  23.4 0.0 collective-permute-start.8
  23.4 0.0 collective-permute-done.4.four
  23.4 2.1 %collective-permute-start.10 = (f32[3,128]{1,0:T(4,128)S(1)}, f32[3,128]{1,0:T(4,128)S(1)}, u32[]{:S(2)}, u32[]{:S(2)}) collective-permute-start(f32[3,128]{1,0:T(4,128)S(1)} %get-tuple-element.84), channel_id=1, source_target_pairs={{1,2},{2,1},{3,0},{0,3},{5,6},{6,5},{7,4},{4,7},{9,10},{10,9},{11,... | collective-permute-start | bytes 4616 | tf_op jit(solution)/shard_map/ppermute | solution.py:30
  25.5 1.2 %shard_map.87 = (f32[2,1,1,5,128,128]{5,4,3,2,1,0:T(8,128)}, f32[3,128,128]{2,1,0:T(8,128)S(1)}, f32[128,128]{1,0:T(8,128)S(1)}, f32[3,128]{1,0:T(4,128)S(1)}) custom-call(f32[3,5,128,128]{3,2,1,0:T(8,128)S(1)} %get-tuple-element.47.held, f32[4,128,128]{2,1,0:T(8,128)S(1)} %get-tuple-element.65.new, bf16[384,640]{1,0:T(8,128)(2,1)S(1)} %get-tuple-element.48.left_high, ...), custom_call_target="tpu_custom_call" | custom-call | flops 125829120 | bytes 6030848 | tf_op jit(solution)/shard_map/pallas_call | solution.py:298
  26.7 1.1 %collective-permute-done.9.c2 = f32[3,128]{1,0:T(4,128)S(1)} collective-permute-done((f32[3,128]{1,0:T(4,128)S(1)}, f32[3,128]{1,0:T(4,128)S(1)}, u32[]{:S(2)}, u32[]{:S(2)}) %collective-permute-start.9) | collective-permute-done | bytes 1568 | tf_op jit(solution)/shard_map/ppermute | solution.py:30
  27.9 0.9 %collective-permute-done.8.c1 = f32[3,128]{1,0:T(4,128)S(1)} collective-permute-done((f32[3,128]{1,0:T(4,128)S(1)}, f32[3,128]{1,0:T(4,128)S(1)}, u32[]{:S(2)}, u32[]{:S(2)}) %collective-permute-start.8) | collective-permute-done | bytes 1568 | tf_op jit(solution)/shard_map/ppermute | solution.py:30
  28.8 0.0 collective-permute-done.10.c4
  28.8 0.0 collective-permute-done.5.one
  28.8 0.0 collective-permute-done.6.two
  28.8 1.2 %shard_map.89 = (f32[2,1,1,5,128,128]{5,4,3,2,1,0:T(8,128)}, f32[3,1,64]{2,1,0:T(1,128)}) custom-call(f32[3,5,128,128]{3,2,1,0:T(8,128)S(1)} %get-tuple-element.47.held, f32[3,1,1,5,128,128]{5,4,3,2,1,0:T(8,128)S(1)} %get-tuple-element.52.der_ref, bf16[64,128]{1,0:T(8,128)(2,1)S(1)} %get-tuple-element.53.members, ...), custom_call_target="tpu_custom_call", output_to_operand_aliasing={{0}: (16, {})} | custom-call | flops 125829120 | bytes 4890880 | tf_op jit(solution)/shard_map/pallas_call | solution.py:298
  (3 shorter events, 0.0 us)
Async XLA Ops:
  1.7 18.2 %collective-permute-start.2 = (f32[4,128,128]{2,1,0:T(8,128)S(1)}, f32[4,128,128]{2,1,0:T(8,128)S(1)}, u32[]{:S(2)}, u32[]{:S(2)}) collective-permute-start(f32[4,128,128]{2,1,0:T(8,128)S(1)} %get-tuple-element.45.message), channel_id=1, source_target_pairs={{0,4},{4,0},{8,12},{12,8},{16,20},{20,16},{24,28},{28,24},{1,5},{5... | collective-permute-start | bytes 786440 | tf_op jit(solution)/shard_map/ppermute | solution.py:30
  4.7 8.9 %collective-permute-start.1 = (f32[4,128,128]{2,1,0:T(8,128)S(1)}, f32[4,128,128]{2,1,0:T(8,128)S(1)}, u32[]{:S(2)}, u32[]{:S(2)}) collective-permute-start(f32[4,128,128]{2,1,0:T(8,128)S(1)} %shard_map.78.message), channel_id=1, source_target_pairs={{1,2},{2,1},{3,0},{0,3},{5,6},{6,5},{7,4},{4,7},{9,10},{10,9},{11,... | collective-permute-start | bytes 786440 | tf_op jit(solution)/shard_map/ppermute | solution.py:30
  5.5 15.0 %collective-permute-start.3 = (f32[4,128,128]{2,1,0:T(8,128)S(1)}, f32[4,128,128]{2,1,0:T(8,128)S(1)}, u32[]{:S(2)}, u32[]{:S(2)}) collective-permute-start(f32[4,128,128]{2,1,0:T(8,128)S(1)} %shard_map.79.message), channel_id=1, source_target_pairs={{4,8},{8,4},{12,16},{16,12},{20,24},{24,20},{28,0},{0,28},{5,9},{9... | collective-permute-start | bytes 786440 | tf_op jit(solution)/shard_map/ppermute | solution.py:30
  10.1 2.3 %collective-permute-start = (f32[8,128,128]{2,1,0:T(8,128)S(1)}, f32[8,128,128]{2,1,0:T(8,128)S(1)}, u32[]{:S(2)}, u32[]{:S(2)}) collective-permute-start(f32[8,128,128]{2,1,0:T(8,128)S(1)} %shard_map.80.after), channel_id=1, source_target_pairs={{0,1},{1,0},{2,3},{3,2},{4,5},{5,4},{6,7},{7,6},{8,9},{9,8},{10,11... | collective-permute-start | bytes 1572872 | tf_op jit(solution)/shard_map/ppermute | solution.py:30
  13.7 9.7 %collective-permute-start.4 = (f32[4,128,128]{2,1,0:T(8,128)S(1)}, f32[4,128,128]{2,1,0:T(8,128)S(1)}, u32[]{:S(2)}, u32[]{:S(2)}) collective-permute-start(f32[4,128,128]{2,1,0:T(8,128)S(1)} %get-tuple-element.73), channel_id=1, source_target_pairs={{1,2},{2,1},{3,0},{0,3},{5,6},{6,5},{7,4},{4,7},{9,10},{10,9},{11,... | collective-permute-start | bytes 786440 | tf_op jit(solution)/shard_map/ppermute | solution.py:30
  14.3 14.5 %collective-permute-start.5 = (f32[4,128,128]{2,1,0:T(8,128)S(1)}, f32[4,128,128]{2,1,0:T(8,128)S(1)}, u32[]{:S(2)}, u32[]{:S(2)}) collective-permute-start(f32[4,128,128]{2,1,0:T(8,128)S(1)} %get-tuple-element.77), channel_id=1, source_target_pairs={{0,4},{4,0},{8,12},{12,8},{16,20},{20,16},{24,28},{28,24},{1,5},{5... | collective-permute-start | bytes 786440 | tf_op jit(solution)/shard_map/ppermute | solution.py:30
  14.7 14.1 %collective-permute-start.6 = (f32[4,128,128]{2,1,0:T(8,128)S(1)}, f32[4,128,128]{2,1,0:T(8,128)S(1)}, u32[]{:S(2)}, u32[]{:S(2)}) collective-permute-start(f32[4,128,128]{2,1,0:T(8,128)S(1)} %get-tuple-element.78), channel_id=1, source_target_pairs={{4,8},{8,4},{12,16},{16,12},{20,24},{24,20},{28,0},{0,28},{5,9},{9... | collective-permute-start | bytes 786440 | tf_op jit(solution)/shard_map/ppermute | solution.py:30
  21.5 2.0 %collective-permute-start.7 = (f32[3,128]{1,0:T(4,128)S(1)}, f32[3,128]{1,0:T(4,128)S(1)}, u32[]{:S(2)}, u32[]{:S(2)}) collective-permute-start(f32[3,128]{1,0:T(4,128)S(1)} %get-tuple-element.79), channel_id=1, source_target_pairs={{0,1},{1,0},{2,3},{3,2},{4,5},{5,4},{6,7},{7,6},{8,9},{9,8},{10,11... | collective-permute-start | bytes 4616 | tf_op jit(solution)/shard_map/ppermute | solution.py:30
  21.6 6.3 %collective-permute-start.9 = (f32[3,128]{1,0:T(4,128)S(1)}, f32[3,128]{1,0:T(4,128)S(1)}, u32[]{:S(2)}, u32[]{:S(2)}) collective-permute-start(f32[3,128]{1,0:T(4,128)S(1)} %get-tuple-element.83), channel_id=1, source_target_pairs={{4,8},{8,4},{12,16},{16,12},{20,24},{24,20},{28,0},{0,28},{5,9},{9... | collective-permute-start | bytes 4616 | tf_op jit(solution)/shard_map/ppermute | solution.py:30
  23.4 5.4 %collective-permute-start.8 = (f32[3,128]{1,0:T(4,128)S(1)}, f32[3,128]{1,0:T(4,128)S(1)}, u32[]{:S(2)}, u32[]{:S(2)}) collective-permute-start(f32[3,128]{1,0:T(4,128)S(1)} %get-tuple-element.82), channel_id=1, source_target_pairs={{0,4},{4,0},{8,12},{12,8},{16,20},{20,16},{24,28},{28,24},{1,5},{5... | collective-permute-start | bytes 4616 | tf_op jit(solution)/shard_map/ppermute | solution.py:30
  23.4 5.3 %collective-permute-start.10 = (f32[3,128]{1,0:T(4,128)S(1)}, f32[3,128]{1,0:T(4,128)S(1)}, u32[]{:S(2)}, u32[]{:S(2)}) collective-permute-start(f32[3,128]{1,0:T(4,128)S(1)} %get-tuple-element.84), channel_id=1, source_target_pairs={{1,2},{2,1},{3,0},{0,3},{5,6},{6,5},{7,4},{4,7},{9,10},{10,9},{11,... | collective-permute-start | bytes 4616 | tf_op jit(solution)/shard_map/ppermute | solution.py:30
